TPU v7x, 128 devices: a whole 4x4x4 slice. The times are simulated.
128 devices in a mesh: img: 64 (over z, y, x), head: 2 (over core).
Axes of the slice: x: 4, y: 4, z: 4, core: 2. Of those that a mesh axis runs over, the one named last changes fastest.
Arguments:
- tokens: bfloat16 [128, 256, 3200], P('img', 'head'), may hold values from -180 to 180
- tap_early: bfloat16 [128, 256, 3200], P('img', 'head'), may hold values from -6 to 6
- tap_mid: bfloat16 [128, 256, 3200], P('img', 'head'), may hold values from -6 to 6
- tile_counts: int32 [51], replicated, may hold values from 1 to 5, 128 in all
- qkv_weight: bfloat16 [3200, 6144], P('img', 'head'), may hold values from -1 to 1
- out_weight: bfloat16 [2048, 3200], P('head'), may hold values from -0.125 to 0.125
- layer_scale: float32 [3200], replicated, may hold values from 0.5 to 4
- layer_logits: float32 [4], replicated, may hold values from -1 to 1
- proj_weight: bfloat16 [3200, 4096], P(None, 'head'), may hold values from -0.109375 to 0.109375
- proj_bias: float32 [4096], P('head'), may hold values from -5 to 5
- grad_out: bfloat16 [384, 256, 4096], P('img', None, 'head'), may hold values from -6 to 6
Outputs:
- owner_rows: bfloat16 [384, 256, 4096], P('img', None, 'head')
- grad_joined: bfloat16 [128, 256, 3200], P('img', 'head')
Inputs may be any that keep to these rules, and one draw needn't show every extreme that they name: `tile_counts`: tiles of the samples in order make up the 128 tiles, 2 to each index of img.
All inputs are finite; a program needn't handle non-finite values.
Results may differ from a plain program's by a relative error of at most 0.017.
Values may be sent and summed in bfloat16 or wider, within the bound.
No kernel may reach another device: no remote copies, remote signals or barrier semaphores. Data moves between devices by JAX's collectives and lax.ppermute only.
A program may use at most 192 MiB of HBM per device.

v0:
```python
import math

import jax
import jax.numpy as jnp
from jax import lax
from jax.sharding import PartitionSpec as P

HEAD_DIM = 128
REACH = 2


inv_root_two = 0.7071067811865476
inv_root_tau = 0.3989422804014327


def from_behind(array, axis, by):
    peers = lax.axis_size(axis)
    pairs = [(i, i + by) for i in range(peers) if 0 <= i + by < peers]
    return lax.ppermute(array, axis, pairs)


def tile_owners(tile_counts, tile_total, tile_group):
    starts = jnp.cumsum(tile_counts) - tile_counts
    tile_index = jnp.arange(tile_total, dtype=jnp.int32)
    start_of = jnp.max(
        jnp.where(starts[None, :] <= tile_index[:, None], starts[None, :], -1), axis=1
    )
    owner_of = start_of // tile_group
    owners_total = tile_total // tile_group
    edge_tiles = jnp.arange(owners_total + 1, dtype=jnp.int32) * tile_group
    first_tile = jnp.min(
        jnp.where(starts[None, :] >= edge_tiles[:, None], starts[None, :], tile_total), axis=1
    )
    return (owner_of, first_tile)


def gelu_slope(values):
    cumulative = 0.5 * (1.0 + jax.scipy.special.erf(values * inv_root_two))
    return cumulative + values * jnp.exp(-0.5 * values * values) * inv_root_tau


def rms_rows(values):
    return values * lax.rsqrt(jnp.mean(values * values, axis=-1, keepdims=True) + 1e-06)


def group_rows(rows_local, row_fn):
    return row_fn(lax.all_gather(rows_local, "head", axis=1, tiled=True), jnp.int32(0))


def group_sums(term_fn, token_share):
    return lax.psum_scatter(
        term_fn(jnp.int32(0), token_share * lax.axis_size("head")).astype(jnp.bfloat16),
        "head",
        scatter_dimension=0,
        tiled=True,
    ).astype(jnp.float32)


def move_tiles(payload, offset):
    return from_behind(payload, "img", offset)


def return_rows(grad_out, owner_of, first_tile, place_index, tile_group, img_count):
    own_tiles = grad_out.shape[0]
    tile_total = tile_group * img_count
    within = jnp.arange(tile_group, dtype=jnp.int32)
    gathered_rows = None
    for distance in range(REACH + 1):
        wanted = (place_index + distance) * tile_group + within
        inside = wanted < tile_total
        clipped = jnp.clip(wanted, 0, tile_total - 1)
        owned_here = jnp.logical_and(inside, owner_of[clipped] == place_index)
        slot_index = jnp.clip(clipped - first_tile[place_index], 0, own_tiles - 1)
        packet = jnp.where(
            owned_here[:, None, None],
            jnp.take(grad_out, slot_index, axis=0),
            jnp.zeros((), grad_out.dtype),
        )
        if distance > 0:
            packet = move_tiles(packet, distance)
        gathered_rows = packet if gathered_rows is None else gathered_rows + packet
    return gathered_rows


def on_device(
    tokens,
    tap_early,
    tap_mid,
    tile_counts,
    qkv_weight,
    out_weight,
    layer_scale,
    layer_logits,
    proj_weight,
    proj_bias,
    grad_out,
):
    tile_group = tokens.shape[0]
    token_share = tokens.shape[1]
    img_count = lax.axis_size("img")
    place_index = lax.axis_index("img")
    owner_of, first_tile = tile_owners(tile_counts, tile_group * img_count, tile_group)
    local_heads = qkv_weight.shape[1] // (3 * HEAD_DIM)
    source_rows = rms_rows(tokens.astype(jnp.float32)).astype(jnp.bfloat16)
    weight_full = lax.all_gather(qkv_weight, "img", axis=0, tiled=True)

    def project_qkv(row_block, row_start):
        return jnp.einsum(
            "tpd,de->pte", row_block, weight_full, preferred_element_type=jnp.float32
        ).astype(jnp.bfloat16)

    qkv_rows = group_rows(source_rows, project_qkv)
    tile_len = qkv_rows.shape[0]
    split_heads = qkv_rows.reshape(tile_len, tile_group, local_heads, 3, HEAD_DIM)
    queries = split_heads[:, :, :, 0]
    keys_all = split_heads[:, :, :, 1]
    values_all = split_heads[:, :, :, 2]
    scores = jnp.einsum(
        "ptnd,qtnd->tnpq", queries, keys_all, preferred_element_type=jnp.float32
    ) / math.sqrt(HEAD_DIM)
    scores = scores - jnp.max(scores, axis=-1, keepdims=True)
    raised = jnp.exp(scores)
    soft_weights = (raised / jnp.sum(raised, axis=-1, keepdims=True)).astype(jnp.bfloat16)
    attended = jnp.einsum(
        "tnpq,qtnd->ptnd", soft_weights, values_all, preferred_element_type=jnp.float32
    ).astype(jnp.bfloat16)
    attended = attended.reshape(tile_len, tile_group, local_heads * HEAD_DIM)

    def out_terms(row_start, row_count):
        return jnp.einsum("ptc,ce->pte", attended, out_weight, preferred_element_type=jnp.float32)

    attended_out = jnp.transpose(group_sums(out_terms, token_share), (1, 0, 2))
    inputs = tokens.astype(jnp.float32)
    layer_out = inputs + layer_scale * attended_out
    raised_logits = jnp.exp(layer_logits)
    mixing = raised_logits / jnp.sum(raised_logits)
    joined_rows = (
        mixing[0] * tap_early.astype(jnp.float32)
        + mixing[1] * tap_mid.astype(jnp.float32)
        + mixing[2] * inputs
        + mixing[3] * layer_out
    )
    centre = jnp.mean(joined_rows, axis=-1, keepdims=True)
    shifted = joined_rows - centre
    inverse_std = lax.rsqrt(jnp.mean(shifted * shifted, axis=-1, keepdims=True) + 1e-05)
    normal_rows = shifted * inverse_std
    z_rows = normal_rows.astype(jnp.bfloat16)

    def project_rows(row_block, row_start):
        return (
            jnp.einsum("tpd,df->ptf", row_block, proj_weight, preferred_element_type=jnp.float32)
            + proj_bias
        )

    preact = group_rows(z_rows, project_rows)
    projected = jnp.transpose(
        jax.nn.gelu(preact, approximate=False).astype(jnp.bfloat16), (1, 0, 2)
    )
    received = [projected]
    for distance in range(1, REACH + 1):
        received.append(move_tiles(projected, -distance))
    stacked = jnp.concatenate(received, axis=0)
    own_tiles = grad_out.shape[0]
    slot_tiles = first_tile[place_index] + jnp.arange(own_tiles, dtype=jnp.int32)
    live_slots = slot_tiles < first_tile[place_index + 1]
    source_index = jnp.clip(
        (slot_tiles // tile_group - place_index) * tile_group + slot_tiles % tile_group,
        0,
        stacked.shape[0] - 1,
    )
    owner_rows = jnp.where(
        live_slots[:, None, None],
        jnp.take(stacked, source_index, axis=0),
        jnp.zeros((), jnp.bfloat16),
    )
    back_rows = return_rows(grad_out, owner_of, first_tile, place_index, tile_group, img_count)
    back_tokens = jnp.transpose(back_rows, (1, 0, 2))
    slope_rows = (back_tokens.astype(jnp.float32) * gelu_slope(preact)).astype(jnp.bfloat16)

    def grad_terms(row_start, row_count):
        return jnp.einsum(
            "ptf,ef->pte", slope_rows, proj_weight, preferred_element_type=jnp.float32
        )

    grad_norm = jnp.transpose(group_sums(grad_terms, token_share), (1, 0, 2))
    grad_joined = (
        grad_norm
        - jnp.mean(grad_norm, axis=-1, keepdims=True)
        - normal_rows * jnp.mean(grad_norm * normal_rows, axis=-1, keepdims=True)
    ) * inverse_std
    return (owner_rows, grad_joined.astype(jnp.bfloat16))


def solution(mesh):
    return jax.shard_map(
        on_device,
        mesh=mesh,
        in_specs=(
            P("img", "head", None),
            P("img", "head", None),
            P("img", "head", None),
            P(),
            P("img", "head"),
            P("head", None),
            P(),
            P(),
            P(None, "head"),
            P("head"),
            P("img", None, "head"),
        ),
        out_specs=(P("img", None, "head"), P("img", "head", None)),
        check_vma=False,
    )
```

profile of v0, /device:TPU:31, one launch (start us, length us, event | category | flops | bytes accessed | tf_op | source)
XLA Modules:
  0.0 460.6 jit_solution(7398375593218561577)
XLA Ops:
  12.9 120.7 %all-gather.9.cloned.1.call-done = bf16[64,50,3072]{2,1,0:T(8,128)(2,1)} async-done(((bf16[1,50,3072]{2,1,0:T(8,128)(2,1)}), bf16[64,50,3072]{2,1,0:T(8,128)(2,1)}) %all-gather.9.cloned.1.call-update) | async-done | bytes 19660816 | tf_op jit(solution)/shard_map/all_gather | solution.py:105
  133.6 21.5 %reshape.335 = bf16[3200,3072,1]{1,0,2:T(8,128)(2,1)} reshape(bf16[64,50,3072]{2,1,0:T(8,128)(2,1)} %all-gather.9.cloned.1.call-done) | data formatting | bytes 39321600
  155.1 16.7 %fusion.32 = bf16[256,2,3072]{2,0,1:T(8,128)(2,1)} fusion(bf16[2,256,3200]{2,1,0:T(8,128)(2,1)} %all-gather.5.cloned.1.call-done, bf16[3200,3072,1]{1,0,2:T(8,128)(2,1)} %reshape.335), kind=kOutput, calls=%fused_computation.55 | convolution fusion | flops 10067902464 | bytes 26083328 | tf_op jit(solution)/shard_map/tpd,de->pte/dot_general | solution.py:108
  175.8 3.2 fusion.83
  180.8 5.1 %fusion.7 = bf16[256,2,3200]{2,0,1:T(8,128)(2,1)} fusion(bf16[256,2,1024]{0,2,1:T(8,128)(2,1)S(1)} %bitcast.89, bf16[1024,3200]{1,0:T(8,128)(2,1)S(1)} %bitcast.88), kind=kOutput, calls=%fused_computation.18 | convolution fusion | flops 3357081600 | bytes 10878976 | tf_op jit(solution)/shard_map/ptc,ce->pte/dot_general | solution.py:130
  187.9 12.1 %reduce-scatter.3.cloned.1.call-done = bf16[128,2,3200]{2,0,1:T(8,128)(2,1)} async-done(((bf16[256,2,3200]{2,0,1:T(8,128)(2,1)}), bf16[128,2,3200]{2,0,1:T(8,128)(2,1)}) %reduce-scatter.3.cloned.1.call-update) | async-done | bytes 1638416 | tf_op jit(solution)/shard_map/reduce_scatter | solution.py:51
  200.0 7.0 %fusion.79 = (f32[2,128]{1,0:T(2,128)S(1)}, f32[2,128,3200]{2,1,0:T(8,128)S(1)}) fusion(bf16[128,2,3200]{2,0,1:T(8,128)(2,1)} %reduce-scatter.3.cloned.1.call-done, f32[3200]{0:T(1024)S(1)} %copy-done.1, f32[]{:T(128)} %bitcast.6, bf16[2,128,3200]{2,1,0:T(8,128)(2,1)} %param.13, f32[]{:T(128)} %bitcast.5, bf16[2,128,3200]{2,1,0:T(8,128)(2,1)} %param.15, ...), kind=kLoop, calls=%fused_computation.161 | loop fusion | flops 11468544 | bytes 9844240 | tf_op jit(solution)/shard_map/reduce_sum | solution.py:143
  211.7 4.8 %gather_fusion.6 = bf16[2,256,2048]{2,1,0:T(8,128)(2,1)} fusion(bf16[6,256,2048]{2,1,0:T(8,128)(2,1)} %param.23, s32[1024]{0:T(1024)S(1)} %pad_clamp_fusion), kind=kCustom, calls=%fused_computation.2.clone | custom fusion | bytes 4194312 | tf_op jit(solution)/shard_map/jit(_take)/gather | solution.py:76
  216.5 3.2 select_select_fusion.1
  219.7 4.0 collective-permute-start.3
  224.4 4.8 %gather_fusion.5 = bf16[2,256,2048]{2,1,0:T(8,128)(2,1)} fusion(bf16[6,256,2048]{2,1,0:T(8,128)(2,1)} %param.23, s32[1024]{0:T(1024)S(1)} %pad_clamp_fusion.2), kind=kCustom, calls=%fused_computation.1.clone | custom fusion | bytes 4194312 | tf_op jit(solution)/shard_map/jit(_take)/gather | solution.py:76
  229.2 3.3 select_select_fusion.2
  232.5 3.9 collective-permute-start.2
  237.7 4.8 %gather_fusion.4 = bf16[2,256,2048]{2,1,0:T(8,128)(2,1)} fusion(bf16[6,256,2048]{2,1,0:T(8,128)(2,1)} %param.23, s32[1024]{0:T(1024)S(1)} %pad_clamp_fusion.4), kind=kCustom, calls=%fused_computation.clone | custom fusion | bytes 4194312 | tf_op jit(solution)/shard_map/jit(_take)/gather | solution.py:76
  242.5 21.3 %fusion.15 = (bf16[2,256,2048]{2,1,0:T(8,128)(2,1)}, f32[2,256,2048]{2,1,0:T(8,128)}) fusion(f32[2048]{0:T(1024)S(1)} %copy-done.3, bf16[2,256,3200]{2,1,0:T(8,128)(2,1)} %all-gather.7.cloned.1.call-done, bf16[3200,2048]{1,0:T(8,128)(2,1)} %param.21), kind=kOutput, calls=%fused_computation.27 | convolution fusion | flops 6780092416 | bytes 22683648 | tf_op jit(solution)/shard_map/tpd,df->ptf/dot_general | solution.py:151
  263.8 6.7 %collective-permute-done.3 = bf16[2,256,2048]{2,1,0:T(8,128)(2,1)} collective-permute-done((bf16[2,256,2048]{2,1,0:T(8,128)(2,1)}, bf16[2,256,2048]{2,1,0:T(8,128)(2,1)}, u32[]{:S(2)}, u32[]{:S(2)}) %collective-permute-start.3) | collective-permute-done | bytes 2097184 | tf_op jit(solution)/shard_map/ppermute | solution.py:19
  270.4 43.8 %collective-permute-done.2 = bf16[2,256,2048]{2,1,0:T(8,128)(2,1)} collective-permute-done((bf16[2,256,2048]{2,1,0:T(8,128)(2,1)}, bf16[2,256,2048]{2,1,0:T(8,128)(2,1)}, u32[]{:S(2)}, u32[]{:S(2)}) %collective-permute-start.2) | collective-permute-done | bytes 2097184 | tf_op jit(solution)/shard_map/ppermute | solution.py:19
  314.2 18.2 %fusion.10 = bf16[256,2,3200]{2,0,1:T(8,128)(2,1)} fusion(bf16[3200,2048]{1,0:T(8,128)(2,1)} %param.21, f32[2,256,2048]{2,1,0:T(8,128)} %get-tuple-element.22, bf16[2,256,2048]{2,1,0:T(8,128)(2,1)} %collective-permute-done.3, bf16[2,256,2048]{2,1,0:T(8,128)(2,1)} %collective-permute-done.2, bf16[2,256,2048]{2,1,0:T(8,128)(2,1)} %gather_fusion.4, ...), kind=kOutput, calls=%fused_computation.19 | convolution fusion | flops 6732447744 | bytes 26877956 | tf_op jit(solution)/shard_map/ptf,ef->pte/dot_general | solution.py:181
  332.5 4.2 collective-permute-start.1
  341.9 43.4 %collective-permute-done.1 = bf16[2,256,2048]{2,1,0:T(8,128)(2,1)S(1)} collective-permute-done((bf16[2,256,2048]{2,1,0:T(8,128)(2,1)}, bf16[2,256,2048]{2,1,0:T(8,128)(2,1)S(1)}, u32[]{:S(2)}, u32[]{:S(2)}) %collective-permute-start.1) | collective-permute-done | bytes 2097184 | tf_op jit(solution)/shard_map/ppermute | solution.py:19
  385.3 46.3 %collective-permute-done = bf16[2,256,2048]{2,1,0:T(8,128)(2,1)S(1)} collective-permute-done((bf16[2,256,2048]{2,1,0:T(8,128)(2,1)}, bf16[2,256,2048]{2,1,0:T(8,128)(2,1)S(1)}, u32[]{:S(2)}, u32[]{:S(2)}) %collective-permute-start) | collective-permute-done | bytes 2097184 | tf_op jit(solution)/shard_map/ppermute | solution.py:19
  431.6 4.5 pad_maximum_fusion
  436.1 6.9 %gather_fusion = bf16[6,256,2048]{2,1,0:T(8,128)(2,1)} fusion(bf16[6,256,2048]{2,1,0:T(8,128)(2,1)} %pad_maximum_fusion, s32[1024]{0:T(1024)S(1)} %pad_clamp_fusion.6), kind=kCustom, calls=%fused_computation.3 | custom fusion | bytes 12582936 | tf_op jit(solution)/shard_map/jit(_take)/gather | solution.py:173
  443.0 6.2 %select_select_fusion = bf16[6,256,2048]{2,1,0:T(8,128)(2,1)} fusion(bf16[6,256,2048]{2,1,0:T(8,128)(2,1)} %gather_fusion, pred[6]{0:T(512)(128)(4,1)S(1)} %get-tuple-element.25, pred[6]{0:T(512)(128)(4,1)S(1)} %get-tuple-element.26), kind=kLoop, calls=%fused_computation.16 | loop fusion | flops 6291456 | bytes 12582924 | tf_op jit(solution)/shard_map/jit(_where)/select_n | solution.py:171
  (74 shorter events, 29.8 us)
Async XLA Ops:
  7.2 126.4 %all-gather.9.cloned.1.call-start = ((), (), s32[]{:S(2)}) async-start(), calls=%async_computation.6 | async-start | bytes 22364160 | tf_op jit(solution)/shard_map/all_gather | solution.py:105
  7.9 147.2 %all-gather.5.cloned.1.call-start = ((), (), s32[]{:S(2)}) async-start(), calls=%async_computation.2 | async-start | bytes 4915200 | tf_op jit(solution)/shard_map/all_gather | solution.py:47
  12.8 187.2 %reduce-scatter.3.cloned.1.call-start = ((), (), s32[]{:S(2)}) async-start(), calls=%async_computation.3 | async-start | bytes 4915200 | tf_op jit(solution)/shard_map/reduce_scatter | solution.py:51
  175.8 3.8 slice-start
  179.1 1.7 slice-start.1
  180.8 5.2 %copy-start.4 = (f32[4]{0:T(128)S(1)}, f32[4]{0:T(128)}, u32[]{:S(2)}) copy-start(f32[4]{0:T(128)} %param.20) | copy-start | bytes 52
  180.8 19.3 %copy-start.1 = (f32[3200]{0:T(1024)S(1)}, f32[3200]{0:T(1024)}, u32[]{:S(2)}) copy-start(f32[3200]{0:T(1024)} %param.19) | copy-start | bytes 38404
  185.9 56.6 %all-gather.7.cloned.1.call-start = ((), (), s32[]{:S(2)}) async-start(), calls=%async_computation.4 | async-start | bytes 4915200 | tf_op jit(solution)/shard_map/all_gather | solution.py:47
  207.0 2.2 copy-start.2
  209.1 240.1 %reduce-scatter.5.cloned.1.call-start = ((), (), s32[]{:S(2)}) async-start(), calls=%async_computation.5 | async-start | bytes 4915200 | tf_op jit(solution)/shard_map/reduce_scatter | solution.py:51
  219.7 50.7 %collective-permute-start.3 = (bf16[2,256,2048]{2,1,0:T(8,128)(2,1)}, bf16[2,256,2048]{2,1,0:T(8,128)(2,1)}, u32[]{:S(2)}, u32[]{:S(2)}) collective-permute-start(bf16[2,256,2048]{2,1,0:T(8,128)(2,1)} %select_select_fusion.1), channel_id=1, source_target_pairs={{0,4},{2,6},{4,8},{6,10},{8,12},{10,14},{12,16},{14,18},{16,20},{1... | collective-permute-start | bytes 6291464 | tf_op jit(solution)/shard_map/ppermute | solution.py:19
  229.2 13.3 %copy-start.3 = (f32[2048]{0:T(1024)S(1)}, f32[2048]{0:T(1024)}, u32[]{:S(2)}) copy-start(f32[2048]{0:T(1024)} %param.22) | copy-start | bytes 24580
  232.5 81.8 %collective-permute-start.2 = (bf16[2,256,2048]{2,1,0:T(8,128)(2,1)}, bf16[2,256,2048]{2,1,0:T(8,128)(2,1)}, u32[]{:S(2)}, u32[]{:S(2)}) collective-permute-start(bf16[2,256,2048]{2,1,0:T(8,128)(2,1)} %select_select_fusion.2), channel_id=1, source_target_pairs={{0,2},{2,4},{4,6},{6,8},{8,10},{10,12},{12,14},{14,16},{16,18},{18... | collective-permute-start | bytes 6291464 | tf_op jit(solution)/shard_map/ppermute | solution.py:19
  332.5 52.8 %collective-permute-start.1 = (bf16[2,256,2048]{2,1,0:T(8,128)(2,1)}, bf16[2,256,2048]{2,1,0:T(8,128)(2,1)S(1)}, u32[]{:S(2)}, u32[]{:S(2)}) collective-permute-start(bf16[2,256,2048]{2,1,0:T(8,128)(2,1)} %get-tuple-element.21), channel_id=1, source_target_pairs={{4,0},{6,2},{8,4},{10,6},{12,8},{14,10},{16,12},{18,14},{20,16},{2... | collective-permute-start | bytes 6291464 | tf_op jit(solution)/shard_map/ppermute | solution.py:19
  336.7 94.9 %collective-permute-start = (bf16[2,256,2048]{2,1,0:T(8,128)(2,1)}, bf16[2,256,2048]{2,1,0:T(8,128)(2,1)S(1)}, u32[]{:S(2)}, u32[]{:S(2)}) collective-permute-start(bf16[2,256,2048]{2,1,0:T(8,128)(2,1)} %get-tuple-element.21), channel_id=1, source_target_pairs={{2,0},{4,2},{6,4},{8,6},{10,8},{12,10},{14,12},{16,14},{18,16},{20... | collective-permute-start | bytes 6291464 | tf_op jit(solution)/shard_map/ppermute | solution.py:19
  449.3 2.5 copy-start
Sparse Core Ops, SparseCore 0:
  10.8 122.8 all-gather.8
  135.8 15.1 all-gather.4
  186.0 13.9 reduce-scatter.2
  209.3 16.3 all-gather.6
  332.6 17.0 reduce-scatter.4
where the time goes:
time: 462 us; the launch traced here: 461 us
  waiting for transfers between devices  274 us (59%)
  matrix products  62.6 us (14%)
  local copies, waits for them, and re-layouts  50.4 us (11%)
  other arithmetic  44.2 us (10%)
  starting transfers between devices  15.5 us (3%)
  between operations  14 us (3%)
    ppermute x4, waiting for transfers between devices, from_behind(): return lax.ppermute(array, axis, pairs)  140 us
    all_gather x1, waiting for transfers between devices, on_device(): weight_full = lax.all_gather(qkv_weight, 'img', axis=0, tiled=True)  121 us
    unnamed x15, local copies, waits for them, and re-layouts  22.7 us
    dot_general x1, matrix products, project_rows(): jnp.einsum('tpd,df->ptf', row_block, proj_weight, preferred_element_type=...  21.3 us
    dot_general x1, matrix products, grad_terms(): jnp.einsum('ptf,ef->pte', slope_rows, proj_weight, preferred_element_type...  18.2 us
    dot_general x1, matrix products, project_qkv(): jnp.einsum('tpd,de->pte', row_block, weight_full, preferred_element_type=...  16.7 us
    ppermute x4, starting transfers between devices, from_behind(): return lax.ppermute(array, axis, pairs)  15.3 us
    gather x3, local copies, waits for them, and re-layouts, return_rows(): jnp.take(grad_out, slot_index, axis=0)  14.3 us
  transfers between devices with their start and end apart: 9, of which 6 were waited for; matrix products, arithmetic and copies ran while one was open for 21% of the time, Pallas kernels for 0%

commit v1 on v0

v1 whole, which is shorter than its diff:
```python
import functools
import math

import jax
import jax.numpy as jnp
from jax import lax
from jax.experimental import pallas as pl
from jax.experimental.pallas import tpu as pltpu
from jax.sharding import Mesh, PartitionSpec as P

HEAD_DIM = 128
LINE = 4
IMG = ("z", "y", "x")
VMEM_BYTES = 56 * 1024 * 1024

inv_root_two = 0.7071067811865476
inv_root_tau = 0.3989422804014327


def swap(array):
    return lax.ppermute(array, "head", [(0, 1), (1, 0)])


def along_z(array, by):
    return lax.ppermute(array, "z", [(i, (i + by) % LINE) for i in range(LINE)])


def along_img(array, by):
    peers = lax.axis_size(IMG)
    pairs = [(i, i + by) for i in range(peers) if 0 <= i + by < peers]
    return lax.ppermute(array, IMG, pairs)


def tile_owners(tile_counts, tile_total, tile_group):
    starts = jnp.cumsum(tile_counts) - tile_counts
    tile_index = jnp.arange(tile_total, dtype=jnp.int32)
    start_of = jnp.max(
        jnp.where(starts[None, :] <= tile_index[:, None], starts[None, :], -1), axis=1
    )
    owner_of = start_of // tile_group
    owners_total = tile_total // tile_group
    edge_tiles = jnp.arange(owners_total + 1, dtype=jnp.int32) * tile_group
    first_tile = jnp.min(
        jnp.where(starts[None, :] >= edge_tiles[:, None], starts[None, :], tile_total), axis=1
    )
    return (owner_of, first_tile)


def norm_kernel(tokens_ref, out_ref, ordered):
    rows = tokens_ref[0].astype(jnp.float32)
    normed = rows * lax.rsqrt(jnp.mean(rows * rows, axis=-1, keepdims=True) + 1e-06)
    groups = LINE * LINE
    share = rows.shape[1] // (LINE * groups)
    for line in range(LINE):
        for group in range(groups):
            source = (line * groups + group) * share
            target = (group * LINE + line) * share
            ordered[:, target : target + share] = normed[:, source : source + share]
    out_ref[0] = ordered[...].astype(jnp.bfloat16)


def norm_rows(tokens):
    tiles, half, depth = tokens.shape
    block = 64
    spec = pl.BlockSpec((1, block, depth), lambda t, r: (t, r, 0))
    return pl.pallas_call(
        norm_kernel,
        grid=(tiles, half // block),
        out_shape=jax.ShapeDtypeStruct(tokens.shape, jnp.bfloat16),
        in_specs=[spec],
        out_specs=spec,
        scratch_shapes=[pltpu.VMEM((block, depth), jnp.float32)],
        compiler_params=pltpu.CompilerParams(vmem_limit_bytes=VMEM_BYTES),
        name="norm",
    )(tokens)


def attend_kernel(own_ref, other_ref, weight_ref, out_ref, total):
    step = pl.program_id(0)
    tiles, half, depth = own_ref.shape
    rows = jnp.concatenate(
        [own_ref[...].reshape(tiles * half, depth), other_ref[...].reshape(tiles * half, depth)], axis=0
    )
    part = jnp.dot(rows, weight_ref[...], preferred_element_type=jnp.float32)

    @pl.when(step == 0)
    def _():
        total[...] = part

    @pl.when(step > 0)
    def _():
        total[...] += part

    @pl.when(step == pl.num_programs(0) - 1)
    def _():
        heads = out_ref.shape[2] // HEAD_DIM
        for tile in range(tiles):
            for head in range(heads):

                def piece(kind):
                    start = (head * 3 + kind) * HEAD_DIM
                    columns = slice(start, start + HEAD_DIM)
                    low = total[tile * half : (tile + 1) * half, columns]
                    high = total[(tiles + tile) * half : (tiles + tile + 1) * half, columns]
                    return jnp.concatenate([low, high], axis=0).astype(jnp.bfloat16)

                scores = lax.dot_general(
                    piece(0), piece(1), (((1,), (1,)), ((), ())), preferred_element_type=jnp.float32
                ) * (1.0 / math.sqrt(HEAD_DIM))
                scores = scores - jnp.max(scores, axis=-1, keepdims=True)
                raised = jnp.exp(scores)
                soft = (raised / jnp.sum(raised, axis=-1, keepdims=True)).astype(jnp.bfloat16)
                mixed = jnp.dot(soft, piece(2), preferred_element_type=jnp.float32)
                out_ref[tile, :, head * HEAD_DIM : (head + 1) * HEAD_DIM] = mixed.astype(jnp.bfloat16)


def attend(own, other, weight):
    tiles, half, depth = own.shape
    width = weight.shape[1]
    out_width = width // 3
    block = 640
    return pl.pallas_call(
        attend_kernel,
        grid=(depth // block,),
        out_shape=jax.ShapeDtypeStruct((tiles, 2 * half, out_width), jnp.bfloat16),
        in_specs=[
            pl.BlockSpec((tiles, half, block), lambda k: (0, 0, k)),
            pl.BlockSpec((tiles, half, block), lambda k: (0, 0, k)),
            pl.BlockSpec((block, width), lambda k: (k, 0)),
        ],
        out_specs=pl.BlockSpec((tiles, 2 * half, out_width), lambda k: (0, 0, 0)),
        scratch_shapes=[pltpu.VMEM((2 * tiles * half, width), jnp.float32)],
        compiler_params=pltpu.CompilerParams(vmem_limit_bytes=VMEM_BYTES),
        cost_estimate=pl.CostEstimate(
            flops=2 * tiles * 2 * half * depth * width,
            bytes_accessed=2 * depth * width + 4 * tiles * half * depth,
            transcendentals=0,
        ),
        name="attend",
    )(own, other, weight)


def out_kernel(line_ref, *refs):
    attended = refs[:LINE]
    weights = refs[LINE : 2 * LINE]
    own_ref, other_ref = refs[2 * LINE :]
    tiles, half, block = own_ref.shape
    for part_ref, start in ((other_ref, half), (own_ref, 0)):
        total = None
        for rows_ref, weight_ref in zip(attended, weights):
            rows = rows_ref[:, start : start + half].reshape(tiles * half, rows_ref.shape[2])
            term = jnp.dot(rows, weight_ref[...], preferred_element_type=jnp.float32)
            total = term if total is None else total + term
        part_ref[...] = total.astype(jnp.bfloat16).reshape(tiles, half, block)


def out_project(line_arg, attended, out_weight):
    tiles, full, share = attended[0].shape
    half = full // 2
    depth = out_weight.shape[1]
    block = 640

    def weight_spec(k):
        return pl.BlockSpec((share, block), lambda n, line: ((line[0] + k) % LINE, n))

    part = pl.BlockSpec((tiles, half, block), lambda n, line: (0, 0, n))
    shape = jax.ShapeDtypeStruct((tiles, half, depth), jnp.bfloat16)
    return pl.pallas_call(
        out_kernel,
        grid_spec=pltpu.PrefetchScalarGridSpec(
            num_scalar_prefetch=1,
            grid=(depth // block,),
            in_specs=[pl.BlockSpec((tiles, full, share), lambda n, line: (0, 0, 0))] * LINE
            + [weight_spec(k) for k in range(LINE)],
            out_specs=[part, part],
        ),
        out_shape=[shape, shape],
        compiler_params=pltpu.CompilerParams(vmem_limit_bytes=VMEM_BYTES),
        cost_estimate=pl.CostEstimate(
            flops=2 * tiles * full * share * LINE * depth,
            bytes_accessed=2 * LINE * share * depth,
            transcendentals=0,
        ),
        name="out",
    )(line_arg, *attended, *([out_weight] * LINE))


def join_kernel(
    mixing_ref, tokens_ref, early_ref, mid_ref, own_ref, other_ref, scale_ref, z_ref, inverse_ref
):
    inputs = tokens_ref[0].astype(jnp.float32)
    attended_out = own_ref[0].astype(jnp.float32) + other_ref[0].astype(jnp.float32)
    layer_out = inputs + scale_ref[...] * attended_out
    joined = (
        mixing_ref[0] * early_ref[0].astype(jnp.float32)
        + mixing_ref[1] * mid_ref[0].astype(jnp.float32)
        + mixing_ref[2] * inputs
        + mixing_ref[3] * layer_out
    )
    centre = jnp.mean(joined, axis=-1, keepdims=True)
    shifted = joined - centre
    inverse = lax.rsqrt(jnp.mean(shifted * shifted, axis=-1, keepdims=True) + 1e-05)
    z_ref[0] = (shifted * inverse).astype(jnp.bfloat16)
    inverse_ref[0] = jnp.broadcast_to(inverse, inverse_ref.shape[1:])


def join_rows(mixing, tokens, early, mid, own, other, scale):
    tiles, half, depth = tokens.shape
    block = 32
    spec = pl.BlockSpec((1, block, depth), lambda t, r: (t, r, 0))
    return pl.pallas_call(
        join_kernel,
        grid=(tiles, half // block),
        out_shape=[
            jax.ShapeDtypeStruct(tokens.shape, jnp.bfloat16),
            jax.ShapeDtypeStruct((tiles, half, 128), jnp.float32),
        ],
        in_specs=[pl.BlockSpec(memory_space=pltpu.SMEM)]
        + [spec] * 5
        + [pl.BlockSpec((1, depth), lambda t, r: (0, 0))],
        out_specs=[spec, pl.BlockSpec((1, block, 128), lambda t, r: (t, r, 0))],
        compiler_params=pltpu.CompilerParams(vmem_limit_bytes=VMEM_BYTES),
        name="join",
    )(mixing, tokens, early, mid, own, other, scale)


def final_kernel(own_ref, other_ref, z_ref, inverse_ref, out_ref):
    grad = own_ref[0].astype(jnp.float32) + other_ref[0].astype(jnp.float32)
    normal = z_ref[0].astype(jnp.float32)
    mean = jnp.mean(grad, axis=-1, keepdims=True)
    along = jnp.mean(grad * normal, axis=-1, keepdims=True)
    out_ref[0] = ((grad - mean - normal * along) * inverse_ref[0, :, :1]).astype(jnp.bfloat16)


def final_rows(own, other, z_rows, inverse):
    tiles, half, depth = own.shape
    block = 32
    spec = pl.BlockSpec((1, block, depth), lambda t, r: (t, r, 0))
    return pl.pallas_call(
        final_kernel,
        grid=(tiles, half // block),
        out_shape=jax.ShapeDtypeStruct(own.shape, jnp.bfloat16),
        in_specs=[spec, spec, spec, pl.BlockSpec((1, block, 128), lambda t, r: (t, r, 0))],
        out_specs=spec,
        compiler_params=pltpu.CompilerParams(vmem_limit_bytes=VMEM_BYTES),
        name="final",
    )(own, other, z_rows, inverse)


def activate(preact):
    raised = jnp.exp(-0.5 * preact * preact)
    step = 1.0 / (1.0 + 0.3275911 * inv_root_two * jnp.abs(preact))
    series = 1.061405429 * step - 1.453152027
    series = series * step + 1.421413741
    series = series * step - 0.284496736
    series = series * step + 0.254829592
    tail = 0.5 * series * step * raised
    return jnp.where(preact >= 0.0, 1.0 - tail, tail), raised * inv_root_tau


def home_kernel(
    core_ref, own_ref, other_ref, weight_ref, bias_ref, back_own_ref, back_other_ref,
    projected_ref, grad_own_ref, grad_other_ref, own_total, other_total,
):
    step = pl.program_id(0)
    core = core_ref[0]
    tiles, half, depth = own_ref.shape
    block = weight_ref.shape[1]

    @pl.when(step == 0)
    def _():
        own_total[...] = jnp.zeros_like(own_total)
        other_total[...] = jnp.zeros_like(other_total)

    parts = (
        (own_ref, back_own_ref, own_total, core),
        (other_ref, back_other_ref, other_total, 1 - core),
    )
    for rows_ref, back_ref, total, place in parts:
        rows = rows_ref[...].reshape(tiles * half, depth)
        preact = jnp.dot(rows, weight_ref[...], preferred_element_type=jnp.float32) + bias_ref[...]
        cumulative, density = activate(preact)
        projected = (preact * cumulative).astype(jnp.bfloat16)
        projected_ref[:, pl.ds(place, 1)] = projected.reshape(tiles, 1, half, block)
        slope = cumulative + preact * density
        back = back_ref[...].reshape(tiles * half, block).astype(jnp.float32)
        slope_rows = (back * slope).astype(jnp.bfloat16)
        total[...] += lax.dot_general(
            slope_rows, weight_ref[...], (((1,), (1,)), ((), ())), preferred_element_type=jnp.float32
        )

    @pl.when(step == pl.num_programs(0) - 1)
    def _():
        grad_own_ref[...] = own_total[...].astype(jnp.bfloat16).reshape(tiles, half, depth)
        grad_other_ref[...] = other_total[...].astype(jnp.bfloat16).reshape(tiles, half, depth)


def home_rows(core, own, other, weight, bias, back):
    tiles, half, depth = own.shape
    width = weight.shape[1]
    block = 512
    back = back.reshape(tiles, 2, half, width)
    whole = pl.BlockSpec((tiles, half, depth), lambda n, c: (0, 0, 0))
    projected, grad_own, grad_other = pl.pallas_call(
        home_kernel,
        grid_spec=pltpu.PrefetchScalarGridSpec(
            num_scalar_prefetch=1,
            grid=(width // block,),
            in_specs=[
                whole,
                whole,
                pl.BlockSpec((depth, block), lambda n, c: (0, n)),
                pl.BlockSpec((1, block), lambda n, c: (0, n)),
                pl.BlockSpec((tiles, 1, half, block), lambda n, c: (0, c[0], 0, n)),
                pl.BlockSpec((tiles, 1, half, block), lambda n, c: (0, 1 - c[0], 0, n)),
            ],
            out_specs=[
                pl.BlockSpec((tiles, 2, half, block), lambda n, c: (0, 0, 0, n)),
                whole,
                whole,
            ],
            scratch_shapes=[
                pltpu.VMEM((tiles * half, depth), jnp.float32),
                pltpu.VMEM((tiles * half, depth), jnp.float32),
            ],
        ),
        out_shape=[
            jax.ShapeDtypeStruct((tiles, 2, half, width), jnp.bfloat16),
            jax.ShapeDtypeStruct((tiles, half, depth), jnp.bfloat16),
            jax.ShapeDtypeStruct((tiles, half, depth), jnp.bfloat16),
        ],
        compiler_params=pltpu.CompilerParams(vmem_limit_bytes=VMEM_BYTES),
        cost_estimate=pl.CostEstimate(
            flops=8 * tiles * half * depth * width,
            bytes_accessed=2 * depth * width,
            transcendentals=0,
        ),
        name="home",
    )(core, own, other, weight, bias, back, back)
    return projected.reshape(tiles, 2 * half, width), grad_own, grad_other


def owner_kernel(core_ref, own_ref, other_ref, weight_ref, bias_ref, projected_ref):
    core = core_ref[0]
    tiles, half, depth = own_ref.shape
    block = weight_ref.shape[1]
    for rows_ref, place in ((own_ref, core), (other_ref, 1 - core)):
        rows = rows_ref[...].reshape(tiles * half, depth)
        preact = jnp.dot(rows, weight_ref[...], preferred_element_type=jnp.float32) + bias_ref[...]
        projected = (preact * activate(preact)[0]).astype(jnp.bfloat16)
        projected_ref[:, pl.ds(place, 1)] = projected.reshape(tiles, 1, half, block)


def owner_project(core, own, other, weight, bias):
    tiles, half, depth = own.shape
    width = weight.shape[1]
    block = 512
    whole = pl.BlockSpec((tiles, half, depth), lambda n, c: (0, 0, 0))
    projected = pl.pallas_call(
        owner_kernel,
        grid_spec=pltpu.PrefetchScalarGridSpec(
            num_scalar_prefetch=1,
            grid=(width // block,),
            in_specs=[
                whole,
                whole,
                pl.BlockSpec((depth, block), lambda n, c: (0, n)),
                pl.BlockSpec((1, block), lambda n, c: (0, n)),
            ],
            out_specs=pl.BlockSpec((tiles, 2, half, block), lambda n, c: (0, 0, 0, n)),
        ),
        out_shape=jax.ShapeDtypeStruct((tiles, 2, half, width), jnp.bfloat16),
        compiler_params=pltpu.CompilerParams(vmem_limit_bytes=VMEM_BYTES),
        cost_estimate=pl.CostEstimate(
            flops=4 * tiles * half * depth * width,
            bytes_accessed=2 * depth * width,
            transcendentals=0,
        ),
        name="owner",
    )(core, own, other, weight, bias)
    return projected.reshape(tiles, 2 * half, width)


def on_device(
    tokens, tap_early, tap_mid, tile_counts, qkv_weight, out_weight, layer_scale, layer_logits,
    proj_weight, proj_bias, grad_out,
):
    tile_group, token_share, depth = tokens.shape
    img_count = lax.axis_size(IMG)
    place = lax.axis_index(IMG)
    line_place = lax.axis_index("z")
    core = lax.axis_index("head")
    core_arg = core.astype(jnp.int32).reshape(1)
    tile_total = tile_group * img_count
    own_tiles = grad_out.shape[0]
    owner_of, first_tile = tile_owners(tile_counts, tile_total, tile_group)
    my_first = first_tile[place]

    far_back = []
    for within in range(tile_group):
        tile = (place + 2) * tile_group + within
        slot = jnp.clip(tile - my_first, 0, own_tiles - 1)
        far_back.append(along_img(lax.dynamic_slice_in_dim(grad_out, slot, 1, axis=0), 2))
    slot = jnp.clip((place + 1) * tile_group - my_first, 0, own_tiles - tile_group)
    near_back = along_img(lax.dynamic_slice_in_dim(grad_out, slot, tile_group, axis=0), 1)

    depth_share, width = qkv_weight.shape
    share = width // LINE
    received = []
    for distance in range(LINE):
        target = (line_place + distance) % LINE
        columns = lax.dynamic_slice_in_dim(qkv_weight, target * share, share, axis=1)
        received.append(along_z(columns, distance) if distance else columns)
    ladder = jnp.stack([received[(LINE - 1 - j) % LINE] for j in range(2 * LINE - 1)], axis=0)
    sent = lax.dynamic_slice_in_dim(ladder, LINE - 1 - line_place, LINE, axis=0)
    gathered = lax.all_gather(sent.reshape(LINE * depth_share, share), ("y", "x"), axis=0, tiled=True)
    weight = gathered

    normed = norm_rows(tokens)
    from_low = along_z(normed, 1)
    from_high = along_z(normed, -1)
    from_low, from_high, far_back[0] = lax.optimization_barrier((from_low, from_high, far_back[0]))
    far_first = along_z(from_low[:1], 1)
    far_second = along_z(from_high[1:], -1)
    far_first, far_second, far_back[1] = lax.optimization_barrier((far_first, far_second, far_back[1]))
    from_far = jnp.concatenate([far_first, far_second], axis=0)
    att_far = along_z(attend(from_far, swap(from_far), weight), 2)
    att_low = along_z(attend(from_low, swap(from_low), weight), -1)
    att_high = along_z(attend(from_high, swap(from_high), weight), 1)
    att_own = attend(normed, swap(normed), weight)
    part_own, part_other = out_project(
        line_place.astype(jnp.int32).reshape(1), [att_own, att_low, att_far, att_high], out_weight
    )
    raised_logits = jnp.exp(layer_logits)
    mixing = raised_logits / jnp.sum(raised_logits)
    z_rows, inverse_std = join_rows(
        mixing, tokens, tap_early, tap_mid, part_own, swap(part_other), layer_scale.reshape(1, -1)
    )

    near = along_img(z_rows, -1)
    far = along_img(z_rows, -2)

    back = []
    for within in range(tile_group):
        tile = place * tile_group + within
        owner = owner_of[tile]
        slot = jnp.clip(tile - my_first, 0, own_tiles - 1)
        here = lax.dynamic_index_in_dim(grad_out, slot, axis=0, keepdims=False)
        back.append(
            jnp.where(
                owner == place,
                here,
                jnp.where(owner == place - 1, near_back[within], far_back[within][0]),
            )
        )
    back_rows = jnp.stack(back, axis=0)

    bias = proj_bias.reshape(1, -1)
    projected, grad_own, grad_other = home_rows(
        core_arg, z_rows, swap(z_rows), proj_weight, bias, back_rows
    )
    grad_joined = final_rows(grad_own, swap(grad_other), z_rows, inverse_std)

    near_projected = owner_project(core_arg, near, swap(near), proj_weight, bias)
    far_projected = owner_project(core_arg, far, swap(far), proj_weight, bias)

    offset = my_first - place * tile_group
    held = first_tile[place + 1] - my_first
    at_hand = [
        source[within]
        for source in (projected, near_projected, far_projected)
        for within in range(tile_group)
    ]
    slots = []
    for slot in range(own_tiles):
        later = at_hand[min(slot + 1, len(at_hand) - 1)]
        picked = jnp.where(offset == 0, at_hand[slot], later)
        slots.append(jnp.where(slot < held, picked, jnp.zeros((), jnp.bfloat16)))
    owner_rows = jnp.stack(slots, axis=0)
    return (owner_rows, grad_joined)


def solution(mesh):
    cores = mesh.devices.shape[-1]
    inner = Mesh(mesh.devices.reshape(LINE, LINE, LINE, cores), IMG + ("head",))
    return jax.shard_map(
        on_device,
        mesh=inner,
        in_specs=(
            P(IMG, "head", None),
            P(IMG, "head", None),
            P(IMG, "head", None),
            P(),
            P(IMG, "head"),
            P("head", None),
            P(),
            P(),
            P(None, "head"),
            P("head"),
            P(IMG, None, "head"),
        ),
        out_specs=(P(IMG, None, "head"), P(IMG, "head", None)),
        check_vma=False,
    )
```

time: 462 us -> 358 us (0.77)
  waiting for transfers between devices: 274 us -> 137 us
  Pallas kernels: 0 us -> 120 us
  matrix products: 62.6 us -> 0 us
  other arithmetic: 44.2 us -> 7.23 us
  starting transfers between devices: 15.5 us -> 52 us
  local copies, waits for them, and re-layouts: 50.4 us -> 17.2 us
  between operations: 14 us -> 22.5 us
    pallas_call x0 -> x11, Pallas kernels: none -> 120 us  [the longest x4 35.1 us: attend(): pl.pallas_call(attend_kernel, grid=(depth // block,), out_shape=jax.Shape...]
    all_gather x3 -> x1, waiting for transfers between devices: 121 us -> 23 us  [on_device(): lax.all_gather(sent.reshape(LINE * depth_share, share), ('y', 'x'), axis=...]
    dot_general x6 -> x0, matrix products: 62.6 us -> none  [the longest x1 21.3 us: project_rows(): jnp.einsum('tpd,df->ptf', row_block, proj_weight, preferred_element_type=...]
    ppermute x4 -> x24, starting transfers between devices: 15.3 us -> 51.9 us  [the longest x5 29.5 us: along_img(): return lax.ppermute(array, IMG, pairs)]
    ppermute x4 -> x24, waiting for transfers between devices: 140 us -> 114 us  [the longest x5 104 us: along_img(): return lax.ppermute(array, IMG, pairs)]
    gather x7 -> x0, local copies, waits for them, and re-layouts: 23.2 us -> none  [the longest x3 14.3 us: return_rows(): jnp.take(grad_out, slot_index, axis=0)]
    unnamed x15 -> x42, local copies, waits for them, and re-layouts: 22.7 us -> 5.79 us
    reduce_scatter x2 -> x0, waiting for transfers between devices: 12.1 us -> none  [group_sums(): lax.psum_scatter(term_fn(jnp.int32(0), token_share * lax.axis_size('head'...]
  transfers between devices with their start and end apart: 9 -> 25, of which waited for: 6 -> 10; matrix products, arithmetic and copies ran while one was open for 21% -> 5% of each run, Pallas kernels for 0% -> 29%
where the time goes in v1:
time: 358 us; the launch traced here: 356 us
  waiting for transfers between devices  137 us (38%)
  Pallas kernels  120 us (34%)
  starting transfers between devices  52 us (15%)
  between operations  22.5 us (6%)
  local copies, waits for them, and re-layouts  17.2 us (5%)
  other arithmetic  7.23 us (2%)
    ppermute x5, waiting for transfers between devices, along_img(): return lax.ppermute(array, IMG, pairs)  104 us
    pallas_call x4, Pallas kernels, attend(): pl.pallas_call(attend_kernel, grid=(depth // block,), out_shape=jax.Shape...  35.1 us
    ppermute x5, starting transfers between devices, along_img(): return lax.ppermute(array, IMG, pairs)  29.5 us
    pallas_call x2, Pallas kernels, owner_project(): pl.pallas_call(owner_kernel, grid_spec=pltpu.PrefetchScalarGridSpec(num_s...  29 us
    pallas_call x1, Pallas kernels, home_rows(): pl.pallas_call(home_kernel, grid_spec=pltpu.PrefetchScalarGridSpec(num_sc...  25 us
    all_gather x1, waiting for transfers between devices, on_device(): lax.all_gather(sent.reshape(LINE * depth_share, share), ('y', 'x'), axis=...  23 us
    ppermute x10, starting transfers between devices, along_z(): return lax.ppermute(array, 'z', [(i, (i + by) % LINE) for i in range(LINE)])  12.6 us
    ppermute x9, starting transfers between devices, swap(): return lax.ppermute(array, 'head', [(0, 1), (1, 0)])  9.84 us
  transfers between devices with their start and end apart: 25, of which 10 were waited for; matrix products, arithmetic and copies ran while one was open for 5% of the time, Pallas kernels for 29%

profile of v1, /device:TPU:31, one launch (start us, length us, event | category | flops | bytes accessed | tf_op | source)
XLA Modules:
  0.0 356.2 jit_solution(11255262035587139894)
XLA Ops:
  8.3 3.8 %collective-permute-start.1 = (bf16[50,768]{1,0:T(8,128)(2,1)S(1)}, bf16[50,768]{1,0:T(8,128)(2,1)S(1)}, u32[]{:S(2)}, u32[]{:S(2)}) collective-permute-start(bf16[50,768]{1,0:T(8,128)(2,1)S(1)} %get-tuple-element.40), channel_id=1, source_target_pairs={{0,96},{32,0},{64,32},{96,64},{1,97},{33,1},{65,33},{97,65},{2,98}... | collective-permute-start | bytes 230408 | tf_op jit(solution)/shard_map/ppermute | solution.py:25
  13.6 4.4 %collective-permute-done.2 = bf16[50,768]{1,0:T(8,128)(2,1)S(1)} collective-permute-done((bf16[50,768]{1,0:T(8,128)(2,1)S(1)}, bf16[50,768]{1,0:T(8,128)(2,1)S(1)}, u32[]{:S(2)}, u32[]{:S(2)}) %collective-permute-start.2) | collective-permute-done | bytes 76832 | tf_op jit(solution)/shard_map/ppermute | solution.py:25
  19.9 6.0 %norm.1.own_ref = bf16[2,128,3200]{2,1,0:T(8,128)(2,1)} custom-call(bf16[2,128,3200]{2,1,0:T(8,128)(2,1)} %tokens_ref.3), custom_call_target="tpu_custom_call" | custom-call | tf_op jit(solution)/shard_map/norm/pallas_call | solution.py:66
  34.0 3.8 %collective-permute-start.11 = (bf16[1,256,2048]{2,1,0:T(8,128)(2,1)S(1)}, bf16[1,256,2048]{2,1,0:T(8,128)(2,1)S(1)}, u32[]{:S(2)}, u32[]{:S(2)}) collective-permute-start(bf16[1,256,2048]{2,1,0:T(8,128)(2,1)S(1)} %get-tuple-element.30), channel_id=1, source_target_pairs={{0,4},{2,6},{4,8},{6,10},{8,12},{10,14},{12,16},{14,18},{16,20},{1... | collective-permute-start | bytes 3145736 | tf_op jit(solution)/shard_map/ppermute | solution.py:31
  37.7 23.9 %collective-permute-done.6 = bf16[1,256,2048]{2,1,0:T(8,128)(2,1)S(1)} collective-permute-done((bf16[1,256,2048]{2,1,0:T(8,128)(2,1)S(1)}, bf16[1,256,2048]{2,1,0:T(8,128)(2,1)S(1)}, u32[]{:S(2)}, u32[]{:S(2)}) %collective-permute-start.6) | collective-permute-done | bytes 1048608 | tf_op jit(solution)/shard_map/ppermute | solution.py:31
  67.7 16.4 %collective-permute-done.11 = bf16[1,256,2048]{2,1,0:T(8,128)(2,1)S(1)} collective-permute-done((bf16[1,256,2048]{2,1,0:T(8,128)(2,1)S(1)}, bf16[1,256,2048]{2,1,0:T(8,128)(2,1)S(1)}, u32[]{:S(2)}, u32[]{:S(2)}) %collective-permute-start.11) | collective-permute-done | bytes 1048608 | tf_op jit(solution)/shard_map/ppermute | solution.py:31
  84.3 4.7 %collective-permute-start.12 = (bf16[2,128,3200]{2,1,0:T(8,128)(2,1)S(1)}, bf16[2,128,3200]{2,1,0:T(8,128)(2,1)}, u32[]{:S(2)}, u32[]{:S(2)}) collective-permute-start(bf16[2,128,3200]{2,1,0:T(8,128)(2,1)S(1)} %constant_dynamic-update-slice_fusion.own_ref), channel_id=1, source_target_pairs={{0,1},{1,0},{2,3},{3,2},{4,5},{5,4},{6,7},{7,6},{8,9},{9,8},{10,11... | collective-permute-start | bytes 4915208 | tf_op jit(solution)/shard_map/ppermute | solution.py:21
  89.6 4.0 %collective-permute-done.12.other_ref = bf16[2,128,3200]{2,1,0:T(8,128)(2,1)} collective-permute-done((bf16[2,128,3200]{2,1,0:T(8,128)(2,1)S(1)}, bf16[2,128,3200]{2,1,0:T(8,128)(2,1)}, u32[]{:S(2)}, u32[]{:S(2)}) %collective-permute-start.12) | collective-permute-done | bytes 1638432 | tf_op jit(solution)/shard_map/ppermute | solution.py:21
  93.7 23.0 %all-gather.2.cloned.1.call-done.weight_ref = bf16[3200,768]{1,0:T(8,128)(2,1)} async-done(((bf16[200,768]{1,0:T(8,128)(2,1)}), bf16[3200,768]{1,0:T(8,128)(2,1)}) %all-gather.2.cloned.1.call-update) | async-done | bytes 4915216 | tf_op jit(solution)/shard_map/all_gather | solution.py:416
  116.7 8.8 %attend.6 = bf16[2,256,256]{2,1,0:T(8,128)(2,1)} custom-call(bf16[2,128,3200]{2,1,0:T(8,128)(2,1)} %copy-done.5, bf16[2,128,3200]{2,1,0:T(8,128)(2,1)} %collective-permute-done.12.other_ref, bf16[3200,768]{1,0:T(8,128)(2,1)} %all-gather.2.cloned.1.call-done.weight_ref), custom_call_target="tpu_custom_call" | custom-call | flops 2516582400 | bytes 8192000 | tf_op jit(solution)/shard_map/attend/pallas_call | solution.py:122
  128.3 8.8 %attend.5 = bf16[2,256,256]{2,1,0:T(8,128)(2,1)} custom-call(bf16[2,128,3200]{2,1,0:T(8,128)(2,1)} %collective-permute-done.4.own_ref, bf16[2,128,3200]{2,1,0:T(8,128)(2,1)} %collective-permute-done.7.other_ref, bf16[3200,768]{1,0:T(8,128)(2,1)} %all-gather.2.cloned.1.call-done.weight_ref), custom_call_target="tpu_custom_call" | custom-call | flops 2516582400 | bytes 8192000 | tf_op jit(solution)/shard_map/attend/pallas_call | solution.py:122
  137.9 8.8 %attend.7 = bf16[2,256,256]{2,1,0:T(8,128)(2,1)} custom-call(bf16[2,128,3200]{2,1,0:T(8,128)(2,1)} %collective-permute-done.5.own_ref, bf16[2,128,3200]{2,1,0:T(8,128)(2,1)} %collective-permute-done.14.other_ref, bf16[3200,768]{1,0:T(8,128)(2,1)} %all-gather.2.cloned.1.call-done.weight_ref), custom_call_target="tpu_custom_call" | custom-call | flops 2516582400 | bytes 8192000 | tf_op jit(solution)/shard_map/attend/pallas_call | solution.py:122
  147.3 8.8 %attend.4.refs_0_ = bf16[2,256,256]{2,1,0:T(8,128)(2,1)} custom-call(bf16[2,128,3200]{2,1,0:T(8,128)(2,1)} %norm.1.own_ref, bf16[2,128,3200]{2,1,0:T(8,128)(2,1)} %collective-permute-done.other_ref, bf16[3200,768]{1,0:T(8,128)(2,1)} %all-gather.2.cloned.1.call-done.weight_ref), custom_call_target="tpu_custom_call" | custom-call | flops 2516582400 | bytes 8192000 | tf_op jit(solution)/shard_map/attend/pallas_call | solution.py:122
  157.1 8.2 %out.1 = (bf16[2,128,3200]{2,1,0:T(8,128)(2,1)}, bf16[2,128,3200]{2,1,0:T(8,128)(2,1)}) custom-call(s32[1]{0:T(128)} %bitcast.4.line_ref, bf16[2,256,256]{2,1,0:T(8,128)(2,1)} %attend.4.refs_0_, bf16[2,256,256]{2,1,0:T(8,128)(2,1)} %copy-done.7, bf16[2,256,256]{2,1,0:T(8,128)(2,1)} %copy-done.6, bf16[2,256,256]{2,1,0:T(8,128)(2,1)} %copy-done.8, ...), custom_call_target="tpu_custom_call" | custom-call | flops 3355443200 | bytes 6553600 | tf_op jit(solution)/shard_map/out/pallas_call | solution.py:168
  167.5 3.2 constant_dynamic-slice_fusion
  170.7 19.6 %collective-permute-start.18 = (bf16[2,256,2048]{2,1,0:T(8,128)(2,1)}, bf16[2,256,2048]{2,1,0:T(8,128)(2,1)S(1)}, u32[]{:S(2)}, u32[]{:S(2)}) collective-permute-start(bf16[2,256,2048]{2,1,0:T(8,128)(2,1)} %constant_dynamic-slice_fusion), channel_id=1, source_target_pairs={{0,2},{2,4},{4,6},{6,8},{8,10},{10,12},{12,14},{14,16},{16,18},{18... | collective-permute-start | bytes 6291464 | tf_op jit(solution)/shard_map/ppermute | solution.py:31
  192.7 8.5 %join.1 = (bf16[2,128,3200]{2,1,0:T(8,128)(2,1)}, f32[2,128,128]{2,1,0:T(8,128)}) custom-call(f32[4]{0:T(128)} %exponential_divide_fusion.mixing_ref, bf16[2,128,3200]{2,1,0:T(8,128)(2,1)} %tokens_ref.3, bf16[2,128,3200]{2,1,0:T(8,128)(2,1)} %early_ref.1, bf16[2,128,3200]{2,1,0:T(8,128)(2,1)} %mid_ref.1, bf16[2,128,3200]{2,1,0:T(8,128)(2,1)} %get-tuple-element.19.own_ref, ...), custom_call_target="tpu_custom_call" | custom-call | tf_op jit(solution)/shard_map/join/pallas_call | solution.py:211
  212.1 33.0 %collective-permute-done.21.own_ref = bf16[2,128,3200]{2,1,0:T(8,128)(2,1)} collective-permute-done((bf16[2,128,3200]{2,1,0:T(8,128)(2,1)}, bf16[2,128,3200]{2,1,0:T(8,128)(2,1)}, u32[]{:S(2)}, u32[]{:S(2)}) %collective-permute-start.21) | collective-permute-done | bytes 1638432 | tf_op jit(solution)/shard_map/ppermute | solution.py:31
  246.9 23.9 %collective-permute-done.18 = bf16[2,256,2048]{2,1,0:T(8,128)(2,1)S(1)} collective-permute-done((bf16[2,256,2048]{2,1,0:T(8,128)(2,1)}, bf16[2,256,2048]{2,1,0:T(8,128)(2,1)S(1)}, u32[]{:S(2)}, u32[]{:S(2)}) %collective-permute-start.18) | collective-permute-done | bytes 2097184 | tf_op jit(solution)/shard_map/ppermute | solution.py:31
  274.2 6.6 %collective-permute-done.19.own_ref = bf16[2,128,3200]{2,1,0:T(8,128)(2,1)} collective-permute-done((bf16[2,128,3200]{2,1,0:T(8,128)(2,1)}, bf16[2,128,3200]{2,1,0:T(8,128)(2,1)}, u32[]{:S(2)}, u32[]{:S(2)}) %collective-permute-start.19) | collective-permute-done | bytes 1638432 | tf_op jit(solution)/shard_map/ppermute | solution.py:31
  281.2 25.0 %home.1 = (bf16[2,2,128,2048]{3,2,1,0:T(8,128)(2,1)}, bf16[2,128,3200]{2,1,0:T(8,128)(2,1)}, bf16[2,128,3200]{2,1,0:T(8,128)(2,1)}) custom-call(s32[1]{0:T(128)} %bitcast.3.core_ref, bf16[2,128,3200]{2,1,0:T(8,128)(2,1)} %get-tuple-element.21.own_ref.z_ref, bf16[2,128,3200]{2,1,0:T(8,128)(2,1)} %collective-permute-done.17.other_ref, ...), custom_call_target="tpu_custom_call" | custom-call | flops 13421772800 | bytes 13107200 | tf_op jit(solution)/shard_map/home/pallas_call | solution.py:304
  307.8 14.2 %owner.3 = bf16[2,2,128,2048]{3,2,1,0:T(8,128)(2,1)} custom-call(s32[1]{0:T(128)} %bitcast.3.core_ref, bf16[2,128,3200]{2,1,0:T(8,128)(2,1)} %collective-permute-done.21.own_ref, bf16[2,128,3200]{2,1,0:T(8,128)(2,1)} %copy-done.12, bf16[3200,2048]{1,0:T(8,128)(2,1)} %weight_ref.5, f32[1,2048]{1,0:T(1,128)} %bitcast.37), custom_call_target="tpu_custom_call" | custom-call | flops 6710886400 | bytes 13107200 | tf_op jit(solution)/shard_map/owner/pallas_call | solution.py:359
  323.1 14.9 %owner.2 = bf16[2,2,128,2048]{3,2,1,0:T(8,128)(2,1)} custom-call(s32[1]{0:T(128)} %bitcast.3.core_ref, bf16[2,128,3200]{2,1,0:T(8,128)(2,1)} %collective-permute-done.19.own_ref, bf16[2,128,3200]{2,1,0:T(8,128)(2,1)} %copy-done.13, bf16[3200,2048]{1,0:T(8,128)(2,1)} %weight_ref.5, f32[1,2048]{1,0:T(1,128)} %bitcast.38), custom_call_target="tpu_custom_call" | custom-call | flops 6710886400 | bytes 13107200 | tf_op jit(solution)/shard_map/owner/pallas_call | solution.py:359
  341.5 7.8 %final.1 = bf16[2,128,3200]{2,1,0:T(8,128)(2,1)} custom-call(bf16[2,128,3200]{2,1,0:T(8,128)(2,1)} %get-tuple-element.25.own_ref, bf16[2,128,3200]{2,1,0:T(8,128)(2,1)} %copy-done.3, bf16[2,128,3200]{2,1,0:T(8,128)(2,1)} %get-tuple-element.21.own_ref.z_ref, f32[2,128,128]{2,1,0:T(8,128)} %get-tuple-element.27.inverse_ref), custom_call_target="tpu_custom_call" | custom-call | tf_op jit(solution)/shard_map/final/pallas_call | solution.py:239
  (106 shorter events, 43.6 us)
Async XLA Ops:
  7.2 109.5 %all-gather.2.cloned.1.call-start = ((), (), s32[]{:S(2)}) async-start(), calls=%async_computation | async-start | bytes 5222400 | tf_op jit(solution)/shard_map/all_gather | solution.py:416
  12.1 5.9 %collective-permute-start.3 = (bf16[50,768]{1,0:T(8,128)(2,1)S(1)}, bf16[50,768]{1,0:T(8,128)(2,1)S(1)}, u32[]{:S(2)}, u32[]{:S(2)}) collective-permute-start(bf16[50,768]{1,0:T(8,128)(2,1)S(1)} %get-tuple-element.38), channel_id=1, source_target_pairs={{0,32},{32,64},{64,96},{96,0},{1,33},{33,65},{65,97},{97,1},{2,34}... | collective-permute-start | bytes 230408 | tf_op jit(solution)/shard_map/ppermute | solution.py:25
  12.1 5.9 %collective-permute-start.2 = (bf16[50,768]{1,0:T(8,128)(2,1)S(1)}, bf16[50,768]{1,0:T(8,128)(2,1)S(1)}, u32[]{:S(2)}, u32[]{:S(2)}) collective-permute-start(bf16[50,768]{1,0:T(8,128)(2,1)S(1)} %get-tuple-element.39), channel_id=1, source_target_pairs={{0,64},{32,96},{64,0},{96,32},{1,65},{33,97},{65,1},{97,33},{2,66}... | collective-permute-start | bytes 230408 | tf_op jit(solution)/shard_map/ppermute | solution.py:25
  25.9 35.7 %collective-permute-start.5 = (bf16[2,128,3200]{2,1,0:T(8,128)(2,1)}, bf16[2,128,3200]{2,1,0:T(8,128)(2,1)}, u32[]{:S(2)}, u32[]{:S(2)}) collective-permute-start(bf16[2,128,3200]{2,1,0:T(8,128)(2,1)} %norm.1.own_ref), channel_id=1, source_target_pairs={{0,96},{32,0},{64,32},{96,64},{1,97},{33,1},{65,33},{97,65},{2,98}... | collective-permute-start | bytes 4915208 | tf_op jit(solution)/shard_map/ppermute | solution.py:25
  27.5 36.2 %collective-permute-start.4 = (bf16[2,128,3200]{2,1,0:T(8,128)(2,1)}, bf16[2,128,3200]{2,1,0:T(8,128)(2,1)}, u32[]{:S(2)}, u32[]{:S(2)}) collective-permute-start(bf16[2,128,3200]{2,1,0:T(8,128)(2,1)} %norm.1.own_ref), channel_id=1, source_target_pairs={{0,32},{32,64},{64,96},{96,0},{1,33},{33,65},{65,97},{97,1},{2,34}... | collective-permute-start | bytes 4915208 | tf_op jit(solution)/shard_map/ppermute | solution.py:25
  31.7 29.9 %collective-permute-start.6 = (bf16[1,256,2048]{2,1,0:T(8,128)(2,1)S(1)}, bf16[1,256,2048]{2,1,0:T(8,128)(2,1)S(1)}, u32[]{:S(2)}, u32[]{:S(2)}) collective-permute-start(bf16[1,256,2048]{2,1,0:T(8,128)(2,1)S(1)} %get-tuple-element.31), channel_id=1, source_target_pairs={{0,4},{2,6},{4,8},{6,10},{8,12},{10,14},{12,16},{14,18},{16,20},{1... | collective-permute-start | bytes 3145736 | tf_op jit(solution)/shard_map/ppermute | solution.py:31
  34.0 50.1 %collective-permute-start.11 = (bf16[1,256,2048]{2,1,0:T(8,128)(2,1)S(1)}, bf16[1,256,2048]{2,1,0:T(8,128)(2,1)S(1)}, u32[]{:S(2)}, u32[]{:S(2)}) collective-permute-start(bf16[1,256,2048]{2,1,0:T(8,128)(2,1)S(1)} %get-tuple-element.30), channel_id=1, source_target_pairs={{0,4},{2,6},{4,8},{6,10},{8,12},{10,14},{12,16},{14,18},{16,20},{1... | collective-permute-start | bytes 3145736 | tf_op jit(solution)/shard_map/ppermute | solution.py:31
  66.2 17.9 %collective-permute-start.10 = (bf16[1,128,3200]{2,1,0:T(8,128)(2,1)S(1)}, bf16[1,128,3200]{2,1,0:T(8,128)(2,1)S(1)}, u32[]{:S(2)}, u32[]{:S(2)}) collective-permute-start(bf16[1,128,3200]{2,1,0:T(8,128)(2,1)S(1)} %slice.37), channel_id=1, source_target_pairs={{0,96},{32,0},{64,32},{96,64},{1,97},{33,1},{65,33},{97,65},{2,98}... | collective-permute-start | bytes 2457608 | tf_op jit(solution)/shard_map/ppermute | solution.py:25
  66.9 17.2 %collective-permute-start.9 = (bf16[1,128,3200]{2,1,0:T(8,128)(2,1)S(1)}, bf16[1,128,3200]{2,1,0:T(8,128)(2,1)S(1)}, u32[]{:S(2)}, u32[]{:S(2)}) collective-permute-start(bf16[1,128,3200]{2,1,0:T(8,128)(2,1)S(1)} %slice.36), channel_id=1, source_target_pairs={{0,32},{32,64},{64,96},{96,0},{1,33},{33,65},{65,97},{97,1},{2,34}... | collective-permute-start | bytes 2457608 | tf_op jit(solution)/shard_map/ppermute | solution.py:25
  84.3 9.4 %collective-permute-start.12 = (bf16[2,128,3200]{2,1,0:T(8,128)(2,1)S(1)}, bf16[2,128,3200]{2,1,0:T(8,128)(2,1)}, u32[]{:S(2)}, u32[]{:S(2)}) collective-permute-start(bf16[2,128,3200]{2,1,0:T(8,128)(2,1)S(1)} %constant_dynamic-update-slice_fusion.own_ref), channel_id=1, source_target_pairs={{0,1},{1,0},{2,3},{3,2},{4,5},{5,4},{6,7},{7,6},{8,9},{9,8},{10,11... | collective-permute-start | bytes 4915208 | tf_op jit(solution)/shard_map/ppermute | solution.py:21
  89.0 39.3 %collective-permute-start.7 = (bf16[2,128,3200]{2,1,0:T(8,128)(2,1)}, bf16[2,128,3200]{2,1,0:T(8,128)(2,1)}, u32[]{:S(2)}, u32[]{:S(2)}) collective-permute-start(bf16[2,128,3200]{2,1,0:T(8,128)(2,1)} %collective-permute-done.4.own_ref), channel_id=1, source_target_pairs={{0,1},{1,0},{2,3},{3,2},{4,5},{5,4},{6,7},{7,6},{8,9},{9,8},{10,11... | collective-permute-start | bytes 4915208 | tf_op jit(solution)/shard_map/ppermute | solution.py:21
  89.1 48.8 %collective-permute-start.14 = (bf16[2,128,3200]{2,1,0:T(8,128)(2,1)}, bf16[2,128,3200]{2,1,0:T(8,128)(2,1)}, u32[]{:S(2)}, u32[]{:S(2)}) collective-permute-start(bf16[2,128,3200]{2,1,0:T(8,128)(2,1)} %collective-permute-done.5.own_ref), channel_id=1, source_target_pairs={{0,1},{1,0},{2,3},{3,2},{4,5},{5,4},{6,7},{7,6},{8,9},{9,8},{10,11... | collective-permute-start | bytes 4915208 | tf_op jit(solution)/shard_map/ppermute | solution.py:21
  89.5 57.8 %collective-permute-start = (bf16[2,128,3200]{2,1,0:T(8,128)(2,1)S(1)}, bf16[2,128,3200]{2,1,0:T(8,128)(2,1)}, u32[]{:S(2)}, u32[]{:S(2)}) collective-permute-start(bf16[2,128,3200]{2,1,0:T(8,128)(2,1)S(1)} %copy-done.2), channel_id=1, source_target_pairs={{0,1},{1,0},{2,3},{3,2},{4,5},{5,4},{6,7},{7,6},{8,9},{9,8},{10,11... | collective-permute-start | bytes 4915208 | tf_op jit(solution)/shard_map/ppermute | solution.py:21
  125.4 30.7 %collective-permute-start.13 = (bf16[2,256,256]{2,1,0:T(8,128)(2,1)}, bf16[2,256,256]{2,1,0:T(8,128)(2,1)S(1)}, u32[]{:S(2)}, u32[]{:S(2)}) collective-permute-start(bf16[2,256,256]{2,1,0:T(8,128)(2,1)} %attend.6), channel_id=1, source_target_pairs={{0,64},{32,96},{64,0},{96,32},{1,65},{33,97},{65,1},{97,33},{2,66}... | collective-permute-start | bytes 786440 | tf_op jit(solution)/shard_map/ppermute | solution.py:25
  137.1 19.1 %collective-permute-start.8 = (bf16[2,256,256]{2,1,0:T(8,128)(2,1)}, bf16[2,256,256]{2,1,0:T(8,128)(2,1)S(1)}, u32[]{:S(2)}, u32[]{:S(2)}) collective-permute-start(bf16[2,256,256]{2,1,0:T(8,128)(2,1)} %attend.5), channel_id=1, source_target_pairs={{0,96},{32,0},{64,32},{96,64},{1,97},{33,1},{65,33},{97,65},{2,98}... | collective-permute-start | bytes 786440 | tf_op jit(solution)/shard_map/ppermute | solution.py:25
  146.7 9.5 %collective-permute-start.15 = (bf16[2,256,256]{2,1,0:T(8,128)(2,1)}, bf16[2,256,256]{2,1,0:T(8,128)(2,1)S(1)}, u32[]{:S(2)}, u32[]{:S(2)}) collective-permute-start(bf16[2,256,256]{2,1,0:T(8,128)(2,1)} %attend.7), channel_id=1, source_target_pairs={{0,32},{32,64},{64,96},{96,0},{1,33},{33,65},{65,97},{97,1},{2,34}... | collective-permute-start | bytes 786440 | tf_op jit(solution)/shard_map/ppermute | solution.py:25
  165.3 27.4 %collective-permute-start.16 = (bf16[2,128,3200]{2,1,0:T(8,128)(2,1)}, bf16[2,128,3200]{2,1,0:T(8,128)(2,1)}, u32[]{:S(2)}, u32[]{:S(2)}) collective-permute-start(bf16[2,128,3200]{2,1,0:T(8,128)(2,1)} %get-tuple-element.20), channel_id=1, source_target_pairs={{0,1},{1,0},{2,3},{3,2},{4,5},{5,4},{6,7},{7,6},{8,9},{9,8},{10,11... | collective-permute-start | bytes 4915208 | tf_op jit(solution)/shard_map/ppermute | solution.py:21
  170.7 100.1 %collective-permute-start.18 = (bf16[2,256,2048]{2,1,0:T(8,128)(2,1)}, bf16[2,256,2048]{2,1,0:T(8,128)(2,1)S(1)}, u32[]{:S(2)}, u32[]{:S(2)}) collective-permute-start(bf16[2,256,2048]{2,1,0:T(8,128)(2,1)} %constant_dynamic-slice_fusion), channel_id=1, source_target_pairs={{0,2},{2,4},{4,6},{6,8},{8,10},{10,12},{12,14},{14,16},{16,18},{18... | collective-permute-start | bytes 6291464 | tf_op jit(solution)/shard_map/ppermute | solution.py:31
  201.2 43.9 %collective-permute-start.21 = (bf16[2,128,3200]{2,1,0:T(8,128)(2,1)}, bf16[2,128,3200]{2,1,0:T(8,128)(2,1)}, u32[]{:S(2)}, u32[]{:S(2)}) collective-permute-start(bf16[2,128,3200]{2,1,0:T(8,128)(2,1)} %get-tuple-element.21.own_ref.z_ref), channel_id=1, source_target_pairs={{4,0},{6,2},{8,4},{10,6},{12,8},{14,10},{16,12},{18,14},{20,16},{2... | collective-permute-start | bytes 4915208 | tf_op jit(solution)/shard_map/ppermute | solution.py:31
  203.1 77.7 %collective-permute-start.19 = (bf16[2,128,3200]{2,1,0:T(8,128)(2,1)}, bf16[2,128,3200]{2,1,0:T(8,128)(2,1)}, u32[]{:S(2)}, u32[]{:S(2)}) collective-permute-start(bf16[2,128,3200]{2,1,0:T(8,128)(2,1)} %get-tuple-element.21.own_ref.z_ref), channel_id=1, source_target_pairs={{2,0},{4,2},{6,4},{8,6},{10,8},{12,10},{14,12},{16,14},{18,16},{20... | collective-permute-start | bytes 4915208 | tf_op jit(solution)/shard_map/ppermute | solution.py:31
  205.0 76.2 %collective-permute-start.17 = (bf16[2,128,3200]{2,1,0:T(8,128)(2,1)}, bf16[2,128,3200]{2,1,0:T(8,128)(2,1)}, u32[]{:S(2)}, u32[]{:S(2)}) collective-permute-start(bf16[2,128,3200]{2,1,0:T(8,128)(2,1)} %get-tuple-element.21.own_ref.z_ref), channel_id=1, source_target_pairs={{0,1},{1,0},{2,3},{3,2},{4,5},{5,4},{6,7},{7,6},{8,9},{9,8},{10,11... | collective-permute-start | bytes 4915208 | tf_op jit(solution)/shard_map/ppermute | solution.py:21
  245.1 61.6 %collective-permute-start.22 = (bf16[2,128,3200]{2,1,0:T(8,128)(2,1)}, bf16[2,128,3200]{2,1,0:T(8,128)(2,1)S(1)}, u32[]{:S(2)}, u32[]{:S(2)}) collective-permute-start(bf16[2,128,3200]{2,1,0:T(8,128)(2,1)} %collective-permute-done.21.own_ref), channel_id=1, source_target_pairs={{0,1},{1,0},{2,3},{3,2},{4,5},{5,4},{6,7},{7,6},{8,9},{9,8},{10,11... | collective-permute-start | bytes 4915208 | tf_op jit(solution)/shard_map/ppermute | solution.py:21
  280.8 41.2 %collective-permute-start.20 = (bf16[2,128,3200]{2,1,0:T(8,128)(2,1)}, bf16[2,128,3200]{2,1,0:T(8,128)(2,1)S(1)}, u32[]{:S(2)}, u32[]{:S(2)}) collective-permute-start(bf16[2,128,3200]{2,1,0:T(8,128)(2,1)} %collective-permute-done.19.own_ref), channel_id=1, source_target_pairs={{0,1},{1,0},{2,3},{3,2},{4,5},{5,4},{6,7},{7,6},{8,9},{9,8},{10,11... | collective-permute-start | bytes 4915208 | tf_op jit(solution)/shard_map/ppermute | solution.py:21
  306.3 34.0 %collective-permute-start.23 = (bf16[2,128,3200]{2,1,0:T(8,128)(2,1)}, bf16[2,128,3200]{2,1,0:T(8,128)(2,1)S(1)}, u32[]{:S(2)}, u32[]{:S(2)}) collective-permute-start(bf16[2,128,3200]{2,1,0:T(8,128)(2,1)} %get-tuple-element.26), channel_id=1, source_target_pairs={{0,1},{1,0},{2,3},{3,2},{4,5},{5,4},{6,7},{7,6},{8,9},{9,8},{10,11... | collective-permute-start | bytes 4915208 | tf_op jit(solution)/shard_map/ppermute | solution.py:21
  (16 other events, 142.7 us)
Sparse Core Ops, SparseCore 0:
  20.0 96.6 all-gather.1

commit v2 on v1

--- a/solution.py
+++ b/solution.py
@@ -29,6 +29,18 @@
     peers = lax.axis_size(IMG)
     pairs = [(i, i + by) for i in range(peers) if 0 <= i + by < peers]
     return lax.ppermute(array, IMG, pairs)
+
+
+def around(place, side):
+    return place - place % LINE + (place % LINE + side) % LINE
+
+
+def two_on(array, by):
+    peers = lax.axis_size(IMG)
+    side = -by // 2
+    ends = [(i, i + by) for i in range(peers) if 0 <= i + by < peers]
+    halfway = lax.ppermute(array, IMG, [(i, around(i, side)) for i, _ in ends])
+    return halfway, lambda held: lax.ppermute(held, IMG, [(around(i, side), j) for i, j in ends])
 
 
 def tile_owners(tile_counts, tile_total, tile_group):
@@ -140,21 +152,20 @@
     )(own, other, weight)
 
 
-def out_kernel(line_ref, *refs):
+def out_kernel(start, line_ref, *refs):
     attended = refs[:LINE]
     weights = refs[LINE : 2 * LINE]
-    own_ref, other_ref = refs[2 * LINE :]
-    tiles, half, block = own_ref.shape
-    for part_ref, start in ((other_ref, half), (own_ref, 0)):
-        total = None
-        for rows_ref, weight_ref in zip(attended, weights):
-            rows = rows_ref[:, start : start + half].reshape(tiles * half, rows_ref.shape[2])
-            term = jnp.dot(rows, weight_ref[...], preferred_element_type=jnp.float32)
-            total = term if total is None else total + term
-        part_ref[...] = total.astype(jnp.bfloat16).reshape(tiles, half, block)
-
-
-def out_project(line_arg, attended, out_weight):
+    part_ref = refs[2 * LINE]
+    tiles, half, block = part_ref.shape
+    total = None
+    for rows_ref, weight_ref in zip(attended, weights):
+        rows = rows_ref[...].reshape(tiles * half, rows_ref.shape[2])
+        term = jnp.dot(rows, weight_ref[...], preferred_element_type=jnp.float32)
+        total = term if total is None else total + term
+    part_ref[...] = total.astype(jnp.bfloat16).reshape(tiles, half, block)
+
+
+def out_project(line_arg, attended, out_weight, part):
     tiles, full, share = attended[0].shape
     half = full // 2
     depth = out_weight.shape[1]
@@ -163,18 +174,16 @@
     def weight_spec(k):
         return pl.BlockSpec((share, block), lambda n, line: ((line[0] + k) % LINE, n))
 
-    part = pl.BlockSpec((tiles, half, block), lambda n, line: (0, 0, n))
-    shape = jax.ShapeDtypeStruct((tiles, half, depth), jnp.bfloat16)
     return pl.pallas_call(
-        out_kernel,
+        functools.partial(out_kernel, part),
         grid_spec=pltpu.PrefetchScalarGridSpec(
             num_scalar_prefetch=1,
             grid=(depth // block,),
-            in_specs=[pl.BlockSpec((tiles, full, share), lambda n, line: (0, 0, 0))] * LINE
+            in_specs=[pl.BlockSpec((tiles, half, share), lambda n, line: (0, part, 0))] * LINE
             + [weight_spec(k) for k in range(LINE)],
-            out_specs=[part, part],
-        ),
-        out_shape=[shape, shape],
+            out_specs=pl.BlockSpec((tiles, half, block), lambda n, line: (0, 0, n)),
+        ),
+        out_shape=jax.ShapeDtypeStruct((tiles, half, depth), jnp.bfloat16),
         compiler_params=pltpu.CompilerParams(vmem_limit_bytes=VMEM_BYTES),
         cost_estimate=pl.CostEstimate(
             flops=2 * tiles * full * share * LINE * depth,
@@ -190,12 +199,11 @@
 ):
     inputs = tokens_ref[0].astype(jnp.float32)
     attended_out = own_ref[0].astype(jnp.float32) + other_ref[0].astype(jnp.float32)
-    layer_out = inputs + scale_ref[...] * attended_out
     joined = (
         mixing_ref[0] * early_ref[0].astype(jnp.float32)
         + mixing_ref[1] * mid_ref[0].astype(jnp.float32)
-        + mixing_ref[2] * inputs
-        + mixing_ref[3] * layer_out
+        + (mixing_ref[2] + mixing_ref[3]) * inputs
+        + (mixing_ref[3] * scale_ref[...]) * attended_out
     )
     centre = jnp.mean(joined, axis=-1, keepdims=True)
     shifted = joined - centre
@@ -206,7 +214,7 @@
 
 def join_rows(mixing, tokens, early, mid, own, other, scale):
     tiles, half, depth = tokens.shape
-    block = 32
+    block = 64
     spec = pl.BlockSpec((1, block, depth), lambda t, r: (t, r, 0))
     return pl.pallas_call(
         join_kernel,
@@ -234,7 +242,7 @@
 
 def final_rows(own, other, z_rows, inverse):
     tiles, half, depth = own.shape
-    block = 32
+    block = 64
     spec = pl.BlockSpec((1, block, depth), lambda t, r: (t, r, 0))
     return pl.pallas_call(
         final_kernel,
@@ -344,11 +352,14 @@
     core = core_ref[0]
     tiles, half, depth = own_ref.shape
     block = weight_ref.shape[1]
-    for rows_ref, place in ((own_ref, core), (other_ref, 1 - core)):
-        rows = rows_ref[...].reshape(tiles * half, depth)
-        preact = jnp.dot(rows, weight_ref[...], preferred_element_type=jnp.float32) + bias_ref[...]
-        projected = (preact * activate(preact)[0]).astype(jnp.bfloat16)
-        projected_ref[:, pl.ds(place, 1)] = projected.reshape(tiles, 1, half, block)
+    rows = jnp.concatenate(
+        [own_ref[...].reshape(tiles * half, depth), other_ref[...].reshape(tiles * half, depth)], axis=0
+    )
+    preact = jnp.dot(rows, weight_ref[...], preferred_element_type=jnp.float32) + bias_ref[...]
+    projected = (preact * activate(preact)[0]).astype(jnp.bfloat16)
+    projected = projected.reshape(2, tiles, 1, half, block)
+    projected_ref[:, pl.ds(core, 1)] = projected[0]
+    projected_ref[:, pl.ds(1 - core, 1)] = projected[1]
 
 
 def owner_project(core, own, other, weight, bias):
@@ -396,14 +407,6 @@
     owner_of, first_tile = tile_owners(tile_counts, tile_total, tile_group)
     my_first = first_tile[place]
 
-    far_back = []
-    for within in range(tile_group):
-        tile = (place + 2) * tile_group + within
-        slot = jnp.clip(tile - my_first, 0, own_tiles - 1)
-        far_back.append(along_img(lax.dynamic_slice_in_dim(grad_out, slot, 1, axis=0), 2))
-    slot = jnp.clip((place + 1) * tile_group - my_first, 0, own_tiles - tile_group)
-    near_back = along_img(lax.dynamic_slice_in_dim(grad_out, slot, tile_group, axis=0), 1)
-
     depth_share, width = qkv_weight.shape
     share = width // LINE
     received = []
@@ -411,34 +414,58 @@
         target = (line_place + distance) % LINE
         columns = lax.dynamic_slice_in_dim(qkv_weight, target * share, share, axis=1)
         received.append(along_z(columns, distance) if distance else columns)
+    normed = norm_rows(tokens)
+    normed, received = lax.optimization_barrier((normed, received))
     ladder = jnp.stack([received[(LINE - 1 - j) % LINE] for j in range(2 * LINE - 1)], axis=0)
     sent = lax.dynamic_slice_in_dim(ladder, LINE - 1 - line_place, LINE, axis=0)
-    gathered = lax.all_gather(sent.reshape(LINE * depth_share, share), ("y", "x"), axis=0, tiled=True)
-    weight = gathered
-
-    normed = norm_rows(tokens)
+    weight = lax.all_gather(sent.reshape(LINE * depth_share, share), ("y", "x"), axis=0, tiled=True)
+
     from_low = along_z(normed, 1)
     from_high = along_z(normed, -1)
-    from_low, from_high, far_back[0] = lax.optimization_barrier((from_low, from_high, far_back[0]))
     far_first = along_z(from_low[:1], 1)
     far_second = along_z(from_high[1:], -1)
-    far_first, far_second, far_back[1] = lax.optimization_barrier((far_first, far_second, far_back[1]))
+    far_first, far_second, weight, first_slot = lax.optimization_barrier(
+        (far_first, far_second, weight, my_first)
+    )
+    packets = []
+    for distance in (1, 2):
+        for within in range(tile_group):
+            tile = (place + distance) * tile_group + within
+            slot = jnp.clip(tile - first_slot, 0, own_tiles - 1)
+            packets.append(lax.dynamic_slice_in_dim(grad_out, slot, 1, axis=0))
+    halfway, far_on = two_on(packets[3], 2)
+    near_back = [along_img(packets[0], 1)]
+
     from_far = jnp.concatenate([far_first, far_second], axis=0)
     att_far = along_z(attend(from_far, swap(from_far), weight), 2)
     att_low = along_z(attend(from_low, swap(from_low), weight), -1)
     att_high = along_z(attend(from_high, swap(from_high), weight), 1)
     att_own = attend(normed, swap(normed), weight)
-    part_own, part_other = out_project(
-        line_place.astype(jnp.int32).reshape(1), [att_own, att_low, att_far, att_high], out_weight
-    )
+    att_own, halfway, near_back[0], packets[1] = lax.optimization_barrier(
+        (att_own, halfway, near_back[0], packets[1])
+    )
+    near_back.append(along_img(packets[1], 1))
+    far_back = [None, far_on(halfway)]
+    attended = [att_own, att_low, att_far, att_high]
+    line_arg = line_place.astype(jnp.int32).reshape(1)
+    part_other = swap(out_project(line_arg, attended, out_weight, 1))
+    part_own = out_project(line_arg, attended, out_weight, 0)
+    part_own, part_other, far_back[1], near_back[1], packets[2] = lax.optimization_barrier(
+        (part_own, part_other, far_back[1], near_back[1], packets[2])
+    )
+    far_back[0] = along_img(packets[2], 2)
     raised_logits = jnp.exp(layer_logits)
     mixing = raised_logits / jnp.sum(raised_logits)
     z_rows, inverse_std = join_rows(
-        mixing, tokens, tap_early, tap_mid, part_own, swap(part_other), layer_scale.reshape(1, -1)
-    )
-
-    near = along_img(z_rows, -1)
-    far = along_img(z_rows, -2)
+        mixing, tokens, tap_early, tap_mid, part_own, part_other, layer_scale.reshape(1, -1)
+    )
+
+    halfway, far_on = two_on(z_rows[1:], -2)
+    far_first = along_img(z_rows[:1], -2)
+    near_first = along_img(z_rows[:1], -1)
+    near_first, halfway, second = lax.optimization_barrier((near_first, halfway, z_rows[1:]))
+    near_second = along_img(second, -1)
+    far_second = far_on(halfway)
 
     back = []
     for within in range(tile_group):
@@ -450,7 +477,7 @@
             jnp.where(
                 owner == place,
                 here,
-                jnp.where(owner == place - 1, near_back[within], far_back[within][0]),
+                jnp.where(owner == place - 1, near_back[within][0], far_back[within][0]),
             )
         )
     back_rows = jnp.stack(back, axis=0)
@@ -459,18 +486,18 @@
     projected, grad_own, grad_other = home_rows(
         core_arg, z_rows, swap(z_rows), proj_weight, bias, back_rows
     )
+    far_first, _ = lax.optimization_barrier((far_first, grad_other))
     grad_joined = final_rows(grad_own, swap(grad_other), z_rows, inverse_std)
-
-    near_projected = owner_project(core_arg, near, swap(near), proj_weight, bias)
-    far_projected = owner_project(core_arg, far, swap(far), proj_weight, bias)
+    far_second, _ = lax.optimization_barrier((far_second, grad_joined))
+    near_second, _ = lax.optimization_barrier((near_second, grad_joined))
+    guests = [
+        owner_project(core_arg, rows, swap(rows), proj_weight, bias)
+        for rows in (near_first, near_second, far_first, far_second)
+    ]
 
     offset = my_first - place * tile_group
     held = first_tile[place + 1] - my_first
-    at_hand = [
-        source[within]
-        for source in (projected, near_projected, far_projected)
-        for within in range(tile_group)
-    ]
+    at_hand = [tile for source in (projected, *guests) for tile in source]
     slots = []
     for slot in range(own_tiles):
         later = at_hand[min(slot + 1, len(at_hand) - 1)]

time: 358 us -> 369 us (1.031)
  waiting for transfers between devices: 137 us -> 116 us
  starting transfers between devices: 52 us -> 69.7 us
  Pallas kernels: 120 us -> 130 us
  local copies, waits for them, and re-layouts: 17.2 us -> 21.3 us
    ppermute x5 -> x6, waiting for transfers between devices: 104 us -> 46.6 us  [along_img(): return lax.ppermute(array, IMG, pairs)]
    ppermute x10, waiting for transfers between devices: 6.65 us -> 50.1 us  [along_z(): return lax.ppermute(array, 'z', [(i, (i + by) % LINE) for i in range(LINE)])]
    all_gather x1, waiting for transfers between devices: 23 us -> 0.01 us  [on_device(): lax.all_gather(sent.reshape(LINE * depth_share, share), ('y', 'x'), axis=...]
    ppermute x0 -> x4, waiting for transfers between devices: none -> 18.7 us  [the longest x2 18.7 us: two_on(): lax.ppermute(held, IMG, [(around(i, side), j) for i, j in ends])]
    ppermute x0 -> x4, starting transfers between devices: none -> 10.7 us  [the longest x2 5.46 us: two_on(): lax.ppermute(held, IMG, [(around(i, side), j) for i, j in ends])]
    pallas_call x2 -> x4, Pallas kernels: 29 us -> 38.4 us  [owner_project(): pl.pallas_call(owner_kernel, grid_spec=pltpu.PrefetchScalarGridSpec(num_s...]
    pallas_call x1 -> x2, Pallas kernels: 8.25 us -> 13.6 us  [out_project(): pl.pallas_call(functools.partial(out_kernel, part), grid_spec=pltpu.Prefe...]
    ppermute x9 -> x11, starting transfers between devices: 9.84 us -> 14.1 us  [swap(): return lax.ppermute(array, 'head', [(0, 1), (1, 0)])]
  transfers between devices with their start and end apart: 25 -> 32, of which waited for: 10 -> 8; matrix products, arithmetic and copies ran while one was open for 5% -> 5% of each run, Pallas kernels for 29% -> 31%
where the time goes in v2:
time: 369 us; the launch traced here: 366 us
  Pallas kernels  130 us (35%)
  waiting for transfers between devices  116 us (31%)
  starting transfers between devices  69.7 us (19%)
  between operations  23.3 us (6%)
  local copies, waits for them, and re-layouts  21.3 us (6%)
  other arithmetic  7.09 us (2%)
    ppermute x10, waiting for transfers between devices, along_z(): return lax.ppermute(array, 'z', [(i, (i + by) % LINE) for i in range(LINE)])  50.1 us
    ppermute x6, waiting for transfers between devices, along_img(): return lax.ppermute(array, IMG, pairs)  46.6 us
    pallas_call x4, Pallas kernels, owner_project(): pl.pallas_call(owner_kernel, grid_spec=pltpu.PrefetchScalarGridSpec(num_s...  38.4 us
    pallas_call x4, Pallas kernels, attend(): pl.pallas_call(attend_kernel, grid=(depth // block,), out_shape=jax.Shape...  35.2 us
    ppermute x6, starting transfers between devices, along_img(): return lax.ppermute(array, IMG, pairs)  33 us
    pallas_call x1, Pallas kernels, home_rows(): pl.pallas_call(home_kernel, grid_spec=pltpu.PrefetchScalarGridSpec(num_sc...  25 us
    ppermute x2, waiting for transfers between devices, two_on(): lax.ppermute(held, IMG, [(around(i, side), j) for i, j in ends])  18.7 us
    ppermute x11, starting transfers between devices, swap(): return lax.ppermute(array, 'head', [(0, 1), (1, 0)])  14.1 us
  transfers between devices with their start and end apart: 32, of which 8 were waited for; matrix products, arithmetic and copies ran while one was open for 5% of the time, Pallas kernels for 31%

profile of v2, /device:TPU:31, one launch (start us, length us, event | category | flops | bytes accessed | tf_op | source)
XLA Modules:
  0.0 366.5 jit_solution(980576132878831884)
XLA Ops:
  13.5 6.0 %norm.1.own_ref = bf16[2,128,3200]{2,1,0:T(8,128)(2,1)} custom-call(bf16[2,128,3200]{2,1,0:T(8,128)(2,1)} %tokens_ref.3), custom_call_target="tpu_custom_call" | custom-call | tf_op jit(solution)/shard_map/norm/pallas_call | solution.py:78
  23.0 34.7 %collective-permute-done.6.own_ref = bf16[2,128,3200]{2,1,0:T(8,128)(2,1)S(1)} collective-permute-done((bf16[2,128,3200]{2,1,0:T(8,128)(2,1)S(1)}, bf16[2,128,3200]{2,1,0:T(8,128)(2,1)S(1)}, u32[]{:S(2)}, u32[]{:S(2)}) %collective-permute-start.6) | collective-permute-done | bytes 1638432 | tf_op jit(solution)/shard_map/ppermute | solution.py:25
  66.3 10.3 %collective-permute-done.7 = bf16[1,128,3200]{2,1,0:T(8,128)(2,1)S(1)} collective-permute-done((bf16[1,128,3200]{2,1,0:T(8,128)(2,1)}, bf16[1,128,3200]{2,1,0:T(8,128)(2,1)S(1)}, u32[]{:S(2)}, u32[]{:S(2)}) %collective-permute-start.7) | collective-permute-done | bytes 819232 | tf_op jit(solution)/shard_map/ppermute | solution.py:25
  76.6 5.1 %collective-permute-done.5 = bf16[1,128,3200]{2,1,0:T(8,128)(2,1)S(1)} collective-permute-done((bf16[1,128,3200]{2,1,0:T(8,128)(2,1)}, bf16[1,128,3200]{2,1,0:T(8,128)(2,1)S(1)}, u32[]{:S(2)}, u32[]{:S(2)}) %collective-permute-start.5) | collective-permute-done | bytes 819232 | tf_op jit(solution)/shard_map/ppermute | solution.py:25
  98.5 8.8 %attend.7 = bf16[2,256,256]{2,1,0:T(8,128)(2,1)} custom-call(bf16[2,128,3200]{2,1,0:T(8,128)(2,1)} %copy-done.20, bf16[2,128,3200]{2,1,0:T(8,128)(2,1)} %collective-permute-done.14.other_ref, bf16[3200,768]{1,0:T(8,128)(2,1)} %all-gather.2.cloned.1.call-done.weight_ref), custom_call_target="tpu_custom_call" | custom-call | flops 2516582400 | bytes 8192000 | tf_op jit(solution)/shard_map/attend/pallas_call | solution.py:134
  107.3 8.8 %attend.5 = bf16[2,256,256]{2,1,0:T(8,128)(2,1)} custom-call(bf16[2,128,3200]{2,1,0:T(8,128)(2,1)} %collective-permute-done.4.own_ref, bf16[2,128,3200]{2,1,0:T(8,128)(2,1)} %collective-permute-done.10.other_ref, bf16[3200,768]{1,0:T(8,128)(2,1)} %all-gather.2.cloned.1.call-done.weight_ref), custom_call_target="tpu_custom_call" | custom-call | flops 2516582400 | bytes 8192000 | tf_op jit(solution)/shard_map/attend/pallas_call | solution.py:134
  118.8 8.8 %attend.6 = bf16[2,256,256]{2,1,0:T(8,128)(2,1)} custom-call(bf16[2,128,3200]{2,1,0:T(8,128)(2,1)} %constant_dynamic-update-slice_fusion.own_ref, bf16[2,128,3200]{2,1,0:T(8,128)(2,1)} %collective-permute-done.12.other_ref, bf16[3200,768]{1,0:T(8,128)(2,1)} %all-gather.2.cloned.1.call-done.weight_ref), custom_call_target="tpu_custom_call" | custom-call | flops 2516582400 | bytes 8192000 | tf_op jit(solution)/shard_map/attend/pallas_call | solution.py:134
  127.6 8.8 %attend.4.refs_0_ = bf16[2,256,256]{2,1,0:T(8,128)(2,1)} custom-call(bf16[2,128,3200]{2,1,0:T(8,128)(2,1)} %norm.1.own_ref, bf16[2,128,3200]{2,1,0:T(8,128)(2,1)} %collective-permute-done.3.other_ref, bf16[3200,768]{1,0:T(8,128)(2,1)} %all-gather.2.cloned.1.call-done.weight_ref), custom_call_target="tpu_custom_call" | custom-call | flops 2516582400 | bytes 8192000 | tf_op jit(solution)/shard_map/attend/pallas_call | solution.py:134
  137.4 6.8 %out.3 = bf16[2,128,3200]{2,1,0:T(8,128)(2,1)} custom-call(s32[1]{0:T(128)} %bitcast.4.line_ref, bf16[2,256,256]{2,1,0:T(8,128)(2,1)} %attend.4.refs_0_, bf16[2,256,256]{2,1,0:T(8,128)(2,1)} %copy-done.8, bf16[2,256,256]{2,1,0:T(8,128)(2,1)} %copy-done.9, bf16[2,256,256]{2,1,0:T(8,128)(2,1)} %copy-done.7, bf16[1024,3200]{1,0:T(8,128)(2,1)} %refs_7_.3, ...), custom_call_target="tpu_custom_call" | custom-call | flops 3355443200 | bytes 6553600 | tf_op jit(solution)/shard_map/out/pallas_call | solution.py:177
  154.3 6.8 %out.2.own_ref = bf16[2,128,3200]{2,1,0:T(8,128)(2,1)} custom-call(s32[1]{0:T(128)} %bitcast.4.line_ref, bf16[2,256,256]{2,1,0:T(8,128)(2,1)} %attend.4.refs_0_, bf16[2,256,256]{2,1,0:T(8,128)(2,1)} %copy-done.8, bf16[2,256,256]{2,1,0:T(8,128)(2,1)} %copy-done.9, bf16[2,256,256]{2,1,0:T(8,128)(2,1)} %copy-done.7, bf16[1024,3200]{1,0:T(8,128)(2,1)} %refs_7_.3, ...), custom_call_target="tpu_custom_call" | custom-call | flops 3355443200 | bytes 6553600 | tf_op jit(solution)/shard_map/out/pallas_call | solution.py:177
  161.1 12.9 %collective-permute-done.17 = bf16[1,256,2048]{2,1,0:T(8,128)(2,1)S(1)} collective-permute-done((bf16[1,256,2048]{2,1,0:T(8,128)(2,1)}, bf16[1,256,2048]{2,1,0:T(8,128)(2,1)S(1)}, u32[]{:S(2)}, u32[]{:S(2)}) %collective-permute-start.17) | collective-permute-done | bytes 1048608 | tf_op jit(solution)/shard_map/ppermute | solution.py:43
  174.0 13.8 %collective-permute-done.18 = bf16[1,256,2048]{2,1,0:T(8,128)(2,1)S(1)} collective-permute-done((bf16[1,256,2048]{2,1,0:T(8,128)(2,1)S(1)}, bf16[1,256,2048]{2,1,0:T(8,128)(2,1)S(1)}, u32[]{:S(2)}, u32[]{:S(2)}) %collective-permute-start.18) | collective-permute-done | bytes 1048608 | tf_op jit(solution)/shard_map/ppermute | solution.py:31
  187.7 11.8 %collective-permute-start.20 = (bf16[1,256,2048]{2,1,0:T(8,128)(2,1)S(1)}, bf16[1,256,2048]{2,1,0:T(8,128)(2,1)}, u32[]{:S(2)}, u32[]{:S(2)}) collective-permute-start(bf16[1,256,2048]{2,1,0:T(8,128)(2,1)S(1)} %get-tuple-element.47), channel_id=1, source_target_pairs={{0,4},{2,6},{4,8},{6,10},{8,12},{10,14},{12,16},{14,18},{16,20},{1... | collective-permute-start | bytes 3145736 | tf_op jit(solution)/shard_map/ppermute | solution.py:31
  204.9 6.3 %join.1 = (bf16[2,128,3200]{2,1,0:T(8,128)(2,1)}, f32[2,128,128]{2,1,0:T(8,128)}) custom-call(f32[4]{0:T(128)} %exponential_divide_fusion.mixing_ref, bf16[2,128,3200]{2,1,0:T(8,128)(2,1)} %tokens_ref.3, bf16[2,128,3200]{2,1,0:T(8,128)(2,1)} %early_ref.1, bf16[2,128,3200]{2,1,0:T(8,128)(2,1)} %mid_ref.1, bf16[2,128,3200]{2,1,0:T(8,128)(2,1)} %out.2.own_ref, ...), custom_call_target="tpu_custom_call" | custom-call | tf_op jit(solution)/shard_map/join/pallas_call | solution.py:219
  215.8 5.4 %collective-permute-start.21 = (bf16[1,128,3200]{2,1,0:T(8,128)(2,1)S(1)}, bf16[1,128,3200]{2,1,0:T(8,128)(2,1)S(1)}, u32[]{:S(2)}, u32[]{:S(2)}) collective-permute-start(bf16[1,128,3200]{2,1,0:T(8,128)(2,1)S(1)} %get-tuple-element.69), channel_id=1, source_target_pairs={{2,0},{4,2},{6,4},{8,6},{10,8},{12,10},{14,12},{16,14},{18,16},{20... | collective-permute-start | bytes 2457608 | tf_op jit(solution)/shard_map/ppermute | solution.py:31
  225.9 25.0 %home.1 = (bf16[2,2,128,2048]{3,2,1,0:T(8,128)(2,1)}, bf16[2,128,3200]{2,1,0:T(8,128)(2,1)}, bf16[2,128,3200]{2,1,0:T(8,128)(2,1)}) custom-call(s32[1]{0:T(128)} %bitcast.3.core_ref, bf16[2,128,3200]{2,1,0:T(8,128)(2,1)} %get-tuple-element.45.own_ref.z_ref, bf16[2,128,3200]{2,1,0:T(8,128)(2,1)} %copy-done.24, bf16[3200,2048]{1,0:T(8,128)(2,1)} %weight_ref.9, ...), custom_call_target="tpu_custom_call" | custom-call | flops 13421772800 | bytes 13107200 | tf_op jit(solution)/shard_map/home/pallas_call | solution.py:312
  253.2 6.3 %collective-permute-start.27 = (bf16[1,128,3200]{2,1,0:T(8,128)(2,1)S(1)}, bf16[1,128,3200]{2,1,0:T(8,128)(2,1)S(1)}, u32[]{:S(2)}, u32[]{:S(2)}) collective-permute-start(bf16[1,128,3200]{2,1,0:T(8,128)(2,1)S(1)} %get-tuple-element.69), channel_id=1, source_target_pairs={{4,0},{6,2},{8,4},{10,6},{12,8},{14,10},{16,12},{18,14},{20,16},{2... | collective-permute-start | bytes 2457608 | tf_op jit(solution)/shard_map/ppermute | solution.py:31
  267.0 13.5 %collective-permute-done.27.own_ref = bf16[1,128,3200]{2,1,0:T(8,128)(2,1)S(1)} collective-permute-done((bf16[1,128,3200]{2,1,0:T(8,128)(2,1)S(1)}, bf16[1,128,3200]{2,1,0:T(8,128)(2,1)S(1)}, u32[]{:S(2)}, u32[]{:S(2)}) %collective-permute-start.27) | collective-permute-done | bytes 819232 | tf_op jit(solution)/shard_map/ppermute | solution.py:31
  287.4 19.4 %collective-permute-done.24.own_ref = bf16[1,128,3200]{2,1,0:T(8,128)(2,1)S(1)} collective-permute-done((bf16[1,128,3200]{2,1,0:T(8,128)(2,1)S(1)}, bf16[1,128,3200]{2,1,0:T(8,128)(2,1)S(1)}, u32[]{:S(2)}, u32[]{:S(2)}) %collective-permute-start.24) | collective-permute-done | bytes 819232 | tf_op jit(solution)/shard_map/ppermute | solution.py:31
  309.5 5.8 %collective-permute-done.29.own_ref = bf16[1,128,3200]{2,1,0:T(8,128)(2,1)S(1)} collective-permute-done((bf16[1,128,3200]{2,1,0:T(8,128)(2,1)}, bf16[1,128,3200]{2,1,0:T(8,128)(2,1)S(1)}, u32[]{:S(2)}, u32[]{:S(2)}) %collective-permute-start.29) | collective-permute-done | bytes 819232 | tf_op jit(solution)/shard_map/ppermute | solution.py:43
  316.2 9.6 %owner.4 = bf16[1,2,128,2048]{3,2,1,0:T(8,128)(2,1)} custom-call(s32[1]{0:T(128)} %bitcast.3.core_ref, bf16[1,128,3200]{2,1,0:T(8,128)(2,1)} %copy-done.16, bf16[1,128,3200]{2,1,0:T(8,128)(2,1)} %collective-permute-done.23.other_ref, bf16[3200,2048]{1,0:T(8,128)(2,1)} %weight_ref.9, f32[1,2048]{1,0:T(1,128)} %bitcast.36), custom_call_target="tpu_custom_call" | custom-call | flops 3355443200 | bytes 13107200 | tf_op jit(solution)/shard_map/owner/pallas_call | solution.py:370
  325.8 9.6 %owner.6 = bf16[1,2,128,2048]{3,2,1,0:T(8,128)(2,1)} custom-call(s32[1]{0:T(128)} %bitcast.3.core_ref, bf16[1,128,3200]{2,1,0:T(8,128)(2,1)} %copy-done.17, bf16[1,128,3200]{2,1,0:T(8,128)(2,1)} %collective-permute-done.28.other_ref, bf16[3200,2048]{1,0:T(8,128)(2,1)} %weight_ref.9, f32[1,2048]{1,0:T(1,128)} %bitcast.37), custom_call_target="tpu_custom_call" | custom-call | flops 3355443200 | bytes 13107200 | tf_op jit(solution)/shard_map/owner/pallas_call | solution.py:370
  335.4 9.6 %owner.5 = bf16[1,2,128,2048]{3,2,1,0:T(8,128)(2,1)} custom-call(s32[1]{0:T(128)} %bitcast.3.core_ref, bf16[1,128,3200]{2,1,0:T(8,128)(2,1)} %copy-done.19, bf16[1,128,3200]{2,1,0:T(8,128)(2,1)} %collective-permute-done.26.other_ref, bf16[3200,2048]{1,0:T(8,128)(2,1)} %weight_ref.9, f32[1,2048]{1,0:T(1,128)} %bitcast.38), custom_call_target="tpu_custom_call" | custom-call | flops 3355443200 | bytes 13107200 | tf_op jit(solution)/shard_map/owner/pallas_call | solution.py:370
  345.0 9.7 %owner.7 = bf16[1,2,128,2048]{3,2,1,0:T(8,128)(2,1)} custom-call(s32[1]{0:T(128)} %bitcast.3.core_ref, bf16[1,128,3200]{2,1,0:T(8,128)(2,1)} %copy-done.18, bf16[1,128,3200]{2,1,0:T(8,128)(2,1)} %collective-permute-done.30.other_ref, bf16[3200,2048]{1,0:T(8,128)(2,1)} %weight_ref.9, f32[1,2048]{1,0:T(1,128)} %bitcast.39), custom_call_target="tpu_custom_call" | custom-call | flops 3355443200 | bytes 13107200 | tf_op jit(solution)/shard_map/owner/pallas_call | solution.py:370
  (145 shorter events, 79.6 us)
Async XLA Ops:
  7.2 74.5 %all-gather.2.cloned.1.call-start = ((), (), s32[]{:S(2)}) async-start(), calls=%async_computation | async-start | bytes 5222400 | tf_op jit(solution)/shard_map/all_gather | solution.py:421
  21.0 36.6 %collective-permute-start.6 = (bf16[2,128,3200]{2,1,0:T(8,128)(2,1)S(1)}, bf16[2,128,3200]{2,1,0:T(8,128)(2,1)S(1)}, u32[]{:S(2)}, u32[]{:S(2)}) collective-permute-start(bf16[2,128,3200]{2,1,0:T(8,128)(2,1)S(1)} %copy-done.4), channel_id=1, source_target_pairs={{0,96},{32,0},{64,32},{96,64},{1,97},{33,1},{65,33},{97,65},{2,98}... | collective-permute-start | bytes 4915208 | tf_op jit(solution)/shard_map/ppermute | solution.py:25
  22.4 38.4 %collective-permute-start.4 = (bf16[2,128,3200]{2,1,0:T(8,128)(2,1)S(1)}, bf16[2,128,3200]{2,1,0:T(8,128)(2,1)}, u32[]{:S(2)}, u32[]{:S(2)}) collective-permute-start(bf16[2,128,3200]{2,1,0:T(8,128)(2,1)S(1)} %copy-done.4), channel_id=1, source_target_pairs={{0,32},{32,64},{64,96},{96,0},{1,33},{33,65},{65,97},{97,1},{2,34}... | collective-permute-start | bytes 4915208 | tf_op jit(solution)/shard_map/ppermute | solution.py:25
  64.0 31.2 %collective-permute-start.14 = (bf16[2,128,3200]{2,1,0:T(8,128)(2,1)}, bf16[2,128,3200]{2,1,0:T(8,128)(2,1)}, u32[]{:S(2)}, u32[]{:S(2)}) collective-permute-start(bf16[2,128,3200]{2,1,0:T(8,128)(2,1)} %copy-done.20), channel_id=1, source_target_pairs={{0,1},{1,0},{2,3},{3,2},{4,5},{5,4},{6,7},{7,6},{8,9},{9,8},{10,11... | collective-permute-start | bytes 4915208 | tf_op jit(solution)/shard_map/ppermute | solution.py:21
  66.3 41.0 %collective-permute-start.10 = (bf16[2,128,3200]{2,1,0:T(8,128)(2,1)}, bf16[2,128,3200]{2,1,0:T(8,128)(2,1)}, u32[]{:S(2)}, u32[]{:S(2)}) collective-permute-start(bf16[2,128,3200]{2,1,0:T(8,128)(2,1)} %collective-permute-done.4.own_ref), channel_id=1, source_target_pairs={{0,1},{1,0},{2,3},{3,2},{4,5},{5,4},{6,7},{7,6},{8,9},{9,8},{10,11... | collective-permute-start | bytes 4915208 | tf_op jit(solution)/shard_map/ppermute | solution.py:21
  83.6 32.6 %collective-permute-start.12 = (bf16[2,128,3200]{2,1,0:T(8,128)(2,1)}, bf16[2,128,3200]{2,1,0:T(8,128)(2,1)}, u32[]{:S(2)}, u32[]{:S(2)}) collective-permute-start(bf16[2,128,3200]{2,1,0:T(8,128)(2,1)} %constant_dynamic-update-slice_fusion.own_ref), channel_id=1, source_target_pairs={{0,1},{1,0},{2,3},{3,2},{4,5},{5,4},{6,7},{7,6},{8,9},{9,8},{10,11... | collective-permute-start | bytes 4915208 | tf_op jit(solution)/shard_map/ppermute | solution.py:21
  86.9 40.8 %collective-permute-start.3 = (bf16[2,128,3200]{2,1,0:T(8,128)(2,1)S(1)}, bf16[2,128,3200]{2,1,0:T(8,128)(2,1)}, u32[]{:S(2)}, u32[]{:S(2)}) collective-permute-start(bf16[2,128,3200]{2,1,0:T(8,128)(2,1)S(1)} %copy-done.4), channel_id=1, source_target_pairs={{0,1},{1,0},{2,3},{3,2},{4,5},{5,4},{6,7},{7,6},{8,9},{9,8},{10,11... | collective-permute-start | bytes 4915208 | tf_op jit(solution)/shard_map/ppermute | solution.py:21
  93.2 43.2 %collective-permute-start.9 = (bf16[1,256,2048]{2,1,0:T(8,128)(2,1)}, bf16[1,256,2048]{2,1,0:T(8,128)(2,1)S(1)}, u32[]{:S(2)}, u32[]{:S(2)}) collective-permute-start(bf16[1,256,2048]{2,1,0:T(8,128)(2,1)} %get-tuple-element.64), channel_id=1, source_target_pairs={{0,2},{2,4},{4,6},{6,8},{8,10},{10,12},{12,14},{14,16},{16,18},{18... | collective-permute-start | bytes 3145736 | tf_op jit(solution)/shard_map/ppermute | solution.py:31
  95.2 41.3 %collective-permute-start.8 = (bf16[1,256,2048]{2,1,0:T(8,128)(2,1)S(1)}, bf16[1,256,2048]{2,1,0:T(8,128)(2,1)}, u32[]{:S(2)}, u32[]{:S(2)}) collective-permute-start(bf16[1,256,2048]{2,1,0:T(8,128)(2,1)S(1)} %get-tuple-element.65), channel_id=1, source_target_pairs={{0,6},{2,0},{4,2},{6,4},{8,14},{10,8},{12,10},{14,12},{16,22},{18,... | collective-permute-start | bytes 3145736 | tf_op jit(solution)/shard_map/ppermute | solution.py:42
  107.3 29.1 %collective-permute-start.15 = (bf16[2,256,256]{2,1,0:T(8,128)(2,1)}, bf16[2,256,256]{2,1,0:T(8,128)(2,1)S(1)}, u32[]{:S(2)}, u32[]{:S(2)}) collective-permute-start(bf16[2,256,256]{2,1,0:T(8,128)(2,1)} %attend.7), channel_id=1, source_target_pairs={{0,32},{32,64},{64,96},{96,0},{1,33},{33,65},{65,97},{97,1},{2,34}... | collective-permute-start | bytes 786440 | tf_op jit(solution)/shard_map/ppermute | solution.py:25
  144.2 43.5 %collective-permute-start.16 = (bf16[2,128,3200]{2,1,0:T(8,128)(2,1)}, bf16[2,128,3200]{2,1,0:T(8,128)(2,1)S(1)}, u32[]{:S(2)}, u32[]{:S(2)}) collective-permute-start(bf16[2,128,3200]{2,1,0:T(8,128)(2,1)} %out.3), channel_id=1, source_target_pairs={{0,1},{1,0},{2,3},{3,2},{4,5},{5,4},{6,7},{7,6},{8,9},{9,8},{10,11... | collective-permute-start | bytes 4915208 | tf_op jit(solution)/shard_map/ppermute | solution.py:21
  145.9 28.1 %collective-permute-start.17 = (bf16[1,256,2048]{2,1,0:T(8,128)(2,1)}, bf16[1,256,2048]{2,1,0:T(8,128)(2,1)S(1)}, u32[]{:S(2)}, u32[]{:S(2)}) collective-permute-start(bf16[1,256,2048]{2,1,0:T(8,128)(2,1)} %collective-permute-done.8), channel_id=1, source_target_pairs={{6,4},{0,6},{2,8},{4,10},{14,12},{8,14},{10,16},{12,18},{22,20},{1... | collective-permute-start | bytes 3145736 | tf_op jit(solution)/shard_map/ppermute | solution.py:43
  148.4 39.4 %collective-permute-start.18 = (bf16[1,256,2048]{2,1,0:T(8,128)(2,1)S(1)}, bf16[1,256,2048]{2,1,0:T(8,128)(2,1)S(1)}, u32[]{:S(2)}, u32[]{:S(2)}) collective-permute-start(bf16[1,256,2048]{2,1,0:T(8,128)(2,1)S(1)} %get-tuple-element.42), channel_id=1, source_target_pairs={{0,2},{2,4},{4,6},{6,8},{8,10},{10,12},{12,14},{14,16},{16,18},{18... | collective-permute-start | bytes 3145736 | tf_op jit(solution)/shard_map/ppermute | solution.py:31
  187.7 33.6 %collective-permute-start.20 = (bf16[1,256,2048]{2,1,0:T(8,128)(2,1)S(1)}, bf16[1,256,2048]{2,1,0:T(8,128)(2,1)}, u32[]{:S(2)}, u32[]{:S(2)}) collective-permute-start(bf16[1,256,2048]{2,1,0:T(8,128)(2,1)S(1)} %get-tuple-element.47), channel_id=1, source_target_pairs={{0,4},{2,6},{4,8},{6,10},{8,12},{10,14},{12,16},{14,18},{16,20},{1... | collective-permute-start | bytes 3145736 | tf_op jit(solution)/shard_map/ppermute | solution.py:31
  213.9 45.5 %collective-permute-start.22 = (bf16[1,128,3200]{2,1,0:T(8,128)(2,1)S(1)}, bf16[1,128,3200]{2,1,0:T(8,128)(2,1)}, u32[]{:S(2)}, u32[]{:S(2)}) collective-permute-start(bf16[1,128,3200]{2,1,0:T(8,128)(2,1)S(1)} %get-tuple-element.52), channel_id=1, source_target_pairs={{4,6},{6,0},{8,10},{10,12},{12,14},{14,8},{16,18},{18,20},{20,22},... | collective-permute-start | bytes 2457608 | tf_op jit(solution)/shard_map/ppermute | solution.py:42
  215.8 43.6 %collective-permute-start.21 = (bf16[1,128,3200]{2,1,0:T(8,128)(2,1)S(1)}, bf16[1,128,3200]{2,1,0:T(8,128)(2,1)S(1)}, u32[]{:S(2)}, u32[]{:S(2)}) collective-permute-start(bf16[1,128,3200]{2,1,0:T(8,128)(2,1)S(1)} %get-tuple-element.69), channel_id=1, source_target_pairs={{2,0},{4,2},{6,4},{8,6},{10,8},{12,10},{14,12},{16,14},{18,16},{20... | collective-permute-start | bytes 2457608 | tf_op jit(solution)/shard_map/ppermute | solution.py:31
  250.9 30.4 %collective-permute-start.25 = (bf16[2,128,3200]{2,1,0:T(8,128)(2,1)}, bf16[2,128,3200]{2,1,0:T(8,128)(2,1)S(1)}, u32[]{:S(2)}, u32[]{:S(2)}) collective-permute-start(bf16[2,128,3200]{2,1,0:T(8,128)(2,1)} %get-tuple-element.54), channel_id=1, source_target_pairs={{0,1},{1,0},{2,3},{3,2},{4,5},{5,4},{6,7},{7,6},{8,9},{9,8},{10,11... | collective-permute-start | bytes 4915208 | tf_op jit(solution)/shard_map/ppermute | solution.py:21
  253.2 27.3 %collective-permute-start.27 = (bf16[1,128,3200]{2,1,0:T(8,128)(2,1)S(1)}, bf16[1,128,3200]{2,1,0:T(8,128)(2,1)S(1)}, u32[]{:S(2)}, u32[]{:S(2)}) collective-permute-start(bf16[1,128,3200]{2,1,0:T(8,128)(2,1)S(1)} %get-tuple-element.69), channel_id=1, source_target_pairs={{4,0},{6,2},{8,4},{10,6},{12,8},{14,10},{16,12},{18,14},{20,16},{2... | collective-permute-start | bytes 2457608 | tf_op jit(solution)/shard_map/ppermute | solution.py:31
  259.5 47.3 %collective-permute-start.24 = (bf16[1,128,3200]{2,1,0:T(8,128)(2,1)S(1)}, bf16[1,128,3200]{2,1,0:T(8,128)(2,1)S(1)}, u32[]{:S(2)}, u32[]{:S(2)}) collective-permute-start(bf16[1,128,3200]{2,1,0:T(8,128)(2,1)S(1)} %get-tuple-element.52), channel_id=1, source_target_pairs={{2,0},{4,2},{6,4},{8,6},{10,8},{12,10},{14,12},{16,14},{18,16},{20... | collective-permute-start | bytes 2457608 | tf_op jit(solution)/shard_map/ppermute | solution.py:31
  263.1 52.2 %collective-permute-start.29 = (bf16[1,128,3200]{2,1,0:T(8,128)(2,1)}, bf16[1,128,3200]{2,1,0:T(8,128)(2,1)S(1)}, u32[]{:S(2)}, u32[]{:S(2)}) collective-permute-start(bf16[1,128,3200]{2,1,0:T(8,128)(2,1)} %collective-permute-done.22), channel_id=1, source_target_pairs={{6,0},{0,2},{10,4},{12,6},{14,8},{8,10},{18,12},{20,14},{22,16},{1... | collective-permute-start | bytes 2457608 | tf_op jit(solution)/shard_map/ppermute | solution.py:43
  266.1 50.1 %collective-permute-start.23 = (bf16[1,128,3200]{2,1,0:T(8,128)(2,1)S(1)}, bf16[1,128,3200]{2,1,0:T(8,128)(2,1)}, u32[]{:S(2)}, u32[]{:S(2)}) collective-permute-start(bf16[1,128,3200]{2,1,0:T(8,128)(2,1)S(1)} %collective-permute-done.21.own_ref), channel_id=1, source_target_pairs={{0,1},{1,0},{2,3},{3,2},{4,5},{5,4},{6,7},{7,6},{8,9},{9,8},{10,11... | collective-permute-start | bytes 2457608 | tf_op jit(solution)/shard_map/ppermute | solution.py:21
  280.5 45.3 %collective-permute-start.28 = (bf16[1,128,3200]{2,1,0:T(8,128)(2,1)S(1)}, bf16[1,128,3200]{2,1,0:T(8,128)(2,1)}, u32[]{:S(2)}, u32[]{:S(2)}) collective-permute-start(bf16[1,128,3200]{2,1,0:T(8,128)(2,1)S(1)} %collective-permute-done.27.own_ref), channel_id=1, source_target_pairs={{0,1},{1,0},{2,3},{3,2},{4,5},{5,4},{6,7},{7,6},{8,9},{9,8},{10,11... | collective-permute-start | bytes 2457608 | tf_op jit(solution)/shard_map/ppermute | solution.py:21
  306.8 28.6 %collective-permute-start.26 = (bf16[1,128,3200]{2,1,0:T(8,128)(2,1)S(1)}, bf16[1,128,3200]{2,1,0:T(8,128)(2,1)}, u32[]{:S(2)}, u32[]{:S(2)}) collective-permute-start(bf16[1,128,3200]{2,1,0:T(8,128)(2,1)S(1)} %collective-permute-done.24.own_ref), channel_id=1, source_target_pairs={{0,1},{1,0},{2,3},{3,2},{4,5},{5,4},{6,7},{7,6},{8,9},{9,8},{10,11... | collective-permute-start | bytes 2457608 | tf_op jit(solution)/shard_map/ppermute | solution.py:21
  315.3 29.7 %collective-permute-start.30 = (bf16[1,128,3200]{2,1,0:T(8,128)(2,1)S(1)}, bf16[1,128,3200]{2,1,0:T(8,128)(2,1)}, u32[]{:S(2)}, u32[]{:S(2)}) collective-permute-start(bf16[1,128,3200]{2,1,0:T(8,128)(2,1)S(1)} %collective-permute-done.29.own_ref), channel_id=1, source_target_pairs={{0,1},{1,0},{2,3},{3,2},{4,5},{5,4},{6,7},{7,6},{8,9},{9,8},{10,11... | collective-permute-start | bytes 2457608 | tf_op jit(solution)/shard_map/ppermute | solution.py:21
  (34 other events, 488.5 us)
Sparse Core Ops, SparseCore 0:
  20.7 53.9 all-gather.1

commit v3 on v2

v3 whole, which is shorter than its diff:
```python
import functools
import math

import jax
import jax.numpy as jnp
from jax import lax
from jax.experimental import pallas as pl
from jax.experimental.pallas import tpu as pltpu
from jax.sharding import Mesh, PartitionSpec as P

HEAD_DIM = 128
LINE = 4
IMG = ("z", "y", "x")
VMEM_BYTES = 56 * 1024 * 1024
SMALL_COST = pl.CostEstimate(flops=1, bytes_accessed=1, transcendentals=0)

inv_root_two = 0.7071067811865476
inv_root_tau = 0.3989422804014327


def swap(array):
    return lax.ppermute(array, "head", [(0, 1), (1, 0)])


def along_z(array, by):
    return lax.ppermute(array, "z", [(i, (i + by) % LINE) for i in range(LINE)])


def along_img(array, by):
    peers = lax.axis_size(IMG)
    pairs = [(i, i + by) for i in range(peers) if 0 <= i + by < peers]
    return lax.ppermute(array, IMG, pairs)


def around(place, side):
    return place - place % LINE + (place % LINE + side) % LINE


def ring_x(array, by):
    peers = lax.axis_size(IMG)
    return lax.ppermute(array, IMG, [(i, around(i, by)) for i in range(peers)])


def next_line(array, columns):
    peers = lax.axis_size(IMG)
    pairs = [(i, i + LINE) for i in range(peers - LINE) if i % LINE < columns]
    return lax.ppermute(array, IMG, pairs)


def two_back(array):
    peers = lax.axis_size(IMG)

    def middle(i):
        return i - LINE + 1 if i % LINE == 1 else around(i, 1)

    ends = [(i, i - 2) for i in range(2, peers)]
    halfway = lax.ppermute(array, IMG, [(i, middle(i)) for i, _ in ends])
    return halfway, lambda held: lax.ppermute(held, IMG, [(middle(i), j) for i, j in ends])


def tile_owners(tile_counts, tile_total, tile_group):
    starts = jnp.cumsum(tile_counts) - tile_counts
    tile_index = jnp.arange(tile_total, dtype=jnp.int32)
    start_of = jnp.max(
        jnp.where(starts[None, :] <= tile_index[:, None], starts[None, :], -1), axis=1
    )
    owner_of = start_of // tile_group
    owners_total = tile_total // tile_group
    edge_tiles = jnp.arange(owners_total + 1, dtype=jnp.int32) * tile_group
    first_tile = jnp.min(
        jnp.where(starts[None, :] >= edge_tiles[:, None], starts[None, :], tile_total), axis=1
    )
    return (owner_of, first_tile)


def norm_kernel(tokens_ref, out_ref, ordered):
    rows = tokens_ref[0].astype(jnp.float32)
    normed = rows * lax.rsqrt(jnp.mean(rows * rows, axis=-1, keepdims=True) + 1e-06)
    groups = LINE * LINE
    share = rows.shape[1] // (LINE * groups)
    for line in range(LINE):
        for group in range(groups):
            source = (line * groups + group) * share
            target = (group * LINE + line) * share
            ordered[:, target : target + share] = normed[:, source : source + share]
    out_ref[0] = ordered[...].astype(jnp.bfloat16)


def norm_rows(tokens):
    tiles, half, depth = tokens.shape
    block = 64
    spec = pl.BlockSpec((1, block, depth), lambda t, r: (t, r, 0))
    return pl.pallas_call(
        norm_kernel,
        grid=(tiles, half // block),
        out_shape=jax.ShapeDtypeStruct(tokens.shape, jnp.bfloat16),
        in_specs=[spec],
        out_specs=spec,
        scratch_shapes=[pltpu.VMEM((block, depth), jnp.float32)],
        compiler_params=pltpu.CompilerParams(vmem_limit_bytes=VMEM_BYTES),
        cost_estimate=SMALL_COST,
        name="norm",
    )(tokens)


def attend_kernel(count, *refs):
    sources, weight_hbm = refs[: 2 * count], refs[2 * count]
    outs = refs[2 * count + 1 : 3 * count + 1]
    rows, weight, qkv, row_sems, weight_sem = refs[3 * count + 1 :]
    _, _, tiles, half, depth = rows.shape
    heads = weight.shape[1] // (3 * HEAD_DIM)

    def fetch(index):
        slot = index % 2
        return [
            pltpu.make_async_copy(sources[2 * index + part], rows.at[slot, part], row_sems.at[slot, part])
            for part in range(2)
        ]

    weight_copy = pltpu.make_async_copy(weight_hbm, weight, weight_sem)
    pending = fetch(0)
    for copy in pending:
        copy.start()
    weight_copy.start()
    for index in range(count):
        current = pending
        if index + 1 < count:
            pending = fetch(index + 1)
            for copy in pending:
                copy.start()
        for copy in current:
            copy.wait()
        if index == 0:
            weight_copy.wait()
        block = rows[index % 2].reshape(2 * tiles * half, depth)
        qkv[...] = jnp.dot(block, weight[...], preferred_element_type=jnp.float32).astype(jnp.bfloat16)
        for tile in range(tiles):
            for head in range(heads):

                def piece(kind):
                    start = (head * 3 + kind) * HEAD_DIM
                    columns = slice(start, start + HEAD_DIM)
                    low = qkv[tile * half : (tile + 1) * half, columns]
                    high = qkv[(tiles + tile) * half : (tiles + tile + 1) * half, columns]
                    return jnp.concatenate([low, high], axis=0)

                scores = lax.dot_general(
                    piece(0), piece(1), (((1,), (1,)), ((), ())), preferred_element_type=jnp.float32
                ) * (1.0 / math.sqrt(HEAD_DIM))
                scores = scores - jnp.max(scores, axis=-1, keepdims=True)
                raised = jnp.exp(scores)
                inverse = 1.0 / jnp.sum(raised, axis=-1, keepdims=True)
                soft = (raised * inverse).astype(jnp.bfloat16)
                mixed = jnp.dot(soft, piece(2), preferred_element_type=jnp.float32)
                outs[index][tile, :, head * HEAD_DIM : (head + 1) * HEAD_DIM] = mixed.astype(jnp.bfloat16)


def attend(pairs, weight):
    count = len(pairs)
    tiles, half, depth = pairs[0][0].shape
    width = weight.shape[1]
    shape = (tiles, 2 * half, width // 3)
    return pl.pallas_call(
        functools.partial(attend_kernel, count),
        out_shape=[jax.ShapeDtypeStruct(shape, jnp.bfloat16)] * count,
        in_specs=[pl.BlockSpec(memory_space=pl.ANY)] * (2 * count + 1),
        out_specs=[pl.BlockSpec(memory_space=pltpu.VMEM)] * count,
        scratch_shapes=[
            pltpu.VMEM((2, 2, tiles, half, depth), jnp.bfloat16),
            pltpu.VMEM((depth, width), jnp.bfloat16),
            pltpu.VMEM((2 * tiles * half, width), jnp.bfloat16),
            pltpu.SemaphoreType.DMA((2, 2)),
            pltpu.SemaphoreType.DMA,
        ],
        compiler_params=pltpu.CompilerParams(vmem_limit_bytes=VMEM_BYTES),
        cost_estimate=SMALL_COST,
        name="attend",
    )(*[rows for pair in pairs for rows in pair], weight)


def out_kernel(start, line_ref, *refs):
    attended = refs[:LINE]
    weights = refs[LINE : 2 * LINE]
    part_ref = refs[2 * LINE]
    tiles, half, block = part_ref.shape
    total = None
    for rows_ref, weight_ref in zip(attended, weights):
        rows = rows_ref[...].reshape(tiles * half, rows_ref.shape[2])
        term = jnp.dot(rows, weight_ref[...], preferred_element_type=jnp.float32)
        total = term if total is None else total + term
    part_ref[...] = total.astype(jnp.bfloat16).reshape(tiles, half, block)


def out_project(line_arg, attended, out_weight, part):
    tiles, full, share = attended[0].shape
    half = full // 2
    depth = out_weight.shape[1]
    block = 640

    def weight_spec(k):
        return pl.BlockSpec((share, block), lambda n, line: ((line[0] + k) % LINE, n))

    return pl.pallas_call(
        functools.partial(out_kernel, part),
        grid_spec=pltpu.PrefetchScalarGridSpec(
            num_scalar_prefetch=1,
            grid=(depth // block,),
            in_specs=[pl.BlockSpec((tiles, half, share), lambda n, line: (0, part, 0))] * LINE
            + [weight_spec(k) for k in range(LINE)],
            out_specs=pl.BlockSpec((tiles, half, block), lambda n, line: (0, 0, n)),
        ),
        out_shape=jax.ShapeDtypeStruct((tiles, half, depth), jnp.bfloat16),
        compiler_params=pltpu.CompilerParams(vmem_limit_bytes=VMEM_BYTES),
        cost_estimate=SMALL_COST,
        name="out",
    )(line_arg, *attended, *([out_weight] * LINE))


def join_kernel(
    mixing_ref, tokens_ref, early_ref, mid_ref, own_ref, other_ref, scale_ref, z_ref, inverse_ref
):
    inputs = tokens_ref[0].astype(jnp.float32)
    attended_out = own_ref[0].astype(jnp.float32) + other_ref[0].astype(jnp.float32)
    joined = (
        mixing_ref[0] * early_ref[0].astype(jnp.float32)
        + mixing_ref[1] * mid_ref[0].astype(jnp.float32)
        + (mixing_ref[2] + mixing_ref[3]) * inputs
        + (mixing_ref[3] * scale_ref[...]) * attended_out
    )
    centre = jnp.mean(joined, axis=-1, keepdims=True)
    shifted = joined - centre
    inverse = lax.rsqrt(jnp.mean(shifted * shifted, axis=-1, keepdims=True) + 1e-05)
    z_ref[0] = (shifted * inverse).astype(jnp.bfloat16)
    inverse_ref[0] = jnp.broadcast_to(inverse, inverse_ref.shape[1:])


def join_rows(mixing, tokens, early, mid, own, other, scale):
    tiles, half, depth = tokens.shape
    block = 64
    spec = pl.BlockSpec((1, block, depth), lambda t, r: (t, r, 0))
    return pl.pallas_call(
        join_kernel,
        grid=(tiles, half // block),
        out_shape=[
            jax.ShapeDtypeStruct(tokens.shape, jnp.bfloat16),
            jax.ShapeDtypeStruct((tiles, half, 128), jnp.float32),
        ],
        in_specs=[pl.BlockSpec(memory_space=pltpu.SMEM)]
        + [spec] * 5
        + [pl.BlockSpec((1, depth), lambda t, r: (0, 0))],
        out_specs=[spec, pl.BlockSpec((1, block, 128), lambda t, r: (t, r, 0))],
        compiler_params=pltpu.CompilerParams(vmem_limit_bytes=VMEM_BYTES),
        cost_estimate=SMALL_COST,
        name="join",
    )(mixing, tokens, early, mid, own, other, scale)


def final_kernel(own_ref, other_ref, z_ref, inverse_ref, out_ref):
    grad = own_ref[0].astype(jnp.float32) + other_ref[0].astype(jnp.float32)
    normal = z_ref[0].astype(jnp.float32)
    mean = jnp.mean(grad, axis=-1, keepdims=True)
    along = jnp.mean(grad * normal, axis=-1, keepdims=True)
    out_ref[0] = ((grad - mean - normal * along) * inverse_ref[0, :, :1]).astype(jnp.bfloat16)


def final_rows(own, other, z_rows, inverse):
    tiles, half, depth = own.shape
    block = 64
    spec = pl.BlockSpec((1, block, depth), lambda t, r: (t, r, 0))
    return pl.pallas_call(
        final_kernel,
        grid=(tiles, half // block),
        out_shape=jax.ShapeDtypeStruct(own.shape, jnp.bfloat16),
        in_specs=[spec, spec, spec, pl.BlockSpec((1, block, 128), lambda t, r: (t, r, 0))],
        out_specs=spec,
        compiler_params=pltpu.CompilerParams(vmem_limit_bytes=VMEM_BYTES),
        cost_estimate=SMALL_COST,
        name="final",
    )(own, other, z_rows, inverse)


def activate(preact):
    raised = jnp.exp(-0.5 * preact * preact)
    step = 1.0 / (1.0 + 0.3275911 * inv_root_two * jnp.abs(preact))
    series = 1.061405429 * step - 1.453152027
    series = series * step + 1.421413741
    series = series * step - 0.284496736
    series = series * step + 0.254829592
    tail = 0.5 * series * step * raised
    return jnp.where(preact >= 0.0, 1.0 - tail, tail), raised * inv_root_tau


def project_kernel(core_ref, own_ref, other_ref, weight_ref, bias_ref, projected_ref, slope_ref):
    core = core_ref[0]
    tiles, half, depth = own_ref.shape
    block = weight_ref.shape[1]
    rows = jnp.concatenate(
        [own_ref[...].reshape(tiles * half, depth), other_ref[...].reshape(tiles * half, depth)], axis=0
    )
    preact = jnp.dot(rows, weight_ref[...], preferred_element_type=jnp.float32) + bias_ref[...]
    cumulative, density = activate(preact)
    projected = (preact * cumulative).astype(jnp.bfloat16).reshape(2, tiles, 1, half, block)
    projected_ref[:, pl.ds(core, 1)] = projected[0]
    projected_ref[:, pl.ds(1 - core, 1)] = projected[1]
    slope_ref[...] = cumulative + preact * density


def home_project(core, own, other, weight, bias):
    tiles, half, depth = own.shape
    width = weight.shape[1]
    block = 512
    whole = pl.BlockSpec((tiles, half, depth), lambda n, c: (0, 0, 0))
    projected, slope = pl.pallas_call(
        project_kernel,
        grid_spec=pltpu.PrefetchScalarGridSpec(
            num_scalar_prefetch=1,
            grid=(width // block,),
            in_specs=[
                whole,
                whole,
                pl.BlockSpec((depth, block), lambda n, c: (0, n)),
                pl.BlockSpec((1, block), lambda n, c: (0, n)),
            ],
            out_specs=[
                pl.BlockSpec((tiles, 2, half, block), lambda n, c: (0, 0, 0, n)),
                pl.BlockSpec((2 * tiles * half, block), lambda n, c: (0, n)),
            ],
        ),
        out_shape=[
            jax.ShapeDtypeStruct((tiles, 2, half, width), jnp.bfloat16),
            jax.ShapeDtypeStruct((2 * tiles * half, width), jnp.float32),
        ],
        compiler_params=pltpu.CompilerParams(vmem_limit_bytes=VMEM_BYTES),
        cost_estimate=SMALL_COST,
        name="project",
    )(core, own, other, weight, bias)
    return projected.reshape(tiles, 2 * half, width), slope


def grad_kernel(core_ref, slope_ref, back_own_ref, back_other_ref, weight_ref, own_ref, other_ref, total):
    step = pl.program_id(0)
    tiles, half, depth = own_ref.shape
    rows, block = slope_ref.shape
    back = jnp.concatenate(
        [ref[...].reshape(tiles * half, block) for ref in (back_own_ref, back_other_ref)], axis=0
    )
    slope_rows = (back.astype(jnp.float32) * slope_ref[...]).astype(jnp.bfloat16)
    term = lax.dot_general(
        slope_rows, weight_ref[...], (((1,), (1,)), ((), ())), preferred_element_type=jnp.float32
    )

    @pl.when(step == 0)
    def _():
        total[...] = term

    @pl.when(step > 0)
    def _():
        total[...] += term

    @pl.when(step == pl.num_programs(0) - 1)
    def _():
        own_ref[...] = total[: tiles * half].astype(jnp.bfloat16).reshape(tiles, half, depth)
        other_ref[...] = total[tiles * half :].astype(jnp.bfloat16).reshape(tiles, half, depth)


def home_grad(core, slope, back, weight):
    tiles, full, width = back.shape
    half = full // 2
    depth = weight.shape[0]
    block = 512
    back = back.reshape(tiles, 2, half, width)
    whole = pl.BlockSpec((tiles, half, depth), lambda n, c: (0, 0, 0))
    shape = jax.ShapeDtypeStruct((tiles, half, depth), jnp.bfloat16)
    return pl.pallas_call(
        grad_kernel,
        grid_spec=pltpu.PrefetchScalarGridSpec(
            num_scalar_prefetch=1,
            grid=(width // block,),
            in_specs=[
                pl.BlockSpec((tiles * full, block), lambda n, c: (0, n)),
                pl.BlockSpec((tiles, 1, half, block), lambda n, c: (0, c[0], 0, n)),
                pl.BlockSpec((tiles, 1, half, block), lambda n, c: (0, 1 - c[0], 0, n)),
                pl.BlockSpec((depth, block), lambda n, c: (0, n)),
            ],
            out_specs=[whole, whole],
            scratch_shapes=[pltpu.VMEM((tiles * full, depth), jnp.float32)],
        ),
        out_shape=[shape, shape],
        compiler_params=pltpu.CompilerParams(vmem_limit_bytes=VMEM_BYTES),
        cost_estimate=SMALL_COST,
        name="grad",
    )(core, slope, back, back, weight)


def owner_kernel(count, core_ref, *refs):
    sources = refs[: 2 * count]
    weight_ref, bias_ref, projected_ref = refs[2 * count :]
    core = core_ref[0]
    _, half, depth = sources[0].shape
    block = weight_ref.shape[1]
    rows = jnp.concatenate([source[0] for source in sources], axis=0)
    preact = jnp.dot(rows, weight_ref[...], preferred_element_type=jnp.float32) + bias_ref[...]
    projected = (preact * activate(preact)[0]).astype(jnp.bfloat16)
    projected = projected.reshape(count, 2, half, block)
    for index in range(count):
        projected_ref[index, pl.ds(core, 1)] = projected[index, :1]
        projected_ref[index, pl.ds(1 - core, 1)] = projected[index, 1:]


def owner_project(core, pairs, weight, bias):
    count = len(pairs)
    _, half, depth = pairs[0][0].shape
    width = weight.shape[1]
    block = 512
    projected = pl.pallas_call(
        functools.partial(owner_kernel, count),
        grid_spec=pltpu.PrefetchScalarGridSpec(
            num_scalar_prefetch=1,
            grid=(width // block,),
            in_specs=[pl.BlockSpec((1, half, depth), lambda n, c: (0, 0, 0))] * (2 * count)
            + [
                pl.BlockSpec((depth, block), lambda n, c: (0, n)),
                pl.BlockSpec((1, block), lambda n, c: (0, n)),
            ],
            out_specs=pl.BlockSpec((count, 2, half, block), lambda n, c: (0, 0, 0, n)),
        ),
        out_shape=jax.ShapeDtypeStruct((count, 2, half, width), jnp.bfloat16),
        compiler_params=pltpu.CompilerParams(vmem_limit_bytes=VMEM_BYTES),
        cost_estimate=SMALL_COST,
        name="owner",
    )(core, *[rows for pair in pairs for rows in pair], weight, bias)
    return projected.reshape(count, 2 * half, width)


def on_device(
    tokens, tap_early, tap_mid, tile_counts, qkv_weight, out_weight, layer_scale, layer_logits,
    proj_weight, proj_bias, grad_out,
):
    tile_group, token_share, depth = tokens.shape
    img_count = lax.axis_size(IMG)
    place = lax.axis_index(IMG)
    line_place = lax.axis_index("z")
    core = lax.axis_index("head")
    core_arg = core.astype(jnp.int32).reshape(1)
    tile_total = tile_group * img_count
    own_tiles = grad_out.shape[0]
    owner_of, first_tile = tile_owners(tile_counts, tile_total, tile_group)
    my_first = first_tile[place]

    depth_share, width = qkv_weight.shape
    share = width // LINE
    received = []
    for distance in range(LINE):
        target = (line_place + distance) % LINE
        columns = lax.dynamic_slice_in_dim(qkv_weight, target * share, share, axis=1)
        received.append(along_z(columns, distance) if distance else columns)
    normed = norm_rows(tokens)
    normed, received = lax.optimization_barrier((normed, received))
    ladder = jnp.stack([received[(LINE - 1 - j) % LINE] for j in range(2 * LINE - 1)], axis=0)
    sent = lax.dynamic_slice_in_dim(ladder, LINE - 1 - line_place, LINE, axis=0)
    weight = lax.all_gather(sent.reshape(LINE * depth_share, share), ("y", "x"), axis=0, tiled=True)

    def packet(distance, within, count, first):
        tile = (place + distance) * tile_group + within
        slot = jnp.clip(tile - first, 0, own_tiles - count)
        return lax.dynamic_slice_in_dim(grad_out, slot, count, axis=0)

    near_line = [ring_x(packet(1, 0, 1, my_first), 1)]
    from_low = along_z(normed, 1)
    from_high = along_z(normed, -1)
    from_low, from_high, near_line[0], second_first = lax.optimization_barrier(
        (from_low, from_high, near_line[0], my_first)
    )
    near_line.append(ring_x(packet(1, 1, 1, second_first), 1))
    far_first = along_z(from_low[:1], 1)
    far_second = along_z(from_high[1:], -1)
    near_next = [next_line(near_line[0], 1)]
    far_first, far_second, weight, near_line[1], near_next[0], far_slot = lax.optimization_barrier(
        (far_first, far_second, weight, near_line[1], near_next[0], my_first)
    )
    far_line = ring_x(packet(2, 0, tile_group, far_slot), 2)
    near_next.append(next_line(near_line[1], 1))

    from_far = jnp.concatenate([far_first, far_second], axis=0)
    att_far, att_low, att_high = attend(
        [(rows, swap(rows)) for rows in (from_far, from_low, from_high)], weight
    )
    (att_own,) = attend([(normed, swap(normed))], weight)
    att_far, att_low, att_high = along_z(att_far, 2), along_z(att_low, -1), along_z(att_high, 1)
    att_own, near_next[1] = lax.optimization_barrier((att_own, near_next[1]))
    attended = [att_own, att_low, att_far, att_high]
    line_arg = line_place.astype(jnp.int32).reshape(1)
    part_other = swap(out_project(line_arg, attended, out_weight, 1))
    part_own = out_project(line_arg, attended, out_weight, 0)
    part_own, part_other, far_line = lax.optimization_barrier((part_own, part_other, far_line))
    far_next = next_line(far_line, 2)
    raised_logits = jnp.exp(layer_logits)
    mixing = raised_logits / jnp.sum(raised_logits)
    z_rows, inverse_std = join_rows(
        mixing, tokens, tap_early, tap_mid, part_own, part_other, layer_scale.reshape(1, -1)
    )

    halfway, far_on = two_back(z_rows[1:])
    far_first = along_img(z_rows[:1], -2)
    near_first = along_img(z_rows[:1], -1)
    bias = proj_bias.reshape(1, -1)
    projected, slope = home_project(core_arg, z_rows, swap(z_rows), proj_weight, bias)
    near_first, far_first, halfway, second, slope = lax.optimization_barrier(
        (near_first, far_first, halfway, z_rows[1:], slope)
    )
    near_second = along_img(second, -1)
    far_second = far_on(halfway)

    def guests(first, second):
        return owner_project(
            core_arg, [(first, swap(first)), (second, swap(second))], proj_weight, bias
        )

    early = guests(near_first, far_first)
    far_next, slope, _ = lax.optimization_barrier((far_next, slope, early))

    column = place % LINE
    back = []
    for within in range(tile_group):
        tile = place * tile_group + within
        owner = owner_of[tile]
        slot = jnp.clip(tile - my_first, 0, own_tiles - 1)
        here = lax.dynamic_index_in_dim(grad_out, slot, axis=0, keepdims=False)
        near = jnp.where(column < 1, near_next[within][0], near_line[within][0])
        far = jnp.where(column < 2, far_next[within], far_line[within])
        back.append(jnp.where(owner == place, here, jnp.where(owner == place - 1, near, far)))
    back_rows = jnp.stack(back, axis=0)
    grad_own, grad_other = home_grad(core_arg, slope, back_rows, proj_weight)
    near_second, far_second, _ = lax.optimization_barrier((near_second, far_second, grad_other))
    late = guests(near_second, far_second)
    grad_joined = final_rows(grad_own, swap(grad_other), z_rows, inverse_std)

    offset = my_first - place * tile_group
    held = first_tile[place + 1] - my_first
    at_hand = [projected[0], projected[1], early[0], late[0], early[1], late[1]]
    slots = []
    for slot in range(own_tiles):
        later = at_hand[min(slot + 1, len(at_hand) - 1)]
        picked = jnp.where(offset == 0, at_hand[slot], later)
        slots.append(jnp.where(slot < held, picked, jnp.zeros((), jnp.bfloat16)))
    owner_rows = jnp.stack(slots, axis=0)
    return (owner_rows, grad_joined)


def solution(mesh):
    cores = mesh.devices.shape[-1]
    inner = Mesh(mesh.devices.reshape(LINE, LINE, LINE, cores), IMG + ("head",))
    return jax.shard_map(
        on_device,
        mesh=inner,
        in_specs=(
            P(IMG, "head", None),
            P(IMG, "head", None),
            P(IMG, "head", None),
            P(),
            P(IMG, "head"),
            P("head", None),
            P(),
            P(),
            P(None, "head"),
            P("head"),
            P(IMG, None, "head"),
        ),
        out_specs=(P(IMG, None, "head"), P(IMG, "head", None)),
        check_vma=False,
    )
```

time: 369 us -> 305 us (0.83)
  waiting for transfers between devices: 116 us -> 71.3 us
  Pallas kernels: 130 us -> 118 us
  starting transfers between devices: 69.7 us -> 60.1 us
    ppermute x10, waiting for transfers between devices: 50.1 us -> 14.5 us  [along_z(): return lax.ppermute(array, 'z', [(i, (i + by) % LINE) for i in range(LINE)])]
    ppermute x6 -> x3, waiting for transfers between devices: 46.6 us -> 11.6 us  [along_img(): return lax.ppermute(array, IMG, pairs)]
    ppermute x4 -> x8, waiting for transfers between devices: 18.7 us -> 44.9 us  [the longest x3 42.6 us: ring_x(): return lax.ppermute(array, IMG, [(i, around(i, by)) for i in range(peers)])]
    ppermute x6 -> x3, starting transfers between devices: 33 us -> 20.6 us  [along_img(): return lax.ppermute(array, IMG, pairs)]
    pallas_call x9 -> x6, Pallas kernels: 98.7 us -> 86.3 us  [the longest x2 28.7 us: owner_project(): pl.pallas_call(functools.partial(owner_kernel, count), grid_spec=pltpu.Pr...]
    unnamed x64 -> x48, local copies, waits for them, and re-layouts: 7.96 us -> 6.87 us
    ppermute x4 -> x8, starting transfers between devices: 10.7 us -> 9.99 us  [the longest x3 4.06 us: next_line(): return lax.ppermute(array, IMG, pairs)]
  transfers between devices with their start and end apart: 32 -> 33, of which waited for: 8 -> 8; matrix products, arithmetic and copies ran while one was open for 5% -> 8% of each run, Pallas kernels for 31% -> 37%
where the time goes in v3:
time: 305 us; the launch traced here: 301 us
  Pallas kernels  118 us (39%)
  waiting for transfers between devices  71.3 us (23%)
  starting transfers between devices  60.1 us (20%)
  between operations  21.8 us (7%)
  local copies, waits for them, and re-layouts  20.9 us (7%)
  other arithmetic  8.68 us (3%)
    ppermute x3, waiting for transfers between devices, ring_x(): return lax.ppermute(array, IMG, [(i, around(i, by)) for i in range(peers)])  42.6 us
    pallas_call x2, Pallas kernels, owner_project(): pl.pallas_call(functools.partial(owner_kernel, count), grid_spec=pltpu.Pr...  28.7 us
    pallas_call x2, Pallas kernels, attend(): pl.pallas_call(functools.partial(attend_kernel, count), out_shape=[jax.Sh...  27.5 us
    ppermute x3, starting transfers between devices, along_img(): return lax.ppermute(array, IMG, pairs)  20.6 us
    ppermute x11, starting transfers between devices, swap(): return lax.ppermute(array, 'head', [(0, 1), (1, 0)])  16.8 us
    pallas_call x1, Pallas kernels, home_project(): pl.pallas_call(project_kernel, grid_spec=pltpu.PrefetchScalarGridSpec(num...  15.2 us
    pallas_call x1, Pallas kernels, home_grad(): pl.pallas_call(grad_kernel, grid_spec=pltpu.PrefetchScalarGridSpec(num_sc...  14.9 us
    ppermute x10, waiting for transfers between devices, along_z(): return lax.ppermute(array, 'z', [(i, (i + by) % LINE) for i in range(LINE)])  14.5 us
  transfers between devices with their start and end apart: 33, of which 8 were waited for; matrix products, arithmetic and copies ran while one was open for 8% of the time, Pallas kernels for 37%

profile of v3, /device:TPU:31, one launch (start us, length us, event | category | flops | bytes accessed | tf_op | source)
XLA Modules:
  0.0 301.3 jit_solution(14844471118319495753)
XLA Ops:
  10.0 3.3 %collective-permute-start.1 = (bf16[50,768]{1,0:T(8,128)(2,1)S(1)}, bf16[50,768]{1,0:T(8,128)(2,1)S(1)}, u32[]{:S(2)}, u32[]{:S(2)}) collective-permute-start(bf16[50,768]{1,0:T(8,128)(2,1)S(1)} %get-tuple-element.91), channel_id=1, source_target_pairs={{0,64},{32,96},{64,0},{96,32},{1,65},{33,97},{65,1},{97,33},{2,66}... | collective-permute-start | bytes 230408 | tf_op jit(solution)/shard_map/ppermute | solution.py:26
  14.1 6.0 %norm.1.refs_0_ = bf16[2,128,3200]{2,1,0:T(8,128)(2,1)} custom-call(bf16[2,128,3200]{2,1,0:T(8,128)(2,1)} %tokens_ref.3), custom_call_target="tpu_custom_call" | custom-call | flops 1 | bytes 1 | tf_op jit(solution)/shard_map/norm/pallas_call | solution.py:93
  28.4 27.9 %collective-permute-done.6 = bf16[1,256,2048]{2,1,0:T(8,128)(2,1)} collective-permute-done((bf16[1,256,2048]{2,1,0:T(8,128)(2,1)}, bf16[1,256,2048]{2,1,0:T(8,128)(2,1)}, u32[]{:S(2)}, u32[]{:S(2)}) %collective-permute-start.6) | collective-permute-done | bytes 1048608 | tf_op jit(solution)/shard_map/ppermute | solution.py:41
  63.8 2.7 collective-permute-start.8
  66.6 5.7 %collective-permute-start.13 = (bf16[2,128,3200]{2,1,0:T(8,128)(2,1)S(1)}, bf16[2,128,3200]{2,1,0:T(8,128)(2,1)}, u32[]{:S(2)}, u32[]{:S(2)}) collective-permute-start(bf16[2,128,3200]{2,1,0:T(8,128)(2,1)S(1)} %collective-permute-done.4.refs_2_), channel_id=1, source_target_pairs={{0,1},{1,0},{2,3},{3,2},{4,5},{5,4},{6,7},{7,6},{8,9},{9,8},{10,11... | collective-permute-start | bytes 4915208 | tf_op jit(solution)/shard_map/ppermute | solution.py:22
  72.3 6.2 %collective-permute-done.7 = bf16[1,128,3200]{2,1,0:T(8,128)(2,1)S(1)} collective-permute-done((bf16[1,128,3200]{2,1,0:T(8,128)(2,1)S(1)}, bf16[1,128,3200]{2,1,0:T(8,128)(2,1)S(1)}, u32[]{:S(2)}, u32[]{:S(2)}) %collective-permute-start.7) | collective-permute-done | bytes 819232 | tf_op jit(solution)/shard_map/ppermute | solution.py:26
  78.5 6.0 %collective-permute-start.14 = (bf16[2,128,3200]{2,1,0:T(8,128)(2,1)}, bf16[2,128,3200]{2,1,0:T(8,128)(2,1)}, u32[]{:S(2)}, u32[]{:S(2)}) collective-permute-start(bf16[2,128,3200]{2,1,0:T(8,128)(2,1)} %collective-permute-done.5.refs_4_), channel_id=1, source_target_pairs={{0,1},{1,0},{2,3},{3,2},{4,5},{5,4},{6,7},{7,6},{8,9},{9,8},{10,11... | collective-permute-start | bytes 4915208 | tf_op jit(solution)/shard_map/ppermute | solution.py:22
  84.5 14.6 %collective-permute-done.9 = bf16[1,256,2048]{2,1,0:T(8,128)(2,1)} collective-permute-done((bf16[1,256,2048]{2,1,0:T(8,128)(2,1)S(1)}, bf16[1,256,2048]{2,1,0:T(8,128)(2,1)}, u32[]{:S(2)}, u32[]{:S(2)}) %collective-permute-start.9) | collective-permute-done | bytes 1048608 | tf_op jit(solution)/shard_map/ppermute | solution.py:41
  110.2 19.0 %attend.3 = (bf16[2,256,256]{2,1,0:T(8,128)(2,1)}, bf16[2,256,256]{2,1,0:T(8,128)(2,1)}, bf16[2,256,256]{2,1,0:T(8,128)(2,1)}) custom-call(bf16[2,128,3200]{2,1,0:T(8,128)(2,1)} %constant_dynamic-update-slice_fusion.refs_0_, bf16[2,128,3200]{2,1,0:T(8,128)(2,1)} %collective-permute-done.12.refs_1_, bf16[2,128,3200]{2,1,0:T(8,128)(2,1)} %copy-done.2, ...), custom_call_target="tpu_custom_call" | custom-call | flops 1 | bytes 1 | tf_op jit(solution)/shard_map/attend/pallas_call | solution.py:163
  130.8 8.5 %attend.2.refs_0_ = bf16[2,256,256]{2,1,0:T(8,128)(2,1)} custom-call(bf16[2,128,3200]{2,1,0:T(8,128)(2,1)} %norm.1.refs_0_, bf16[2,128,3200]{2,1,0:T(8,128)(2,1)} %collective-permute-done.3.refs_1_, bf16[3200,768]{1,0:T(8,128)(2,1)} %all-gather.2.cloned.1.call-done.refs_2_.refs_6_), custom_call_target="tpu_custom_call" | custom-call | flops 1 | bytes 1 | tf_op jit(solution)/shard_map/attend/pallas_call | solution.py:163
  139.3 5.9 %collective-permute-done.17.refs_3_ = bf16[2,256,256]{2,1,0:T(8,128)(2,1)S(1)} collective-permute-done((bf16[2,256,256]{2,1,0:T(8,128)(2,1)}, bf16[2,256,256]{2,1,0:T(8,128)(2,1)S(1)}, u32[]{:S(2)}, u32[]{:S(2)}) %collective-permute-start.17) | collective-permute-done | bytes 262176 | tf_op jit(solution)/shard_map/ppermute | solution.py:26
  146.0 6.8 %out.3 = bf16[2,128,3200]{2,1,0:T(8,128)(2,1)} custom-call(s32[1]{0:T(128)} %bitcast.4.line_ref, bf16[2,256,256]{2,1,0:T(8,128)(2,1)} %attend.2.refs_0_, bf16[2,256,256]{2,1,0:T(8,128)(2,1)} %copy-done.6, bf16[2,256,256]{2,1,0:T(8,128)(2,1)} %copy-done.7, bf16[2,256,256]{2,1,0:T(8,128)(2,1)} %copy-done.8, bf16[1024,3200]{1,0:T(8,128)(2,1)} %refs_7_.3, ...), custom_call_target="tpu_custom_call" | custom-call | flops 1 | bytes 1 | tf_op jit(solution)/shard_map/out/pallas_call | solution.py:203
  153.8 6.8 %out.2.own_ref = bf16[2,128,3200]{2,1,0:T(8,128)(2,1)} custom-call(s32[1]{0:T(128)} %bitcast.4.line_ref, bf16[2,256,256]{2,1,0:T(8,128)(2,1)} %attend.2.refs_0_, bf16[2,256,256]{2,1,0:T(8,128)(2,1)} %copy-done.6, bf16[2,256,256]{2,1,0:T(8,128)(2,1)} %copy-done.7, bf16[2,256,256]{2,1,0:T(8,128)(2,1)} %copy-done.8, bf16[1024,3200]{1,0:T(8,128)(2,1)} %refs_7_.3, ...), custom_call_target="tpu_custom_call" | custom-call | flops 1 | bytes 1 | tf_op jit(solution)/shard_map/out/pallas_call | solution.py:203
  163.1 6.3 %join.1 = (bf16[2,128,3200]{2,1,0:T(8,128)(2,1)}, f32[2,128,128]{2,1,0:T(8,128)}) custom-call(f32[4]{0:T(128)} %exponential_divide_fusion.mixing_ref, bf16[2,128,3200]{2,1,0:T(8,128)(2,1)} %tokens_ref.3, bf16[2,128,3200]{2,1,0:T(8,128)(2,1)} %early_ref.1, bf16[2,128,3200]{2,1,0:T(8,128)(2,1)} %mid_ref.1, bf16[2,128,3200]{2,1,0:T(8,128)(2,1)} %out.2.own_ref, ...), custom_call_target="tpu_custom_call" | custom-call | flops 1 | bytes 1 | tf_op jit(solution)/shard_map/join/pallas_call | solution.py:241
  171.9 10.2 %collective-permute-start.21 = (bf16[1,128,3200]{2,1,0:T(8,128)(2,1)}, bf16[1,128,3200]{2,1,0:T(8,128)(2,1)}, u32[]{:S(2)}, u32[]{:S(2)}) collective-permute-start(bf16[1,128,3200]{2,1,0:T(8,128)(2,1)} %get-tuple-element.87), channel_id=1, source_target_pairs={{2,0},{4,2},{6,4},{8,6},{10,8},{12,10},{14,12},{16,14},{18,16},{20... | collective-permute-start | bytes 2457608 | tf_op jit(solution)/shard_map/ppermute | solution.py:32
  182.1 5.3 %collective-permute-start.22 = (bf16[1,128,3200]{2,1,0:T(8,128)(2,1)}, bf16[1,128,3200]{2,1,0:T(8,128)(2,1)}, u32[]{:S(2)}, u32[]{:S(2)}) collective-permute-start(bf16[1,128,3200]{2,1,0:T(8,128)(2,1)} %get-tuple-element.87), channel_id=1, source_target_pairs={{4,0},{6,2},{8,4},{10,6},{12,8},{14,10},{16,12},{18,14},{20,16},{2... | collective-permute-start | bytes 2457608 | tf_op jit(solution)/shard_map/ppermute | solution.py:32
  194.0 15.2 %project.1 = (bf16[2,2,128,2048]{3,2,1,0:T(8,128)(2,1)}, f32[512,2048]{1,0:T(8,128)}) custom-call(s32[1]{0:T(128)} %bitcast.3.core_ref, bf16[2,128,3200]{2,1,0:T(8,128)(2,1)} %get-tuple-element.60.own_ref.z_ref, bf16[2,128,3200]{2,1,0:T(8,128)(2,1)} %collective-permute-done.20.other_ref, bf16[3200,2048]{1,0:T(8,128)(2,1)} %refs_4_.7, f32[1,2048]{1,0:T(1,128)} %bitcast.35), custom_call_target="tpu_custom_call" | custom-call | flops 1 | bytes 1 | tf_op jit(solution)/shard_map/project/pallas_call | solution.py:313
  209.2 11.6 %collective-permute-done.22.refs_2_ = bf16[1,128,3200]{2,1,0:T(8,128)(2,1)} collective-permute-done((bf16[1,128,3200]{2,1,0:T(8,128)(2,1)}, bf16[1,128,3200]{2,1,0:T(8,128)(2,1)}, u32[]{:S(2)}, u32[]{:S(2)}) %collective-permute-start.22) | collective-permute-done | bytes 819232 | tf_op jit(solution)/shard_map/ppermute | solution.py:32
  223.9 5.1 %collective-permute-start.26 = (bf16[1,128,3200]{2,1,0:T(8,128)(2,1)S(1)}, bf16[1,128,3200]{2,1,0:T(8,128)(2,1)}, u32[]{:S(2)}, u32[]{:S(2)}) collective-permute-start(bf16[1,128,3200]{2,1,0:T(8,128)(2,1)S(1)} %get-tuple-element.65), channel_id=1, source_target_pairs={{2,0},{4,2},{6,4},{8,6},{10,8},{12,10},{14,12},{16,14},{18,16},{20... | collective-permute-start | bytes 2457608 | tf_op jit(solution)/shard_map/ppermute | solution.py:32
  231.2 3.3 %select_select_fusion.4 = (bf16[1,256,2048]{2,1,0:T(8,128)(2,1)S(1)}, bf16[1,256,2048]{2,1,0:T(8,128)(2,1)S(1)}) fusion(bf16[2,256,2048]{2,1,0:T(8,128)(2,1)} %collective-permute-done.19, bf16[2,256,2048]{2,1,0:T(8,128)(2,1)S(1)} %collective-permute-done.28, bf16[1,256,2048]{2,1,0:T(8,128)(2,1)} %collective-permute-done.10, ...), kind=kLoop, calls=%fused_computation.5 | loop fusion | flops 4194304 | bytes 12582926 | tf_op jit(solution)/shard_map/jit(_where)/select_n | solution.py:531
  236.0 14.9 %grad.1 = (bf16[2,128,3200]{2,1,0:T(8,128)(2,1)}, bf16[2,128,3200]{2,1,0:T(8,128)(2,1)}) custom-call(s32[1]{0:T(128)} %bitcast.3.core_ref, f32[512,2048]{1,0:T(8,128)} %get-tuple-element.69.slope_ref, bf16[2,2,128,2048]{3,2,1,0:T(8,128)(2,1)} %pad_maximum_fusion.back_own_ref.back_other_ref, ...), custom_call_target="tpu_custom_call" | custom-call | flops 1 | bytes 1 | tf_op jit(solution)/shard_map/grad/pallas_call | solution.py:374
  254.2 14.4 %owner.2 = bf16[2,2,128,2048]{3,2,1,0:T(8,128)(2,1)} custom-call(s32[1]{0:T(128)} %bitcast.3.core_ref, bf16[1,128,3200]{2,1,0:T(8,128)(2,1)} %collective-permute-done.21.refs_0_, bf16[1,128,3200]{2,1,0:T(8,128)(2,1)} %collective-permute-done.24.refs_1_, bf16[1,128,3200]{2,1,0:T(8,128)(2,1)} %collective-permute-done.22.refs_2_, ...), custom_call_target="tpu_custom_call" | custom-call | flops 1 | bytes 1 | tf_op jit(solution)/shard_map/owner/pallas_call | solution.py:415
  270.5 14.3 %owner.3 = bf16[2,2,128,2048]{3,2,1,0:T(8,128)(2,1)} custom-call(s32[1]{0:T(128)} %bitcast.3.core_ref, bf16[1,128,3200]{2,1,0:T(8,128)(2,1)} %collective-permute-done.26.refs_0_, bf16[1,128,3200]{2,1,0:T(8,128)(2,1)} %copy-done.12, bf16[1,128,3200]{2,1,0:T(8,128)(2,1)} %collective-permute-done.27.refs_2_, bf16[1,128,3200]{2,1,0:T(8,128)(2,1)} %copy-done.13, ...), custom_call_target="tpu_custom_call" | custom-call | flops 1 | bytes 1 | tf_op jit(solution)/shard_map/owner/pallas_call | solution.py:415
  288.3 6.2 %final.1 = bf16[2,128,3200]{2,1,0:T(8,128)(2,1)} custom-call(bf16[2,128,3200]{2,1,0:T(8,128)(2,1)} %get-tuple-element.76.own_ref, bf16[2,128,3200]{2,1,0:T(8,128)(2,1)} %copy-done.4, bf16[2,128,3200]{2,1,0:T(8,128)(2,1)} %get-tuple-element.60.own_ref.z_ref, f32[2,128,128]{2,1,0:T(8,128)} %get-tuple-element.77.inverse_ref), custom_call_target="tpu_custom_call" | custom-call | flops 1 | bytes 1 | tf_op jit(solution)/shard_map/final/pallas_call | solution.py:270
  (130 shorter events, 53.3 us)
Async XLA Ops:
  7.2 92.0 %all-gather.2.cloned.1.call-start = ((), (), s32[]{:S(2)}) async-start(), calls=%async_computation | async-start | bytes 5222400 | tf_op jit(solution)/shard_map/all_gather | solution.py:461
  21.6 37.1 %collective-permute-start.4 = (bf16[2,128,3200]{2,1,0:T(8,128)(2,1)S(1)}, bf16[2,128,3200]{2,1,0:T(8,128)(2,1)S(1)}, u32[]{:S(2)}, u32[]{:S(2)}) collective-permute-start(bf16[2,128,3200]{2,1,0:T(8,128)(2,1)S(1)} %copy-done.1), channel_id=1, source_target_pairs={{0,32},{32,64},{64,96},{96,0},{1,33},{33,65},{65,97},{97,1},{2,34}... | collective-permute-start | bytes 4915208 | tf_op jit(solution)/shard_map/ppermute | solution.py:26
  22.4 36.4 %collective-permute-start.5 = (bf16[2,128,3200]{2,1,0:T(8,128)(2,1)S(1)}, bf16[2,128,3200]{2,1,0:T(8,128)(2,1)}, u32[]{:S(2)}, u32[]{:S(2)}) collective-permute-start(bf16[2,128,3200]{2,1,0:T(8,128)(2,1)S(1)} %copy-done.1), channel_id=1, source_target_pairs={{0,96},{32,0},{64,32},{96,64},{1,97},{33,1},{65,33},{97,65},{2,98}... | collective-permute-start | bytes 4915208 | tf_op jit(solution)/shard_map/ppermute | solution.py:26
  28.2 28.1 %collective-permute-start.6 = (bf16[1,256,2048]{2,1,0:T(8,128)(2,1)}, bf16[1,256,2048]{2,1,0:T(8,128)(2,1)}, u32[]{:S(2)}, u32[]{:S(2)}) collective-permute-start(bf16[1,256,2048]{2,1,0:T(8,128)(2,1)} %constant_dynamic-slice_fusion.3), channel_id=1, source_target_pairs={{0,2},{2,4},{4,6},{6,0},{8,10},{10,12},{12,14},{14,8},{16,18},{18,... | collective-permute-start | bytes 3145736 | tf_op jit(solution)/shard_map/ppermute | solution.py:41
  60.6 38.5 %collective-permute-start.9 = (bf16[1,256,2048]{2,1,0:T(8,128)(2,1)S(1)}, bf16[1,256,2048]{2,1,0:T(8,128)(2,1)}, u32[]{:S(2)}, u32[]{:S(2)}) collective-permute-start(bf16[1,256,2048]{2,1,0:T(8,128)(2,1)S(1)} %constant_dynamic-slice_fusion.1), channel_id=1, source_target_pairs={{0,2},{2,4},{4,6},{6,0},{8,10},{10,12},{12,14},{14,8},{16,18},{18,... | collective-permute-start | bytes 3145736 | tf_op jit(solution)/shard_map/ppermute | solution.py:41
  60.8 38.3 %collective-permute-start.10 = (bf16[1,256,2048]{2,1,0:T(8,128)(2,1)}, bf16[1,256,2048]{2,1,0:T(8,128)(2,1)}, u32[]{:S(2)}, u32[]{:S(2)}) collective-permute-start(bf16[1,256,2048]{2,1,0:T(8,128)(2,1)} %collective-permute-done.6), channel_id=1, source_target_pairs={{0,8},{8,16},{16,24},{24,32},{32,40},{40,48},{48,56},{56,64},{64,7... | collective-permute-start | bytes 3145736 | tf_op jit(solution)/shard_map/ppermute | solution.py:47
  63.8 20.7 %collective-permute-start.8 = (bf16[1,128,3200]{2,1,0:T(8,128)(2,1)S(1)}, bf16[1,128,3200]{2,1,0:T(8,128)(2,1)S(1)}, u32[]{:S(2)}, u32[]{:S(2)}) collective-permute-start(bf16[1,128,3200]{2,1,0:T(8,128)(2,1)S(1)} %slice.51), channel_id=1, source_target_pairs={{0,96},{32,0},{64,32},{96,64},{1,97},{33,1},{65,33},{97,65},{2,98}... | collective-permute-start | bytes 2457608 | tf_op jit(solution)/shard_map/ppermute | solution.py:26
  66.6 41.9 %collective-permute-start.13 = (bf16[2,128,3200]{2,1,0:T(8,128)(2,1)S(1)}, bf16[2,128,3200]{2,1,0:T(8,128)(2,1)}, u32[]{:S(2)}, u32[]{:S(2)}) collective-permute-start(bf16[2,128,3200]{2,1,0:T(8,128)(2,1)S(1)} %collective-permute-done.4.refs_2_), channel_id=1, source_target_pairs={{0,1},{1,0},{2,3},{3,2},{4,5},{5,4},{6,7},{7,6},{8,9},{9,8},{10,11... | collective-permute-start | bytes 4915208 | tf_op jit(solution)/shard_map/ppermute | solution.py:22
  78.5 31.4 %collective-permute-start.14 = (bf16[2,128,3200]{2,1,0:T(8,128)(2,1)}, bf16[2,128,3200]{2,1,0:T(8,128)(2,1)}, u32[]{:S(2)}, u32[]{:S(2)}) collective-permute-start(bf16[2,128,3200]{2,1,0:T(8,128)(2,1)} %collective-permute-done.5.refs_4_), channel_id=1, source_target_pairs={{0,1},{1,0},{2,3},{3,2},{4,5},{5,4},{6,7},{7,6},{8,9},{9,8},{10,11... | collective-permute-start | bytes 4915208 | tf_op jit(solution)/shard_map/ppermute | solution.py:22
  104.5 26.2 %collective-permute-start.3 = (bf16[2,128,3200]{2,1,0:T(8,128)(2,1)S(1)}, bf16[2,128,3200]{2,1,0:T(8,128)(2,1)}, u32[]{:S(2)}, u32[]{:S(2)}) collective-permute-start(bf16[2,128,3200]{2,1,0:T(8,128)(2,1)S(1)} %copy-done.1), channel_id=1, source_target_pairs={{0,1},{1,0},{2,3},{3,2},{4,5},{5,4},{6,7},{7,6},{8,9},{9,8},{10,11... | collective-permute-start | bytes 4915208 | tf_op jit(solution)/shard_map/ppermute | solution.py:22
  104.5 34.8 %collective-permute-start.11 = (bf16[1,256,2048]{2,1,0:T(8,128)(2,1)}, bf16[1,256,2048]{2,1,0:T(8,128)(2,1)}, u32[]{:S(2)}, u32[]{:S(2)}) collective-permute-start(bf16[1,256,2048]{2,1,0:T(8,128)(2,1)} %collective-permute-done.9), channel_id=1, source_target_pairs={{0,8},{8,16},{16,24},{24,32},{32,40},{40,48},{48,56},{56,64},{64,7... | collective-permute-start | bytes 3145736 | tf_op jit(solution)/shard_map/ppermute | solution.py:47
  108.5 52.1 %collective-permute-start.19 = (bf16[2,256,2048]{2,1,0:T(8,128)(2,1)S(1)}, bf16[2,256,2048]{2,1,0:T(8,128)(2,1)}, u32[]{:S(2)}, u32[]{:S(2)}) collective-permute-start(bf16[2,256,2048]{2,1,0:T(8,128)(2,1)S(1)} %constant_dynamic-slice_fusion), channel_id=1, source_target_pairs={{0,4},{2,6},{4,0},{6,2},{8,12},{10,14},{12,8},{14,10},{16,20},{18,... | collective-permute-start | bytes 6291464 | tf_op jit(solution)/shard_map/ppermute | solution.py:41
  160.6 70.6 %collective-permute-start.28 = (bf16[2,256,2048]{2,1,0:T(8,128)(2,1)}, bf16[2,256,2048]{2,1,0:T(8,128)(2,1)S(1)}, u32[]{:S(2)}, u32[]{:S(2)}) collective-permute-start(bf16[2,256,2048]{2,1,0:T(8,128)(2,1)} %collective-permute-done.19), channel_id=1, source_target_pairs={{0,8},{2,10},{8,16},{10,18},{16,24},{18,26},{24,32},{26,34},{32,40... | collective-permute-start | bytes 6291464 | tf_op jit(solution)/shard_map/ppermute | solution.py:47
  169.4 24.6 %collective-permute-start.20 = (bf16[2,128,3200]{2,1,0:T(8,128)(2,1)}, bf16[2,128,3200]{2,1,0:T(8,128)(2,1)}, u32[]{:S(2)}, u32[]{:S(2)}) collective-permute-start(bf16[2,128,3200]{2,1,0:T(8,128)(2,1)} %get-tuple-element.60.own_ref.z_ref), channel_id=1, source_target_pairs={{0,1},{1,0},{2,3},{3,2},{4,5},{5,4},{6,7},{7,6},{8,9},{9,8},{10,11... | collective-permute-start | bytes 4915208 | tf_op jit(solution)/shard_map/ppermute | solution.py:22
  171.9 37.2 %collective-permute-start.21 = (bf16[1,128,3200]{2,1,0:T(8,128)(2,1)}, bf16[1,128,3200]{2,1,0:T(8,128)(2,1)}, u32[]{:S(2)}, u32[]{:S(2)}) collective-permute-start(bf16[1,128,3200]{2,1,0:T(8,128)(2,1)} %get-tuple-element.87), channel_id=1, source_target_pairs={{2,0},{4,2},{6,4},{8,6},{10,8},{12,10},{14,12},{16,14},{18,16},{20... | collective-permute-start | bytes 2457608 | tf_op jit(solution)/shard_map/ppermute | solution.py:32
  182.1 38.6 %collective-permute-start.22 = (bf16[1,128,3200]{2,1,0:T(8,128)(2,1)}, bf16[1,128,3200]{2,1,0:T(8,128)(2,1)}, u32[]{:S(2)}, u32[]{:S(2)}) collective-permute-start(bf16[1,128,3200]{2,1,0:T(8,128)(2,1)} %get-tuple-element.87), channel_id=1, source_target_pairs={{4,0},{6,2},{8,4},{10,6},{12,8},{14,10},{16,12},{18,14},{20,16},{2... | collective-permute-start | bytes 2457608 | tf_op jit(solution)/shard_map/ppermute | solution.py:32
  187.4 35.6 %collective-permute-start.23 = (bf16[1,128,3200]{2,1,0:T(8,128)(2,1)S(1)}, bf16[1,128,3200]{2,1,0:T(8,128)(2,1)}, u32[]{:S(2)}, u32[]{:S(2)}) collective-permute-start(bf16[1,128,3200]{2,1,0:T(8,128)(2,1)S(1)} %get-tuple-element.65), channel_id=1, source_target_pairs={{4,6},{6,0},{8,10},{10,4},{12,14},{14,8},{16,18},{18,12},{20,22},{... | collective-permute-start | bytes 2457608 | tf_op jit(solution)/shard_map/ppermute | solution.py:57
  223.1 31.2 %collective-permute-start.24 = (bf16[1,128,3200]{2,1,0:T(8,128)(2,1)}, bf16[1,128,3200]{2,1,0:T(8,128)(2,1)}, u32[]{:S(2)}, u32[]{:S(2)}) collective-permute-start(bf16[1,128,3200]{2,1,0:T(8,128)(2,1)} %collective-permute-done.21.refs_0_), channel_id=1, source_target_pairs={{0,1},{1,0},{2,3},{3,2},{4,5},{5,4},{6,7},{7,6},{8,9},{9,8},{10,11... | collective-permute-start | bytes 2457608 | tf_op jit(solution)/shard_map/ppermute | solution.py:22
  223.9 30.3 %collective-permute-start.25 = (bf16[1,128,3200]{2,1,0:T(8,128)(2,1)}, bf16[1,128,3200]{2,1,0:T(8,128)(2,1)}, u32[]{:S(2)}, u32[]{:S(2)}) collective-permute-start(bf16[1,128,3200]{2,1,0:T(8,128)(2,1)} %collective-permute-done.22.refs_2_), channel_id=1, source_target_pairs={{0,1},{1,0},{2,3},{3,2},{4,5},{5,4},{6,7},{7,6},{8,9},{9,8},{10,11... | collective-permute-start | bytes 2457608 | tf_op jit(solution)/shard_map/ppermute | solution.py:22
  223.9 27.0 %collective-permute-start.26 = (bf16[1,128,3200]{2,1,0:T(8,128)(2,1)S(1)}, bf16[1,128,3200]{2,1,0:T(8,128)(2,1)}, u32[]{:S(2)}, u32[]{:S(2)}) collective-permute-start(bf16[1,128,3200]{2,1,0:T(8,128)(2,1)S(1)} %get-tuple-element.65), channel_id=1, source_target_pairs={{2,0},{4,2},{6,4},{8,6},{10,8},{12,10},{14,12},{16,14},{18,16},{20... | collective-permute-start | bytes 2457608 | tf_op jit(solution)/shard_map/ppermute | solution.py:32
  229.0 21.9 %collective-permute-start.27 = (bf16[1,128,3200]{2,1,0:T(8,128)(2,1)}, bf16[1,128,3200]{2,1,0:T(8,128)(2,1)}, u32[]{:S(2)}, u32[]{:S(2)}) collective-permute-start(bf16[1,128,3200]{2,1,0:T(8,128)(2,1)} %collective-permute-done.23), channel_id=1, source_target_pairs={{6,0},{0,2},{10,4},{4,6},{14,8},{8,10},{18,12},{12,14},{22,16},{16... | collective-permute-start | bytes 2457608 | tf_op jit(solution)/shard_map/ppermute | solution.py:58
  251.0 17.7 %collective-permute-start.29 = (bf16[1,128,3200]{2,1,0:T(8,128)(2,1)}, bf16[1,128,3200]{2,1,0:T(8,128)(2,1)S(1)}, u32[]{:S(2)}, u32[]{:S(2)}) collective-permute-start(bf16[1,128,3200]{2,1,0:T(8,128)(2,1)} %collective-permute-done.26.refs_0_), channel_id=1, source_target_pairs={{0,1},{1,0},{2,3},{3,2},{4,5},{5,4},{6,7},{7,6},{8,9},{9,8},{10,11... | collective-permute-start | bytes 2457608 | tf_op jit(solution)/shard_map/ppermute | solution.py:22
  251.9 16.8 %collective-permute-start.30 = (bf16[1,128,3200]{2,1,0:T(8,128)(2,1)}, bf16[1,128,3200]{2,1,0:T(8,128)(2,1)S(1)}, u32[]{:S(2)}, u32[]{:S(2)}) collective-permute-start(bf16[1,128,3200]{2,1,0:T(8,128)(2,1)} %collective-permute-done.27.refs_2_), channel_id=1, source_target_pairs={{0,1},{1,0},{2,3},{3,2},{4,5},{5,4},{6,7},{7,6},{8,9},{9,8},{10,11... | collective-permute-start | bytes 2457608 | tf_op jit(solution)/shard_map/ppermute | solution.py:22
  253.7 33.4 %collective-permute-start.31 = (bf16[2,128,3200]{2,1,0:T(8,128)(2,1)}, bf16[2,128,3200]{2,1,0:T(8,128)(2,1)S(1)}, u32[]{:S(2)}, u32[]{:S(2)}) collective-permute-start(bf16[2,128,3200]{2,1,0:T(8,128)(2,1)} %get-tuple-element.73), channel_id=1, source_target_pairs={{0,1},{1,0},{2,3},{3,2},{4,5},{5,4},{6,7},{7,6},{8,9},{9,8},{10,11... | collective-permute-start | bytes 4915208 | tf_op jit(solution)/shard_map/ppermute | solution.py:22
  (27 other events, 218.5 us)
Sparse Core Ops, SparseCore 0:
  21.2 70.6 all-gather.1

commit v4 on v3

--- a/solution.py
+++ b/solution.py
@@ -36,24 +36,15 @@
     return place - place % LINE + (place % LINE + side) % LINE
 
 
-def ring_x(array, by):
+def two_on(array, by):
     peers = lax.axis_size(IMG)
-    return lax.ppermute(array, IMG, [(i, around(i, by)) for i in range(peers)])
-
-
-def next_line(array, columns):
-    peers = lax.axis_size(IMG)
-    pairs = [(i, i + LINE) for i in range(peers - LINE) if i % LINE < columns]
-    return lax.ppermute(array, IMG, pairs)
-
-
-def two_back(array):
-    peers = lax.axis_size(IMG)
+    side = -by // 2
+    turning = 2 if by > 0 else 1
 
     def middle(i):
-        return i - LINE + 1 if i % LINE == 1 else around(i, 1)
-
-    ends = [(i, i - 2) for i in range(2, peers)]
+        return i + side + LINE * (by // 2) if i % LINE == turning else around(i, side)
+
+    ends = [(i, i + by) for i in range(peers) if 0 <= i + by < peers]
     halfway = lax.ppermute(array, IMG, [(i, middle(i)) for i, _ in ends])
     return halfway, lambda held: lax.ppermute(held, IMG, [(middle(i), j) for i, j in ends])
 
@@ -103,19 +94,27 @@
     )(tokens)
 
 
-def attend_kernel(count, *refs):
-    sources, weight_hbm = refs[: 2 * count], refs[2 * count]
-    outs = refs[2 * count + 1 : 3 * count + 1]
-    rows, weight, qkv, row_sems, weight_sem = refs[3 * count + 1 :]
+def attend_kernel(layout, *refs):
+    count = len(layout)
+    pieces = sum(2 * len(tiles) for tiles in layout)
+    sources, weight_hbm = list(refs[:pieces]), refs[pieces]
+    outs = refs[pieces + 1 : pieces + 1 + count]
+    rows, weight, qkv, row_sems, weight_sem = refs[pieces + 1 + count :]
     _, _, tiles, half, depth = rows.shape
     heads = weight.shape[1] // (3 * HEAD_DIM)
 
     def fetch(index):
         slot = index % 2
-        return [
-            pltpu.make_async_copy(sources[2 * index + part], rows.at[slot, part], row_sems.at[slot, part])
-            for part in range(2)
-        ]
+        copies = []
+        for part in range(2):
+            start = 0
+            for place, length in enumerate(layout[index]):
+                target = rows.at[slot, part, pl.ds(start, length)]
+                copies.append(
+                    pltpu.make_async_copy(sources.pop(0), target, row_sems.at[slot, part, place])
+                )
+                start += length
+        return copies
 
     weight_copy = pltpu.make_async_copy(weight_hbm, weight, weight_sem)
     pending = fetch(0)
@@ -155,39 +154,43 @@
                 outs[index][tile, :, head * HEAD_DIM : (head + 1) * HEAD_DIM] = mixed.astype(jnp.bfloat16)
 
 
-def attend(pairs, weight):
-    count = len(pairs)
-    tiles, half, depth = pairs[0][0].shape
+def attend(sources, weight):
+    layout = tuple(tuple(array.shape[0] for array in own) for own, _ in sources)
+    tiles = sum(layout[0])
+    _, half, depth = sources[0][0][0].shape
     width = weight.shape[1]
     shape = (tiles, 2 * half, width // 3)
+    arrays = [array for own, other in sources for array in (*own, *other)]
     return pl.pallas_call(
-        functools.partial(attend_kernel, count),
-        out_shape=[jax.ShapeDtypeStruct(shape, jnp.bfloat16)] * count,
-        in_specs=[pl.BlockSpec(memory_space=pl.ANY)] * (2 * count + 1),
-        out_specs=[pl.BlockSpec(memory_space=pltpu.VMEM)] * count,
+        functools.partial(attend_kernel, layout),
+        out_shape=[jax.ShapeDtypeStruct(shape, jnp.bfloat16)] * len(layout),
+        in_specs=[pl.BlockSpec(memory_space=pl.ANY)] * (len(arrays) + 1),
+        out_specs=[pl.BlockSpec(memory_space=pltpu.VMEM)] * len(layout),
         scratch_shapes=[
             pltpu.VMEM((2, 2, tiles, half, depth), jnp.bfloat16),
             pltpu.VMEM((depth, width), jnp.bfloat16),
             pltpu.VMEM((2 * tiles * half, width), jnp.bfloat16),
-            pltpu.SemaphoreType.DMA((2, 2)),
+            pltpu.SemaphoreType.DMA((2, 2, tiles)),
             pltpu.SemaphoreType.DMA,
         ],
         compiler_params=pltpu.CompilerParams(vmem_limit_bytes=VMEM_BYTES),
         cost_estimate=SMALL_COST,
         name="attend",
-    )(*[rows for pair in pairs for rows in pair], weight)
-
-
-def out_kernel(start, line_ref, *refs):
-    attended = refs[:LINE]
-    weights = refs[LINE : 2 * LINE]
-    part_ref = refs[2 * LINE]
+    )(*arrays, weight)
+
+
+def out_kernel(line_ref, *refs):
+    attended, weight_ref, part_ref, rows = refs[:LINE], refs[LINE], refs[LINE + 1], refs[LINE + 2]
     tiles, half, block = part_ref.shape
-    total = None
-    for rows_ref, weight_ref in zip(attended, weights):
-        rows = rows_ref[...].reshape(tiles * half, rows_ref.shape[2])
-        term = jnp.dot(rows, weight_ref[...], preferred_element_type=jnp.float32)
-        total = term if total is None else total + term
+    share = attended[0].shape[2]
+
+    @pl.when(pl.program_id(0) == 0)
+    def _():
+        for distance, source in enumerate(attended):
+            start = pl.multiple_of(lax.rem(line_ref[0] + distance, LINE) * share, share)
+            rows[:, pl.ds(start, share)] = source[...].reshape(tiles * half, share)
+
+    total = jnp.dot(rows[...], weight_ref[...], preferred_element_type=jnp.float32)
     part_ref[...] = total.astype(jnp.bfloat16).reshape(tiles, half, block)
 
 
@@ -196,24 +199,21 @@
     half = full // 2
     depth = out_weight.shape[1]
     block = 640
-
-    def weight_spec(k):
-        return pl.BlockSpec((share, block), lambda n, line: ((line[0] + k) % LINE, n))
-
     return pl.pallas_call(
-        functools.partial(out_kernel, part),
+        out_kernel,
         grid_spec=pltpu.PrefetchScalarGridSpec(
             num_scalar_prefetch=1,
             grid=(depth // block,),
             in_specs=[pl.BlockSpec((tiles, half, share), lambda n, line: (0, part, 0))] * LINE
-            + [weight_spec(k) for k in range(LINE)],
+            + [pl.BlockSpec((LINE * share, block), lambda n, line: (0, n))],
             out_specs=pl.BlockSpec((tiles, half, block), lambda n, line: (0, 0, n)),
+            scratch_shapes=[pltpu.VMEM((tiles * half, LINE * share), jnp.bfloat16)],
         ),
         out_shape=jax.ShapeDtypeStruct((tiles, half, depth), jnp.bfloat16),
         compiler_params=pltpu.CompilerParams(vmem_limit_bytes=VMEM_BYTES),
         cost_estimate=SMALL_COST,
         name="out",
-    )(line_arg, *attended, *([out_weight] * LINE))
+    )(line_arg, *attended, out_weight)
 
 
 def join_kernel(
@@ -234,49 +234,56 @@
     inverse_ref[0] = jnp.broadcast_to(inverse, inverse_ref.shape[1:])
 
 
-def join_rows(mixing, tokens, early, mid, own, other, scale):
-    tiles, half, depth = tokens.shape
+def join_rows(tile, mixing, tokens, early, mid, own, other, scale):
+    _, half, depth = tokens.shape
     block = 64
-    spec = pl.BlockSpec((1, block, depth), lambda t, r: (t, r, 0))
+    spec = pl.BlockSpec((1, block, depth), lambda r: (tile, r, 0))
     return pl.pallas_call(
         join_kernel,
-        grid=(tiles, half // block),
+        grid=(half // block,),
         out_shape=[
-            jax.ShapeDtypeStruct(tokens.shape, jnp.bfloat16),
-            jax.ShapeDtypeStruct((tiles, half, 128), jnp.float32),
+            jax.ShapeDtypeStruct((1, half, depth), jnp.bfloat16),
+            jax.ShapeDtypeStruct((1, half, 128), jnp.float32),
         ],
         in_specs=[pl.BlockSpec(memory_space=pltpu.SMEM)]
         + [spec] * 5
-        + [pl.BlockSpec((1, depth), lambda t, r: (0, 0))],
-        out_specs=[spec, pl.BlockSpec((1, block, 128), lambda t, r: (t, r, 0))],
+        + [pl.BlockSpec((1, depth), lambda r: (0, 0))],
+        out_specs=[
+            pl.BlockSpec((1, block, depth), lambda r: (0, r, 0)),
+            pl.BlockSpec((1, block, 128), lambda r: (0, r, 0)),
+        ],
         compiler_params=pltpu.CompilerParams(vmem_limit_bytes=VMEM_BYTES),
         cost_estimate=SMALL_COST,
         name="join",
     )(mixing, tokens, early, mid, own, other, scale)
 
 
-def final_kernel(own_ref, other_ref, z_ref, inverse_ref, out_ref):
+def final_kernel(own_ref, other_ref, z_ref, later_z_ref, inverse_ref, later_inverse_ref, out_ref):
+    first = pl.program_id(0) == 0
     grad = own_ref[0].astype(jnp.float32) + other_ref[0].astype(jnp.float32)
-    normal = z_ref[0].astype(jnp.float32)
+    normal = jnp.where(first, z_ref[0], later_z_ref[0]).astype(jnp.float32)
+    inverse = jnp.where(first, inverse_ref[0, :, :1], later_inverse_ref[0, :, :1])
     mean = jnp.mean(grad, axis=-1, keepdims=True)
     along = jnp.mean(grad * normal, axis=-1, keepdims=True)
-    out_ref[0] = ((grad - mean - normal * along) * inverse_ref[0, :, :1]).astype(jnp.bfloat16)
-
-
-def final_rows(own, other, z_rows, inverse):
+    out_ref[0] = ((grad - mean - normal * along) * inverse).astype(jnp.bfloat16)
+
+
+def final_rows(own, other, z_tiles, inverse_tiles):
     tiles, half, depth = own.shape
     block = 64
     spec = pl.BlockSpec((1, block, depth), lambda t, r: (t, r, 0))
+    z_spec = pl.BlockSpec((1, block, depth), lambda t, r: (0, r, 0))
+    inverse_spec = pl.BlockSpec((1, block, 128), lambda t, r: (0, r, 0))
     return pl.pallas_call(
         final_kernel,
         grid=(tiles, half // block),
         out_shape=jax.ShapeDtypeStruct(own.shape, jnp.bfloat16),
-        in_specs=[spec, spec, spec, pl.BlockSpec((1, block, 128), lambda t, r: (t, r, 0))],
+        in_specs=[spec, spec, z_spec, z_spec, inverse_spec, inverse_spec],
         out_specs=spec,
         compiler_params=pltpu.CompilerParams(vmem_limit_bytes=VMEM_BYTES),
         cost_estimate=SMALL_COST,
         name="final",
-    )(own, other, z_rows, inverse)
+    )(own, other, *z_tiles, *inverse_tiles)
 
 
 def activate(preact):
@@ -290,13 +297,12 @@
     return jnp.where(preact >= 0.0, 1.0 - tail, tail), raised * inv_root_tau
 
 
-def project_kernel(core_ref, own_ref, other_ref, weight_ref, bias_ref, projected_ref, slope_ref):
+def project_kernel(core_ref, *refs):
+    sources = refs[:-4]
+    weight_ref, bias_ref, projected_ref, slope_ref = refs[-4:]
     core = core_ref[0]
-    tiles, half, depth = own_ref.shape
-    block = weight_ref.shape[1]
-    rows = jnp.concatenate(
-        [own_ref[...].reshape(tiles * half, depth), other_ref[...].reshape(tiles * half, depth)], axis=0
-    )
+    tiles, _, half, block = projected_ref.shape
+    rows = jnp.concatenate([source[0] for source in sources], axis=0)
     preact = jnp.dot(rows, weight_ref[...], preferred_element_type=jnp.float32) + bias_ref[...]
     cumulative, density = activate(preact)
     projected = (preact * cumulative).astype(jnp.bfloat16).reshape(2, tiles, 1, half, block)
@@ -306,18 +312,17 @@
 
 
 def home_project(core, own, other, weight, bias):
-    tiles, half, depth = own.shape
+    tiles = len(own)
+    _, half, depth = own[0].shape
     width = weight.shape[1]
     block = 512
-    whole = pl.BlockSpec((tiles, half, depth), lambda n, c: (0, 0, 0))
     projected, slope = pl.pallas_call(
         project_kernel,
         grid_spec=pltpu.PrefetchScalarGridSpec(
             num_scalar_prefetch=1,
             grid=(width // block,),
-            in_specs=[
-                whole,
-                whole,
+            in_specs=[pl.BlockSpec((1, half, depth), lambda n, c: (0, 0, 0))] * (2 * tiles)
+            + [
                 pl.BlockSpec((depth, block), lambda n, c: (0, n)),
                 pl.BlockSpec((1, block), lambda n, c: (0, n)),
             ],
@@ -333,7 +338,7 @@
         compiler_params=pltpu.CompilerParams(vmem_limit_bytes=VMEM_BYTES),
         cost_estimate=SMALL_COST,
         name="project",
-    )(core, own, other, weight, bias)
+    )(core, *own, *other, weight, bias)
     return projected.reshape(tiles, 2 * half, width), slope
 
 
@@ -465,75 +470,84 @@
         slot = jnp.clip(tile - first, 0, own_tiles - count)
         return lax.dynamic_slice_in_dim(grad_out, slot, count, axis=0)
 
-    near_line = [ring_x(packet(1, 0, 1, my_first), 1)]
     from_low = along_z(normed, 1)
     from_high = along_z(normed, -1)
-    from_low, from_high, near_line[0], second_first = lax.optimization_barrier(
-        (from_low, from_high, near_line[0], my_first)
-    )
-    near_line.append(ring_x(packet(1, 1, 1, second_first), 1))
+
+    def packet(distance, within, count):
+        tile = (place + distance) * tile_group + within
+        slot = jnp.clip(tile - my_first, 0, own_tiles - count)
+        return lax.dynamic_slice_in_dim(grad_out, slot, count, axis=0)
+
+    packets = [packet(distance, within, 1) for distance in (1, 2) for within in range(tile_group)]
+    from_low, from_high, packets = lax.optimization_barrier((from_low, from_high, packets))
     far_first = along_z(from_low[:1], 1)
     far_second = along_z(from_high[1:], -1)
-    near_next = [next_line(near_line[0], 1)]
-    far_first, far_second, weight, near_line[1], near_next[0], far_slot = lax.optimization_barrier(
-        (far_first, far_second, weight, near_line[1], near_next[0], my_first)
-    )
-    far_line = ring_x(packet(2, 0, tile_group, far_slot), 2)
-    near_next.append(next_line(near_line[1], 1))
-
-    from_far = jnp.concatenate([far_first, far_second], axis=0)
-    att_far, att_low, att_high = attend(
-        [(rows, swap(rows)) for rows in (from_far, from_low, from_high)], weight
-    )
-    (att_own,) = attend([(normed, swap(normed))], weight)
+    weight, packets = lax.optimization_barrier((weight, packets))
+    halfway, far_on = two_on(packets[3], 2)
+    far_back = [along_img(packets[2], 2), None]
+    near_back = [along_img(packets[0], 1), along_img(packets[1], 1)]
+
+    far_others = [swap(far_first), swap(far_second)]
+    att_low, att_high = attend(
+        [([rows], [swap(rows)]) for rows in (from_low, from_high)], weight
+    )
+    far_first, far_second, att_low = lax.optimization_barrier((far_first, far_second, att_low))
+    (att_far,) = attend([([far_first, far_second], far_others)], weight)
+    (att_own,) = attend([([normed], [swap(normed)])], weight)
     att_far, att_low, att_high = along_z(att_far, 2), along_z(att_low, -1), along_z(att_high, 1)
-    att_own, near_next[1] = lax.optimization_barrier((att_own, near_next[1]))
+    att_own, halfway, near_back[0] = lax.optimization_barrier((att_own, halfway, near_back[0]))
+    far_back[1] = far_on(halfway)
     attended = [att_own, att_low, att_far, att_high]
     line_arg = line_place.astype(jnp.int32).reshape(1)
     part_other = swap(out_project(line_arg, attended, out_weight, 1))
     part_own = out_project(line_arg, attended, out_weight, 0)
-    part_own, part_other, far_line = lax.optimization_barrier((part_own, part_other, far_line))
-    far_next = next_line(far_line, 2)
     raised_logits = jnp.exp(layer_logits)
     mixing = raised_logits / jnp.sum(raised_logits)
-    z_rows, inverse_std = join_rows(
-        mixing, tokens, tap_early, tap_mid, part_own, part_other, layer_scale.reshape(1, -1)
-    )
-
-    halfway, far_on = two_back(z_rows[1:])
-    far_first = along_img(z_rows[:1], -2)
-    near_first = along_img(z_rows[:1], -1)
+    scale = layer_scale.reshape(1, -1)
+    joined = [
+        join_rows(tile, mixing, tokens, tap_early, tap_mid, part_own, part_other, scale)
+        for tile in range(tile_group)
+    ]
+    z_tiles = [z_rows for z_rows, _ in joined]
+    inverse_tiles = [inverse for _, inverse in joined]
+
+    near_first = along_img(z_tiles[0], -1)
+    far_first = along_img(z_tiles[0], -2)
+    halfway, far_on = two_on(z_tiles[1], -2)
     bias = proj_bias.reshape(1, -1)
-    projected, slope = home_project(core_arg, z_rows, swap(z_rows), proj_weight, bias)
-    near_first, far_first, halfway, second, slope = lax.optimization_barrier(
-        (near_first, far_first, halfway, z_rows[1:], slope)
-    )
-    near_second = along_img(second, -1)
-    far_second = far_on(halfway)
-
-    def guests(first, second):
-        return owner_project(
-            core_arg, [(first, swap(first)), (second, swap(second))], proj_weight, bias
-        )
-
-    early = guests(near_first, far_first)
-    far_next, slope, _ = lax.optimization_barrier((far_next, slope, early))
-
-    column = place % LINE
+    projected, slope = home_project(
+        core_arg, z_tiles, [swap(z_rows) for z_rows in z_tiles], proj_weight, bias
+    )
+    slope, near_back[1], far_back[1] = lax.optimization_barrier((slope, near_back[1], far_back[1]))
+
     back = []
     for within in range(tile_group):
         tile = place * tile_group + within
         owner = owner_of[tile]
         slot = jnp.clip(tile - my_first, 0, own_tiles - 1)
         here = lax.dynamic_index_in_dim(grad_out, slot, axis=0, keepdims=False)
-        near = jnp.where(column < 1, near_next[within][0], near_line[within][0])
-        far = jnp.where(column < 2, far_next[within], far_line[within])
+        near, far = near_back[within][0], far_back[within][0]
         back.append(jnp.where(owner == place, here, jnp.where(owner == place - 1, near, far)))
     back_rows = jnp.stack(back, axis=0)
     grad_own, grad_other = home_grad(core_arg, slope, back_rows, proj_weight)
-    near_second, far_second, _ = lax.optimization_barrier((near_second, far_second, grad_other))
+
+    near_first, far_first, halfway, second, grad_other = lax.optimization_barrier(
+        (near_first, far_first, halfway, z_tiles[1], grad_other)
+    )
+    near_second = along_img(second, -1)
+    far_second = far_on(halfway)
+
+    def guests(first, second):
+        return owner_project(
+            core_arg, [(first, swap(first)), (second, swap(second))], proj_weight, bias
+        )
+
+    early = guests(near_first, far_first)
+    grad_joined = final_rows(grad_own, swap(grad_other), z_tiles, inverse_tiles)
+    near_second, far_second, early, grad_joined = lax.optimization_barrier(
+        (near_second, far_second, early, grad_joined)
+    )
     late = guests(near_second, far_second)
-    grad_joined = final_rows(grad_own, swap(grad_other), z_rows, inverse_std)
 
     offset = my_first - place * tile_group
     held = first_tile[place + 1] - my_first

time: 305 us -> 293 us (0.961)
  waiting for transfers between devices: 71.3 us -> 58.8 us
  Pallas kernels: 118 us -> 123 us
    ppermute x8 -> x4, waiting for transfers between devices: 44.9 us -> 0.01 us  [the longest x2 0.01 us: two_on(): halfway = lax.ppermute(array, IMG, [(i, middle(i)) for i, _ in ends])]
    ppermute x10, waiting for transfers between devices: 14.5 us -> 45.1 us  [along_z(): return lax.ppermute(array, 'z', [(i, (i + by) % LINE) for i in range(LINE)])]
    ppermute x11 -> x13, starting transfers between devices: 16.8 us -> 8.67 us  [swap(): return lax.ppermute(array, 'head', [(0, 1), (1, 0)])]
    pallas_call x5 -> x7, Pallas kernels: 47.4 us -> 53.2 us  [the longest x3 31.7 us: attend(): pl.pallas_call(functools.partial(attend_kernel, layout), out_shape=[jax.S...]
    ppermute x8 -> x4, starting transfers between devices: 9.99 us -> 15 us  [the longest x2 8.53 us: two_on(): lax.ppermute(held, IMG, [(middle(i), j) for i, j in ends])]
    ppermute x10, starting transfers between devices: 12.8 us -> 15.8 us  [along_z(): return lax.ppermute(array, 'z', [(i, (i + by) % LINE) for i in range(LINE)])]
    unnamed x48 -> x63, local copies, waits for them, and re-layouts: 6.87 us -> 9.02 us
    ppermute x3 -> x6, starting transfers between devices: 20.6 us -> 19.9 us  [along_img(): return lax.ppermute(array, IMG, pairs)]
  transfers between devices with their start and end apart: 33 -> 34, of which waited for: 8 -> 7; matrix products, arithmetic and copies ran while one was open for 8% -> 5% of each run, Pallas kernels for 37% -> 35%
where the time goes in v4:
time: 293 us; the launch traced here: 291 us
  Pallas kernels  123 us (42%)
  starting transfers between devices  59.4 us (20%)
  waiting for transfers between devices  58.8 us (20%)
  between operations  22.3 us (8%)
  local copies, waits for them, and re-layouts  20.5 us (7%)
  other arithmetic  6.95 us (2%)
    ppermute x10, waiting for transfers between devices, along_z(): return lax.ppermute(array, 'z', [(i, (i + by) % LINE) for i in range(LINE)])  45.1 us
    pallas_call x3, Pallas kernels, attend(): pl.pallas_call(functools.partial(attend_kernel, layout), out_shape=[jax.S...  31.7 us
    pallas_call x2, Pallas kernels, owner_project(): pl.pallas_call(functools.partial(owner_kernel, count), grid_spec=pltpu.Pr...  28.6 us
    ppermute x6, starting transfers between devices, along_img(): return lax.ppermute(array, IMG, pairs)  19.9 us
    ppermute x10, starting transfers between devices, along_z(): return lax.ppermute(array, 'z', [(i, (i + by) % LINE) for i in range(LINE)])  15.8 us
    pallas_call x1, Pallas kernels, home_project(): pl.pallas_call(project_kernel, grid_spec=pltpu.PrefetchScalarGridSpec(num...  15.2 us
    pallas_call x1, Pallas kernels, home_grad(): pl.pallas_call(grad_kernel, grid_spec=pltpu.PrefetchScalarGridSpec(num_sc...  14.9 us
    pallas_call x2, Pallas kernels, out_project(): pl.pallas_call(out_kernel, grid_spec=pltpu.PrefetchScalarGridSpec(num_sca...  13.9 us
  transfers between devices with their start and end apart: 34, of which 7 were waited for; matrix products, arithmetic and copies ran while one was open for 5% of the time, Pallas kernels for 35%

profile of v4, /device:TPU:31, one launch (start us, length us, event | category | flops | bytes accessed | tf_op | source)
XLA Modules:
  0.0 291.4 jit_solution(15475550164968514348)
XLA Ops:
  10.0 3.3 %collective-permute-start.1 = (bf16[50,768]{1,0:T(8,128)(2,1)S(1)}, bf16[50,768]{1,0:T(8,128)(2,1)S(1)}, u32[]{:S(2)}, u32[]{:S(2)}) collective-permute-start(bf16[50,768]{1,0:T(8,128)(2,1)S(1)} %get-tuple-element.111), channel_id=1, source_target_pairs={{0,64},{32,96},{64,0},{96,32},{1,65},{33,97},{65,1},{97,33},{2,66}... | collective-permute-start | bytes 230408 | tf_op jit(solution)/shard_map/ppermute | solution.py:26
  14.1 6.0 %norm.1.refs_0_ = bf16[2,128,3200]{2,1,0:T(8,128)(2,1)} custom-call(bf16[2,128,3200]{2,1,0:T(8,128)(2,1)} %tokens_ref.5), custom_call_target="tpu_custom_call" | custom-call | flops 1 | bytes 1 | tf_op jit(solution)/shard_map/norm/pallas_call | solution.py:84
  27.6 4.4 %constant_dynamic-slice_fusion = (bf16[1,256,2048]{2,1,0:T(8,128)(2,1)}, bf16[1,256,2048]{2,1,0:T(8,128)(2,1)}, bf16[1,256,2048]{2,1,0:T(8,128)(2,1)}, bf16[1,256,2048]{2,1,0:T(8,128)(2,1)}) fusion(bf16[6,256,2048]{2,1,0:T(8,128)(2,1)} %param.21, s32[]{:T(128)S(6)} %min.22, s32[]{:T(128)S(6)} %min.21, s32[]{:T(128)S(6)} %min.20, s32[]{:T(128)S(6)} %min.19), kind=kLoop, calls=%fused_computation.30 | loop fusion | bytes 8388624 | tf_op jit(solution)/shard_map/dynamic_slice | solution.py:479
  31.9 26.8 %collective-permute-done.4.refs_0_ = bf16[2,128,3200]{2,1,0:T(8,128)(2,1)S(1)} collective-permute-done((bf16[2,128,3200]{2,1,0:T(8,128)(2,1)S(1)}, bf16[2,128,3200]{2,1,0:T(8,128)(2,1)S(1)}, u32[]{:S(2)}, u32[]{:S(2)}) %collective-permute-start.4) | collective-permute-done | bytes 1638432 | tf_op jit(solution)/shard_map/ppermute | solution.py:26
  66.2 15.8 %collective-permute-done.8.refs_0_ = bf16[1,128,3200]{2,1,0:T(8,128)(2,1)} collective-permute-done((bf16[1,128,3200]{2,1,0:T(8,128)(2,1)S(1)}, bf16[1,128,3200]{2,1,0:T(8,128)(2,1)}, u32[]{:S(2)}, u32[]{:S(2)}) %collective-permute-start.8) | collective-permute-done | bytes 819232 | tf_op jit(solution)/shard_map/ppermute | solution.py:26
  86.2 5.3 %collective-permute-start.7 = (bf16[1,256,2048]{2,1,0:T(8,128)(2,1)}, bf16[1,256,2048]{2,1,0:T(8,128)(2,1)S(1)}, u32[]{:S(2)}, u32[]{:S(2)}) collective-permute-start(bf16[1,256,2048]{2,1,0:T(8,128)(2,1)} %get-tuple-element.57), channel_id=1, source_target_pairs={{0,2},{2,4},{4,6},{6,8},{8,10},{10,12},{12,14},{14,16},{16,18},{18... | collective-permute-start | bytes 3145736 | tf_op jit(solution)/shard_map/ppermute | solution.py:32
  91.5 14.6 %attend.4 = (bf16[2,256,256]{2,1,0:T(8,128)(2,1)}, bf16[2,256,256]{2,1,0:T(8,128)(2,1)}) custom-call(bf16[2,128,3200]{2,1,0:T(8,128)(2,1)} %copy-done.3, bf16[2,128,3200]{2,1,0:T(8,128)(2,1)} %collective-permute-done.10.refs_1_, bf16[2,128,3200]{2,1,0:T(8,128)(2,1)} %collective-permute-done.5.refs_2_, bf16[2,128,3200]{2,1,0:T(8,128)(2,1)} %collective-permute-done.11.refs_3_, ...), custom_call_target="tpu_custom_call" | custom-call | flops 1 | bytes 1 | tf_op jit(solution)/shard_map/attend/pallas_call | solution.py:164
  106.2 8.6 %attend.5 = bf16[2,256,256]{2,1,0:T(8,128)(2,1)} custom-call(bf16[1,128,3200]{2,1,0:T(8,128)(2,1)} %collective-permute-done.8.refs_0_, bf16[1,128,3200]{2,1,0:T(8,128)(2,1)} %collective-permute-done.9.refs_1_, bf16[1,128,3200]{2,1,0:T(8,128)(2,1)} %collective-permute-done.13.refs_2_, bf16[1,128,3200]{2,1,0:T(8,128)(2,1)} %collective-permute-done.14.refs_3_, ...), custom_call_target="tpu_custom_call" | custom-call | flops 1 | bytes 1 | tf_op jit(solution)/shard_map/attend/pallas_call | solution.py:164
  114.8 3.1 %collective-permute-start.15 = (bf16[2,256,256]{2,1,0:T(8,128)(2,1)}, bf16[2,256,256]{2,1,0:T(8,128)(2,1)S(1)}, u32[]{:S(2)}, u32[]{:S(2)}) collective-permute-start(bf16[2,256,256]{2,1,0:T(8,128)(2,1)} %attend.5), channel_id=1, source_target_pairs={{0,64},{32,96},{64,0},{96,32},{1,65},{33,97},{65,1},{97,33},{2,66}... | collective-permute-start | bytes 786440 | tf_op jit(solution)/shard_map/ppermute | solution.py:26
  119.4 8.5 %attend.3.refs_0_ = bf16[2,256,256]{2,1,0:T(8,128)(2,1)} custom-call(bf16[2,128,3200]{2,1,0:T(8,128)(2,1)} %norm.1.refs_0_, bf16[2,128,3200]{2,1,0:T(8,128)(2,1)} %collective-permute-done.3.refs_1_, bf16[3200,768]{1,0:T(8,128)(2,1)} %all-gather.2.cloned.1.call-done.refs_2_.refs_4_), custom_call_target="tpu_custom_call" | custom-call | flops 1 | bytes 1 | tf_op jit(solution)/shard_map/attend/pallas_call | solution.py:164
  131.2 7.1 %out.3 = bf16[2,128,3200]{2,1,0:T(8,128)(2,1)} custom-call(s32[1]{0:T(128)} %bitcast.4.line_ref, bf16[2,256,256]{2,1,0:T(8,128)(2,1)} %attend.3.refs_0_, bf16[2,256,256]{2,1,0:T(8,128)(2,1)} %copy-done.13, bf16[2,256,256]{2,1,0:T(8,128)(2,1)} %copy-done.12, bf16[2,256,256]{2,1,0:T(8,128)(2,1)} %copy-done.14, bf16[1024,3200]{1,0:T(8,128)(2,1)} %refs_4_.6), custom_call_target="tpu_custom_call" | custom-call | flops 1 | bytes 1 | tf_op jit(solution)/shard_map/out/pallas_call | solution.py:202
  138.8 3.8 %collective-permute-start.23 = (bf16[1,256,2048]{2,1,0:T(8,128)(2,1)S(1)}, bf16[1,256,2048]{2,1,0:T(8,128)(2,1)}, u32[]{:S(2)}, u32[]{:S(2)}) collective-permute-start(bf16[1,256,2048]{2,1,0:T(8,128)(2,1)S(1)} %copy-done.10), channel_id=1, source_target_pairs={{0,2},{2,4},{4,6},{6,8},{8,10},{10,12},{12,14},{14,16},{16,18},{18... | collective-permute-start | bytes 3145736 | tf_op jit(solution)/shard_map/ppermute | solution.py:32
  149.3 6.9 %out.2.own_ref = bf16[2,128,3200]{2,1,0:T(8,128)(2,1)} custom-call(s32[1]{0:T(128)} %bitcast.4.line_ref, bf16[2,256,256]{2,1,0:T(8,128)(2,1)} %attend.3.refs_0_, bf16[2,256,256]{2,1,0:T(8,128)(2,1)} %copy-done.13, bf16[2,256,256]{2,1,0:T(8,128)(2,1)} %copy-done.12, bf16[2,256,256]{2,1,0:T(8,128)(2,1)} %copy-done.14, bf16[1024,3200]{1,0:T(8,128)(2,1)} %refs_4_.6), custom_call_target="tpu_custom_call" | custom-call | flops 1 | bytes 1 | tf_op jit(solution)/shard_map/out/pallas_call | solution.py:202
  157.4 3.7 %join.3 = (bf16[1,128,3200]{2,1,0:T(8,128)(2,1)}, f32[1,128,128]{2,1,0:T(8,128)}) custom-call(f32[4]{0:T(128)} %exponential_divide_fusion.mixing_ref, bf16[2,128,3200]{2,1,0:T(8,128)(2,1)} %tokens_ref.5, bf16[2,128,3200]{2,1,0:T(8,128)(2,1)} %early_ref.3, bf16[2,128,3200]{2,1,0:T(8,128)(2,1)} %mid_ref.3, bf16[2,128,3200]{2,1,0:T(8,128)(2,1)} %out.2.own_ref, ...), custom_call_target="tpu_custom_call" | custom-call | flops 1 | bytes 1 | tf_op jit(solution)/shard_map/join/pallas_call | solution.py:241
  161.8 3.8 %join.2 = (bf16[1,128,3200]{2,1,0:T(8,128)(2,1)}, f32[1,128,128]{2,1,0:T(8,128)}) custom-call(f32[4]{0:T(128)} %exponential_divide_fusion.mixing_ref, bf16[2,128,3200]{2,1,0:T(8,128)(2,1)} %tokens_ref.5, bf16[2,128,3200]{2,1,0:T(8,128)(2,1)} %early_ref.3, bf16[2,128,3200]{2,1,0:T(8,128)(2,1)} %mid_ref.3, bf16[2,128,3200]{2,1,0:T(8,128)(2,1)} %out.2.own_ref, ...), custom_call_target="tpu_custom_call" | custom-call | flops 1 | bytes 1 | tf_op jit(solution)/shard_map/join/pallas_call | solution.py:241
  170.1 4.0 %collective-permute-start.22 = (bf16[1,128,3200]{2,1,0:T(8,128)(2,1)S(1)}, bf16[1,128,3200]{2,1,0:T(8,128)(2,1)}, u32[]{:S(2)}, u32[]{:S(2)}) collective-permute-start(bf16[1,128,3200]{2,1,0:T(8,128)(2,1)S(1)} %copy-done.4), channel_id=1, source_target_pairs={{4,6},{6,0},{8,10},{10,4},{12,14},{14,8},{16,18},{18,12},{20,22},{... | collective-permute-start | bytes 2457608 | tf_op jit(solution)/shard_map/ppermute | solution.py:48
  176.1 15.2 %project.1 = (bf16[2,2,128,2048]{3,2,1,0:T(8,128)(2,1)}, f32[512,2048]{1,0:T(8,128)}) custom-call(s32[1]{0:T(128)} %bitcast.3.core_ref, bf16[1,128,3200]{2,1,0:T(8,128)(2,1)} %get-tuple-element.66.refs_0_.z_ref, bf16[1,128,3200]{2,1,0:T(8,128)(2,1)} %get-tuple-element.78.refs_1_.later_z_ref, bf16[1,128,3200]{2,1,0:T(8,128)(2,1)} %collective-permute-done.18.refs_2_, ...), custom_call_target="tpu_custom_call" | custom-call | flops 1 | bytes 1 | tf_op jit(solution)/shard_map/project/pallas_call | solution.py:319
  191.3 5.1 %collective-permute-start.21 = (bf16[1,128,3200]{2,1,0:T(8,128)(2,1)S(1)}, bf16[1,128,3200]{2,1,0:T(8,128)(2,1)S(1)}, u32[]{:S(2)}, u32[]{:S(2)}) collective-permute-start(bf16[1,128,3200]{2,1,0:T(8,128)(2,1)S(1)} %copy-done.6), channel_id=1, source_target_pairs={{4,0},{6,2},{8,4},{10,6},{12,8},{14,10},{16,12},{18,14},{20,16},{2... | collective-permute-start | bytes 2457608 | tf_op jit(solution)/shard_map/ppermute | solution.py:32
  200.5 14.9 %grad.1 = (bf16[2,128,3200]{2,1,0:T(8,128)(2,1)}, bf16[2,128,3200]{2,1,0:T(8,128)(2,1)}) custom-call(s32[1]{0:T(128)} %bitcast.3.core_ref, f32[512,2048]{1,0:T(8,128)} %get-tuple-element.72.slope_ref, bf16[2,2,128,2048]{3,2,1,0:T(8,128)(2,1)} %pad_maximum_fusion.back_own_ref.back_other_ref, ...), custom_call_target="tpu_custom_call" | custom-call | flops 1 | bytes 1 | tf_op jit(solution)/shard_map/grad/pallas_call | solution.py:379
  215.4 12.1 %collective-permute-done.21.refs_2_ = bf16[1,128,3200]{2,1,0:T(8,128)(2,1)S(1)} collective-permute-done((bf16[1,128,3200]{2,1,0:T(8,128)(2,1)S(1)}, bf16[1,128,3200]{2,1,0:T(8,128)(2,1)S(1)}, u32[]{:S(2)}, u32[]{:S(2)}) %collective-permute-start.21) | collective-permute-done | bytes 819232 | tf_op jit(solution)/shard_map/ppermute | solution.py:32
  231.0 6.0 %collective-permute-start.27 = (bf16[1,128,3200]{2,1,0:T(8,128)(2,1)}, bf16[1,128,3200]{2,1,0:T(8,128)(2,1)}, u32[]{:S(2)}, u32[]{:S(2)}) collective-permute-start(bf16[1,128,3200]{2,1,0:T(8,128)(2,1)} %collective-permute-done.22), channel_id=1, source_target_pairs={{6,0},{0,2},{10,4},{4,6},{14,8},{8,10},{18,12},{12,14},{22,16},{16... | collective-permute-start | bytes 2457608 | tf_op jit(solution)/shard_map/ppermute | solution.py:49
  238.8 14.4 %owner.2 = bf16[2,2,128,2048]{3,2,1,0:T(8,128)(2,1)} custom-call(s32[1]{0:T(128)} %bitcast.3.core_ref, bf16[1,128,3200]{2,1,0:T(8,128)(2,1)} %copy-done.15, bf16[1,128,3200]{2,1,0:T(8,128)(2,1)} %copy-done.18, bf16[1,128,3200]{2,1,0:T(8,128)(2,1)} %copy-done.17, bf16[1,128,3200]{2,1,0:T(8,128)(2,1)} %copy-done.19, bf16[3200,2048]{1,0:T(8,128)(2,1)} %refs_4_.9, ...), custom_call_target="tpu_custom_call" | custom-call | flops 1 | bytes 1 | tf_op jit(solution)/shard_map/owner/pallas_call | solution.py:420
  254.4 5.4 %final.1 = bf16[2,128,3200]{2,1,0:T(8,128)(2,1)} custom-call(bf16[2,128,3200]{2,1,0:T(8,128)(2,1)} %get-tuple-element.82.own_ref, bf16[2,128,3200]{2,1,0:T(8,128)(2,1)} %copy-done.8, bf16[1,128,3200]{2,1,0:T(8,128)(2,1)} %get-tuple-element.66.refs_0_.z_ref, bf16[1,128,3200]{2,1,0:T(8,128)(2,1)} %get-tuple-element.78.refs_1_.later_z_ref, ...), custom_call_target="tpu_custom_call" | custom-call | flops 1 | bytes 1 | tf_op jit(solution)/shard_map/final/pallas_call | solution.py:277
  263.9 14.3 %owner.3 = bf16[2,2,128,2048]{3,2,1,0:T(8,128)(2,1)} custom-call(s32[1]{0:T(128)} %bitcast.3.core_ref, bf16[1,128,3200]{2,1,0:T(8,128)(2,1)} %copy-done.16, bf16[1,128,3200]{2,1,0:T(8,128)(2,1)} %collective-permute-done.31.refs_1_, bf16[1,128,3200]{2,1,0:T(8,128)(2,1)} %collective-permute-done.27.refs_2_, ...), custom_call_target="tpu_custom_call" | custom-call | flops 1 | bytes 1 | tf_op jit(solution)/shard_map/owner/pallas_call | solution.py:420
  (147 shorter events, 56.1 us)
Async XLA Ops:
  7.2 76.6 %all-gather.2.cloned.1.call-start = ((), (), s32[]{:S(2)}) async-start(), calls=%async_computation | async-start | bytes 5222400 | tf_op jit(solution)/shard_map/all_gather | solution.py:466
  21.6 37.1 %collective-permute-start.4 = (bf16[2,128,3200]{2,1,0:T(8,128)(2,1)S(1)}, bf16[2,128,3200]{2,1,0:T(8,128)(2,1)S(1)}, u32[]{:S(2)}, u32[]{:S(2)}) collective-permute-start(bf16[2,128,3200]{2,1,0:T(8,128)(2,1)S(1)} %copy-done.1), channel_id=1, source_target_pairs={{0,32},{32,64},{64,96},{96,0},{1,33},{33,65},{65,97},{97,1},{2,34}... | collective-permute-start | bytes 4915208 | tf_op jit(solution)/shard_map/ppermute | solution.py:26
  22.4 36.4 %collective-permute-start.5 = (bf16[2,128,3200]{2,1,0:T(8,128)(2,1)S(1)}, bf16[2,128,3200]{2,1,0:T(8,128)(2,1)}, u32[]{:S(2)}, u32[]{:S(2)}) collective-permute-start(bf16[2,128,3200]{2,1,0:T(8,128)(2,1)S(1)} %copy-done.1), channel_id=1, source_target_pairs={{0,96},{32,0},{64,32},{96,64},{1,97},{33,1},{65,33},{97,65},{2,98}... | collective-permute-start | bytes 4915208 | tf_op jit(solution)/shard_map/ppermute | solution.py:26
  58.7 25.0 %collective-permute-start.10 = (bf16[2,128,3200]{2,1,0:T(8,128)(2,1)S(1)}, bf16[2,128,3200]{2,1,0:T(8,128)(2,1)}, u32[]{:S(2)}, u32[]{:S(2)}) collective-permute-start(bf16[2,128,3200]{2,1,0:T(8,128)(2,1)S(1)} %collective-permute-done.4.refs_0_), channel_id=1, source_target_pairs={{0,1},{1,0},{2,3},{3,2},{4,5},{5,4},{6,7},{7,6},{8,9},{9,8},{10,11... | collective-permute-start | bytes 4915208 | tf_op jit(solution)/shard_map/ppermute | solution.py:22
  61.0 25.2 %collective-permute-start.11 = (bf16[2,128,3200]{2,1,0:T(8,128)(2,1)}, bf16[2,128,3200]{2,1,0:T(8,128)(2,1)}, u32[]{:S(2)}, u32[]{:S(2)}) collective-permute-start(bf16[2,128,3200]{2,1,0:T(8,128)(2,1)} %collective-permute-done.5.refs_2_), channel_id=1, source_target_pairs={{0,1},{1,0},{2,3},{3,2},{4,5},{5,4},{6,7},{7,6},{8,9},{9,8},{10,11... | collective-permute-start | bytes 4915208 | tf_op jit(solution)/shard_map/ppermute | solution.py:22
  61.2 20.8 %collective-permute-start.8 = (bf16[1,128,3200]{2,1,0:T(8,128)(2,1)S(1)}, bf16[1,128,3200]{2,1,0:T(8,128)(2,1)}, u32[]{:S(2)}, u32[]{:S(2)}) collective-permute-start(bf16[1,128,3200]{2,1,0:T(8,128)(2,1)S(1)} %slice.28), channel_id=1, source_target_pairs={{0,32},{32,64},{64,96},{96,0},{1,33},{33,65},{65,97},{97,1},{2,34}... | collective-permute-start | bytes 2457608 | tf_op jit(solution)/shard_map/ppermute | solution.py:26
  62.5 20.7 %collective-permute-start.9 = (bf16[1,128,3200]{2,1,0:T(8,128)(2,1)S(1)}, bf16[1,128,3200]{2,1,0:T(8,128)(2,1)}, u32[]{:S(2)}, u32[]{:S(2)}) collective-permute-start(bf16[1,128,3200]{2,1,0:T(8,128)(2,1)S(1)} %slice.29), channel_id=1, source_target_pairs={{0,96},{32,0},{64,32},{96,64},{1,97},{33,1},{65,33},{97,65},{2,98}... | collective-permute-start | bytes 2457608 | tf_op jit(solution)/shard_map/ppermute | solution.py:26
  65.3 53.4 %collective-permute-start.3 = (bf16[2,128,3200]{2,1,0:T(8,128)(2,1)S(1)}, bf16[2,128,3200]{2,1,0:T(8,128)(2,1)}, u32[]{:S(2)}, u32[]{:S(2)}) collective-permute-start(bf16[2,128,3200]{2,1,0:T(8,128)(2,1)S(1)} %copy-done.1), channel_id=1, source_target_pairs={{0,1},{1,0},{2,3},{3,2},{4,5},{5,4},{6,7},{7,6},{8,9},{9,8},{10,11... | collective-permute-start | bytes 4915208 | tf_op jit(solution)/shard_map/ppermute | solution.py:22
  82.0 24.1 %collective-permute-start.13 = (bf16[1,128,3200]{2,1,0:T(8,128)(2,1)}, bf16[1,128,3200]{2,1,0:T(8,128)(2,1)}, u32[]{:S(2)}, u32[]{:S(2)}) collective-permute-start(bf16[1,128,3200]{2,1,0:T(8,128)(2,1)} %collective-permute-done.8.refs_0_), channel_id=1, source_target_pairs={{0,1},{1,0},{2,3},{3,2},{4,5},{5,4},{6,7},{7,6},{8,9},{9,8},{10,11... | collective-permute-start | bytes 2457608 | tf_op jit(solution)/shard_map/ppermute | solution.py:22
  83.3 22.9 %collective-permute-start.14 = (bf16[1,128,3200]{2,1,0:T(8,128)(2,1)}, bf16[1,128,3200]{2,1,0:T(8,128)(2,1)}, u32[]{:S(2)}, u32[]{:S(2)}) collective-permute-start(bf16[1,128,3200]{2,1,0:T(8,128)(2,1)} %collective-permute-done.9.refs_1_), channel_id=1, source_target_pairs={{0,1},{1,0},{2,3},{3,2},{4,5},{5,4},{6,7},{7,6},{8,9},{9,8},{10,11... | collective-permute-start | bytes 2457608 | tf_op jit(solution)/shard_map/ppermute | solution.py:22
  83.7 44.1 %collective-permute-start.6 = (bf16[1,256,2048]{2,1,0:T(8,128)(2,1)}, bf16[1,256,2048]{2,1,0:T(8,128)(2,1)}, u32[]{:S(2)}, u32[]{:S(2)}) collective-permute-start(bf16[1,256,2048]{2,1,0:T(8,128)(2,1)} %get-tuple-element.56), channel_id=1, source_target_pairs={{0,6},{2,0},{4,10},{6,4},{8,14},{10,8},{12,18},{14,12},{16,22},{18... | collective-permute-start | bytes 3145736 | tf_op jit(solution)/shard_map/ppermute | solution.py:48
  86.2 41.7 %collective-permute-start.7 = (bf16[1,256,2048]{2,1,0:T(8,128)(2,1)}, bf16[1,256,2048]{2,1,0:T(8,128)(2,1)S(1)}, u32[]{:S(2)}, u32[]{:S(2)}) collective-permute-start(bf16[1,256,2048]{2,1,0:T(8,128)(2,1)} %get-tuple-element.57), channel_id=1, source_target_pairs={{0,2},{2,4},{4,6},{6,8},{8,10},{10,12},{12,14},{14,16},{16,18},{18... | collective-permute-start | bytes 3145736 | tf_op jit(solution)/shard_map/ppermute | solution.py:32
  114.8 13.2 %collective-permute-start.15 = (bf16[2,256,256]{2,1,0:T(8,128)(2,1)}, bf16[2,256,256]{2,1,0:T(8,128)(2,1)S(1)}, u32[]{:S(2)}, u32[]{:S(2)}) collective-permute-start(bf16[2,256,256]{2,1,0:T(8,128)(2,1)} %attend.5), channel_id=1, source_target_pairs={{0,64},{32,96},{64,0},{96,32},{1,65},{33,97},{65,1},{97,33},{2,66}... | collective-permute-start | bytes 786440 | tf_op jit(solution)/shard_map/ppermute | solution.py:26
  118.7 11.8 %collective-permute-start.16 = (bf16[2,256,256]{2,1,0:T(8,128)(2,1)S(1)}, bf16[2,256,256]{2,1,0:T(8,128)(2,1)S(1)}, u32[]{:S(2)}, u32[]{:S(2)}) collective-permute-start(bf16[2,256,256]{2,1,0:T(8,128)(2,1)S(1)} %copy-done.23), channel_id=1, source_target_pairs={{0,32},{32,64},{64,96},{96,0},{1,33},{33,65},{65,97},{97,1},{2,34}... | collective-permute-start | bytes 786440 | tf_op jit(solution)/shard_map/ppermute | solution.py:26
  138.2 18.0 %collective-permute-start.17 = (bf16[2,128,3200]{2,1,0:T(8,128)(2,1)}, bf16[2,128,3200]{2,1,0:T(8,128)(2,1)S(1)}, u32[]{:S(2)}, u32[]{:S(2)}) collective-permute-start(bf16[2,128,3200]{2,1,0:T(8,128)(2,1)} %out.3), channel_id=1, source_target_pairs={{0,1},{1,0},{2,3},{3,2},{4,5},{5,4},{6,7},{7,6},{8,9},{9,8},{10,11... | collective-permute-start | bytes 4915208 | tf_op jit(solution)/shard_map/ppermute | solution.py:22
  138.8 52.5 %collective-permute-start.23 = (bf16[1,256,2048]{2,1,0:T(8,128)(2,1)S(1)}, bf16[1,256,2048]{2,1,0:T(8,128)(2,1)}, u32[]{:S(2)}, u32[]{:S(2)}) collective-permute-start(bf16[1,256,2048]{2,1,0:T(8,128)(2,1)S(1)} %copy-done.10), channel_id=1, source_target_pairs={{0,2},{2,4},{4,6},{6,8},{8,10},{10,12},{12,14},{14,16},{16,18},{18... | collective-permute-start | bytes 3145736 | tf_op jit(solution)/shard_map/ppermute | solution.py:32
  142.5 53.9 %collective-permute-start.25 = (bf16[1,256,2048]{2,1,0:T(8,128)(2,1)S(1)}, bf16[1,256,2048]{2,1,0:T(8,128)(2,1)}, u32[]{:S(2)}, u32[]{:S(2)}) collective-permute-start(bf16[1,256,2048]{2,1,0:T(8,128)(2,1)S(1)} %copy-done.9), channel_id=1, source_target_pairs={{0,4},{2,6},{4,8},{6,10},{8,12},{10,14},{12,16},{14,18},{16,20},{1... | collective-permute-start | bytes 3145736 | tf_op jit(solution)/shard_map/ppermute | solution.py:32
  144.5 51.9 %collective-permute-start.24 = (bf16[1,256,2048]{2,1,0:T(8,128)(2,1)}, bf16[1,256,2048]{2,1,0:T(8,128)(2,1)}, u32[]{:S(2)}, u32[]{:S(2)}) collective-permute-start(bf16[1,256,2048]{2,1,0:T(8,128)(2,1)} %collective-permute-done.6), channel_id=1, source_target_pairs={{6,4},{0,6},{10,8},{4,10},{14,12},{8,14},{18,16},{12,18},{22,20},{... | collective-permute-start | bytes 3145736 | tf_op jit(solution)/shard_map/ppermute | solution.py:49
  170.1 45.2 %collective-permute-start.22 = (bf16[1,128,3200]{2,1,0:T(8,128)(2,1)S(1)}, bf16[1,128,3200]{2,1,0:T(8,128)(2,1)}, u32[]{:S(2)}, u32[]{:S(2)}) collective-permute-start(bf16[1,128,3200]{2,1,0:T(8,128)(2,1)S(1)} %copy-done.4), channel_id=1, source_target_pairs={{4,6},{6,0},{8,10},{10,4},{12,14},{14,8},{16,18},{18,12},{20,22},{... | collective-permute-start | bytes 2457608 | tf_op jit(solution)/shard_map/ppermute | solution.py:48
  174.2 41.2 %collective-permute-start.20 = (bf16[1,128,3200]{2,1,0:T(8,128)(2,1)}, bf16[1,128,3200]{2,1,0:T(8,128)(2,1)S(1)}, u32[]{:S(2)}, u32[]{:S(2)}) collective-permute-start(bf16[1,128,3200]{2,1,0:T(8,128)(2,1)} %get-tuple-element.66.refs_0_.z_ref), channel_id=1, source_target_pairs={{2,0},{4,2},{6,4},{8,6},{10,8},{12,10},{14,12},{16,14},{18,16},{20... | collective-permute-start | bytes 2457608 | tf_op jit(solution)/shard_map/ppermute | solution.py:32
  191.3 36.2 %collective-permute-start.21 = (bf16[1,128,3200]{2,1,0:T(8,128)(2,1)S(1)}, bf16[1,128,3200]{2,1,0:T(8,128)(2,1)S(1)}, u32[]{:S(2)}, u32[]{:S(2)}) collective-permute-start(bf16[1,128,3200]{2,1,0:T(8,128)(2,1)S(1)} %copy-done.6), channel_id=1, source_target_pairs={{4,0},{6,2},{8,4},{10,6},{12,8},{14,10},{16,12},{18,14},{20,16},{2... | collective-permute-start | bytes 2457608 | tf_op jit(solution)/shard_map/ppermute | solution.py:32
  227.5 25.7 %collective-permute-start.30 = (bf16[2,128,3200]{2,1,0:T(8,128)(2,1)}, bf16[2,128,3200]{2,1,0:T(8,128)(2,1)S(1)}, u32[]{:S(2)}, u32[]{:S(2)}) collective-permute-start(bf16[2,128,3200]{2,1,0:T(8,128)(2,1)} %get-tuple-element.83), channel_id=1, source_target_pairs={{0,1},{1,0},{2,3},{3,2},{4,5},{5,4},{6,7},{7,6},{8,9},{9,8},{10,11... | collective-permute-start | bytes 4915208 | tf_op jit(solution)/shard_map/ppermute | solution.py:22
  229.1 30.7 %collective-permute-start.26 = (bf16[1,128,3200]{2,1,0:T(8,128)(2,1)S(1)}, bf16[1,128,3200]{2,1,0:T(8,128)(2,1)S(1)}, u32[]{:S(2)}, u32[]{:S(2)}) collective-permute-start(bf16[1,128,3200]{2,1,0:T(8,128)(2,1)S(1)} %copy-done.5), channel_id=1, source_target_pairs={{2,0},{4,2},{6,4},{8,6},{10,8},{12,10},{14,12},{16,14},{18,16},{20... | collective-permute-start | bytes 2457608 | tf_op jit(solution)/shard_map/ppermute | solution.py:32
  231.0 28.8 %collective-permute-start.27 = (bf16[1,128,3200]{2,1,0:T(8,128)(2,1)}, bf16[1,128,3200]{2,1,0:T(8,128)(2,1)}, u32[]{:S(2)}, u32[]{:S(2)}) collective-permute-start(bf16[1,128,3200]{2,1,0:T(8,128)(2,1)} %collective-permute-done.22), channel_id=1, source_target_pairs={{6,0},{0,2},{10,4},{4,6},{14,8},{8,10},{18,12},{12,14},{22,16},{16... | collective-permute-start | bytes 2457608 | tf_op jit(solution)/shard_map/ppermute | solution.py:49
  (36 other events, 305.5 us)
Sparse Core Ops, SparseCore 0:
  21.2 52.7 all-gather.1

commit v5 on v4

--- a/solution.py
+++ b/solution.py
@@ -30,23 +30,6 @@
     peers = lax.axis_size(IMG)
     pairs = [(i, i + by) for i in range(peers) if 0 <= i + by < peers]
     return lax.ppermute(array, IMG, pairs)
-
-
-def around(place, side):
-    return place - place % LINE + (place % LINE + side) % LINE
-
-
-def two_on(array, by):
-    peers = lax.axis_size(IMG)
-    side = -by // 2
-    turning = 2 if by > 0 else 1
-
-    def middle(i):
-        return i + side + LINE * (by // 2) if i % LINE == turning else around(i, side)
-
-    ends = [(i, i + by) for i in range(peers) if 0 <= i + by < peers]
-    halfway = lax.ppermute(array, IMG, [(i, middle(i)) for i, _ in ends])
-    return halfway, lambda held: lax.ppermute(held, IMG, [(middle(i), j) for i, j in ends])
 
 
 def tile_owners(tile_counts, tile_total, tile_group):
@@ -151,7 +134,8 @@
                 inverse = 1.0 / jnp.sum(raised, axis=-1, keepdims=True)
                 soft = (raised * inverse).astype(jnp.bfloat16)
                 mixed = jnp.dot(soft, piece(2), preferred_element_type=jnp.float32)
-                outs[index][tile, :, head * HEAD_DIM : (head + 1) * HEAD_DIM] = mixed.astype(jnp.bfloat16)
+                columns = slice(head * HEAD_DIM, (head + 1) * HEAD_DIM)
+                outs[index][:, tile, :, columns] = mixed.astype(jnp.bfloat16).reshape(2, half, HEAD_DIM)
 
 
 def attend(sources, weight):
@@ -159,7 +143,7 @@
     tiles = sum(layout[0])
     _, half, depth = sources[0][0][0].shape
     width = weight.shape[1]
-    shape = (tiles, 2 * half, width // 3)
+    shape = (2, tiles, half, width // 3)
     arrays = [array for own, other in sources for array in (*own, *other)]
     return pl.pallas_call(
         functools.partial(attend_kernel, layout),
@@ -179,111 +163,117 @@
     )(*arrays, weight)
 
 
-def out_kernel(line_ref, *refs):
-    attended, weight_ref, part_ref, rows = refs[:LINE], refs[LINE], refs[LINE + 1], refs[LINE + 2]
-    tiles, half, block = part_ref.shape
-    share = attended[0].shape[2]
-
-    @pl.when(pl.program_id(0) == 0)
+def join_kernel(line_ref, mixing_ref, *refs):
+    own, other = refs[:LINE], refs[LINE : 2 * LINE]
+    own_weight_ref, other_weight_ref, scale_ref = refs[2 * LINE : 2 * LINE + 3]
+    inputs_hbm = refs[2 * LINE + 3 : 2 * LINE + 6]
+    z_ref, first_ref, second_ref, inverse_ref, rows, total, inputs, sems = refs[2 * LINE + 6 :]
+    step = pl.program_id(0)
+    _, tiles, half, share = own[0].shape
+    block = own_weight_ref.shape[1]
+    copies = [
+        pltpu.make_async_copy(source, inputs.at[i], sems.at[i]) for i, source in enumerate(inputs_hbm)
+    ]
+
+    @pl.when(step == 0)
     def _():
-        for distance, source in enumerate(attended):
+        for copy in copies:
+            copy.start()
+        for distance in range(LINE):
             start = pl.multiple_of(lax.rem(line_ref[0] + distance, LINE) * share, share)
-            rows[:, pl.ds(start, share)] = source[...].reshape(tiles * half, share)
-
-    total = jnp.dot(rows[...], weight_ref[...], preferred_element_type=jnp.float32)
-    part_ref[...] = total.astype(jnp.bfloat16).reshape(tiles, half, block)
-
-
-def out_project(line_arg, attended, out_weight, part):
-    tiles, full, share = attended[0].shape
-    half = full // 2
-    depth = out_weight.shape[1]
+            rows[0, :, pl.ds(start, share)] = own[distance][0].reshape(tiles * half, share)
+            rows[1, :, pl.ds(start, share)] = other[distance][...].reshape(tiles * half, share)
+
+    part = jnp.dot(rows[0], own_weight_ref[...], preferred_element_type=jnp.float32)
+    part += jnp.dot(rows[1], other_weight_ref[...], preferred_element_type=jnp.float32)
+    total[:, pl.ds(pl.multiple_of(step * block, block), block)] = part
+
+    @pl.when(step == pl.num_programs(0) - 1)
+    def _():
+        for copy in copies:
+            copy.wait()
+        chunk = 64
+        scale = mixing_ref[3] * scale_ref[...]
+        for tile in range(tiles):
+            for start in range(0, half, chunk):
+                span = slice(start, start + chunk)
+                joined = (
+                    (mixing_ref[2] + mixing_ref[3]) * inputs[0, tile, span].astype(jnp.float32)
+                    + mixing_ref[0] * inputs[1, tile, span].astype(jnp.float32)
+                    + mixing_ref[1] * inputs[2, tile, span].astype(jnp.float32)
+                    + scale * total[tile * half + start : tile * half + start + chunk]
+                )
+                centre = jnp.mean(joined, axis=-1, keepdims=True)
+                shifted = joined - centre
+                inverse = lax.rsqrt(jnp.mean(shifted * shifted, axis=-1, keepdims=True) + 1e-05)
+                z_rows = (shifted * inverse).astype(jnp.bfloat16)
+                z_ref[tile, span] = z_rows
+                (first_ref, second_ref)[tile][0, span] = z_rows
+                inverse_ref[tile, span] = jnp.broadcast_to(inverse, (chunk, 128))
+
+
+def join_rows(line_arg, mixing, attended, swapped, weights, scale, inputs):
+    _, tiles, half, share = attended[0].shape
+    depth = weights[0].shape[1]
     block = 640
+    weight_spec = pl.BlockSpec((LINE * share, block), lambda n, line: (0, n))
     return pl.pallas_call(
-        out_kernel,
+        join_kernel,
         grid_spec=pltpu.PrefetchScalarGridSpec(
             num_scalar_prefetch=1,
             grid=(depth // block,),
-            in_specs=[pl.BlockSpec((tiles, half, share), lambda n, line: (0, part, 0))] * LINE
-            + [pl.BlockSpec((LINE * share, block), lambda n, line: (0, n))],
-            out_specs=pl.BlockSpec((tiles, half, block), lambda n, line: (0, 0, n)),
-            scratch_shapes=[pltpu.VMEM((tiles * half, LINE * share), jnp.bfloat16)],
+            in_specs=[pl.BlockSpec(memory_space=pltpu.SMEM)]
+            + [pl.BlockSpec((1, tiles, half, share), lambda n, line: (0, 0, 0, 0))] * LINE
+            + [pl.BlockSpec((tiles, half, share), lambda n, line: (0, 0, 0))] * LINE
+            + [weight_spec, weight_spec, pl.BlockSpec((1, depth), lambda n, line: (0, 0))]
+            + [pl.BlockSpec(memory_space=pl.ANY)] * 3,
+            out_specs=[
+                pl.BlockSpec((tiles, half, depth), lambda n, line: (0, 0, 0)),
+                pl.BlockSpec((1, half, depth), lambda n, line: (0, 0, 0)),
+                pl.BlockSpec((1, half, depth), lambda n, line: (0, 0, 0)),
+                pl.BlockSpec((tiles, half, 128), lambda n, line: (0, 0, 0)),
+            ],
+            scratch_shapes=[
+                pltpu.VMEM((2, tiles * half, LINE * share), jnp.bfloat16),
+                pltpu.VMEM((tiles * half, depth), jnp.float32),
+                pltpu.VMEM((3, tiles, half, depth), jnp.bfloat16),
+                pltpu.SemaphoreType.DMA((3,)),
+            ],
         ),
-        out_shape=jax.ShapeDtypeStruct((tiles, half, depth), jnp.bfloat16),
-        compiler_params=pltpu.CompilerParams(vmem_limit_bytes=VMEM_BYTES),
-        cost_estimate=SMALL_COST,
-        name="out",
-    )(line_arg, *attended, out_weight)
-
-
-def join_kernel(
-    mixing_ref, tokens_ref, early_ref, mid_ref, own_ref, other_ref, scale_ref, z_ref, inverse_ref
-):
-    inputs = tokens_ref[0].astype(jnp.float32)
-    attended_out = own_ref[0].astype(jnp.float32) + other_ref[0].astype(jnp.float32)
-    joined = (
-        mixing_ref[0] * early_ref[0].astype(jnp.float32)
-        + mixing_ref[1] * mid_ref[0].astype(jnp.float32)
-        + (mixing_ref[2] + mixing_ref[3]) * inputs
-        + (mixing_ref[3] * scale_ref[...]) * attended_out
-    )
-    centre = jnp.mean(joined, axis=-1, keepdims=True)
-    shifted = joined - centre
-    inverse = lax.rsqrt(jnp.mean(shifted * shifted, axis=-1, keepdims=True) + 1e-05)
-    z_ref[0] = (shifted * inverse).astype(jnp.bfloat16)
-    inverse_ref[0] = jnp.broadcast_to(inverse, inverse_ref.shape[1:])
-
-
-def join_rows(tile, mixing, tokens, early, mid, own, other, scale):
-    _, half, depth = tokens.shape
-    block = 64
-    spec = pl.BlockSpec((1, block, depth), lambda r: (tile, r, 0))
-    return pl.pallas_call(
-        join_kernel,
-        grid=(half // block,),
         out_shape=[
+            jax.ShapeDtypeStruct((tiles, half, depth), jnp.bfloat16),
             jax.ShapeDtypeStruct((1, half, depth), jnp.bfloat16),
-            jax.ShapeDtypeStruct((1, half, 128), jnp.float32),
+            jax.ShapeDtypeStruct((1, half, depth), jnp.bfloat16),
+            jax.ShapeDtypeStruct((tiles, half, 128), jnp.float32),
         ],
-        in_specs=[pl.BlockSpec(memory_space=pltpu.SMEM)]
-        + [spec] * 5
-        + [pl.BlockSpec((1, depth), lambda r: (0, 0))],
-        out_specs=[
-            pl.BlockSpec((1, block, depth), lambda r: (0, r, 0)),
-            pl.BlockSpec((1, block, 128), lambda r: (0, r, 0)),
-        ],
         compiler_params=pltpu.CompilerParams(vmem_limit_bytes=VMEM_BYTES),
         cost_estimate=SMALL_COST,
         name="join",
-    )(mixing, tokens, early, mid, own, other, scale)
-
-
-def final_kernel(own_ref, other_ref, z_ref, later_z_ref, inverse_ref, later_inverse_ref, out_ref):
-    first = pl.program_id(0) == 0
+    )(line_arg, mixing, *attended, *swapped, *weights, scale, *inputs)
+
+
+def final_kernel(own_ref, other_ref, z_ref, inverse_ref, out_ref):
     grad = own_ref[0].astype(jnp.float32) + other_ref[0].astype(jnp.float32)
-    normal = jnp.where(first, z_ref[0], later_z_ref[0]).astype(jnp.float32)
-    inverse = jnp.where(first, inverse_ref[0, :, :1], later_inverse_ref[0, :, :1])
+    normal = z_ref[0].astype(jnp.float32)
     mean = jnp.mean(grad, axis=-1, keepdims=True)
     along = jnp.mean(grad * normal, axis=-1, keepdims=True)
-    out_ref[0] = ((grad - mean - normal * along) * inverse).astype(jnp.bfloat16)
-
-
-def final_rows(own, other, z_tiles, inverse_tiles):
+    out_ref[0] = ((grad - mean - normal * along) * inverse_ref[0, :, :1]).astype(jnp.bfloat16)
+
+
+def final_rows(own, other, z_rows, inverse):
     tiles, half, depth = own.shape
     block = 64
     spec = pl.BlockSpec((1, block, depth), lambda t, r: (t, r, 0))
-    z_spec = pl.BlockSpec((1, block, depth), lambda t, r: (0, r, 0))
-    inverse_spec = pl.BlockSpec((1, block, 128), lambda t, r: (0, r, 0))
     return pl.pallas_call(
         final_kernel,
         grid=(tiles, half // block),
         out_shape=jax.ShapeDtypeStruct(own.shape, jnp.bfloat16),
-        in_specs=[spec, spec, z_spec, z_spec, inverse_spec, inverse_spec],
+        in_specs=[spec, spec, spec, pl.BlockSpec((1, block, 128), lambda t, r: (t, r, 0))],
         out_specs=spec,
         compiler_params=pltpu.CompilerParams(vmem_limit_bytes=VMEM_BYTES),
         cost_estimate=SMALL_COST,
         name="final",
-    )(own, other, *z_tiles, *inverse_tiles)
+    )(own, other, z_rows, inverse)
 
 
 def activate(preact):
@@ -297,12 +287,13 @@
     return jnp.where(preact >= 0.0, 1.0 - tail, tail), raised * inv_root_tau
 
 
-def project_kernel(core_ref, *refs):
-    sources = refs[:-4]
-    weight_ref, bias_ref, projected_ref, slope_ref = refs[-4:]
+def project_kernel(core_ref, own_ref, other_ref, weight_ref, bias_ref, projected_ref, slope_ref):
     core = core_ref[0]
-    tiles, _, half, block = projected_ref.shape
-    rows = jnp.concatenate([source[0] for source in sources], axis=0)
+    tiles, half, depth = own_ref.shape
+    block = weight_ref.shape[1]
+    rows = jnp.concatenate(
+        [own_ref[...].reshape(tiles * half, depth), other_ref[...].reshape(tiles * half, depth)], axis=0
+    )
     preact = jnp.dot(rows, weight_ref[...], preferred_element_type=jnp.float32) + bias_ref[...]
     cumulative, density = activate(preact)
     projected = (preact * cumulative).astype(jnp.bfloat16).reshape(2, tiles, 1, half, block)
@@ -312,17 +303,18 @@
 
 
 def home_project(core, own, other, weight, bias):
-    tiles = len(own)
-    _, half, depth = own[0].shape
+    tiles, half, depth = own.shape
     width = weight.shape[1]
     block = 512
+    whole = pl.BlockSpec((tiles, half, depth), lambda n, c: (0, 0, 0))
     projected, slope = pl.pallas_call(
         project_kernel,
         grid_spec=pltpu.PrefetchScalarGridSpec(
             num_scalar_prefetch=1,
             grid=(width // block,),
-            in_specs=[pl.BlockSpec((1, half, depth), lambda n, c: (0, 0, 0))] * (2 * tiles)
-            + [
+            in_specs=[
+                whole,
+                whole,
                 pl.BlockSpec((depth, block), lambda n, c: (0, n)),
                 pl.BlockSpec((1, block), lambda n, c: (0, n)),
             ],
@@ -338,7 +330,7 @@
         compiler_params=pltpu.CompilerParams(vmem_limit_bytes=VMEM_BYTES),
         cost_estimate=SMALL_COST,
         name="project",
-    )(core, *own, *other, weight, bias)
+    )(core, own, other, weight, bias)
     return projected.reshape(tiles, 2 * half, width), slope
 
 
@@ -401,20 +393,18 @@
     sources = refs[: 2 * count]
     weight_ref, bias_ref, projected_ref = refs[2 * count :]
     core = core_ref[0]
-    _, half, depth = sources[0].shape
+    _, half, _ = sources[0].shape
     block = weight_ref.shape[1]
     rows = jnp.concatenate([source[0] for source in sources], axis=0)
     preact = jnp.dot(rows, weight_ref[...], preferred_element_type=jnp.float32) + bias_ref[...]
-    projected = (preact * activate(preact)[0]).astype(jnp.bfloat16)
-    projected = projected.reshape(count, 2, half, block)
-    for index in range(count):
-        projected_ref[index, pl.ds(core, 1)] = projected[index, :1]
-        projected_ref[index, pl.ds(1 - core, 1)] = projected[index, 1:]
-
-
-def owner_project(core, pairs, weight, bias):
-    count = len(pairs)
-    _, half, depth = pairs[0][0].shape
+    projected = (preact * activate(preact)[0]).astype(jnp.bfloat16).reshape(2, count, 1, half, block)
+    projected_ref[:, pl.ds(core, 1)] = projected[0]
+    projected_ref[:, pl.ds(1 - core, 1)] = projected[1]
+
+
+def owner_project(core, own, weight, bias):
+    count = len(own)
+    _, half, depth = own[0].shape
     width = weight.shape[1]
     block = 512
     projected = pl.pallas_call(
@@ -433,7 +423,7 @@
         compiler_params=pltpu.CompilerParams(vmem_limit_bytes=VMEM_BYTES),
         cost_estimate=SMALL_COST,
         name="owner",
-    )(core, *[rows for pair in pairs for rows in pair], weight, bias)
+    )(core, *own, *[swap(rows) for rows in own], weight, bias)
     return projected.reshape(count, 2 * half, width)
 
 
@@ -478,47 +468,52 @@
         slot = jnp.clip(tile - my_first, 0, own_tiles - count)
         return lax.dynamic_slice_in_dim(grad_out, slot, count, axis=0)
 
-    packets = [packet(distance, within, 1) for distance in (1, 2) for within in range(tile_group)]
-    from_low, from_high, packets = lax.optimization_barrier((from_low, from_high, packets))
+    packets = [packet(2, 0, 1), packet(2, 1, 1), packet(1, 0, tile_group)]
+    other_weight = swap(out_weight)
+    from_low, from_high, packets, other_weight = lax.optimization_barrier(
+        (from_low, from_high, packets, other_weight)
+    )
     far_first = along_z(from_low[:1], 1)
     far_second = along_z(from_high[1:], -1)
-    weight, packets = lax.optimization_barrier((weight, packets))
-    halfway, far_on = two_on(packets[3], 2)
-    far_back = [along_img(packets[2], 2), None]
-    near_back = [along_img(packets[0], 1), along_img(packets[1], 1)]
-
-    far_others = [swap(far_first), swap(far_second)]
-    att_low, att_high = attend(
-        [([rows], [swap(rows)]) for rows in (from_low, from_high)], weight
-    )
-    far_first, far_second, att_low = lax.optimization_barrier((far_first, far_second, att_low))
-    (att_far,) = attend([([far_first, far_second], far_others)], weight)
-    (att_own,) = attend([([normed], [swap(normed)])], weight)
-    att_far, att_low, att_high = along_z(att_far, 2), along_z(att_low, -1), along_z(att_high, 1)
-    att_own, halfway, near_back[0] = lax.optimization_barrier((att_own, halfway, near_back[0]))
-    far_back[1] = far_on(halfway)
-    attended = [att_own, att_low, att_far, att_high]
-    line_arg = line_place.astype(jnp.int32).reshape(1)
-    part_other = swap(out_project(line_arg, attended, out_weight, 1))
-    part_own = out_project(line_arg, attended, out_weight, 0)
+    far_first, far_second, weight, packets = lax.optimization_barrier(
+        (far_first, far_second, weight, packets)
+    )
+    far_back = [along_img(packets[0], 2), along_img(packets[1], 2)]
+    near_back = along_img(packets[2], 1)
+
+    att_low, att_high, att_own = attend(
+        [([rows], [swap(rows)]) for rows in (from_low, from_high, normed)], weight
+    )
+    far_first, far_second, att_own, far_back[0] = lax.optimization_barrier(
+        (far_first, far_second, att_own, far_back[0])
+    )
+    (att_far,) = attend(
+        [([far_first, far_second], [swap(far_first), swap(far_second)])], weight
+    )
+    attended = [att_own, along_z(att_low, -1), along_z(att_far, 2), along_z(att_high, 1)]
     raised_logits = jnp.exp(layer_logits)
     mixing = raised_logits / jnp.sum(raised_logits)
-    scale = layer_scale.reshape(1, -1)
-    joined = [
-        join_rows(tile, mixing, tokens, tap_early, tap_mid, part_own, part_other, scale)
-        for tile in range(tile_group)
-    ]
-    z_tiles = [z_rows for z_rows, _ in joined]
-    inverse_tiles = [inverse for _, inverse in joined]
-
-    near_first = along_img(z_tiles[0], -1)
-    far_first = along_img(z_tiles[0], -2)
-    halfway, far_on = two_on(z_tiles[1], -2)
+    z_rows, z_first, z_second, inverse_std = join_rows(
+        line_place.astype(jnp.int32).reshape(1),
+        mixing,
+        attended,
+        [swap(rows[1]) for rows in attended],
+        [out_weight, other_weight],
+        layer_scale.reshape(1, -1),
+        [tokens, tap_early, tap_mid],
+    )
+
+    near = [along_img(z_first, -1)]
+    far = [along_img(z_first, -2)]
     bias = proj_bias.reshape(1, -1)
-    projected, slope = home_project(
-        core_arg, z_tiles, [swap(z_rows) for z_rows in z_tiles], proj_weight, bias
-    )
-    slope, near_back[1], far_back[1] = lax.optimization_barrier((slope, near_back[1], far_back[1]))
+    projected, slope = home_project(core_arg, z_rows, swap(z_rows), proj_weight, bias)
+    near[0], far[0], second, slope = lax.optimization_barrier((near[0], far[0], z_second, slope))
+    near.append(along_img(second, -1))
+    far.append(along_img(second, -2))
+    early = owner_project(core_arg, [near[0], far[0]], proj_weight, bias)
+    slope, early, near_back, far_back[1] = lax.optimization_barrier(
+        (slope, early, near_back, far_back[1])
+    )
 
     back = []
     for within in range(tile_group):
@@ -526,28 +521,14 @@
         owner = owner_of[tile]
         slot = jnp.clip(tile - my_first, 0, own_tiles - 1)
         here = lax.dynamic_index_in_dim(grad_out, slot, axis=0, keepdims=False)
-        near, far = near_back[within][0], far_back[within][0]
-        back.append(jnp.where(owner == place, here, jnp.where(owner == place - 1, near, far)))
+        other = jnp.where(owner == place - 1, near_back[within], far_back[within][0])
+        back.append(jnp.where(owner == place, here, other))
     back_rows = jnp.stack(back, axis=0)
     grad_own, grad_other = home_grad(core_arg, slope, back_rows, proj_weight)
 
-    near_first, far_first, halfway, second, grad_other = lax.optimization_barrier(
-        (near_first, far_first, halfway, z_tiles[1], grad_other)
-    )
-    near_second = along_img(second, -1)
-    far_second = far_on(halfway)
-
-    def guests(first, second):
-        return owner_project(
-            core_arg, [(first, swap(first)), (second, swap(second))], proj_weight, bias
-        )
-
-    early = guests(near_first, far_first)
-    grad_joined = final_rows(grad_own, swap(grad_other), z_tiles, inverse_tiles)
-    near_second, far_second, early, grad_joined = lax.optimization_barrier(
-        (near_second, far_second, early, grad_joined)
-    )
-    late = guests(near_second, far_second)
+    grad_joined = final_rows(grad_own, swap(grad_other), z_rows, inverse_std)
+    near[1], far[1], grad_joined = lax.optimization_barrier((near[1], far[1], grad_joined))
+    late = owner_project(core_arg, [near[1], far[1]], proj_weight, bias)
 
     offset = my_first - place * tile_group
     held = first_tile[place + 1] - my_first

time: 293 us -> 350 us (1.19)
  waiting for transfers between devices: 58.8 us -> 128 us
  Pallas kernels: 123 us -> 110 us
  starting transfers between devices: 59.4 us -> 55.8 us
    ppermute x6 -> x7, waiting for transfers between devices: 12.1 us -> 74.6 us  [along_img(): return lax.ppermute(array, IMG, pairs)]
    ppermute x4 -> x0, starting transfers between devices: 15 us -> none  [the longest x2 8.53 us: two_on(): lax.ppermute(held, IMG, [(middle(i), j) for i, j in ends])]
    pallas_call x4 -> x1, Pallas kernels: 21.5 us -> 13 us  [join_rows(): pl.pallas_call(join_kernel, grid_spec=pltpu.PrefetchScalarGridSpec(num_sc...]
    ppermute x6 -> x7, starting transfers between devices: 19.9 us -> 26.6 us  [along_img(): return lax.ppermute(array, IMG, pairs)]
    ppermute x10, waiting for transfers between devices: 45.1 us -> 51.7 us  [along_z(): return lax.ppermute(array, 'z', [(i, (i + by) % LINE) for i in range(LINE)])]
    ppermute x13 -> x16, starting transfers between devices: 8.67 us -> 13.3 us  [swap(): return lax.ppermute(array, 'head', [(0, 1), (1, 0)])]
    pallas_call x3 -> x2, Pallas kernels: 31.7 us -> 27.5 us  [attend(): pl.pallas_call(functools.partial(attend_kernel, layout), out_shape=[jax.S...]
    unnamed x63 -> x59, local copies, waits for them, and re-layouts: 9.02 us -> 7.39 us
  transfers between devices with their start and end apart: 34 -> 34, of which waited for: 7 -> 11; matrix products, arithmetic and copies ran while one was open for 5% -> 4% of each run, Pallas kernels for 35% -> 20%
where the time goes in v5:
time: 350 us; the launch traced here: 345 us
  waiting for transfers between devices  128 us (37%)
  Pallas kernels  110 us (31%)
  starting transfers between devices  55.8 us (16%)
  between operations  22.8 us (7%)
  local copies, waits for them, and re-layouts  21.6 us (6%)
  other arithmetic  6.72 us (2%)
    ppermute x7, waiting for transfers between devices, along_img(): return lax.ppermute(array, IMG, pairs)  74.6 us
    ppermute x10, waiting for transfers between devices, along_z(): return lax.ppermute(array, 'z', [(i, (i + by) % LINE) for i in range(LINE)])  51.7 us
    pallas_call x2, Pallas kernels, owner_project(): pl.pallas_call(functools.partial(owner_kernel, count), grid_spec=pltpu.Pr...  28.7 us
    pallas_call x2, Pallas kernels, attend(): pl.pallas_call(functools.partial(attend_kernel, layout), out_shape=[jax.S...  27.5 us
    ppermute x7, starting transfers between devices, along_img(): return lax.ppermute(array, IMG, pairs)  26.6 us
    ppermute x10, starting transfers between devices, along_z(): return lax.ppermute(array, 'z', [(i, (i + by) % LINE) for i in range(LINE)])  15.9 us
    pallas_call x1, Pallas kernels, home_project(): pl.pallas_call(project_kernel, grid_spec=pltpu.PrefetchScalarGridSpec(num...  15.1 us
    pallas_call x1, Pallas kernels, home_grad(): pl.pallas_call(grad_kernel, grid_spec=pltpu.PrefetchScalarGridSpec(num_sc...  15 us
  transfers between devices with their start and end apart: 34, of which 11 were waited for; matrix products, arithmetic and copies ran while one was open for 4% of the time, Pallas kernels for 20%

profile of v5, /device:TPU:31, one launch (start us, length us, event | category | flops | bytes accessed | tf_op | source)
XLA Modules:
  0.0 345.0 jit_solution(11079047018084542432)
XLA Ops:
  10.0 3.3 collective-permute-start.1
  14.1 6.0 %norm.1.refs_4_ = bf16[2,128,3200]{2,1,0:T(8,128)(2,1)} custom-call(bf16[2,128,3200]{2,1,0:T(8,128)(2,1)} %refs_11_.1), custom_call_target="tpu_custom_call" | custom-call | flops 1 | bytes 1 | tf_op jit(solution)/shard_map/norm/pallas_call | solution.py:67
  28.4 3.2 constant_dynamic-slice_fusion.1
  31.6 3.2 constant_dynamic-slice_fusion.2
  34.8 26.1 %collective-permute-done.3.refs_0_ = bf16[2,128,3200]{2,1,0:T(8,128)(2,1)S(1)} collective-permute-done((bf16[2,128,3200]{2,1,0:T(8,128)(2,1)S(1)}, bf16[2,128,3200]{2,1,0:T(8,128)(2,1)S(1)}, u32[]{:S(2)}, u32[]{:S(2)}) %collective-permute-start.3) | collective-permute-done | bytes 1638432 | tf_op jit(solution)/shard_map/ppermute | solution.py:26
  67.3 13.7 %collective-permute-done.6.refs_0_ = bf16[1,128,3200]{2,1,0:T(8,128)(2,1)} collective-permute-done((bf16[1,128,3200]{2,1,0:T(8,128)(2,1)S(1)}, bf16[1,128,3200]{2,1,0:T(8,128)(2,1)}, u32[]{:S(2)}, u32[]{:S(2)}) %collective-permute-start.6) | collective-permute-done | bytes 819232 | tf_op jit(solution)/shard_map/ppermute | solution.py:26
  81.6 3.5 %collective-permute-start.11 = (bf16[1,256,2048]{2,1,0:T(8,128)(2,1)}, bf16[1,256,2048]{2,1,0:T(8,128)(2,1)S(1)}, u32[]{:S(2)}, u32[]{:S(2)}) collective-permute-start(bf16[1,256,2048]{2,1,0:T(8,128)(2,1)} %get-tuple-element.59), channel_id=1, source_target_pairs={{0,4},{2,6},{4,8},{6,10},{8,12},{10,14},{12,16},{14,18},{16,20},{1... | collective-permute-start | bytes 3145736 | tf_op jit(solution)/shard_map/ppermute | solution.py:32
  85.1 19.0 %attend.2 = (bf16[2,2,128,256]{3,2,1,0:T(8,128)(2,1)}, bf16[2,2,128,256]{3,2,1,0:T(8,128)(2,1)}, bf16[2,2,128,256]{3,2,1,0:T(8,128)(2,1)}) custom-call(bf16[2,128,3200]{2,1,0:T(8,128)(2,1)} %copy-done.2, bf16[2,128,3200]{2,1,0:T(8,128)(2,1)} %collective-permute-done.8.refs_1_, bf16[2,128,3200]{2,1,0:T(8,128)(2,1)} %collective-permute-done.4.refs_2_, ...), custom_call_target="tpu_custom_call" | custom-call | flops 1 | bytes 1 | tf_op jit(solution)/shard_map/attend/pallas_call | solution.py:148
  104.1 3.6 %collective-permute-done.11 = bf16[1,256,2048]{2,1,0:T(8,128)(2,1)S(1)} collective-permute-done((bf16[1,256,2048]{2,1,0:T(8,128)(2,1)}, bf16[1,256,2048]{2,1,0:T(8,128)(2,1)S(1)}, u32[]{:S(2)}, u32[]{:S(2)}) %collective-permute-start.11) | collective-permute-done | bytes 1048608 | tf_op jit(solution)/shard_map/ppermute | solution.py:32
  115.3 4.2 %collective-permute-done.12.refs_1_ = bf16[2,2,128,256]{3,2,1,0:T(8,128)(2,1)S(1)} collective-permute-done((bf16[2,2,128,256]{3,2,1,0:T(8,128)(2,1)}, bf16[2,2,128,256]{3,2,1,0:T(8,128)(2,1)S(1)}, u32[]{:S(2)}, u32[]{:S(2)}) %collective-permute-start.12) | collective-permute-done | bytes 262176 | tf_op jit(solution)/shard_map/ppermute | solution.py:26
  122.9 8.5 %attend.3 = bf16[2,2,128,256]{3,2,1,0:T(8,128)(2,1)} custom-call(bf16[1,128,3200]{2,1,0:T(8,128)(2,1)} %collective-permute-done.6.refs_0_, bf16[1,128,3200]{2,1,0:T(8,128)(2,1)} %collective-permute-done.7.refs_1_, bf16[1,128,3200]{2,1,0:T(8,128)(2,1)} %copy-done.8, bf16[1,128,3200]{2,1,0:T(8,128)(2,1)} %copy-done.9, ...), custom_call_target="tpu_custom_call" | custom-call | flops 1 | bytes 1 | tf_op jit(solution)/shard_map/attend/pallas_call | solution.py:148
  134.1 7.1 %collective-permute-done.15.refs_2_ = bf16[2,2,128,256]{3,2,1,0:T(8,128)(2,1)S(1)} collective-permute-done((bf16[2,2,128,256]{3,2,1,0:T(8,128)(2,1)}, bf16[2,2,128,256]{3,2,1,0:T(8,128)(2,1)S(1)}, u32[]{:S(2)}, u32[]{:S(2)}) %collective-permute-start.15) | collective-permute-done | bytes 262176 | tf_op jit(solution)/shard_map/ppermute | solution.py:26
  144.1 13.0 %join.1 = (bf16[2,128,3200]{2,1,0:T(8,128)(2,1)}, bf16[1,128,3200]{2,1,0:T(8,128)(2,1)}, bf16[1,128,3200]{2,1,0:T(8,128)(2,1)}, f32[2,128,128]{2,1,0:T(8,128)}) custom-call(s32[1]{0:T(128)} %bitcast.4.line_ref, f32[4]{0:T(128)} %exponential_divide_fusion.mixing_ref, bf16[2,2,128,256]{3,2,1,0:T(8,128)(2,1)} %get-tuple-element.60.refs_0_, ...), custom_call_target="tpu_custom_call" | custom-call | flops 1 | bytes 1 | tf_op jit(solution)/shard_map/join/pallas_call | solution.py:220
  157.2 5.3 %collective-permute-start.26 = (bf16[2,256,2048]{2,1,0:T(8,128)(2,1)}, bf16[2,256,2048]{2,1,0:T(8,128)(2,1)S(1)}, u32[]{:S(2)}, u32[]{:S(2)}) collective-permute-start(bf16[2,256,2048]{2,1,0:T(8,128)(2,1)} %constant_dynamic-slice_fusion.1), channel_id=1, source_target_pairs={{0,2},{2,4},{4,6},{6,8},{8,10},{10,12},{12,14},{14,16},{16,18},{18... | collective-permute-start | bytes 6291464 | tf_op jit(solution)/shard_map/ppermute | solution.py:32
  166.4 7.8 %collective-permute-start.27 = (bf16[1,256,2048]{2,1,0:T(8,128)(2,1)S(1)}, bf16[1,256,2048]{2,1,0:T(8,128)(2,1)}, u32[]{:S(2)}, u32[]{:S(2)}) collective-permute-start(bf16[1,256,2048]{2,1,0:T(8,128)(2,1)S(1)} %copy-done.5), channel_id=1, source_target_pairs={{0,4},{2,6},{4,8},{6,10},{8,12},{10,14},{12,16},{14,18},{16,20},{1... | collective-permute-start | bytes 3145736 | tf_op jit(solution)/shard_map/ppermute | solution.py:32
  174.3 15.1 %project.1 = (bf16[2,2,128,2048]{3,2,1,0:T(8,128)(2,1)}, f32[512,2048]{1,0:T(8,128)}) custom-call(s32[1]{0:T(128)} %bitcast.3.core_ref, bf16[2,128,3200]{2,1,0:T(8,128)(2,1)} %get-tuple-element.66.own_ref.z_ref, bf16[2,128,3200]{2,1,0:T(8,128)(2,1)} %collective-permute-done.21.other_ref, bf16[3200,2048]{1,0:T(8,128)(2,1)} %refs_4_.3, f32[1,2048]{1,0:T(1,128)} %bitcast.54), custom_call_target="tpu_custom_call" | custom-call | flops 1 | bytes 1 | tf_op jit(solution)/shard_map/project/pallas_call | solution.py:310
  189.4 38.6 %collective-permute-done.22.refs_0_ = bf16[1,128,3200]{2,1,0:T(8,128)(2,1)} collective-permute-done((bf16[1,128,3200]{2,1,0:T(8,128)(2,1)}, bf16[1,128,3200]{2,1,0:T(8,128)(2,1)}, u32[]{:S(2)}, u32[]{:S(2)}) %collective-permute-start.22) | collective-permute-done | bytes 819232 | tf_op jit(solution)/shard_map/ppermute | solution.py:32
  234.5 14.4 %owner.2 = bf16[2,2,128,2048]{3,2,1,0:T(8,128)(2,1)} custom-call(s32[1]{0:T(128)} %bitcast.3.core_ref, bf16[1,128,3200]{2,1,0:T(8,128)(2,1)} %collective-permute-done.22.refs_0_, bf16[1,128,3200]{2,1,0:T(8,128)(2,1)} %collective-permute-done.23.refs_1_, bf16[1,128,3200]{2,1,0:T(8,128)(2,1)} %collective-permute-done.24.refs_2_, ...), custom_call_target="tpu_custom_call" | custom-call | flops 1 | bytes 1 | tf_op jit(solution)/shard_map/owner/pallas_call | solution.py:410
  252.6 15.0 %grad.1 = (bf16[2,128,3200]{2,1,0:T(8,128)(2,1)}, bf16[2,128,3200]{2,1,0:T(8,128)(2,1)}) custom-call(s32[1]{0:T(128)} %bitcast.3.core_ref, f32[512,2048]{1,0:T(8,128)} %get-tuple-element.78.slope_ref, bf16[2,2,128,2048]{3,2,1,0:T(8,128)(2,1)} %pad_maximum_fusion.back_own_ref.back_other_ref, ...), custom_call_target="tpu_custom_call" | custom-call | flops 1 | bytes 1 | tf_op jit(solution)/shard_map/grad/pallas_call | solution.py:371
  270.0 4.2 %collective-permute-start.29 = (bf16[1,128,3200]{2,1,0:T(8,128)(2,1)S(1)}, bf16[1,128,3200]{2,1,0:T(8,128)(2,1)}, u32[]{:S(2)}, u32[]{:S(2)}) collective-permute-start(bf16[1,128,3200]{2,1,0:T(8,128)(2,1)S(1)} %copy-done.22), channel_id=1, source_target_pairs={{4,0},{6,2},{8,4},{10,6},{12,8},{14,10},{16,12},{18,14},{20,16},{2... | collective-permute-start | bytes 2457608 | tf_op jit(solution)/shard_map/ppermute | solution.py:32
  275.4 5.0 %final.1 = bf16[2,128,3200]{2,1,0:T(8,128)(2,1)} custom-call(bf16[2,128,3200]{2,1,0:T(8,128)(2,1)} %get-tuple-element.82.own_ref, bf16[2,128,3200]{2,1,0:T(8,128)(2,1)} %copy-done.4, bf16[2,128,3200]{2,1,0:T(8,128)(2,1)} %get-tuple-element.66.own_ref.z_ref, f32[2,128,128]{2,1,0:T(8,128)} %get-tuple-element.84.inverse_ref), custom_call_target="tpu_custom_call" | custom-call | flops 1 | bytes 1 | tf_op jit(solution)/shard_map/final/pallas_call | solution.py:267
  280.5 13.6 %collective-permute-done.28.refs_0_ = bf16[1,128,3200]{2,1,0:T(8,128)(2,1)S(1)} collective-permute-done((bf16[1,128,3200]{2,1,0:T(8,128)(2,1)S(1)}, bf16[1,128,3200]{2,1,0:T(8,128)(2,1)S(1)}, u32[]{:S(2)}, u32[]{:S(2)}) %collective-permute-start.28) | collective-permute-done | bytes 819232 | tf_op jit(solution)/shard_map/ppermute | solution.py:32
  294.1 18.8 %collective-permute-done.29.refs_1_ = bf16[1,128,3200]{2,1,0:T(8,128)(2,1)} collective-permute-done((bf16[1,128,3200]{2,1,0:T(8,128)(2,1)S(1)}, bf16[1,128,3200]{2,1,0:T(8,128)(2,1)}, u32[]{:S(2)}, u32[]{:S(2)}) %collective-permute-start.29) | collective-permute-done | bytes 819232 | tf_op jit(solution)/shard_map/ppermute | solution.py:32
  317.1 14.3 %owner.3 = bf16[2,2,128,2048]{3,2,1,0:T(8,128)(2,1)} custom-call(s32[1]{0:T(128)} %bitcast.3.core_ref, bf16[1,128,3200]{2,1,0:T(8,128)(2,1)} %copy-done.10, bf16[1,128,3200]{2,1,0:T(8,128)(2,1)} %collective-permute-done.29.refs_1_, bf16[1,128,3200]{2,1,0:T(8,128)(2,1)} %collective-permute-done.31.refs_2_, ...), custom_call_target="tpu_custom_call" | custom-call | flops 1 | bytes 1 | tf_op jit(solution)/shard_map/owner/pallas_call | solution.py:410
  (144 shorter events, 55.6 us)
Async XLA Ops:
  7.2 74.4 %all-gather.2.cloned.1.call-start = ((), (), s32[]{:S(2)}) async-start(), calls=%async_computation | async-start | bytes 5222400 | tf_op jit(solution)/shard_map/all_gather | solution.py:456
  8.3 11.8 %collective-permute-start = (bf16[50,768]{1,0:T(8,128)(2,1)S(1)}, bf16[50,768]{1,0:T(8,128)(2,1)S(1)}, u32[]{:S(2)}, u32[]{:S(2)}) collective-permute-start(bf16[50,768]{1,0:T(8,128)(2,1)S(1)} %get-tuple-element.105), channel_id=1, source_target_pairs={{0,32},{32,64},{64,96},{96,0},{1,33},{33,65},{65,97},{97,1},{2,34}... | collective-permute-start | bytes 230408 | tf_op jit(solution)/shard_map/ppermute | solution.py:26
  10.0 10.1 %collective-permute-start.1 = (bf16[50,768]{1,0:T(8,128)(2,1)S(1)}, bf16[50,768]{1,0:T(8,128)(2,1)S(1)}, u32[]{:S(2)}, u32[]{:S(2)}) collective-permute-start(bf16[50,768]{1,0:T(8,128)(2,1)S(1)} %get-tuple-element.107), channel_id=1, source_target_pairs={{0,64},{32,96},{64,0},{96,32},{1,65},{33,97},{65,1},{97,33},{2,66}... | collective-permute-start | bytes 230408 | tf_op jit(solution)/shard_map/ppermute | solution.py:26
  21.1 39.9 %collective-permute-start.5 = (bf16[1024,3200]{1,0:T(8,128)(2,1)}, bf16[1024,3200]{1,0:T(8,128)(2,1)}, u32[]{:S(2)}, u32[]{:S(2)}) collective-permute-start(bf16[1024,3200]{1,0:T(8,128)(2,1)} %refs_8_.1), channel_id=1, source_target_pairs={{0,1},{1,0},{2,3},{3,2},{4,5},{5,4},{6,7},{7,6},{8,9},{9,8},{10,11... | collective-permute-start | bytes 19660808 | tf_op jit(solution)/shard_map/ppermute | solution.py:22
  22.7 38.3 %collective-permute-start.3 = (bf16[2,128,3200]{2,1,0:T(8,128)(2,1)S(1)}, bf16[2,128,3200]{2,1,0:T(8,128)(2,1)S(1)}, u32[]{:S(2)}, u32[]{:S(2)}) collective-permute-start(bf16[2,128,3200]{2,1,0:T(8,128)(2,1)S(1)} %copy-done.1), channel_id=1, source_target_pairs={{0,32},{32,64},{64,96},{96,0},{1,33},{33,65},{65,97},{97,1},{2,34}... | collective-permute-start | bytes 4915208 | tf_op jit(solution)/shard_map/ppermute | solution.py:26
  23.4 37.5 %collective-permute-start.4 = (bf16[2,128,3200]{2,1,0:T(8,128)(2,1)S(1)}, bf16[2,128,3200]{2,1,0:T(8,128)(2,1)}, u32[]{:S(2)}, u32[]{:S(2)}) collective-permute-start(bf16[2,128,3200]{2,1,0:T(8,128)(2,1)S(1)} %copy-done.1), channel_id=1, source_target_pairs={{0,96},{32,0},{64,32},{96,64},{1,97},{33,1},{65,33},{97,65},{2,98}... | collective-permute-start | bytes 4915208 | tf_op jit(solution)/shard_map/ppermute | solution.py:26
  61.0 20.0 %collective-permute-start.6 = (bf16[1,128,3200]{2,1,0:T(8,128)(2,1)S(1)}, bf16[1,128,3200]{2,1,0:T(8,128)(2,1)}, u32[]{:S(2)}, u32[]{:S(2)}) collective-permute-start(bf16[1,128,3200]{2,1,0:T(8,128)(2,1)S(1)} %slice.46), channel_id=1, source_target_pairs={{0,32},{32,64},{64,96},{96,0},{1,33},{33,65},{65,97},{97,1},{2,34}... | collective-permute-start | bytes 2457608 | tf_op jit(solution)/shard_map/ppermute | solution.py:26
  62.8 18.8 %collective-permute-start.7 = (bf16[1,128,3200]{2,1,0:T(8,128)(2,1)S(1)}, bf16[1,128,3200]{2,1,0:T(8,128)(2,1)}, u32[]{:S(2)}, u32[]{:S(2)}) collective-permute-start(bf16[1,128,3200]{2,1,0:T(8,128)(2,1)S(1)} %slice.47), channel_id=1, source_target_pairs={{0,96},{32,0},{64,32},{96,64},{1,97},{33,1},{65,33},{97,65},{2,98}... | collective-permute-start | bytes 2457608 | tf_op jit(solution)/shard_map/ppermute | solution.py:26
  65.1 19.9 %collective-permute-start.10 = (bf16[2,128,3200]{2,1,0:T(8,128)(2,1)S(1)}, bf16[2,128,3200]{2,1,0:T(8,128)(2,1)}, u32[]{:S(2)}, u32[]{:S(2)}) collective-permute-start(bf16[2,128,3200]{2,1,0:T(8,128)(2,1)S(1)} %copy-done.1), channel_id=1, source_target_pairs={{0,1},{1,0},{2,3},{3,2},{4,5},{5,4},{6,7},{7,6},{8,9},{9,8},{10,11... | collective-permute-start | bytes 4915208 | tf_op jit(solution)/shard_map/ppermute | solution.py:22
  66.8 18.3 %collective-permute-start.8 = (bf16[2,128,3200]{2,1,0:T(8,128)(2,1)S(1)}, bf16[2,128,3200]{2,1,0:T(8,128)(2,1)}, u32[]{:S(2)}, u32[]{:S(2)}) collective-permute-start(bf16[2,128,3200]{2,1,0:T(8,128)(2,1)S(1)} %collective-permute-done.3.refs_0_), channel_id=1, source_target_pairs={{0,1},{1,0},{2,3},{3,2},{4,5},{5,4},{6,7},{7,6},{8,9},{9,8},{10,11... | collective-permute-start | bytes 4915208 | tf_op jit(solution)/shard_map/ppermute | solution.py:22
  66.8 18.3 %collective-permute-start.9 = (bf16[2,128,3200]{2,1,0:T(8,128)(2,1)}, bf16[2,128,3200]{2,1,0:T(8,128)(2,1)}, u32[]{:S(2)}, u32[]{:S(2)}) collective-permute-start(bf16[2,128,3200]{2,1,0:T(8,128)(2,1)} %collective-permute-done.4.refs_2_), channel_id=1, source_target_pairs={{0,1},{1,0},{2,3},{3,2},{4,5},{5,4},{6,7},{7,6},{8,9},{9,8},{10,11... | collective-permute-start | bytes 4915208 | tf_op jit(solution)/shard_map/ppermute | solution.py:22
  81.6 26.2 %collective-permute-start.11 = (bf16[1,256,2048]{2,1,0:T(8,128)(2,1)}, bf16[1,256,2048]{2,1,0:T(8,128)(2,1)S(1)}, u32[]{:S(2)}, u32[]{:S(2)}) collective-permute-start(bf16[1,256,2048]{2,1,0:T(8,128)(2,1)} %get-tuple-element.59), channel_id=1, source_target_pairs={{0,4},{2,6},{4,8},{6,10},{8,12},{10,14},{12,16},{14,18},{16,20},{1... | collective-permute-start | bytes 3145736 | tf_op jit(solution)/shard_map/ppermute | solution.py:32
  107.8 13.3 %collective-permute-start.13 = (bf16[1,128,3200]{2,1,0:T(8,128)(2,1)}, bf16[1,128,3200]{2,1,0:T(8,128)(2,1)S(1)}, u32[]{:S(2)}, u32[]{:S(2)}) collective-permute-start(bf16[1,128,3200]{2,1,0:T(8,128)(2,1)} %collective-permute-done.6.refs_0_), channel_id=1, source_target_pairs={{0,1},{1,0},{2,3},{3,2},{4,5},{5,4},{6,7},{7,6},{8,9},{9,8},{10,11... | collective-permute-start | bytes 2457608 | tf_op jit(solution)/shard_map/ppermute | solution.py:22
  110.8 10.4 %collective-permute-start.14 = (bf16[1,128,3200]{2,1,0:T(8,128)(2,1)}, bf16[1,128,3200]{2,1,0:T(8,128)(2,1)S(1)}, u32[]{:S(2)}, u32[]{:S(2)}) collective-permute-start(bf16[1,128,3200]{2,1,0:T(8,128)(2,1)} %collective-permute-done.7.refs_1_), channel_id=1, source_target_pairs={{0,1},{1,0},{2,3},{3,2},{4,5},{5,4},{6,7},{7,6},{8,9},{9,8},{10,11... | collective-permute-start | bytes 2457608 | tf_op jit(solution)/shard_map/ppermute | solution.py:22
  114.0 19.4 %collective-permute-start.16 = (bf16[2,2,128,256]{3,2,1,0:T(8,128)(2,1)}, bf16[2,2,128,256]{3,2,1,0:T(8,128)(2,1)S(1)}, u32[]{:S(2)}, u32[]{:S(2)}) collective-permute-start(bf16[2,2,128,256]{3,2,1,0:T(8,128)(2,1)} %get-tuple-element.64), channel_id=1, source_target_pairs={{0,32},{32,64},{64,96},{96,0},{1,33},{33,65},{65,97},{97,1},{2,34}... | collective-permute-start | bytes 786440 | tf_op jit(solution)/shard_map/ppermute | solution.py:26
  119.5 23.8 %collective-permute-start.18 = (bf16[2,128,256]{2,1,0:T(8,128)(2,1)S(1)}, bf16[2,128,256]{2,1,0:T(8,128)(2,1)S(1)}, u32[]{:S(2)}, u32[]{:S(2)}) collective-permute-start(bf16[2,128,256]{2,1,0:T(8,128)(2,1)S(1)} %slice_bitcast_fusion.2), channel_id=1, source_target_pairs={{0,1},{1,0},{2,3},{3,2},{4,5},{5,4},{6,7},{7,6},{8,9},{9,8},{10,11... | collective-permute-start | bytes 393224 | tf_op jit(solution)/shard_map/ppermute | solution.py:22
  133.4 9.9 %collective-permute-start.20 = (bf16[2,128,256]{2,1,0:T(8,128)(2,1)S(1)}, bf16[2,128,256]{2,1,0:T(8,128)(2,1)S(1)}, u32[]{:S(2)}, u32[]{:S(2)}) collective-permute-start(bf16[2,128,256]{2,1,0:T(8,128)(2,1)S(1)} %slice_bitcast_fusion), channel_id=1, source_target_pairs={{0,1},{1,0},{2,3},{3,2},{4,5},{5,4},{6,7},{7,6},{8,9},{9,8},{10,11... | collective-permute-start | bytes 393224 | tf_op jit(solution)/shard_map/ppermute | solution.py:22
  157.1 17.2 %collective-permute-start.21 = (bf16[2,128,3200]{2,1,0:T(8,128)(2,1)}, bf16[2,128,3200]{2,1,0:T(8,128)(2,1)}, u32[]{:S(2)}, u32[]{:S(2)}) collective-permute-start(bf16[2,128,3200]{2,1,0:T(8,128)(2,1)} %get-tuple-element.66.own_ref.z_ref), channel_id=1, source_target_pairs={{0,1},{1,0},{2,3},{3,2},{4,5},{5,4},{6,7},{7,6},{8,9},{9,8},{10,11... | collective-permute-start | bytes 4915208 | tf_op jit(solution)/shard_map/ppermute | solution.py:22
  157.2 91.7 %collective-permute-start.26 = (bf16[2,256,2048]{2,1,0:T(8,128)(2,1)}, bf16[2,256,2048]{2,1,0:T(8,128)(2,1)S(1)}, u32[]{:S(2)}, u32[]{:S(2)}) collective-permute-start(bf16[2,256,2048]{2,1,0:T(8,128)(2,1)} %constant_dynamic-slice_fusion.1), channel_id=1, source_target_pairs={{0,2},{2,4},{4,6},{6,8},{8,10},{10,12},{12,14},{14,16},{16,18},{18... | collective-permute-start | bytes 6291464 | tf_op jit(solution)/shard_map/ppermute | solution.py:32
  162.5 65.5 %collective-permute-start.22 = (bf16[1,128,3200]{2,1,0:T(8,128)(2,1)}, bf16[1,128,3200]{2,1,0:T(8,128)(2,1)}, u32[]{:S(2)}, u32[]{:S(2)}) collective-permute-start(bf16[1,128,3200]{2,1,0:T(8,128)(2,1)} %get-tuple-element.68), channel_id=1, source_target_pairs={{2,0},{4,2},{6,4},{8,6},{10,8},{12,10},{14,12},{16,14},{18,16},{20... | collective-permute-start | bytes 2457608 | tf_op jit(solution)/shard_map/ppermute | solution.py:32
  164.5 63.5 %collective-permute-start.23 = (bf16[1,128,3200]{2,1,0:T(8,128)(2,1)}, bf16[1,128,3200]{2,1,0:T(8,128)(2,1)}, u32[]{:S(2)}, u32[]{:S(2)}) collective-permute-start(bf16[1,128,3200]{2,1,0:T(8,128)(2,1)} %get-tuple-element.68), channel_id=1, source_target_pairs={{4,0},{6,2},{8,4},{10,6},{12,8},{14,10},{16,12},{18,14},{20,16},{2... | collective-permute-start | bytes 2457608 | tf_op jit(solution)/shard_map/ppermute | solution.py:32
  166.4 82.5 %collective-permute-start.27 = (bf16[1,256,2048]{2,1,0:T(8,128)(2,1)S(1)}, bf16[1,256,2048]{2,1,0:T(8,128)(2,1)}, u32[]{:S(2)}, u32[]{:S(2)}) collective-permute-start(bf16[1,256,2048]{2,1,0:T(8,128)(2,1)S(1)} %copy-done.5), channel_id=1, source_target_pairs={{0,4},{2,6},{4,8},{6,10},{8,12},{10,14},{12,16},{14,18},{16,20},{1... | collective-permute-start | bytes 3145736 | tf_op jit(solution)/shard_map/ppermute | solution.py:32
  268.1 26.0 %collective-permute-start.28 = (bf16[1,128,3200]{2,1,0:T(8,128)(2,1)S(1)}, bf16[1,128,3200]{2,1,0:T(8,128)(2,1)S(1)}, u32[]{:S(2)}, u32[]{:S(2)}) collective-permute-start(bf16[1,128,3200]{2,1,0:T(8,128)(2,1)S(1)} %copy-done.22), channel_id=1, source_target_pairs={{2,0},{4,2},{6,4},{8,6},{10,8},{12,10},{14,12},{16,14},{18,16},{20... | collective-permute-start | bytes 2457608 | tf_op jit(solution)/shard_map/ppermute | solution.py:32
  270.0 42.8 %collective-permute-start.29 = (bf16[1,128,3200]{2,1,0:T(8,128)(2,1)S(1)}, bf16[1,128,3200]{2,1,0:T(8,128)(2,1)}, u32[]{:S(2)}, u32[]{:S(2)}) collective-permute-start(bf16[1,128,3200]{2,1,0:T(8,128)(2,1)S(1)} %copy-done.22), channel_id=1, source_target_pairs={{4,0},{6,2},{8,4},{10,6},{12,8},{14,10},{16,12},{18,14},{20,16},{2... | collective-permute-start | bytes 2457608 | tf_op jit(solution)/shard_map/ppermute | solution.py:32
  (34 other events, 396.3 us)
Sparse Core Ops, SparseCore 0:
  21.2 52.7 all-gather.1

commit v6 on v5

--- a/solution.py
+++ b/solution.py
@@ -167,7 +167,7 @@
     own, other = refs[:LINE], refs[LINE : 2 * LINE]
     own_weight_ref, other_weight_ref, scale_ref = refs[2 * LINE : 2 * LINE + 3]
     inputs_hbm = refs[2 * LINE + 3 : 2 * LINE + 6]
-    z_ref, first_ref, second_ref, inverse_ref, rows, total, inputs, sems = refs[2 * LINE + 6 :]
+    z_ref, inverse_ref, rows, total, inputs, sems = refs[2 * LINE + 6 :]
     step = pl.program_id(0)
     _, tiles, half, share = own[0].shape
     block = own_weight_ref.shape[1]
@@ -206,9 +206,7 @@
                 centre = jnp.mean(joined, axis=-1, keepdims=True)
                 shifted = joined - centre
                 inverse = lax.rsqrt(jnp.mean(shifted * shifted, axis=-1, keepdims=True) + 1e-05)
-                z_rows = (shifted * inverse).astype(jnp.bfloat16)
-                z_ref[tile, span] = z_rows
-                (first_ref, second_ref)[tile][0, span] = z_rows
+                z_ref[tile, span] = (shifted * inverse).astype(jnp.bfloat16)
                 inverse_ref[tile, span] = jnp.broadcast_to(inverse, (chunk, 128))
 
 
@@ -229,8 +227,6 @@
             + [pl.BlockSpec(memory_space=pl.ANY)] * 3,
             out_specs=[
                 pl.BlockSpec((tiles, half, depth), lambda n, line: (0, 0, 0)),
-                pl.BlockSpec((1, half, depth), lambda n, line: (0, 0, 0)),
-                pl.BlockSpec((1, half, depth), lambda n, line: (0, 0, 0)),
                 pl.BlockSpec((tiles, half, 128), lambda n, line: (0, 0, 0)),
             ],
             scratch_shapes=[
@@ -242,8 +238,6 @@
         ),
         out_shape=[
             jax.ShapeDtypeStruct((tiles, half, depth), jnp.bfloat16),
-            jax.ShapeDtypeStruct((1, half, depth), jnp.bfloat16),
-            jax.ShapeDtypeStruct((1, half, depth), jnp.bfloat16),
             jax.ShapeDtypeStruct((tiles, half, 128), jnp.float32),
         ],
         compiler_params=pltpu.CompilerParams(vmem_limit_bytes=VMEM_BYTES),
@@ -389,42 +383,86 @@
     )(core, slope, back, back, weight)
 
 
-def owner_kernel(count, core_ref, *refs):
-    sources = refs[: 2 * count]
-    weight_ref, bias_ref, projected_ref = refs[2 * count :]
+def owner_kernel(core_ref, own_ref, other_ref, weight_ref, bias_ref, projected_ref):
     core = core_ref[0]
-    _, half, _ = sources[0].shape
+    tiles, half, depth = own_ref.shape
     block = weight_ref.shape[1]
-    rows = jnp.concatenate([source[0] for source in sources], axis=0)
+    rows = jnp.concatenate(
+        [own_ref[...].reshape(tiles * half, depth), other_ref[...].reshape(tiles * half, depth)], axis=0
+    )
     preact = jnp.dot(rows, weight_ref[...], preferred_element_type=jnp.float32) + bias_ref[...]
-    projected = (preact * activate(preact)[0]).astype(jnp.bfloat16).reshape(2, count, 1, half, block)
+    projected = (preact * activate(preact)[0]).astype(jnp.bfloat16).reshape(2, tiles, 1, half, block)
     projected_ref[:, pl.ds(core, 1)] = projected[0]
     projected_ref[:, pl.ds(1 - core, 1)] = projected[1]
 
 
-def owner_project(core, own, weight, bias):
-    count = len(own)
-    _, half, depth = own[0].shape
+def owner_project(core, own, other, weight, bias):
+    tiles, half, depth = own.shape
     width = weight.shape[1]
     block = 512
+    whole = pl.BlockSpec((tiles, half, depth), lambda n, c: (0, 0, 0))
     projected = pl.pallas_call(
-        functools.partial(owner_kernel, count),
+        owner_kernel,
         grid_spec=pltpu.PrefetchScalarGridSpec(
             num_scalar_prefetch=1,
             grid=(width // block,),
-            in_specs=[pl.BlockSpec((1, half, depth), lambda n, c: (0, 0, 0))] * (2 * count)
-            + [
+            in_specs=[
+                whole,
+                whole,
                 pl.BlockSpec((depth, block), lambda n, c: (0, n)),
                 pl.BlockSpec((1, block), lambda n, c: (0, n)),
             ],
-            out_specs=pl.BlockSpec((count, 2, half, block), lambda n, c: (0, 0, 0, n)),
+            out_specs=pl.BlockSpec((tiles, 2, half, block), lambda n, c: (0, 0, 0, n)),
         ),
-        out_shape=jax.ShapeDtypeStruct((count, 2, half, width), jnp.bfloat16),
+        out_shape=jax.ShapeDtypeStruct((tiles, 2, half, width), jnp.bfloat16),
         compiler_params=pltpu.CompilerParams(vmem_limit_bytes=VMEM_BYTES),
         cost_estimate=SMALL_COST,
         name="owner",
-    )(core, *own, *[swap(rows) for rows in own], weight, bias)
-    return projected.reshape(count, 2 * half, width)
+    )(core, own, other, weight, bias)
+    return projected.reshape(tiles, 2 * half, width)
+
+
+def place_kernel(first_slot, split, slots_ref, *refs):
+    low_ref, high_ref, out_ref = refs[0], refs[1], refs[-1]
+    slot = pl.program_id(0) + first_slot
+    index = slot + slots_ref[0]
+    rows = jnp.where(index < split, low_ref[...], high_ref[...])
+    out_ref[...] = jnp.where(slot < slots_ref[1], rows, jnp.zeros_like(rows))
+
+
+def place_tiles(slots, low, high, own_tiles, held):
+    tiles, full, width = low.shape
+    count = own_tiles // 2
+    first_slot = 0 if held is None else count
+    split = tiles if held is None else 2 * tiles
+
+    def spec(start):
+        def at(k, s):
+            return (jnp.clip(k + first_slot + s[0] - start, 0, tiles - 1), 0, 0)
+
+        return pl.BlockSpec((1, full, width), at)
+
+    in_specs = [spec(split - tiles), spec(split)]
+    operands = [low, high]
+    aliases = {}
+    if held is not None:
+        in_specs.append(pl.BlockSpec(memory_space=pl.ANY))
+        operands.append(held)
+        aliases = {3: 0}
+    return pl.pallas_call(
+        functools.partial(place_kernel, first_slot, split),
+        grid_spec=pltpu.PrefetchScalarGridSpec(
+            num_scalar_prefetch=1,
+            grid=(count,),
+            in_specs=in_specs,
+            out_specs=pl.BlockSpec((1, full, width), lambda k, s: (k + first_slot, 0, 0)),
+        ),
+        out_shape=jax.ShapeDtypeStruct((own_tiles, full, width), jnp.bfloat16),
+        input_output_aliases=aliases,
+        compiler_params=pltpu.CompilerParams(vmem_limit_bytes=VMEM_BYTES),
+        cost_estimate=SMALL_COST,
+        name="place",
+    )(slots, *operands)
 
 
 def on_device(
@@ -468,7 +506,7 @@
         slot = jnp.clip(tile - my_first, 0, own_tiles - count)
         return lax.dynamic_slice_in_dim(grad_out, slot, count, axis=0)
 
-    packets = [packet(2, 0, 1), packet(2, 1, 1), packet(1, 0, tile_group)]
+    packets = [packet(2, 0, tile_group), packet(1, 0, tile_group)]
     other_weight = swap(out_weight)
     from_low, from_high, packets, other_weight = lax.optimization_barrier(
         (from_low, from_high, packets, other_weight)
@@ -478,42 +516,44 @@
     far_first, far_second, weight, packets = lax.optimization_barrier(
         (far_first, far_second, weight, packets)
     )
-    far_back = [along_img(packets[0], 2), along_img(packets[1], 2)]
-    near_back = along_img(packets[2], 1)
-
-    att_low, att_high, att_own = attend(
-        [([rows], [swap(rows)]) for rows in (from_low, from_high, normed)], weight
-    )
-    far_first, far_second, att_own, far_back[0] = lax.optimization_barrier(
-        (far_first, far_second, att_own, far_back[0])
-    )
-    (att_far,) = attend(
-        [([far_first, far_second], [swap(far_first), swap(far_second)])], weight
-    )
+    far_back = along_img(packets[0], 2)
+    near_back = along_img(packets[1], 1)
+
+    far_others = [swap(far_first), swap(far_second)]
+    att_far, att_low, att_high = attend(
+        [([far_first, far_second], far_others)]
+        + [([rows], [swap(rows)]) for rows in (from_low, from_high)],
+        weight,
+    )
+    normed_other = swap(normed)
+    normed, att_far = lax.optimization_barrier((normed, att_far))
+    (att_own,) = attend([([normed], [normed_other])], weight)
     attended = [att_own, along_z(att_low, -1), along_z(att_far, 2), along_z(att_high, 1)]
+    swapped = [swap(rows[1]) for rows in attended]
+    swapped, far_back = lax.optimization_barrier((swapped, far_back))
     raised_logits = jnp.exp(layer_logits)
     mixing = raised_logits / jnp.sum(raised_logits)
-    z_rows, z_first, z_second, inverse_std = join_rows(
+    z_rows, inverse_std = join_rows(
         line_place.astype(jnp.int32).reshape(1),
         mixing,
         attended,
-        [swap(rows[1]) for rows in attended],
+        swapped,
         [out_weight, other_weight],
         layer_scale.reshape(1, -1),
         [tokens, tap_early, tap_mid],
     )
 
-    near = [along_img(z_first, -1)]
-    far = [along_img(z_first, -2)]
+    near = along_img(z_rows, -1)
     bias = proj_bias.reshape(1, -1)
     projected, slope = home_project(core_arg, z_rows, swap(z_rows), proj_weight, bias)
-    near[0], far[0], second, slope = lax.optimization_barrier((near[0], far[0], z_second, slope))
-    near.append(along_img(second, -1))
-    far.append(along_img(second, -2))
-    early = owner_project(core_arg, [near[0], far[0]], proj_weight, bias)
-    slope, early, near_back, far_back[1] = lax.optimization_barrier(
-        (slope, early, near_back, far_back[1])
-    )
+    near, z_later, slope = lax.optimization_barrier((near, z_rows, slope))
+    far = along_img(z_later, -2)
+    near_projected = owner_project(core_arg, near, swap(near), proj_weight, bias)
+    offset = my_first - place * tile_group
+    held = first_tile[place + 1] - my_first
+    slots = jnp.stack([offset, held]).astype(jnp.int32)
+    owner_rows = place_tiles(slots, projected, near_projected, own_tiles, None)
+    slope, near_projected, near_back = lax.optimization_barrier((slope, near_projected, near_back))
 
     back = []
     for within in range(tile_group):
@@ -521,24 +561,16 @@
         owner = owner_of[tile]
         slot = jnp.clip(tile - my_first, 0, own_tiles - 1)
         here = lax.dynamic_index_in_dim(grad_out, slot, axis=0, keepdims=False)
-        other = jnp.where(owner == place - 1, near_back[within], far_back[within][0])
+        other = jnp.where(owner == place - 1, near_back[within], far_back[within])
         back.append(jnp.where(owner == place, here, other))
     back_rows = jnp.stack(back, axis=0)
     grad_own, grad_other = home_grad(core_arg, slope, back_rows, proj_weight)
 
     grad_joined = final_rows(grad_own, swap(grad_other), z_rows, inverse_std)
-    near[1], far[1], grad_joined = lax.optimization_barrier((near[1], far[1], grad_joined))
-    late = owner_project(core_arg, [near[1], far[1]], proj_weight, bias)
-
-    offset = my_first - place * tile_group
-    held = first_tile[place + 1] - my_first
-    at_hand = [projected[0], projected[1], early[0], late[0], early[1], late[1]]
-    slots = []
-    for slot in range(own_tiles):
-        later = at_hand[min(slot + 1, len(at_hand) - 1)]
-        picked = jnp.where(offset == 0, at_hand[slot], later)
-        slots.append(jnp.where(slot < held, picked, jnp.zeros((), jnp.bfloat16)))
-    owner_rows = jnp.stack(slots, axis=0)
+    far, near_projected, grad_other = lax.optimization_barrier((far, near_projected, grad_other))
+    far_other, grad_joined = lax.optimization_barrier((swap(far), grad_joined))
+    far_projected = owner_project(core_arg, far, far_other, proj_weight, bias)
+    owner_rows = place_tiles(slots, near_projected, far_projected, own_tiles, owner_rows)
     return (owner_rows, grad_joined)
 
 

time: 350 us -> 315 us (0.900)
  waiting for transfers between devices: 128 us -> 97.7 us
  Pallas kernels: 110 us -> 120 us
  starting transfers between devices: 55.8 us -> 49 us
  local copies, waits for them, and re-layouts: 21.6 us -> 15.1 us
    ppermute x7 -> x4, waiting for transfers between devices: 74.6 us -> 41.5 us  [along_img(): return lax.ppermute(array, IMG, pairs)]
    pallas_call x2 -> x4, Pallas kernels: 28.7 us -> 38.7 us  [the longest x2 28.9 us: owner_project(): pl.pallas_call(owner_kernel, grid_spec=pltpu.PrefetchScalarGridSpec(num_s...]
    ppermute x7 -> x4, starting transfers between devices: 26.6 us -> 23.2 us  [along_img(): return lax.ppermute(array, IMG, pairs)]
    ppermute x16 -> x14, starting transfers between devices: 13.3 us -> 10 us  [swap(): return lax.ppermute(array, 'head', [(0, 1), (1, 0)])]
    unnamed x59 -> x48, local copies, waits for them, and re-layouts: 7.39 us -> 4.16 us
  transfers between devices with their start and end apart: 34 -> 29, of which waited for: 11 -> 8; matrix products, arithmetic and copies ran while one was open for 4% -> 5% of each run, Pallas kernels for 20% -> 29%
where the time goes in v6:
time: 315 us; the launch traced here: 310 us
  Pallas kernels  120 us (38%)
  waiting for transfers between devices  97.7 us (31%)
  starting transfers between devices  49 us (16%)
  between operations  21.3 us (7%)
  local copies, waits for them, and re-layouts  15.1 us (5%)
  other arithmetic  6.69 us (2%)
    ppermute x10, waiting for transfers between devices, along_z(): return lax.ppermute(array, 'z', [(i, (i + by) % LINE) for i in range(LINE)])  53.2 us
    ppermute x4, waiting for transfers between devices, along_img(): return lax.ppermute(array, IMG, pairs)  41.5 us
    pallas_call x2, Pallas kernels, owner_project(): pl.pallas_call(owner_kernel, grid_spec=pltpu.PrefetchScalarGridSpec(num_s...  28.9 us
    pallas_call x2, Pallas kernels, attend(): pl.pallas_call(functools.partial(attend_kernel, layout), out_shape=[jax.S...  27.5 us
    ppermute x4, starting transfers between devices, along_img(): return lax.ppermute(array, IMG, pairs)  23.2 us
    ppermute x10, starting transfers between devices, along_z(): return lax.ppermute(array, 'z', [(i, (i + by) % LINE) for i in range(LINE)])  15.8 us
    pallas_call x1, Pallas kernels, home_project(): pl.pallas_call(project_kernel, grid_spec=pltpu.PrefetchScalarGridSpec(num...  15.3 us
    pallas_call x1, Pallas kernels, home_grad(): pl.pallas_call(grad_kernel, grid_spec=pltpu.PrefetchScalarGridSpec(num_sc...  14.9 us
  transfers between devices with their start and end apart: 29, of which 8 were waited for; matrix products, arithmetic and copies ran while one was open for 5% of the time, Pallas kernels for 29%

profile of v6, /device:TPU:31, one launch (start us, length us, event | category | flops | bytes accessed | tf_op | source)
XLA Modules:
  0.0 309.6 jit_solution(122714244805392876)
XLA Ops:
  10.0 3.3 %collective-permute-start.1 = (bf16[50,768]{1,0:T(8,128)(2,1)S(1)}, bf16[50,768]{1,0:T(8,128)(2,1)S(1)}, u32[]{:S(2)}, u32[]{:S(2)}) collective-permute-start(bf16[50,768]{1,0:T(8,128)(2,1)S(1)} %get-tuple-element.91), channel_id=1, source_target_pairs={{0,64},{32,96},{64,0},{96,32},{1,65},{33,97},{65,1},{97,33},{2,66}... | collective-permute-start | bytes 230408 | tf_op jit(solution)/shard_map/ppermute | solution.py:26
  14.1 6.0 %norm.1.refs_0_ = bf16[2,128,3200]{2,1,0:T(8,128)(2,1)} custom-call(bf16[2,128,3200]{2,1,0:T(8,128)(2,1)} %refs_11_.1), custom_call_target="tpu_custom_call" | custom-call | flops 1 | bytes 1 | tf_op jit(solution)/shard_map/norm/pallas_call | solution.py:67
  27.6 4.8 %constant_dynamic-slice_fusion.1 = (bf16[2,256,2048]{2,1,0:T(8,128)(2,1)}, bf16[2,256,2048]{2,1,0:T(8,128)(2,1)}) fusion(bf16[6,256,2048]{2,1,0:T(8,128)(2,1)} %param.21, s32[]{:T(128)S(6)} %min.14, s32[]{:T(128)S(6)} %min.13), kind=kLoop, calls=%fused_computation.18 | loop fusion | bytes 8388616 | tf_op jit(solution)/shard_map/dynamic_slice | solution.py:507
  32.5 28.5 %collective-permute-done.3.refs_4_ = bf16[2,128,3200]{2,1,0:T(8,128)(2,1)S(1)} collective-permute-done((bf16[2,128,3200]{2,1,0:T(8,128)(2,1)S(1)}, bf16[2,128,3200]{2,1,0:T(8,128)(2,1)S(1)}, u32[]{:S(2)}, u32[]{:S(2)}) %collective-permute-start.3) | collective-permute-done | bytes 1638432 | tf_op jit(solution)/shard_map/ppermute | solution.py:26
  63.6 2.8 collective-permute-start.7
  66.9 16.7 %collective-permute-done.6.refs_0_ = bf16[1,128,3200]{2,1,0:T(8,128)(2,1)} collective-permute-done((bf16[1,128,3200]{2,1,0:T(8,128)(2,1)S(1)}, bf16[1,128,3200]{2,1,0:T(8,128)(2,1)}, u32[]{:S(2)}, u32[]{:S(2)}) %collective-permute-start.6) | collective-permute-done | bytes 819232 | tf_op jit(solution)/shard_map/ppermute | solution.py:26
  83.8 4.4 %collective-permute-start.20 = (bf16[2,256,2048]{2,1,0:T(8,128)(2,1)}, bf16[2,256,2048]{2,1,0:T(8,128)(2,1)S(1)}, u32[]{:S(2)}, u32[]{:S(2)}) collective-permute-start(bf16[2,256,2048]{2,1,0:T(8,128)(2,1)} %get-tuple-element.60), channel_id=1, source_target_pairs={{0,4},{2,6},{4,8},{6,10},{8,12},{10,14},{12,16},{14,18},{16,20},{1... | collective-permute-start | bytes 6291464 | tf_op jit(solution)/shard_map/ppermute | solution.py:32
  93.6 19.0 %attend.2 = (bf16[2,2,128,256]{3,2,1,0:T(8,128)(2,1)}, bf16[2,2,128,256]{3,2,1,0:T(8,128)(2,1)}, bf16[2,2,128,256]{3,2,1,0:T(8,128)(2,1)}) custom-call(bf16[1,128,3200]{2,1,0:T(8,128)(2,1)} %collective-permute-done.6.refs_0_, bf16[1,128,3200]{2,1,0:T(8,128)(2,1)} %collective-permute-done.7.refs_1_, bf16[1,128,3200]{2,1,0:T(8,128)(2,1)} %copy-done.8, ...), custom_call_target="tpu_custom_call" | custom-call | flops 1 | bytes 1 | tf_op jit(solution)/shard_map/attend/pallas_call | solution.py:148
  112.6 3.1 collective-permute-start.14
  117.8 8.6 %attend.3.refs_0_ = bf16[2,2,128,256]{3,2,1,0:T(8,128)(2,1)} custom-call(bf16[2,128,3200]{2,1,0:T(8,128)(2,1)} %norm.1.refs_0_, bf16[2,128,3200]{2,1,0:T(8,128)(2,1)} %collective-permute-done.12.refs_1_, bf16[3200,768]{1,0:T(8,128)(2,1)} %all-gather.2.cloned.1.call-done.refs_8_.refs_2_), custom_call_target="tpu_custom_call" | custom-call | flops 1 | bytes 1 | tf_op jit(solution)/shard_map/attend/pallas_call | solution.py:148
  129.8 7.8 %collective-permute-done.15.refs_3_ = bf16[2,2,128,256]{3,2,1,0:T(8,128)(2,1)S(1)} collective-permute-done((bf16[2,2,128,256]{3,2,1,0:T(8,128)(2,1)S(1)}, bf16[2,2,128,256]{3,2,1,0:T(8,128)(2,1)S(1)}, u32[]{:S(2)}, u32[]{:S(2)}) %collective-permute-start.15) | collective-permute-done | bytes 262176 | tf_op jit(solution)/shard_map/ppermute | solution.py:26
  140.4 12.4 %join.1 = (bf16[2,128,3200]{2,1,0:T(8,128)(2,1)}, f32[2,128,128]{2,1,0:T(8,128)}) custom-call(s32[1]{0:T(128)} %bitcast.5.line_ref, f32[4]{0:T(128)} %exponential_divide_fusion.mixing_ref, bf16[2,2,128,256]{3,2,1,0:T(8,128)(2,1)} %attend.3.refs_0_, bf16[2,2,128,256]{3,2,1,0:T(8,128)(2,1)} %copy-done.11, bf16[2,2,128,256]{3,2,1,0:T(8,128)(2,1)} %copy-done.10, ...), custom_call_target="tpu_custom_call" | custom-call | flops 1 | bytes 1 | tf_op jit(solution)/shard_map/join/pallas_call | solution.py:218
  155.0 14.7 %collective-permute-start.25 = (bf16[2,256,2048]{2,1,0:T(8,128)(2,1)}, bf16[2,256,2048]{2,1,0:T(8,128)(2,1)}, u32[]{:S(2)}, u32[]{:S(2)}) collective-permute-start(bf16[2,256,2048]{2,1,0:T(8,128)(2,1)} %get-tuple-element.71), channel_id=1, source_target_pairs={{0,2},{2,4},{4,6},{6,8},{8,10},{10,12},{12,14},{14,16},{16,18},{18... | collective-permute-start | bytes 6291464 | tf_op jit(solution)/shard_map/ppermute | solution.py:32
  170.9 15.3 %project.1 = (bf16[2,2,128,2048]{3,2,1,0:T(8,128)(2,1)}, f32[512,2048]{1,0:T(8,128)}) custom-call(s32[1]{0:T(128)} %bitcast.14.core_ref, bf16[2,128,3200]{2,1,0:T(8,128)(2,1)} %get-tuple-element.68.own_ref.z_ref, bf16[2,128,3200]{2,1,0:T(8,128)(2,1)} %copy-done.7, bf16[3200,2048]{1,0:T(8,128)(2,1)} %weight_ref.7, f32[1,2048]{1,0:T(1,128)} %bitcast.40), custom_call_target="tpu_custom_call" | custom-call | flops 1 | bytes 1 | tf_op jit(solution)/shard_map/project/pallas_call | solution.py:304
  186.1 17.8 %collective-permute-done.21.own_ref = bf16[2,128,3200]{2,1,0:T(8,128)(2,1)} collective-permute-done((bf16[2,128,3200]{2,1,0:T(8,128)(2,1)}, bf16[2,128,3200]{2,1,0:T(8,128)(2,1)}, u32[]{:S(2)}, u32[]{:S(2)}) %collective-permute-start.21) | collective-permute-done | bytes 1638432 | tf_op jit(solution)/shard_map/ppermute | solution.py:32
  204.8 2.2 collective-permute-start.23
  211.5 14.5 %owner.2 = bf16[2,2,128,2048]{3,2,1,0:T(8,128)(2,1)} custom-call(s32[1]{0:T(128)} %bitcast.14.core_ref, bf16[2,128,3200]{2,1,0:T(8,128)(2,1)} %collective-permute-done.21.own_ref, bf16[2,128,3200]{2,1,0:T(8,128)(2,1)} %collective-permute-done.24.other_ref, bf16[3200,2048]{1,0:T(8,128)(2,1)} %weight_ref.7, f32[1,2048]{1,0:T(1,128)} %bitcast.41), custom_call_target="tpu_custom_call" | custom-call | flops 1 | bytes 1 | tf_op jit(solution)/shard_map/owner/pallas_call | solution.py:404
  226.0 23.7 %collective-permute-done.25 = bf16[2,256,2048]{2,1,0:T(8,128)(2,1)} collective-permute-done((bf16[2,256,2048]{2,1,0:T(8,128)(2,1)}, bf16[2,256,2048]{2,1,0:T(8,128)(2,1)}, u32[]{:S(2)}, u32[]{:S(2)}) %collective-permute-start.25) | collective-permute-done | bytes 2097184 | tf_op jit(solution)/shard_map/ppermute | solution.py:32
  249.7 2.4 select_select_fusion.1
  253.7 14.9 %grad.1 = (bf16[2,128,3200]{2,1,0:T(8,128)(2,1)}, bf16[2,128,3200]{2,1,0:T(8,128)(2,1)}) custom-call(s32[1]{0:T(128)} %bitcast.14.core_ref, f32[512,2048]{1,0:T(8,128)} %get-tuple-element.73.slope_ref, bf16[2,2,128,2048]{3,2,1,0:T(8,128)(2,1)} %pad_maximum_fusion.back_own_ref.back_other_ref, ...), custom_call_target="tpu_custom_call" | custom-call | flops 1 | bytes 1 | tf_op jit(solution)/shard_map/grad/pallas_call | solution.py:365
  272.5 5.4 %place.2.refs_2_ = bf16[6,256,2048]{2,1,0:T(8,128)(2,1)} custom-call(s32[2]{0:T(128)} %pad_add_fusion.slots_ref, bf16[2,256,2048]{2,1,0:T(8,128)(2,1)} %bitcast.39, bf16[2,256,2048]{2,1,0:T(8,128)(2,1)} %bitcast.34), custom_call_target="tpu_custom_call" | custom-call | flops 1 | bytes 1 | tf_op jit(solution)/shard_map/place/pallas_call | solution.py:452
  277.9 4.9 %final.1 = bf16[2,128,3200]{2,1,0:T(8,128)(2,1)} custom-call(bf16[2,128,3200]{2,1,0:T(8,128)(2,1)} %get-tuple-element.79.own_ref, bf16[2,128,3200]{2,1,0:T(8,128)(2,1)} %collective-permute-done.27.other_ref, bf16[2,128,3200]{2,1,0:T(8,128)(2,1)} %get-tuple-element.68.own_ref.z_ref, f32[2,128,128]{2,1,0:T(8,128)} %get-tuple-element.80.inverse_ref), custom_call_target="tpu_custom_call" | custom-call | flops 1 | bytes 1 | tf_op jit(solution)/shard_map/final/pallas_call | solution.py:261
  284.0 14.4 %owner.3 = bf16[2,2,128,2048]{3,2,1,0:T(8,128)(2,1)} custom-call(s32[1]{0:T(128)} %bitcast.14.core_ref, bf16[2,128,3200]{2,1,0:T(8,128)(2,1)} %copy-done.5, bf16[2,128,3200]{2,1,0:T(8,128)(2,1)} %copy-done.6, bf16[3200,2048]{1,0:T(8,128)(2,1)} %weight_ref.7, f32[1,2048]{1,0:T(1,128)} %bitcast.42), custom_call_target="tpu_custom_call" | custom-call | flops 1 | bytes 1 | tf_op jit(solution)/shard_map/owner/pallas_call | solution.py:404
  298.4 4.4 %place.3 = bf16[6,256,2048]{2,1,0:T(8,128)(2,1)} custom-call(s32[2]{0:T(128)} %pad_add_fusion.slots_ref, bf16[2,256,2048]{2,1,0:T(8,128)(2,1)} %bitcast.35, bf16[2,256,2048]{2,1,0:T(8,128)(2,1)} %bitcast.36, bf16[6,256,2048]{2,1,0:T(8,128)(2,1)} %place.2.refs_2_), custom_call_target="tpu_custom_call", output_to_operand_aliasing={{}: (3, {})} | custom-call | flops 1 | bytes 1 | tf_op jit(solution)/shard_map/place/pallas_call | solution.py:452
  (121 shorter events, 36.5 us)
Async XLA Ops:
  7.2 76.6 %all-gather.2.cloned.1.call-start = ((), (), s32[]{:S(2)}) async-start(), calls=%async_computation | async-start | bytes 5222400 | tf_op jit(solution)/shard_map/all_gather | solution.py:494
  8.3 11.8 %collective-permute-start = (bf16[50,768]{1,0:T(8,128)(2,1)S(1)}, bf16[50,768]{1,0:T(8,128)(2,1)S(1)}, u32[]{:S(2)}, u32[]{:S(2)}) collective-permute-start(bf16[50,768]{1,0:T(8,128)(2,1)S(1)} %get-tuple-element.89), channel_id=1, source_target_pairs={{0,32},{32,64},{64,96},{96,0},{1,33},{33,65},{65,97},{97,1},{2,34}... | collective-permute-start | bytes 230408 | tf_op jit(solution)/shard_map/ppermute | solution.py:26
  10.0 10.1 %collective-permute-start.1 = (bf16[50,768]{1,0:T(8,128)(2,1)S(1)}, bf16[50,768]{1,0:T(8,128)(2,1)S(1)}, u32[]{:S(2)}, u32[]{:S(2)}) collective-permute-start(bf16[50,768]{1,0:T(8,128)(2,1)S(1)} %get-tuple-element.91), channel_id=1, source_target_pairs={{0,64},{32,96},{64,0},{96,32},{1,65},{33,97},{65,1},{97,33},{2,66}... | collective-permute-start | bytes 230408 | tf_op jit(solution)/shard_map/ppermute | solution.py:26
  21.1 39.9 %collective-permute-start.5 = (bf16[1024,3200]{1,0:T(8,128)(2,1)}, bf16[1024,3200]{1,0:T(8,128)(2,1)}, u32[]{:S(2)}, u32[]{:S(2)}) collective-permute-start(bf16[1024,3200]{1,0:T(8,128)(2,1)} %refs_8_.1), channel_id=1, source_target_pairs={{0,1},{1,0},{2,3},{3,2},{4,5},{5,4},{6,7},{7,6},{8,9},{9,8},{10,11... | collective-permute-start | bytes 19660808 | tf_op jit(solution)/shard_map/ppermute | solution.py:22
  22.7 38.3 %collective-permute-start.3 = (bf16[2,128,3200]{2,1,0:T(8,128)(2,1)S(1)}, bf16[2,128,3200]{2,1,0:T(8,128)(2,1)S(1)}, u32[]{:S(2)}, u32[]{:S(2)}) collective-permute-start(bf16[2,128,3200]{2,1,0:T(8,128)(2,1)S(1)} %copy-done.1), channel_id=1, source_target_pairs={{0,32},{32,64},{64,96},{96,0},{1,33},{33,65},{65,97},{97,1},{2,34}... | collective-permute-start | bytes 4915208 | tf_op jit(solution)/shard_map/ppermute | solution.py:26
  23.4 37.5 %collective-permute-start.4 = (bf16[2,128,3200]{2,1,0:T(8,128)(2,1)S(1)}, bf16[2,128,3200]{2,1,0:T(8,128)(2,1)}, u32[]{:S(2)}, u32[]{:S(2)}) collective-permute-start(bf16[2,128,3200]{2,1,0:T(8,128)(2,1)S(1)} %copy-done.1), channel_id=1, source_target_pairs={{0,96},{32,0},{64,32},{96,64},{1,97},{33,1},{65,33},{97,65},{2,98}... | collective-permute-start | bytes 4915208 | tf_op jit(solution)/shard_map/ppermute | solution.py:26
  61.0 28.3 %collective-permute-start.10 = (bf16[2,128,3200]{2,1,0:T(8,128)(2,1)S(1)}, bf16[2,128,3200]{2,1,0:T(8,128)(2,1)}, u32[]{:S(2)}, u32[]{:S(2)}) collective-permute-start(bf16[2,128,3200]{2,1,0:T(8,128)(2,1)S(1)} %collective-permute-done.3.refs_4_), channel_id=1, source_target_pairs={{0,1},{1,0},{2,3},{3,2},{4,5},{5,4},{6,7},{7,6},{8,9},{9,8},{10,11... | collective-permute-start | bytes 4915208 | tf_op jit(solution)/shard_map/ppermute | solution.py:22
  62.3 21.3 %collective-permute-start.6 = (bf16[1,128,3200]{2,1,0:T(8,128)(2,1)S(1)}, bf16[1,128,3200]{2,1,0:T(8,128)(2,1)}, u32[]{:S(2)}, u32[]{:S(2)}) collective-permute-start(bf16[1,128,3200]{2,1,0:T(8,128)(2,1)S(1)} %slice.30), channel_id=1, source_target_pairs={{0,32},{32,64},{64,96},{96,0},{1,33},{33,65},{65,97},{97,1},{2,34}... | collective-permute-start | bytes 2457608 | tf_op jit(solution)/shard_map/ppermute | solution.py:26
  63.6 20.2 %collective-permute-start.7 = (bf16[1,128,3200]{2,1,0:T(8,128)(2,1)S(1)}, bf16[1,128,3200]{2,1,0:T(8,128)(2,1)}, u32[]{:S(2)}, u32[]{:S(2)}) collective-permute-start(bf16[1,128,3200]{2,1,0:T(8,128)(2,1)S(1)} %slice.31), channel_id=1, source_target_pairs={{0,96},{32,0},{64,32},{96,64},{1,97},{33,1},{65,33},{97,65},{2,98}... | collective-permute-start | bytes 2457608 | tf_op jit(solution)/shard_map/ppermute | solution.py:26
  66.4 23.2 %collective-permute-start.11 = (bf16[2,128,3200]{2,1,0:T(8,128)(2,1)}, bf16[2,128,3200]{2,1,0:T(8,128)(2,1)}, u32[]{:S(2)}, u32[]{:S(2)}) collective-permute-start(bf16[2,128,3200]{2,1,0:T(8,128)(2,1)} %collective-permute-done.4.refs_6_), channel_id=1, source_target_pairs={{0,1},{1,0},{2,3},{3,2},{4,5},{5,4},{6,7},{7,6},{8,9},{9,8},{10,11... | collective-permute-start | bytes 4915208 | tf_op jit(solution)/shard_map/ppermute | solution.py:22
  66.9 50.9 %collective-permute-start.12 = (bf16[2,128,3200]{2,1,0:T(8,128)(2,1)S(1)}, bf16[2,128,3200]{2,1,0:T(8,128)(2,1)}, u32[]{:S(2)}, u32[]{:S(2)}) collective-permute-start(bf16[2,128,3200]{2,1,0:T(8,128)(2,1)S(1)} %copy-done.1), channel_id=1, source_target_pairs={{0,1},{1,0},{2,3},{3,2},{4,5},{5,4},{6,7},{7,6},{8,9},{9,8},{10,11... | collective-permute-start | bytes 4915208 | tf_op jit(solution)/shard_map/ppermute | solution.py:22
  83.8 55.9 %collective-permute-start.20 = (bf16[2,256,2048]{2,1,0:T(8,128)(2,1)}, bf16[2,256,2048]{2,1,0:T(8,128)(2,1)S(1)}, u32[]{:S(2)}, u32[]{:S(2)}) collective-permute-start(bf16[2,256,2048]{2,1,0:T(8,128)(2,1)} %get-tuple-element.60), channel_id=1, source_target_pairs={{0,4},{2,6},{4,8},{6,10},{8,12},{10,14},{12,16},{14,18},{16,20},{1... | collective-permute-start | bytes 6291464 | tf_op jit(solution)/shard_map/ppermute | solution.py:32
  112.6 16.5 %collective-permute-start.14 = (bf16[2,2,128,256]{3,2,1,0:T(8,128)(2,1)}, bf16[2,2,128,256]{3,2,1,0:T(8,128)(2,1)S(1)}, u32[]{:S(2)}, u32[]{:S(2)}) collective-permute-start(bf16[2,2,128,256]{3,2,1,0:T(8,128)(2,1)} %get-tuple-element.58), channel_id=1, source_target_pairs={{0,64},{32,96},{64,0},{96,32},{1,65},{33,97},{65,1},{97,33},{2,66}... | collective-permute-start | bytes 786440 | tf_op jit(solution)/shard_map/ppermute | solution.py:26
  116.9 12.7 %collective-permute-start.13 = (bf16[2,2,128,256]{3,2,1,0:T(8,128)(2,1)}, bf16[2,2,128,256]{3,2,1,0:T(8,128)(2,1)S(1)}, u32[]{:S(2)}, u32[]{:S(2)}) collective-permute-start(bf16[2,2,128,256]{3,2,1,0:T(8,128)(2,1)} %get-tuple-element.57), channel_id=1, source_target_pairs={{0,96},{32,0},{64,32},{96,64},{1,97},{33,1},{65,33},{97,65},{2,98}... | collective-permute-start | bytes 786440 | tf_op jit(solution)/shard_map/ppermute | solution.py:26
  127.3 12.4 %collective-permute-start.16 = (bf16[2,128,256]{2,1,0:T(8,128)(2,1)S(1)}, bf16[2,128,256]{2,1,0:T(8,128)(2,1)S(1)}, u32[]{:S(2)}, u32[]{:S(2)}) collective-permute-start(bf16[2,128,256]{2,1,0:T(8,128)(2,1)S(1)} %slice_bitcast_fusion.3), channel_id=1, source_target_pairs={{0,1},{1,0},{2,3},{3,2},{4,5},{5,4},{6,7},{7,6},{8,9},{9,8},{10,11... | collective-permute-start | bytes 393224 | tf_op jit(solution)/shard_map/ppermute | solution.py:22
  128.5 9.1 %collective-permute-start.15 = (bf16[2,2,128,256]{3,2,1,0:T(8,128)(2,1)S(1)}, bf16[2,2,128,256]{3,2,1,0:T(8,128)(2,1)S(1)}, u32[]{:S(2)}, u32[]{:S(2)}) collective-permute-start(bf16[2,2,128,256]{3,2,1,0:T(8,128)(2,1)S(1)} %copy-done.19), channel_id=1, source_target_pairs={{0,32},{32,64},{64,96},{96,0},{1,33},{33,65},{65,97},{97,1},{2,34}... | collective-permute-start | bytes 786440 | tf_op jit(solution)/shard_map/ppermute | solution.py:26
  129.1 10.5 %collective-permute-start.18 = (bf16[2,128,256]{2,1,0:T(8,128)(2,1)S(1)}, bf16[2,128,256]{2,1,0:T(8,128)(2,1)S(1)}, u32[]{:S(2)}, u32[]{:S(2)}) collective-permute-start(bf16[2,128,256]{2,1,0:T(8,128)(2,1)S(1)} %slice_bitcast_fusion.1), channel_id=1, source_target_pairs={{0,1},{1,0},{2,3},{3,2},{4,5},{5,4},{6,7},{7,6},{8,9},{9,8},{10,11... | collective-permute-start | bytes 393224 | tf_op jit(solution)/shard_map/ppermute | solution.py:22
  129.6 10.1 %collective-permute-start.17 = (bf16[2,128,256]{2,1,0:T(8,128)(2,1)S(1)}, bf16[2,128,256]{2,1,0:T(8,128)(2,1)S(1)}, u32[]{:S(2)}, u32[]{:S(2)}) collective-permute-start(bf16[2,128,256]{2,1,0:T(8,128)(2,1)S(1)} %slice_bitcast_fusion.2), channel_id=1, source_target_pairs={{0,1},{1,0},{2,3},{3,2},{4,5},{5,4},{6,7},{7,6},{8,9},{9,8},{10,11... | collective-permute-start | bytes 393224 | tf_op jit(solution)/shard_map/ppermute | solution.py:22
  152.8 16.9 %collective-permute-start.22 = (bf16[2,128,3200]{2,1,0:T(8,128)(2,1)}, bf16[2,128,3200]{2,1,0:T(8,128)(2,1)S(1)}, u32[]{:S(2)}, u32[]{:S(2)}) collective-permute-start(bf16[2,128,3200]{2,1,0:T(8,128)(2,1)} %get-tuple-element.68.own_ref.z_ref), channel_id=1, source_target_pairs={{0,1},{1,0},{2,3},{3,2},{4,5},{5,4},{6,7},{7,6},{8,9},{9,8},{10,11... | collective-permute-start | bytes 4915208 | tf_op jit(solution)/shard_map/ppermute | solution.py:22
  153.0 50.9 %collective-permute-start.21 = (bf16[2,128,3200]{2,1,0:T(8,128)(2,1)}, bf16[2,128,3200]{2,1,0:T(8,128)(2,1)}, u32[]{:S(2)}, u32[]{:S(2)}) collective-permute-start(bf16[2,128,3200]{2,1,0:T(8,128)(2,1)} %get-tuple-element.68.own_ref.z_ref), channel_id=1, source_target_pairs={{2,0},{4,2},{6,4},{8,6},{10,8},{12,10},{14,12},{16,14},{18,16},{20... | collective-permute-start | bytes 4915208 | tf_op jit(solution)/shard_map/ppermute | solution.py:32
  155.0 94.8 %collective-permute-start.25 = (bf16[2,256,2048]{2,1,0:T(8,128)(2,1)}, bf16[2,256,2048]{2,1,0:T(8,128)(2,1)}, u32[]{:S(2)}, u32[]{:S(2)}) collective-permute-start(bf16[2,256,2048]{2,1,0:T(8,128)(2,1)} %get-tuple-element.71), channel_id=1, source_target_pairs={{0,2},{2,4},{4,6},{6,8},{8,10},{10,12},{12,14},{14,16},{16,18},{18... | collective-permute-start | bytes 6291464 | tf_op jit(solution)/shard_map/ppermute | solution.py:32
  204.8 65.0 %collective-permute-start.23 = (bf16[2,128,3200]{2,1,0:T(8,128)(2,1)S(1)}, bf16[2,128,3200]{2,1,0:T(8,128)(2,1)S(1)}, u32[]{:S(2)}, u32[]{:S(2)}) collective-permute-start(bf16[2,128,3200]{2,1,0:T(8,128)(2,1)S(1)} %copy-done), channel_id=1, source_target_pairs={{4,0},{6,2},{8,4},{10,6},{12,8},{14,10},{16,12},{18,14},{20,16},{2... | collective-permute-start | bytes 4915208 | tf_op jit(solution)/shard_map/ppermute | solution.py:32
  268.6 9.2 %collective-permute-start.27 = (bf16[2,128,3200]{2,1,0:T(8,128)(2,1)}, bf16[2,128,3200]{2,1,0:T(8,128)(2,1)}, u32[]{:S(2)}, u32[]{:S(2)}) collective-permute-start(bf16[2,128,3200]{2,1,0:T(8,128)(2,1)} %get-tuple-element.76), channel_id=1, source_target_pairs={{0,1},{1,0},{2,3},{3,2},{4,5},{5,4},{6,7},{7,6},{8,9},{9,8},{10,11... | collective-permute-start | bytes 4915208 | tf_op jit(solution)/shard_map/ppermute | solution.py:22
  269.9 12.9 %collective-permute-start.26 = (bf16[2,128,3200]{2,1,0:T(8,128)(2,1)S(1)}, bf16[2,128,3200]{2,1,0:T(8,128)(2,1)S(1)}, u32[]{:S(2)}, u32[]{:S(2)}) collective-permute-start(bf16[2,128,3200]{2,1,0:T(8,128)(2,1)S(1)} %collective-permute-done.23.own_ref), channel_id=1, source_target_pairs={{0,1},{1,0},{2,3},{3,2},{4,5},{5,4},{6,7},{7,6},{8,9},{9,8},{10,11... | collective-permute-start | bytes 4915208 | tf_op jit(solution)/shard_map/ppermute | solution.py:22
  (26 other events, 302.6 us)
Sparse Core Ops, SparseCore 0:
  21.2 52.7 all-gather.1

commit v7 on v6

--- a/solution.py
+++ b/solution.py
@@ -437,10 +437,10 @@
     split = tiles if held is None else 2 * tiles
 
     def spec(start):
-        def at(k, s):
-            return (jnp.clip(k + first_slot + s[0] - start, 0, tiles - 1), 0, 0)
-
-        return pl.BlockSpec((1, full, width), at)
+        def at(k, r, s):
+            return (jnp.clip(k + first_slot + s[0] - start, 0, tiles - 1), r, 0)
+
+        return pl.BlockSpec((1, full // 2, width), at)
 
     in_specs = [spec(split - tiles), spec(split)]
     operands = [low, high]
@@ -453,9 +453,9 @@
         functools.partial(place_kernel, first_slot, split),
         grid_spec=pltpu.PrefetchScalarGridSpec(
             num_scalar_prefetch=1,
-            grid=(count,),
+            grid=(count, 2),
             in_specs=in_specs,
-            out_specs=pl.BlockSpec((1, full, width), lambda k, s: (k + first_slot, 0, 0)),
+            out_specs=pl.BlockSpec((1, full // 2, width), lambda k, r, s: (k + first_slot, r, 0)),
         ),
         out_shape=jax.ShapeDtypeStruct((own_tiles, full, width), jnp.bfloat16),
         input_output_aliases=aliases,
@@ -493,11 +493,6 @@
     sent = lax.dynamic_slice_in_dim(ladder, LINE - 1 - line_place, LINE, axis=0)
     weight = lax.all_gather(sent.reshape(LINE * depth_share, share), ("y", "x"), axis=0, tiled=True)
 
-    def packet(distance, within, count, first):
-        tile = (place + distance) * tile_group + within
-        slot = jnp.clip(tile - first, 0, own_tiles - count)
-        return lax.dynamic_slice_in_dim(grad_out, slot, count, axis=0)
-
     from_low = along_z(normed, 1)
     from_high = along_z(normed, -1)
 
@@ -513,22 +508,18 @@
     )
     far_first = along_z(from_low[:1], 1)
     far_second = along_z(from_high[1:], -1)
-    far_first, far_second, weight, packets = lax.optimization_barrier(
-        (far_first, far_second, weight, packets)
-    )
+    weight, packets = lax.optimization_barrier((weight, packets))
     far_back = along_img(packets[0], 2)
-    near_back = along_img(packets[1], 1)
 
     far_others = [swap(far_first), swap(far_second)]
-    att_far, att_low, att_high = attend(
+    att_far, att_low, att_high, att_own = attend(
         [([far_first, far_second], far_others)]
-        + [([rows], [swap(rows)]) for rows in (from_low, from_high)],
+        + [([rows], [swap(rows)]) for rows in (from_low, from_high, normed)],
         weight,
     )
-    normed_other = swap(normed)
-    normed, att_far = lax.optimization_barrier((normed, att_far))
-    (att_own,) = attend([([normed], [normed_other])], weight)
     attended = [att_own, along_z(att_low, -1), along_z(att_far, 2), along_z(att_high, 1)]
+    attended[2], near_packet = lax.optimization_barrier((attended[2], packets[1]))
+    near_back = along_img(near_packet, 1)
     swapped = [swap(rows[1]) for rows in attended]
     swapped, far_back = lax.optimization_barrier((swapped, far_back))
     raised_logits = jnp.exp(layer_logits)
@@ -546,14 +537,7 @@
     near = along_img(z_rows, -1)
     bias = proj_bias.reshape(1, -1)
     projected, slope = home_project(core_arg, z_rows, swap(z_rows), proj_weight, bias)
-    near, z_later, slope = lax.optimization_barrier((near, z_rows, slope))
-    far = along_img(z_later, -2)
-    near_projected = owner_project(core_arg, near, swap(near), proj_weight, bias)
-    offset = my_first - place * tile_group
-    held = first_tile[place + 1] - my_first
-    slots = jnp.stack([offset, held]).astype(jnp.int32)
-    owner_rows = place_tiles(slots, projected, near_projected, own_tiles, None)
-    slope, near_projected, near_back = lax.optimization_barrier((slope, near_projected, near_back))
+    slope, near_back = lax.optimization_barrier((slope, near_back))
 
     back = []
     for within in range(tile_group):
@@ -566,10 +550,16 @@
     back_rows = jnp.stack(back, axis=0)
     grad_own, grad_other = home_grad(core_arg, slope, back_rows, proj_weight)
 
+    near, z_later, grad_other = lax.optimization_barrier((near, z_rows, grad_other))
+    far = along_img(z_later, -2)
+    near_projected = owner_project(core_arg, near, swap(near), proj_weight, bias)
+    offset = my_first - place * tile_group
+    held = first_tile[place + 1] - my_first
+    slots = jnp.stack([offset, held]).astype(jnp.int32)
+    owner_rows = place_tiles(slots, projected, near_projected, own_tiles, None)
     grad_joined = final_rows(grad_own, swap(grad_other), z_rows, inverse_std)
-    far, near_projected, grad_other = lax.optimization_barrier((far, near_projected, grad_other))
-    far_other, grad_joined = lax.optimization_barrier((swap(far), grad_joined))
-    far_projected = owner_project(core_arg, far, far_other, proj_weight, bias)
+    far, grad_joined, owner_rows = lax.optimization_barrier((far, grad_joined, owner_rows))
+    far_projected = owner_project(core_arg, far, swap(far), proj_weight, bias)
     owner_rows = place_tiles(slots, near_projected, far_projected, own_tiles, owner_rows)
     return (owner_rows, grad_joined)
 

time: 315 us -> 320 us (1.016); the launches traced: 310 us -> 319 us
  waiting for transfers between devices: 97.7 us -> 111 us
  starting transfers between devices: 49 us -> 44.3 us
    ppermute x4, waiting for transfers between devices: 41.5 us -> 64.4 us  [along_img(): return lax.ppermute(array, IMG, pairs)]
    ppermute x10, waiting for transfers between devices: 53.2 us -> 35.5 us  [along_z(): return lax.ppermute(array, 'z', [(i, (i + by) % LINE) for i in range(LINE)])]
    ppermute x4, starting transfers between devices: 23.2 us -> 14 us  [along_img(): return lax.ppermute(array, IMG, pairs)]
    all_gather x1, waiting for transfers between devices: 0.01 us -> 5.39 us  [on_device(): lax.all_gather(sent.reshape(LINE * depth_share, share), ('y', 'x'), axis=...]
    ppermute x14, starting transfers between devices: 10 us -> 14.6 us  [swap(): return lax.ppermute(array, 'head', [(0, 1), (1, 0)])]
    pallas_call x2, Pallas kernels: 9.79 us -> 13.1 us  [place_tiles(): pl.pallas_call(functools.partial(place_kernel, first_slot, split), grid_s...]
    pallas_call x2 -> x1, Pallas kernels: 27.5 us -> 24.6 us  [attend(): pl.pallas_call(functools.partial(attend_kernel, layout), out_shape=[jax.S...]
  transfers between devices with their start and end apart: 29 -> 29, of which waited for: 8 -> 12; matrix products, arithmetic and copies ran while one was open for 5% -> 5% of each run, Pallas kernels for 29% -> 31%
where the time goes in v7:
time: 320 us; the launch traced here: 319 us
  Pallas kernels  120 us (38%)
  waiting for transfers between devices  111 us (35%)
  starting transfers between devices  44.3 us (14%)
  between operations  21.7 us (7%)
  local copies, waits for them, and re-layouts  15.7 us (5%)
  other arithmetic  6.13 us (2%)
    ppermute x4, waiting for transfers between devices, along_img(): return lax.ppermute(array, IMG, pairs)  64.4 us
    ppermute x10, waiting for transfers between devices, along_z(): return lax.ppermute(array, 'z', [(i, (i + by) % LINE) for i in range(LINE)])  35.5 us
    pallas_call x2, Pallas kernels, owner_project(): pl.pallas_call(owner_kernel, grid_spec=pltpu.PrefetchScalarGridSpec(num_s...  28.8 us
    pallas_call x1, Pallas kernels, attend(): pl.pallas_call(functools.partial(attend_kernel, layout), out_shape=[jax.S...  24.6 us
    ppermute x10, starting transfers between devices, along_z(): return lax.ppermute(array, 'z', [(i, (i + by) % LINE) for i in range(LINE)])  15.7 us
    pallas_call x1, Pallas kernels, home_project(): pl.pallas_call(project_kernel, grid_spec=pltpu.PrefetchScalarGridSpec(num...  15.3 us
    pallas_call x1, Pallas kernels, home_grad(): pl.pallas_call(grad_kernel, grid_spec=pltpu.PrefetchScalarGridSpec(num_sc...  15 us
    ppermute x14, starting transfers between devices, swap(): return lax.ppermute(array, 'head', [(0, 1), (1, 0)])  14.6 us
  transfers between devices with their start and end apart: 29, of which 12 were waited for; matrix products, arithmetic and copies ran while one was open for 5% of the time, Pallas kernels for 31%

profile of v7, /device:TPU:31, one launch (start us, length us, event | category | flops | bytes accessed | tf_op | source)
XLA Modules:
  0.0 318.7 jit_solution(18376232170619302920)
XLA Ops:
  10.0 3.3 %collective-permute-start.1 = (bf16[50,768]{1,0:T(8,128)(2,1)S(1)}, bf16[50,768]{1,0:T(8,128)(2,1)S(1)}, u32[]{:S(2)}, u32[]{:S(2)}) collective-permute-start(bf16[50,768]{1,0:T(8,128)(2,1)S(1)} %get-tuple-element.85), channel_id=1, source_target_pairs={{0,64},{32,96},{64,0},{96,32},{1,65},{33,97},{65,1},{97,33},{2,66}... | collective-permute-start | bytes 230408 | tf_op jit(solution)/shard_map/ppermute | solution.py:26
  14.1 6.0 %norm.1.refs_8_ = bf16[2,128,3200]{2,1,0:T(8,128)(2,1)} custom-call(bf16[2,128,3200]{2,1,0:T(8,128)(2,1)} %refs_11_.1), custom_call_target="tpu_custom_call" | custom-call | flops 1 | bytes 1 | tf_op jit(solution)/shard_map/norm/pallas_call | solution.py:67
  28.8 4.9 %constant_dynamic-slice_fusion.1 = (bf16[2,256,2048]{2,1,0:T(8,128)(2,1)}, bf16[2,256,2048]{2,1,0:T(8,128)(2,1)}) fusion(bf16[6,256,2048]{2,1,0:T(8,128)(2,1)} %param.21, s32[]{:T(128)S(6)} %min.14, s32[]{:T(128)S(6)} %min.13), kind=kLoop, calls=%fused_computation.18 | loop fusion | bytes 8388616 | tf_op jit(solution)/shard_map/dynamic_slice | solution.py:502
  33.7 27.3 %collective-permute-done.3.refs_4_ = bf16[2,128,3200]{2,1,0:T(8,128)(2,1)S(1)} collective-permute-done((bf16[2,128,3200]{2,1,0:T(8,128)(2,1)S(1)}, bf16[2,128,3200]{2,1,0:T(8,128)(2,1)S(1)}, u32[]{:S(2)}, u32[]{:S(2)}) %collective-permute-start.3) | collective-permute-done | bytes 1638432 | tf_op jit(solution)/shard_map/ppermute | solution.py:26
  64.2 2.7 collective-permute-start.7
  68.6 5.4 %all-gather.2.cloned.1.call-done.refs_10_ = bf16[3200,768]{1,0:T(8,128)(2,1)} async-done(((bf16[200,768]{1,0:T(8,128)(2,1)}), bf16[3200,768]{1,0:T(8,128)(2,1)}) %all-gather.2.cloned.1.call-update) | async-done | bytes 4915216 | tf_op jit(solution)/shard_map/all_gather | solution.py:494
  74.0 5.9 %collective-permute-start.20 = (bf16[2,256,2048]{2,1,0:T(8,128)(2,1)}, bf16[2,256,2048]{2,1,0:T(8,128)(2,1)S(1)}, u32[]{:S(2)}, u32[]{:S(2)}) collective-permute-start(bf16[2,256,2048]{2,1,0:T(8,128)(2,1)} %get-tuple-element.56), channel_id=1, source_target_pairs={{0,4},{2,6},{4,8},{6,10},{8,12},{10,14},{12,16},{14,18},{16,20},{1... | collective-permute-start | bytes 6291464 | tf_op jit(solution)/shard_map/ppermute | solution.py:32
  88.8 24.6 %attend.1 = (bf16[2,2,128,256]{3,2,1,0:T(8,128)(2,1)}, bf16[2,2,128,256]{3,2,1,0:T(8,128)(2,1)}, bf16[2,2,128,256]{3,2,1,0:T(8,128)(2,1)}, bf16[2,2,128,256]{3,2,1,0:T(8,128)(2,1)}) custom-call(bf16[1,128,3200]{2,1,0:T(8,128)(2,1)} %collective-permute-done.6.refs_0_, bf16[1,128,3200]{2,1,0:T(8,128)(2,1)} %collective-permute-done.7.refs_1_, ...), custom_call_target="tpu_custom_call" | custom-call | flops 1 | bytes 1 | tf_op jit(solution)/shard_map/attend/pallas_call | solution.py:148
  113.4 3.1 collective-permute-start.14
  124.8 4.6 %collective-permute-done.13.refs_1_ = bf16[2,2,128,256]{3,2,1,0:T(8,128)(2,1)S(1)} collective-permute-done((bf16[2,2,128,256]{3,2,1,0:T(8,128)(2,1)}, bf16[2,2,128,256]{3,2,1,0:T(8,128)(2,1)S(1)}, u32[]{:S(2)}, u32[]{:S(2)}) %collective-permute-start.13) | collective-permute-done | bytes 262176 | tf_op jit(solution)/shard_map/ppermute | solution.py:26
  129.4 2.3 collective-permute-start.23
  134.8 12.4 %join.1 = (bf16[2,128,3200]{2,1,0:T(8,128)(2,1)}, f32[2,128,128]{2,1,0:T(8,128)}) custom-call(s32[1]{0:T(128)} %bitcast.6.line_ref, f32[4]{0:T(128)} %exponential_divide_fusion.mixing_ref, bf16[2,2,128,256]{3,2,1,0:T(8,128)(2,1)} %get-tuple-element.50.refs_0_, bf16[2,2,128,256]{3,2,1,0:T(8,128)(2,1)} %copy-done.10, bf16[2,2,128,256]{3,2,1,0:T(8,128)(2,1)} %copy-done.9, ...), custom_call_target="tpu_custom_call" | custom-call | flops 1 | bytes 1 | tf_op jit(solution)/shard_map/join/pallas_call | solution.py:218
  147.7 3.6 %collective-permute-start.21 = (bf16[2,128,3200]{2,1,0:T(8,128)(2,1)}, bf16[2,128,3200]{2,1,0:T(8,128)(2,1)}, u32[]{:S(2)}, u32[]{:S(2)}) collective-permute-start(bf16[2,128,3200]{2,1,0:T(8,128)(2,1)} %get-tuple-element.70.own_ref.z_ref), channel_id=1, source_target_pairs={{2,0},{4,2},{6,4},{8,6},{10,8},{12,10},{14,12},{16,14},{18,16},{20... | collective-permute-start | bytes 4915208 | tf_op jit(solution)/shard_map/ppermute | solution.py:32
  156.0 15.3 %project.1 = (bf16[2,2,128,2048]{3,2,1,0:T(8,128)(2,1)}, f32[512,2048]{1,0:T(8,128)}) custom-call(s32[1]{0:T(128)} %bitcast.5.core_ref, bf16[2,128,3200]{2,1,0:T(8,128)(2,1)} %get-tuple-element.70.own_ref.z_ref, bf16[2,128,3200]{2,1,0:T(8,128)(2,1)} %collective-permute-done.22.other_ref, bf16[3200,2048]{1,0:T(8,128)(2,1)} %weight_ref.7, f32[1,2048]{1,0:T(1,128)} %bitcast.40), custom_call_target="tpu_custom_call" | custom-call | flops 1 | bytes 1 | tf_op jit(solution)/shard_map/project/pallas_call | solution.py:304
  171.3 6.2 %collective-permute-done.23 = bf16[2,256,2048]{2,1,0:T(8,128)(2,1)S(1)} collective-permute-done((bf16[2,256,2048]{2,1,0:T(8,128)(2,1)}, bf16[2,256,2048]{2,1,0:T(8,128)(2,1)S(1)}, u32[]{:S(2)}, u32[]{:S(2)}) %collective-permute-start.23) | collective-permute-done | bytes 2097184 | tf_op jit(solution)/shard_map/ppermute | solution.py:32
  180.8 15.0 %grad.1 = (bf16[2,128,3200]{2,1,0:T(8,128)(2,1)}, bf16[2,128,3200]{2,1,0:T(8,128)(2,1)}) custom-call(s32[1]{0:T(128)} %bitcast.5.core_ref, f32[512,2048]{1,0:T(8,128)} %get-tuple-element.65.slope_ref, bf16[2,2,128,2048]{3,2,1,0:T(8,128)(2,1)} %pad_maximum_fusion.back_own_ref.back_other_ref, ...), custom_call_target="tpu_custom_call" | custom-call | flops 1 | bytes 1 | tf_op jit(solution)/shard_map/grad/pallas_call | solution.py:365
  195.8 45.6 %collective-permute-done.21.own_ref = bf16[2,128,3200]{2,1,0:T(8,128)(2,1)} collective-permute-done((bf16[2,128,3200]{2,1,0:T(8,128)(2,1)}, bf16[2,128,3200]{2,1,0:T(8,128)(2,1)}, u32[]{:S(2)}, u32[]{:S(2)}) %collective-permute-start.21) | collective-permute-done | bytes 1638432 | tf_op jit(solution)/shard_map/ppermute | solution.py:32
  246.7 14.4 %owner.2 = bf16[2,2,128,2048]{3,2,1,0:T(8,128)(2,1)} custom-call(s32[1]{0:T(128)} %bitcast.5.core_ref, bf16[2,128,3200]{2,1,0:T(8,128)(2,1)} %collective-permute-done.21.own_ref, bf16[2,128,3200]{2,1,0:T(8,128)(2,1)} %collective-permute-done.24.other_ref, bf16[3200,2048]{1,0:T(8,128)(2,1)} %weight_ref.7, f32[1,2048]{1,0:T(1,128)} %bitcast.41), custom_call_target="tpu_custom_call" | custom-call | flops 1 | bytes 1 | tf_op jit(solution)/shard_map/owner/pallas_call | solution.py:404
  261.1 6.6 %place.2.refs_2_ = bf16[6,256,2048]{2,1,0:T(8,128)(2,1)} custom-call(s32[2]{0:T(128)} %pad_add_fusion.slots_ref, bf16[2,256,2048]{2,1,0:T(8,128)(2,1)} %bitcast.39, bf16[2,256,2048]{2,1,0:T(8,128)(2,1)} %bitcast.34), custom_call_target="tpu_custom_call" | custom-call | flops 1 | bytes 1 | tf_op jit(solution)/shard_map/place/pallas_call | solution.py:452
  267.7 4.9 %final.1 = bf16[2,128,3200]{2,1,0:T(8,128)(2,1)} custom-call(bf16[2,128,3200]{2,1,0:T(8,128)(2,1)} %get-tuple-element.71.own_ref, bf16[2,128,3200]{2,1,0:T(8,128)(2,1)} %collective-permute-done.26.other_ref, bf16[2,128,3200]{2,1,0:T(8,128)(2,1)} %get-tuple-element.70.own_ref.z_ref, f32[2,128,128]{2,1,0:T(8,128)} %get-tuple-element.73.inverse_ref), custom_call_target="tpu_custom_call" | custom-call | flops 1 | bytes 1 | tf_op jit(solution)/shard_map/final/pallas_call | solution.py:261
  272.6 12.7 %collective-permute-done.25.own_ref = bf16[2,128,3200]{2,1,0:T(8,128)(2,1)S(1)} collective-permute-done((bf16[2,128,3200]{2,1,0:T(8,128)(2,1)S(1)}, bf16[2,128,3200]{2,1,0:T(8,128)(2,1)S(1)}, u32[]{:S(2)}, u32[]{:S(2)}) %collective-permute-start.25) | collective-permute-done | bytes 1638432 | tf_op jit(solution)/shard_map/ppermute | solution.py:32
  286.6 3.1 collective-permute-done.27.other_ref
  290.9 14.4 %owner.3 = bf16[2,2,128,2048]{3,2,1,0:T(8,128)(2,1)} custom-call(s32[1]{0:T(128)} %bitcast.5.core_ref, bf16[2,128,3200]{2,1,0:T(8,128)(2,1)} %copy-done.5, bf16[2,128,3200]{2,1,0:T(8,128)(2,1)} %copy-done.6, bf16[3200,2048]{1,0:T(8,128)(2,1)} %weight_ref.7, f32[1,2048]{1,0:T(1,128)} %bitcast.42), custom_call_target="tpu_custom_call" | custom-call | flops 1 | bytes 1 | tf_op jit(solution)/shard_map/owner/pallas_call | solution.py:404
  305.3 6.6 %place.3 = bf16[6,256,2048]{2,1,0:T(8,128)(2,1)} custom-call(s32[2]{0:T(128)} %pad_add_fusion.slots_ref, bf16[2,256,2048]{2,1,0:T(8,128)(2,1)} %bitcast.35, bf16[2,256,2048]{2,1,0:T(8,128)(2,1)} %bitcast.36, bf16[6,256,2048]{2,1,0:T(8,128)(2,1)} %place.2.refs_2_), custom_call_target="tpu_custom_call", output_to_operand_aliasing={{}: (3, {})} | custom-call | flops 1 | bytes 1 | tf_op jit(solution)/shard_map/place/pallas_call | solution.py:452
  (116 shorter events, 46.3 us)
Async XLA Ops:
  7.2 66.8 %all-gather.2.cloned.1.call-start = ((), (), s32[]{:S(2)}) async-start(), calls=%async_computation | async-start | bytes 5222400 | tf_op jit(solution)/shard_map/all_gather | solution.py:494
  8.3 11.8 %collective-permute-start = (bf16[50,768]{1,0:T(8,128)(2,1)S(1)}, bf16[50,768]{1,0:T(8,128)(2,1)S(1)}, u32[]{:S(2)}, u32[]{:S(2)}) collective-permute-start(bf16[50,768]{1,0:T(8,128)(2,1)S(1)} %get-tuple-element.83), channel_id=1, source_target_pairs={{0,32},{32,64},{64,96},{96,0},{1,33},{33,65},{65,97},{97,1},{2,34}... | collective-permute-start | bytes 230408 | tf_op jit(solution)/shard_map/ppermute | solution.py:26
  10.0 10.1 %collective-permute-start.1 = (bf16[50,768]{1,0:T(8,128)(2,1)S(1)}, bf16[50,768]{1,0:T(8,128)(2,1)S(1)}, u32[]{:S(2)}, u32[]{:S(2)}) collective-permute-start(bf16[50,768]{1,0:T(8,128)(2,1)S(1)} %get-tuple-element.85), channel_id=1, source_target_pairs={{0,64},{32,96},{64,0},{96,32},{1,65},{33,97},{65,1},{97,33},{2,66}... | collective-permute-start | bytes 230408 | tf_op jit(solution)/shard_map/ppermute | solution.py:26
  13.3 6.8 %collective-permute-start.2 = (bf16[50,768]{1,0:T(8,128)(2,1)S(1)}, bf16[50,768]{1,0:T(8,128)(2,1)S(1)}, u32[]{:S(2)}, u32[]{:S(2)}) collective-permute-start(bf16[50,768]{1,0:T(8,128)(2,1)S(1)} %get-tuple-element.82), channel_id=1, source_target_pairs={{0,96},{32,0},{64,32},{96,64},{1,97},{33,1},{65,33},{97,65},{2,98}... | collective-permute-start | bytes 230408 | tf_op jit(solution)/shard_map/ppermute | solution.py:26
  21.1 39.9 %collective-permute-start.5 = (bf16[1024,3200]{1,0:T(8,128)(2,1)}, bf16[1024,3200]{1,0:T(8,128)(2,1)}, u32[]{:S(2)}, u32[]{:S(2)}) collective-permute-start(bf16[1024,3200]{1,0:T(8,128)(2,1)} %refs_8_.1), channel_id=1, source_target_pairs={{0,1},{1,0},{2,3},{3,2},{4,5},{5,4},{6,7},{7,6},{8,9},{9,8},{10,11... | collective-permute-start | bytes 19660808 | tf_op jit(solution)/shard_map/ppermute | solution.py:22
  22.7 38.3 %collective-permute-start.3 = (bf16[2,128,3200]{2,1,0:T(8,128)(2,1)S(1)}, bf16[2,128,3200]{2,1,0:T(8,128)(2,1)S(1)}, u32[]{:S(2)}, u32[]{:S(2)}) collective-permute-start(bf16[2,128,3200]{2,1,0:T(8,128)(2,1)S(1)} %copy-done), channel_id=1, source_target_pairs={{0,32},{32,64},{64,96},{96,0},{1,33},{33,65},{65,97},{97,1},{2,34}... | collective-permute-start | bytes 4915208 | tf_op jit(solution)/shard_map/ppermute | solution.py:26
  23.4 37.5 %collective-permute-start.4 = (bf16[2,128,3200]{2,1,0:T(8,128)(2,1)S(1)}, bf16[2,128,3200]{2,1,0:T(8,128)(2,1)}, u32[]{:S(2)}, u32[]{:S(2)}) collective-permute-start(bf16[2,128,3200]{2,1,0:T(8,128)(2,1)S(1)} %copy-done), channel_id=1, source_target_pairs={{0,96},{32,0},{64,32},{96,64},{1,97},{33,1},{65,33},{97,65},{2,98}... | collective-permute-start | bytes 4915208 | tf_op jit(solution)/shard_map/ppermute | solution.py:26
  25.4 48.6 %collective-permute-start.12 = (bf16[2,128,3200]{2,1,0:T(8,128)(2,1)S(1)}, bf16[2,128,3200]{2,1,0:T(8,128)(2,1)}, u32[]{:S(2)}, u32[]{:S(2)}) collective-permute-start(bf16[2,128,3200]{2,1,0:T(8,128)(2,1)S(1)} %copy-done), channel_id=1, source_target_pairs={{0,1},{1,0},{2,3},{3,2},{4,5},{5,4},{6,7},{7,6},{8,9},{9,8},{10,11... | collective-permute-start | bytes 4915208 | tf_op jit(solution)/shard_map/ppermute | solution.py:22
  62.0 20.1 %collective-permute-start.6 = (bf16[1,128,3200]{2,1,0:T(8,128)(2,1)}, bf16[1,128,3200]{2,1,0:T(8,128)(2,1)}, u32[]{:S(2)}, u32[]{:S(2)}) collective-permute-start(bf16[1,128,3200]{2,1,0:T(8,128)(2,1)} %slice.30), channel_id=1, source_target_pairs={{0,32},{32,64},{64,96},{96,0},{1,33},{33,65},{65,97},{97,1},{2,34}... | collective-permute-start | bytes 2457608 | tf_op jit(solution)/shard_map/ppermute | solution.py:26
  64.2 20.0 %collective-permute-start.7 = (bf16[1,128,3200]{2,1,0:T(8,128)(2,1)}, bf16[1,128,3200]{2,1,0:T(8,128)(2,1)}, u32[]{:S(2)}, u32[]{:S(2)}) collective-permute-start(bf16[1,128,3200]{2,1,0:T(8,128)(2,1)} %slice.31), channel_id=1, source_target_pairs={{0,96},{32,0},{64,32},{96,64},{1,97},{33,1},{65,33},{97,65},{2,98}... | collective-permute-start | bytes 2457608 | tf_op jit(solution)/shard_map/ppermute | solution.py:26
  66.9 20.9 %collective-permute-start.10 = (bf16[2,128,3200]{2,1,0:T(8,128)(2,1)S(1)}, bf16[2,128,3200]{2,1,0:T(8,128)(2,1)}, u32[]{:S(2)}, u32[]{:S(2)}) collective-permute-start(bf16[2,128,3200]{2,1,0:T(8,128)(2,1)S(1)} %collective-permute-done.3.refs_4_), channel_id=1, source_target_pairs={{0,1},{1,0},{2,3},{3,2},{4,5},{5,4},{6,7},{7,6},{8,9},{9,8},{10,11... | collective-permute-start | bytes 4915208 | tf_op jit(solution)/shard_map/ppermute | solution.py:22
  68.6 19.2 %collective-permute-start.11 = (bf16[2,128,3200]{2,1,0:T(8,128)(2,1)}, bf16[2,128,3200]{2,1,0:T(8,128)(2,1)}, u32[]{:S(2)}, u32[]{:S(2)}) collective-permute-start(bf16[2,128,3200]{2,1,0:T(8,128)(2,1)} %collective-permute-done.4.refs_6_), channel_id=1, source_target_pairs={{0,1},{1,0},{2,3},{3,2},{4,5},{5,4},{6,7},{7,6},{8,9},{9,8},{10,11... | collective-permute-start | bytes 4915208 | tf_op jit(solution)/shard_map/ppermute | solution.py:22
  74.0 60.1 %collective-permute-start.20 = (bf16[2,256,2048]{2,1,0:T(8,128)(2,1)}, bf16[2,256,2048]{2,1,0:T(8,128)(2,1)S(1)}, u32[]{:S(2)}, u32[]{:S(2)}) collective-permute-start(bf16[2,256,2048]{2,1,0:T(8,128)(2,1)} %get-tuple-element.56), channel_id=1, source_target_pairs={{0,4},{2,6},{4,8},{6,10},{8,12},{10,14},{12,16},{14,18},{16,20},{1... | collective-permute-start | bytes 6291464 | tf_op jit(solution)/shard_map/ppermute | solution.py:32
  113.4 9.4 %collective-permute-start.14 = (bf16[2,2,128,256]{3,2,1,0:T(8,128)(2,1)}, bf16[2,2,128,256]{3,2,1,0:T(8,128)(2,1)S(1)}, u32[]{:S(2)}, u32[]{:S(2)}) collective-permute-start(bf16[2,2,128,256]{3,2,1,0:T(8,128)(2,1)} %get-tuple-element.52), channel_id=1, source_target_pairs={{0,64},{32,96},{64,0},{96,32},{1,65},{33,97},{65,1},{97,33},{2,66}... | collective-permute-start | bytes 786440 | tf_op jit(solution)/shard_map/ppermute | solution.py:26
  117.8 11.6 %collective-permute-start.13 = (bf16[2,2,128,256]{3,2,1,0:T(8,128)(2,1)}, bf16[2,2,128,256]{3,2,1,0:T(8,128)(2,1)S(1)}, u32[]{:S(2)}, u32[]{:S(2)}) collective-permute-start(bf16[2,2,128,256]{3,2,1,0:T(8,128)(2,1)} %get-tuple-element.51), channel_id=1, source_target_pairs={{0,96},{32,0},{64,32},{96,64},{1,97},{33,1},{65,33},{97,65},{2,98}... | collective-permute-start | bytes 786440 | tf_op jit(solution)/shard_map/ppermute | solution.py:26
  118.4 13.3 %collective-permute-start.15 = (bf16[2,2,128,256]{3,2,1,0:T(8,128)(2,1)}, bf16[2,2,128,256]{3,2,1,0:T(8,128)(2,1)S(1)}, u32[]{:S(2)}, u32[]{:S(2)}) collective-permute-start(bf16[2,2,128,256]{3,2,1,0:T(8,128)(2,1)} %get-tuple-element.55), channel_id=1, source_target_pairs={{0,32},{32,64},{64,96},{96,0},{1,33},{33,65},{65,97},{97,1},{2,34}... | collective-permute-start | bytes 786440 | tf_op jit(solution)/shard_map/ppermute | solution.py:26
  120.2 12.5 %collective-permute-start.16 = (bf16[2,128,256]{2,1,0:T(8,128)(2,1)S(1)}, bf16[2,128,256]{2,1,0:T(8,128)(2,1)S(1)}, u32[]{:S(2)}, u32[]{:S(2)}) collective-permute-start(bf16[2,128,256]{2,1,0:T(8,128)(2,1)S(1)} %slice_bitcast_fusion.3), channel_id=1, source_target_pairs={{0,1},{1,0},{2,3},{3,2},{4,5},{5,4},{6,7},{7,6},{8,9},{9,8},{10,11... | collective-permute-start | bytes 393224 | tf_op jit(solution)/shard_map/ppermute | solution.py:22
  122.9 11.0 %collective-permute-start.18 = (bf16[2,128,256]{2,1,0:T(8,128)(2,1)S(1)}, bf16[2,128,256]{2,1,0:T(8,128)(2,1)S(1)}, u32[]{:S(2)}, u32[]{:S(2)}) collective-permute-start(bf16[2,128,256]{2,1,0:T(8,128)(2,1)S(1)} %slice_bitcast_fusion.2), channel_id=1, source_target_pairs={{0,1},{1,0},{2,3},{3,2},{4,5},{5,4},{6,7},{7,6},{8,9},{9,8},{10,11... | collective-permute-start | bytes 393224 | tf_op jit(solution)/shard_map/ppermute | solution.py:22
  129.4 48.0 %collective-permute-start.23 = (bf16[2,256,2048]{2,1,0:T(8,128)(2,1)}, bf16[2,256,2048]{2,1,0:T(8,128)(2,1)S(1)}, u32[]{:S(2)}, u32[]{:S(2)}) collective-permute-start(bf16[2,256,2048]{2,1,0:T(8,128)(2,1)} %get-tuple-element.64), channel_id=1, source_target_pairs={{0,2},{2,4},{4,6},{6,8},{8,10},{10,12},{12,14},{14,16},{16,18},{18... | collective-permute-start | bytes 6291464 | tf_op jit(solution)/shard_map/ppermute | solution.py:32
  147.2 8.8 %collective-permute-start.22 = (bf16[2,128,3200]{2,1,0:T(8,128)(2,1)}, bf16[2,128,3200]{2,1,0:T(8,128)(2,1)}, u32[]{:S(2)}, u32[]{:S(2)}) collective-permute-start(bf16[2,128,3200]{2,1,0:T(8,128)(2,1)} %get-tuple-element.70.own_ref.z_ref), channel_id=1, source_target_pairs={{0,1},{1,0},{2,3},{3,2},{4,5},{5,4},{6,7},{7,6},{8,9},{9,8},{10,11... | collective-permute-start | bytes 4915208 | tf_op jit(solution)/shard_map/ppermute | solution.py:22
  147.7 93.7 %collective-permute-start.21 = (bf16[2,128,3200]{2,1,0:T(8,128)(2,1)}, bf16[2,128,3200]{2,1,0:T(8,128)(2,1)}, u32[]{:S(2)}, u32[]{:S(2)}) collective-permute-start(bf16[2,128,3200]{2,1,0:T(8,128)(2,1)} %get-tuple-element.70.own_ref.z_ref), channel_id=1, source_target_pairs={{2,0},{4,2},{6,4},{8,6},{10,8},{12,10},{14,12},{16,14},{18,16},{20... | collective-permute-start | bytes 4915208 | tf_op jit(solution)/shard_map/ppermute | solution.py:32
  241.3 5.4 %collective-permute-start.24 = (bf16[2,128,3200]{2,1,0:T(8,128)(2,1)}, bf16[2,128,3200]{2,1,0:T(8,128)(2,1)}, u32[]{:S(2)}, u32[]{:S(2)}) collective-permute-start(bf16[2,128,3200]{2,1,0:T(8,128)(2,1)} %collective-permute-done.21.own_ref), channel_id=1, source_target_pairs={{0,1},{1,0},{2,3},{3,2},{4,5},{5,4},{6,7},{7,6},{8,9},{9,8},{10,11... | collective-permute-start | bytes 4915208 | tf_op jit(solution)/shard_map/ppermute | solution.py:22
  242.0 25.7 %collective-permute-start.26 = (bf16[2,128,3200]{2,1,0:T(8,128)(2,1)}, bf16[2,128,3200]{2,1,0:T(8,128)(2,1)}, u32[]{:S(2)}, u32[]{:S(2)}) collective-permute-start(bf16[2,128,3200]{2,1,0:T(8,128)(2,1)} %get-tuple-element.72), channel_id=1, source_target_pairs={{0,1},{1,0},{2,3},{3,2},{4,5},{5,4},{6,7},{7,6},{8,9},{9,8},{10,11... | collective-permute-start | bytes 4915208 | tf_op jit(solution)/shard_map/ppermute | solution.py:22
  242.0 43.2 %collective-permute-start.25 = (bf16[2,128,3200]{2,1,0:T(8,128)(2,1)S(1)}, bf16[2,128,3200]{2,1,0:T(8,128)(2,1)S(1)}, u32[]{:S(2)}, u32[]{:S(2)}) collective-permute-start(bf16[2,128,3200]{2,1,0:T(8,128)(2,1)S(1)} %copy-done.1), channel_id=1, source_target_pairs={{4,0},{6,2},{8,4},{10,6},{12,8},{14,10},{16,12},{18,14},{20,16},{2... | collective-permute-start | bytes 4915208 | tf_op jit(solution)/shard_map/ppermute | solution.py:32
  (24 other events, 282.8 us)
Sparse Core Ops, SparseCore 0:
  21.2 52.7 all-gather.1

commit v8 on v7

--- a/solution.py
+++ b/solution.py
@@ -422,47 +422,101 @@
     return projected.reshape(tiles, 2 * half, width)
 
 
-def place_kernel(first_slot, split, slots_ref, *refs):
-    low_ref, high_ref, out_ref = refs[0], refs[1], refs[-1]
-    slot = pl.program_id(0) + first_slot
+def place_kernel(slots_ref, home_ref, near_ref, out_ref):
+    slot = pl.program_id(0)
     index = slot + slots_ref[0]
-    rows = jnp.where(index < split, low_ref[...], high_ref[...])
-    out_ref[...] = jnp.where(slot < slots_ref[1], rows, jnp.zeros_like(rows))
-
-
-def place_tiles(slots, low, high, own_tiles, held):
-    tiles, full, width = low.shape
-    count = own_tiles // 2
-    first_slot = 0 if held is None else count
-    split = tiles if held is None else 2 * tiles
+    tiles = 2
+    live = jnp.logical_and(slot < slots_ref[1], index < 2 * tiles)
+
+    @pl.when(jnp.logical_and(live, index < tiles))
+    def _():
+        out_ref[...] = home_ref[...]
+
+    @pl.when(jnp.logical_and(live, index >= tiles))
+    def _():
+        out_ref[...] = near_ref[...]
+
+    @pl.when(jnp.logical_not(live))
+    def _():
+        out_ref[...] = jnp.zeros_like(out_ref)
+
+
+def place_tiles(slots, home, near, own_tiles):
+    tiles, full, width = home.shape
 
     def spec(start):
-        def at(k, r, s):
-            return (jnp.clip(k + first_slot + s[0] - start, 0, tiles - 1), r, 0)
-
-        return pl.BlockSpec((1, full // 2, width), at)
-
-    in_specs = [spec(split - tiles), spec(split)]
-    operands = [low, high]
-    aliases = {}
-    if held is not None:
-        in_specs.append(pl.BlockSpec(memory_space=pl.ANY))
-        operands.append(held)
-        aliases = {3: 0}
+        def at(k, s):
+            return (jnp.clip(k + s[0] - start, 0, tiles - 1), 0, 0)
+
+        return pl.BlockSpec((1, full, width), at)
+
     return pl.pallas_call(
-        functools.partial(place_kernel, first_slot, split),
+        place_kernel,
         grid_spec=pltpu.PrefetchScalarGridSpec(
             num_scalar_prefetch=1,
-            grid=(count, 2),
-            in_specs=in_specs,
-            out_specs=pl.BlockSpec((1, full // 2, width), lambda k, r, s: (k + first_slot, r, 0)),
+            grid=(own_tiles,),
+            in_specs=[spec(0), spec(tiles)],
+            out_specs=pl.BlockSpec((1, full, width), lambda k, s: (k, 0, 0)),
         ),
         out_shape=jax.ShapeDtypeStruct((own_tiles, full, width), jnp.bfloat16),
-        input_output_aliases=aliases,
         compiler_params=pltpu.CompilerParams(vmem_limit_bytes=VMEM_BYTES),
         cost_estimate=SMALL_COST,
         name="place",
-    )(slots, *operands)
+    )(slots, home, near)
+
+
+def owner_slots_kernel(slots_ref, own_ref, other_ref, weight_ref, bias_ref, held_ref, out_ref, projected):
+    tile = pl.program_id(1)
+    core = slots_ref[2]
+    tiles, half, depth = own_ref.shape
+    block = weight_ref.shape[1]
+
+    @pl.when(tile == 0)
+    def _():
+        rows = jnp.concatenate(
+            [own_ref[...].reshape(tiles * half, depth), other_ref[...].reshape(tiles * half, depth)],
+            axis=0,
+        )
+        preact = jnp.dot(rows, weight_ref[...], preferred_element_type=jnp.float32) + bias_ref[...]
+        values = (preact * activate(preact)[0]).astype(jnp.bfloat16).reshape(2, tiles, 1, half, block)
+        projected[:, pl.ds(core, 1)] = values[0]
+        projected[:, pl.ds(1 - core, 1)] = values[1]
+
+    slot = 2 * tiles + tile - slots_ref[0]
+    rows = projected[pl.ds(tile, 1)]
+    out_ref[...] = jnp.where(slot < slots_ref[1], rows, jnp.zeros_like(rows))
+
+
+def owner_slots(slots, own, other, weight, bias, held):
+    tiles, half, depth = own.shape
+    own_tiles, full, width = held.shape
+    block = 512
+    whole = pl.BlockSpec((tiles, half, depth), lambda n, t, s: (0, 0, 0))
+    shape = (own_tiles, 2, half, width)
+    out = pl.pallas_call(
+        owner_slots_kernel,
+        grid_spec=pltpu.PrefetchScalarGridSpec(
+            num_scalar_prefetch=1,
+            grid=(width // block, tiles),
+            in_specs=[
+                whole,
+                whole,
+                pl.BlockSpec((depth, block), lambda n, t, s: (0, n)),
+                pl.BlockSpec((1, block), lambda n, t, s: (0, n)),
+                pl.BlockSpec(memory_space=pl.ANY),
+            ],
+            out_specs=pl.BlockSpec(
+                (1, 2, half, block), lambda n, t, s: (2 * tiles + t - s[0], 0, 0, n)
+            ),
+            scratch_shapes=[pltpu.VMEM((tiles, 2, half, block), jnp.bfloat16)],
+        ),
+        out_shape=jax.ShapeDtypeStruct(shape, jnp.bfloat16),
+        input_output_aliases={5: 0},
+        compiler_params=pltpu.CompilerParams(vmem_limit_bytes=VMEM_BYTES),
+        cost_estimate=SMALL_COST,
+        name="slots",
+    )(slots, own, other, weight, bias, held.reshape(shape))
+    return out.reshape(own_tiles, full, width)
 
 
 def on_device(
@@ -518,7 +572,7 @@
         weight,
     )
     attended = [att_own, along_z(att_low, -1), along_z(att_far, 2), along_z(att_high, 1)]
-    attended[2], near_packet = lax.optimization_barrier((attended[2], packets[1]))
+    attended, near_packet = lax.optimization_barrier((attended, packets[1]))
     near_back = along_img(near_packet, 1)
     swapped = [swap(rows[1]) for rows in attended]
     swapped, far_back = lax.optimization_barrier((swapped, far_back))
@@ -553,14 +607,13 @@
     near, z_later, grad_other = lax.optimization_barrier((near, z_rows, grad_other))
     far = along_img(z_later, -2)
     near_projected = owner_project(core_arg, near, swap(near), proj_weight, bias)
-    offset = my_first - place * tile_group
+    offset = jnp.clip(my_first - place * tile_group, 0, 1)
     held = first_tile[place + 1] - my_first
-    slots = jnp.stack([offset, held]).astype(jnp.int32)
-    owner_rows = place_tiles(slots, projected, near_projected, own_tiles, None)
+    slots = jnp.stack([offset, held, core]).astype(jnp.int32)
+    owner_rows = place_tiles(slots, projected, near_projected, own_tiles)
     grad_joined = final_rows(grad_own, swap(grad_other), z_rows, inverse_std)
     far, grad_joined, owner_rows = lax.optimization_barrier((far, grad_joined, owner_rows))
-    far_projected = owner_project(core_arg, far, swap(far), proj_weight, bias)
-    owner_rows = place_tiles(slots, near_projected, far_projected, own_tiles, owner_rows)
+    owner_rows = owner_slots(slots, far, swap(far), proj_weight, bias, owner_rows)
     return (owner_rows, grad_joined)
 
 

time: 320 us -> 299 us (0.934)
  waiting for transfers between devices: 111 us -> 76.4 us
  starting transfers between devices: 44.3 us -> 57.1 us
    ppermute x4, waiting for transfers between devices: 64.4 us -> 19.6 us  [along_img(): return lax.ppermute(array, IMG, pairs)]
    ppermute x10, waiting for transfers between devices: 35.5 us -> 53.5 us  [along_z(): return lax.ppermute(array, 'z', [(i, (i + by) % LINE) for i in range(LINE)])]
    ppermute x4, starting transfers between devices: 14 us -> 30.4 us  [along_img(): return lax.ppermute(array, IMG, pairs)]
    pallas_call x2, Pallas kernels: 13.1 us -> 28.2 us  [the longest x1 21.5 us: owner_slots(): pl.pallas_call(owner_slots_kernel, grid_spec=pltpu.PrefetchScalarGridSpec...]
    pallas_call x2 -> x1, Pallas kernels: 28.8 us -> 14.4 us  [owner_project(): pl.pallas_call(owner_kernel, grid_spec=pltpu.PrefetchScalarGridSpec(num_s...]
    all_gather x1, waiting for transfers between devices: 5.39 us -> 0.01 us  [on_device(): lax.all_gather(sent.reshape(LINE * depth_share, share), ('y', 'x'), axis=...]
  transfers between devices with their start and end apart: 29 -> 29, of which waited for: 12 -> 9; matrix products, arithmetic and copies ran while one was open for 5% -> 5% of each run, Pallas kernels for 31% -> 34%
where the time goes in v8:
time: 299 us; the launch traced here: 296 us
  Pallas kernels  121 us (40%)
  waiting for transfers between devices  76.4 us (26%)
  starting transfers between devices  57.1 us (19%)
  between operations  21.9 us (7%)
  local copies, waits for them, and re-layouts  13.4 us (4%)
  other arithmetic  6.17 us (2%)
    ppermute x10, waiting for transfers between devices, along_z(): return lax.ppermute(array, 'z', [(i, (i + by) % LINE) for i in range(LINE)])  53.5 us
    ppermute x4, starting transfers between devices, along_img(): return lax.ppermute(array, IMG, pairs)  30.4 us
    pallas_call x1, Pallas kernels, attend(): pl.pallas_call(functools.partial(attend_kernel, layout), out_shape=[jax.S...  24.6 us
    pallas_call x1, Pallas kernels, owner_slots(): pl.pallas_call(owner_slots_kernel, grid_spec=pltpu.PrefetchScalarGridSpec...  21.5 us
    ppermute x4, waiting for transfers between devices, along_img(): return lax.ppermute(array, IMG, pairs)  19.6 us
    pallas_call x1, Pallas kernels, home_project(): pl.pallas_call(project_kernel, grid_spec=pltpu.PrefetchScalarGridSpec(num...  15.3 us
    ppermute x10, starting transfers between devices, along_z(): return lax.ppermute(array, 'z', [(i, (i + by) % LINE) for i in range(LINE)])  15 us
    pallas_call x1, Pallas kernels, home_grad(): pl.pallas_call(grad_kernel, grid_spec=pltpu.PrefetchScalarGridSpec(num_sc...  15 us
  transfers between devices with their start and end apart: 29, of which 9 were waited for; matrix products, arithmetic and copies ran while one was open for 5% of the time, Pallas kernels for 34%

profile of v8, /device:TPU:31, one launch (start us, length us, event | category | flops | bytes accessed | tf_op | source)
XLA Modules:
  0.0 295.7 jit_solution(681866452888139122)
XLA Ops:
  10.0 3.3 %collective-permute-start.1 = (bf16[50,768]{1,0:T(8,128)(2,1)S(1)}, bf16[50,768]{1,0:T(8,128)(2,1)S(1)}, u32[]{:S(2)}, u32[]{:S(2)}) collective-permute-start(bf16[50,768]{1,0:T(8,128)(2,1)S(1)} %get-tuple-element.91), channel_id=1, source_target_pairs={{0,64},{32,96},{64,0},{96,32},{1,65},{33,97},{65,1},{97,33},{2,66}... | collective-permute-start | bytes 230408 | tf_op jit(solution)/shard_map/ppermute | solution.py:26
  14.1 6.0 %norm.1.refs_8_ = bf16[2,128,3200]{2,1,0:T(8,128)(2,1)} custom-call(bf16[2,128,3200]{2,1,0:T(8,128)(2,1)} %refs_11_.1), custom_call_target="tpu_custom_call" | custom-call | flops 1 | bytes 1 | tf_op jit(solution)/shard_map/norm/pallas_call | solution.py:67
  28.9 4.9 %constant_dynamic-slice_fusion.1 = (bf16[2,256,2048]{2,1,0:T(8,128)(2,1)}, bf16[2,256,2048]{2,1,0:T(8,128)(2,1)}) fusion(bf16[6,256,2048]{2,1,0:T(8,128)(2,1)} %param.21, s32[]{:T(128)S(6)} %min.18, s32[]{:T(128)S(6)} %min.17), kind=kLoop, calls=%fused_computation.18 | loop fusion | bytes 8388616 | tf_op jit(solution)/shard_map/dynamic_slice | solution.py:556
  33.7 27.3 %collective-permute-done.3.refs_4_ = bf16[2,128,3200]{2,1,0:T(8,128)(2,1)S(1)} collective-permute-done((bf16[2,128,3200]{2,1,0:T(8,128)(2,1)S(1)}, bf16[2,128,3200]{2,1,0:T(8,128)(2,1)S(1)}, u32[]{:S(2)}, u32[]{:S(2)}) %collective-permute-start.3) | collective-permute-done | bytes 1638432 | tf_op jit(solution)/shard_map/ppermute | solution.py:26
  62.8 2.3 collective-permute-start.7
  66.8 14.2 %collective-permute-done.6.refs_0_ = bf16[1,128,3200]{2,1,0:T(8,128)(2,1)} collective-permute-done((bf16[1,128,3200]{2,1,0:T(8,128)(2,1)S(1)}, bf16[1,128,3200]{2,1,0:T(8,128)(2,1)}, u32[]{:S(2)}, u32[]{:S(2)}) %collective-permute-start.6) | collective-permute-done | bytes 819232 | tf_op jit(solution)/shard_map/ppermute | solution.py:26
  81.0 2.1 collective-permute-start.8
  83.7 3.9 %collective-permute-start.20 = (bf16[2,256,2048]{2,1,0:T(8,128)(2,1)}, bf16[2,256,2048]{2,1,0:T(8,128)(2,1)S(1)}, u32[]{:S(2)}, u32[]{:S(2)}) collective-permute-start(bf16[2,256,2048]{2,1,0:T(8,128)(2,1)} %get-tuple-element.62), channel_id=1, source_target_pairs={{0,4},{2,6},{4,8},{6,10},{8,12},{10,14},{12,16},{14,18},{16,20},{1... | collective-permute-start | bytes 6291464 | tf_op jit(solution)/shard_map/ppermute | solution.py:32
  87.6 24.6 %attend.1 = (bf16[2,2,128,256]{3,2,1,0:T(8,128)(2,1)}, bf16[2,2,128,256]{3,2,1,0:T(8,128)(2,1)}, bf16[2,2,128,256]{3,2,1,0:T(8,128)(2,1)}, bf16[2,2,128,256]{3,2,1,0:T(8,128)(2,1)}) custom-call(bf16[1,128,3200]{2,1,0:T(8,128)(2,1)} %collective-permute-done.6.refs_0_, bf16[1,128,3200]{2,1,0:T(8,128)(2,1)} %collective-permute-done.7.refs_1_, ...), custom_call_target="tpu_custom_call" | custom-call | flops 1 | bytes 1 | tf_op jit(solution)/shard_map/attend/pallas_call | solution.py:148
  117.7 2.4 collective-permute-done.13.refs_1_
  120.2 2.9 collective-permute-done.14.refs_2_
  123.1 6.6 %collective-permute-done.15.refs_3_ = bf16[2,2,128,256]{3,2,1,0:T(8,128)(2,1)S(1)} collective-permute-done((bf16[2,2,128,256]{3,2,1,0:T(8,128)(2,1)}, bf16[2,2,128,256]{3,2,1,0:T(8,128)(2,1)S(1)}, u32[]{:S(2)}, u32[]{:S(2)}) %collective-permute-start.15) | collective-permute-done | bytes 262176 | tf_op jit(solution)/shard_map/ppermute | solution.py:26
  131.4 22.5 %collective-permute-start.23 = (bf16[2,256,2048]{2,1,0:T(8,128)(2,1)}, bf16[2,256,2048]{2,1,0:T(8,128)(2,1)S(1)}, u32[]{:S(2)}, u32[]{:S(2)}) collective-permute-start(bf16[2,256,2048]{2,1,0:T(8,128)(2,1)} %get-tuple-element.70), channel_id=1, source_target_pairs={{0,2},{2,4},{4,6},{6,8},{8,10},{10,12},{12,14},{14,16},{16,18},{18... | collective-permute-start | bytes 6291464 | tf_op jit(solution)/shard_map/ppermute | solution.py:32
  156.9 12.4 %join.1 = (bf16[2,128,3200]{2,1,0:T(8,128)(2,1)}, f32[2,128,128]{2,1,0:T(8,128)}) custom-call(s32[1]{0:T(128)} %bitcast.6.line_ref, f32[4]{0:T(128)} %exponential_divide_fusion.mixing_ref, bf16[2,2,128,256]{3,2,1,0:T(8,128)(2,1)} %get-tuple-element.58.refs_0_, bf16[2,2,128,256]{3,2,1,0:T(8,128)(2,1)} %copy-done.7, bf16[2,2,128,256]{3,2,1,0:T(8,128)(2,1)} %copy-done.8, ...), custom_call_target="tpu_custom_call" | custom-call | flops 1 | bytes 1 | tf_op jit(solution)/shard_map/join/pallas_call | solution.py:218
  176.4 15.3 %project.1 = (bf16[2,2,128,2048]{3,2,1,0:T(8,128)(2,1)}, f32[512,2048]{1,0:T(8,128)}) custom-call(s32[1]{0:T(128)} %bitcast.5.core_ref, bf16[2,128,3200]{2,1,0:T(8,128)(2,1)} %get-tuple-element.75.own_ref.z_ref, bf16[2,128,3200]{2,1,0:T(8,128)(2,1)} %collective-permute-done.22.other_ref, bf16[3200,2048]{1,0:T(8,128)(2,1)} %weight_ref.7, f32[1,2048]{1,0:T(1,128)} %bitcast.41), custom_call_target="tpu_custom_call" | custom-call | flops 1 | bytes 1 | tf_op jit(solution)/shard_map/project/pallas_call | solution.py:304
  191.7 7.0 %collective-permute-done.23 = bf16[2,256,2048]{2,1,0:T(8,128)(2,1)S(1)} collective-permute-done((bf16[2,256,2048]{2,1,0:T(8,128)(2,1)}, bf16[2,256,2048]{2,1,0:T(8,128)(2,1)S(1)}, u32[]{:S(2)}, u32[]{:S(2)}) %collective-permute-start.23) | collective-permute-done | bytes 2097184 | tf_op jit(solution)/shard_map/ppermute | solution.py:32
  202.1 15.0 %grad.1 = (bf16[2,128,3200]{2,1,0:T(8,128)(2,1)}, bf16[2,128,3200]{2,1,0:T(8,128)(2,1)}) custom-call(s32[1]{0:T(128)} %bitcast.5.core_ref, f32[512,2048]{1,0:T(8,128)} %get-tuple-element.71.slope_ref, bf16[2,2,128,2048]{3,2,1,0:T(8,128)(2,1)} %pad_maximum_fusion.back_own_ref.back_other_ref, ...), custom_call_target="tpu_custom_call" | custom-call | flops 1 | bytes 1 | tf_op jit(solution)/shard_map/grad/pallas_call | solution.py:365
  218.5 2.2 collective-permute-start.24
  223.3 14.4 %owner.1 = bf16[2,2,128,2048]{3,2,1,0:T(8,128)(2,1)} custom-call(s32[1]{0:T(128)} %bitcast.5.core_ref, bf16[2,128,3200]{2,1,0:T(8,128)(2,1)} %collective-permute-done.21.own_ref, bf16[2,128,3200]{2,1,0:T(8,128)(2,1)} %collective-permute-done.26.other_ref, bf16[3200,2048]{1,0:T(8,128)(2,1)} %weight_ref.7, f32[1,2048]{1,0:T(1,128)} %bitcast.42), custom_call_target="tpu_custom_call" | custom-call | flops 1 | bytes 1 | tf_op jit(solution)/shard_map/owner/pallas_call | solution.py:404
  237.7 6.7 %place.1 = bf16[6,256,2048]{2,1,0:T(8,128)(2,1)} custom-call(s32[3]{0:T(128)} %pad_add_fusion.slots_ref, bf16[2,256,2048]{2,1,0:T(8,128)(2,1)} %bitcast.40, bf16[2,256,2048]{2,1,0:T(8,128)(2,1)} %bitcast.37), custom_call_target="tpu_custom_call" | custom-call | flops 1 | bytes 1 | tf_op jit(solution)/shard_map/place/pallas_call | solution.py:453
  244.4 4.9 %final.1 = bf16[2,128,3200]{2,1,0:T(8,128)(2,1)} custom-call(bf16[2,128,3200]{2,1,0:T(8,128)(2,1)} %get-tuple-element.76.own_ref, bf16[2,128,3200]{2,1,0:T(8,128)(2,1)} %collective-permute-done.25.other_ref, bf16[2,128,3200]{2,1,0:T(8,128)(2,1)} %get-tuple-element.75.own_ref.z_ref, f32[2,128,128]{2,1,0:T(8,128)} %get-tuple-element.78.inverse_ref), custom_call_target="tpu_custom_call" | custom-call | flops 1 | bytes 1 | tf_op jit(solution)/shard_map/final/pallas_call | solution.py:261
  249.3 12.5 %collective-permute-done.24.own_ref = bf16[2,128,3200]{2,1,0:T(8,128)(2,1)S(1)} collective-permute-done((bf16[2,128,3200]{2,1,0:T(8,128)(2,1)S(1)}, bf16[2,128,3200]{2,1,0:T(8,128)(2,1)S(1)}, u32[]{:S(2)}, u32[]{:S(2)}) %collective-permute-start.24) | collective-permute-done | bytes 1638432 | tf_op jit(solution)/shard_map/ppermute | solution.py:32
  263.1 3.1 %collective-permute-done.27.other_ref = bf16[2,128,3200]{2,1,0:T(8,128)(2,1)S(1)} collective-permute-done((bf16[2,128,3200]{2,1,0:T(8,128)(2,1)S(1)}, bf16[2,128,3200]{2,1,0:T(8,128)(2,1)S(1)}, u32[]{:S(2)}, u32[]{:S(2)}) %collective-permute-start.27) | collective-permute-done | bytes 1638432 | tf_op jit(solution)/shard_map/ppermute | solution.py:22
  267.4 21.5 %slots.1 = bf16[6,2,128,2048]{3,2,1,0:T(8,128)(2,1)} custom-call(s32[3]{0:T(128)} %pad_add_fusion.slots_ref, bf16[2,128,3200]{2,1,0:T(8,128)(2,1)} %copy-done.5, bf16[2,128,3200]{2,1,0:T(8,128)(2,1)} %copy-done.6, bf16[3200,2048]{1,0:T(8,128)(2,1)} %weight_ref.7, f32[1,2048]{1,0:T(1,128)} %bitcast.43, ...), custom_call_target="tpu_custom_call", output_to_operand_aliasing={{}: (5, {})} | custom-call | flops 1 | bytes 1 | tf_op jit(solution)/shard_map/slots/pallas_call | solution.py:496
  (111 shorter events, 35.8 us)
Async XLA Ops:
  7.2 76.5 %all-gather.2.cloned.1.call-start = ((), (), s32[]{:S(2)}) async-start(), calls=%async_computation | async-start | bytes 5222400 | tf_op jit(solution)/shard_map/all_gather | solution.py:548
  8.3 11.8 %collective-permute-start = (bf16[50,768]{1,0:T(8,128)(2,1)S(1)}, bf16[50,768]{1,0:T(8,128)(2,1)S(1)}, u32[]{:S(2)}, u32[]{:S(2)}) collective-permute-start(bf16[50,768]{1,0:T(8,128)(2,1)S(1)} %get-tuple-element.89), channel_id=1, source_target_pairs={{0,32},{32,64},{64,96},{96,0},{1,33},{33,65},{65,97},{97,1},{2,34}... | collective-permute-start | bytes 230408 | tf_op jit(solution)/shard_map/ppermute | solution.py:26
  10.0 10.1 %collective-permute-start.1 = (bf16[50,768]{1,0:T(8,128)(2,1)S(1)}, bf16[50,768]{1,0:T(8,128)(2,1)S(1)}, u32[]{:S(2)}, u32[]{:S(2)}) collective-permute-start(bf16[50,768]{1,0:T(8,128)(2,1)S(1)} %get-tuple-element.91), channel_id=1, source_target_pairs={{0,64},{32,96},{64,0},{96,32},{1,65},{33,97},{65,1},{97,33},{2,66}... | collective-permute-start | bytes 230408 | tf_op jit(solution)/shard_map/ppermute | solution.py:26
  13.3 6.8 %collective-permute-start.2 = (bf16[50,768]{1,0:T(8,128)(2,1)S(1)}, bf16[50,768]{1,0:T(8,128)(2,1)S(1)}, u32[]{:S(2)}, u32[]{:S(2)}) collective-permute-start(bf16[50,768]{1,0:T(8,128)(2,1)S(1)} %get-tuple-element.88), channel_id=1, source_target_pairs={{0,96},{32,0},{64,32},{96,64},{1,97},{33,1},{65,33},{97,65},{2,98}... | collective-permute-start | bytes 230408 | tf_op jit(solution)/shard_map/ppermute | solution.py:26
  21.1 39.9 %collective-permute-start.5 = (bf16[1024,3200]{1,0:T(8,128)(2,1)}, bf16[1024,3200]{1,0:T(8,128)(2,1)}, u32[]{:S(2)}, u32[]{:S(2)}) collective-permute-start(bf16[1024,3200]{1,0:T(8,128)(2,1)} %refs_8_.1), channel_id=1, source_target_pairs={{0,1},{1,0},{2,3},{3,2},{4,5},{5,4},{6,7},{7,6},{8,9},{9,8},{10,11... | collective-permute-start | bytes 19660808 | tf_op jit(solution)/shard_map/ppermute | solution.py:22
  22.7 38.3 %collective-permute-start.3 = (bf16[2,128,3200]{2,1,0:T(8,128)(2,1)S(1)}, bf16[2,128,3200]{2,1,0:T(8,128)(2,1)S(1)}, u32[]{:S(2)}, u32[]{:S(2)}) collective-permute-start(bf16[2,128,3200]{2,1,0:T(8,128)(2,1)S(1)} %copy-done), channel_id=1, source_target_pairs={{0,32},{32,64},{64,96},{96,0},{1,33},{33,65},{65,97},{97,1},{2,34}... | collective-permute-start | bytes 4915208 | tf_op jit(solution)/shard_map/ppermute | solution.py:26
  23.5 37.5 %collective-permute-start.4 = (bf16[2,128,3200]{2,1,0:T(8,128)(2,1)S(1)}, bf16[2,128,3200]{2,1,0:T(8,128)(2,1)}, u32[]{:S(2)}, u32[]{:S(2)}) collective-permute-start(bf16[2,128,3200]{2,1,0:T(8,128)(2,1)S(1)} %copy-done), channel_id=1, source_target_pairs={{0,96},{32,0},{64,32},{96,64},{1,97},{33,1},{65,33},{97,65},{2,98}... | collective-permute-start | bytes 4915208 | tf_op jit(solution)/shard_map/ppermute | solution.py:26
  25.4 58.3 %collective-permute-start.12 = (bf16[2,128,3200]{2,1,0:T(8,128)(2,1)S(1)}, bf16[2,128,3200]{2,1,0:T(8,128)(2,1)}, u32[]{:S(2)}, u32[]{:S(2)}) collective-permute-start(bf16[2,128,3200]{2,1,0:T(8,128)(2,1)S(1)} %copy-done), channel_id=1, source_target_pairs={{0,1},{1,0},{2,3},{3,2},{4,5},{5,4},{6,7},{7,6},{8,9},{9,8},{10,11... | collective-permute-start | bytes 4915208 | tf_op jit(solution)/shard_map/ppermute | solution.py:22
  61.1 20.0 %collective-permute-start.6 = (bf16[1,128,3200]{2,1,0:T(8,128)(2,1)S(1)}, bf16[1,128,3200]{2,1,0:T(8,128)(2,1)}, u32[]{:S(2)}, u32[]{:S(2)}) collective-permute-start(bf16[1,128,3200]{2,1,0:T(8,128)(2,1)S(1)} %slice.30), channel_id=1, source_target_pairs={{0,32},{32,64},{64,96},{96,0},{1,33},{33,65},{65,97},{97,1},{2,34}... | collective-permute-start | bytes 2457608 | tf_op jit(solution)/shard_map/ppermute | solution.py:26
  62.8 20.3 %collective-permute-start.7 = (bf16[1,128,3200]{2,1,0:T(8,128)(2,1)S(1)}, bf16[1,128,3200]{2,1,0:T(8,128)(2,1)}, u32[]{:S(2)}, u32[]{:S(2)}) collective-permute-start(bf16[1,128,3200]{2,1,0:T(8,128)(2,1)S(1)} %slice.31), channel_id=1, source_target_pairs={{0,96},{32,0},{64,32},{96,64},{1,97},{33,1},{65,33},{97,65},{2,98}... | collective-permute-start | bytes 2457608 | tf_op jit(solution)/shard_map/ppermute | solution.py:26
  65.1 22.4 %collective-permute-start.10 = (bf16[2,128,3200]{2,1,0:T(8,128)(2,1)S(1)}, bf16[2,128,3200]{2,1,0:T(8,128)(2,1)}, u32[]{:S(2)}, u32[]{:S(2)}) collective-permute-start(bf16[2,128,3200]{2,1,0:T(8,128)(2,1)S(1)} %collective-permute-done.3.refs_4_), channel_id=1, source_target_pairs={{0,1},{1,0},{2,3},{3,2},{4,5},{5,4},{6,7},{7,6},{8,9},{9,8},{10,11... | collective-permute-start | bytes 4915208 | tf_op jit(solution)/shard_map/ppermute | solution.py:22
  66.8 20.8 %collective-permute-start.11 = (bf16[2,128,3200]{2,1,0:T(8,128)(2,1)}, bf16[2,128,3200]{2,1,0:T(8,128)(2,1)}, u32[]{:S(2)}, u32[]{:S(2)}) collective-permute-start(bf16[2,128,3200]{2,1,0:T(8,128)(2,1)} %collective-permute-done.4.refs_6_), channel_id=1, source_target_pairs={{0,1},{1,0},{2,3},{3,2},{4,5},{5,4},{6,7},{7,6},{8,9},{9,8},{10,11... | collective-permute-start | bytes 4915208 | tf_op jit(solution)/shard_map/ppermute | solution.py:22
  81.0 6.5 %collective-permute-start.8 = (bf16[1,128,3200]{2,1,0:T(8,128)(2,1)}, bf16[1,128,3200]{2,1,0:T(8,128)(2,1)}, u32[]{:S(2)}, u32[]{:S(2)}) collective-permute-start(bf16[1,128,3200]{2,1,0:T(8,128)(2,1)} %collective-permute-done.6.refs_0_), channel_id=1, source_target_pairs={{0,1},{1,0},{2,3},{3,2},{4,5},{5,4},{6,7},{7,6},{8,9},{9,8},{10,11... | collective-permute-start | bytes 2457608 | tf_op jit(solution)/shard_map/ppermute | solution.py:22
  83.7 72.5 %collective-permute-start.20 = (bf16[2,256,2048]{2,1,0:T(8,128)(2,1)}, bf16[2,256,2048]{2,1,0:T(8,128)(2,1)S(1)}, u32[]{:S(2)}, u32[]{:S(2)}) collective-permute-start(bf16[2,256,2048]{2,1,0:T(8,128)(2,1)} %get-tuple-element.62), channel_id=1, source_target_pairs={{0,4},{2,6},{4,8},{6,10},{8,12},{10,14},{12,16},{14,18},{16,20},{1... | collective-permute-start | bytes 6291464 | tf_op jit(solution)/shard_map/ppermute | solution.py:32
  112.3 7.9 %collective-permute-start.13 = (bf16[2,2,128,256]{3,2,1,0:T(8,128)(2,1)}, bf16[2,2,128,256]{3,2,1,0:T(8,128)(2,1)S(1)}, u32[]{:S(2)}, u32[]{:S(2)}) collective-permute-start(bf16[2,2,128,256]{3,2,1,0:T(8,128)(2,1)} %get-tuple-element.54), channel_id=1, source_target_pairs={{0,96},{32,0},{64,32},{96,64},{1,97},{33,1},{65,33},{97,65},{2,98}... | collective-permute-start | bytes 786440 | tf_op jit(solution)/shard_map/ppermute | solution.py:26
  114.1 9.0 %collective-permute-start.14 = (bf16[2,2,128,256]{3,2,1,0:T(8,128)(2,1)}, bf16[2,2,128,256]{3,2,1,0:T(8,128)(2,1)S(1)}, u32[]{:S(2)}, u32[]{:S(2)}) collective-permute-start(bf16[2,2,128,256]{3,2,1,0:T(8,128)(2,1)} %get-tuple-element.55), channel_id=1, source_target_pairs={{0,64},{32,96},{64,0},{96,32},{1,65},{33,97},{65,1},{97,33},{2,66}... | collective-permute-start | bytes 786440 | tf_op jit(solution)/shard_map/ppermute | solution.py:26
  115.7 14.0 %collective-permute-start.15 = (bf16[2,2,128,256]{3,2,1,0:T(8,128)(2,1)}, bf16[2,2,128,256]{3,2,1,0:T(8,128)(2,1)S(1)}, u32[]{:S(2)}, u32[]{:S(2)}) collective-permute-start(bf16[2,2,128,256]{3,2,1,0:T(8,128)(2,1)} %get-tuple-element.56), channel_id=1, source_target_pairs={{0,32},{32,64},{64,96},{96,0},{1,33},{33,65},{65,97},{97,1},{2,34}... | collective-permute-start | bytes 786440 | tf_op jit(solution)/shard_map/ppermute | solution.py:26
  130.7 24.0 %collective-permute-start.16 = (bf16[2,128,256]{2,1,0:T(8,128)(2,1)S(1)}, bf16[2,128,256]{2,1,0:T(8,128)(2,1)S(1)}, u32[]{:S(2)}, u32[]{:S(2)}) collective-permute-start(bf16[2,128,256]{2,1,0:T(8,128)(2,1)S(1)} %slice_bitcast_fusion.3), channel_id=1, source_target_pairs={{0,1},{1,0},{2,3},{3,2},{4,5},{5,4},{6,7},{7,6},{8,9},{9,8},{10,11... | collective-permute-start | bytes 393224 | tf_op jit(solution)/shard_map/ppermute | solution.py:22
  131.3 24.7 %collective-permute-start.17 = (bf16[2,128,256]{2,1,0:T(8,128)(2,1)S(1)}, bf16[2,128,256]{2,1,0:T(8,128)(2,1)S(1)}, u32[]{:S(2)}, u32[]{:S(2)}) collective-permute-start(bf16[2,128,256]{2,1,0:T(8,128)(2,1)S(1)} %slice_bitcast_fusion.2), channel_id=1, source_target_pairs={{0,1},{1,0},{2,3},{3,2},{4,5},{5,4},{6,7},{7,6},{8,9},{9,8},{10,11... | collective-permute-start | bytes 393224 | tf_op jit(solution)/shard_map/ppermute | solution.py:22
  131.4 67.3 %collective-permute-start.23 = (bf16[2,256,2048]{2,1,0:T(8,128)(2,1)}, bf16[2,256,2048]{2,1,0:T(8,128)(2,1)S(1)}, u32[]{:S(2)}, u32[]{:S(2)}) collective-permute-start(bf16[2,256,2048]{2,1,0:T(8,128)(2,1)} %get-tuple-element.70), channel_id=1, source_target_pairs={{0,2},{2,4},{4,6},{6,8},{8,10},{10,12},{12,14},{14,16},{16,18},{18... | collective-permute-start | bytes 6291464 | tf_op jit(solution)/shard_map/ppermute | solution.py:32
  169.3 7.1 %collective-permute-start.22 = (bf16[2,128,3200]{2,1,0:T(8,128)(2,1)}, bf16[2,128,3200]{2,1,0:T(8,128)(2,1)}, u32[]{:S(2)}, u32[]{:S(2)}) collective-permute-start(bf16[2,128,3200]{2,1,0:T(8,128)(2,1)} %get-tuple-element.75.own_ref.z_ref), channel_id=1, source_target_pairs={{0,1},{1,0},{2,3},{3,2},{4,5},{5,4},{6,7},{7,6},{8,9},{9,8},{10,11... | collective-permute-start | bytes 4915208 | tf_op jit(solution)/shard_map/ppermute | solution.py:22
  169.8 47.3 %collective-permute-start.21 = (bf16[2,128,3200]{2,1,0:T(8,128)(2,1)}, bf16[2,128,3200]{2,1,0:T(8,128)(2,1)}, u32[]{:S(2)}, u32[]{:S(2)}) collective-permute-start(bf16[2,128,3200]{2,1,0:T(8,128)(2,1)} %get-tuple-element.75.own_ref.z_ref), channel_id=1, source_target_pairs={{2,0},{4,2},{6,4},{8,6},{10,8},{12,10},{14,12},{16,14},{18,16},{20... | collective-permute-start | bytes 4915208 | tf_op jit(solution)/shard_map/ppermute | solution.py:32
  218.4 26.0 %collective-permute-start.25 = (bf16[2,128,3200]{2,1,0:T(8,128)(2,1)}, bf16[2,128,3200]{2,1,0:T(8,128)(2,1)}, u32[]{:S(2)}, u32[]{:S(2)}) collective-permute-start(bf16[2,128,3200]{2,1,0:T(8,128)(2,1)} %get-tuple-element.77), channel_id=1, source_target_pairs={{0,1},{1,0},{2,3},{3,2},{4,5},{5,4},{6,7},{7,6},{8,9},{9,8},{10,11... | collective-permute-start | bytes 4915208 | tf_op jit(solution)/shard_map/ppermute | solution.py:22
  218.5 43.3 %collective-permute-start.24 = (bf16[2,128,3200]{2,1,0:T(8,128)(2,1)S(1)}, bf16[2,128,3200]{2,1,0:T(8,128)(2,1)S(1)}, u32[]{:S(2)}, u32[]{:S(2)}) collective-permute-start(bf16[2,128,3200]{2,1,0:T(8,128)(2,1)S(1)} %copy-done.1), channel_id=1, source_target_pairs={{4,0},{6,2},{8,4},{10,6},{12,8},{14,10},{16,12},{18,14},{20,16},{2... | collective-permute-start | bytes 4915208 | tf_op jit(solution)/shard_map/ppermute | solution.py:32
  (22 other events, 318.7 us)
Sparse Core Ops, SparseCore 0:
  21.2 52.7 all-gather.1

commit v9 on v4

--- a/solution.py
+++ b/solution.py
@@ -488,11 +488,11 @@
     near_back = [along_img(packets[0], 1), along_img(packets[1], 1)]
 
     far_others = [swap(far_first), swap(far_second)]
-    att_low, att_high = attend(
-        [([rows], [swap(rows)]) for rows in (from_low, from_high)], weight
-    )
-    far_first, far_second, att_low = lax.optimization_barrier((far_first, far_second, att_low))
-    (att_far,) = attend([([far_first, far_second], far_others)], weight)
+    att_far, att_low, att_high = attend(
+        [([far_first, far_second], far_others)]
+        + [([rows], [swap(rows)]) for rows in (from_low, from_high)],
+        weight,
+    )
     (att_own,) = attend([([normed], [swap(normed)])], weight)
     att_far, att_low, att_high = along_z(att_far, 2), along_z(att_low, -1), along_z(att_high, 1)
     att_own, halfway, near_back[0] = lax.optimization_barrier((att_own, halfway, near_back[0]))

time: 293 us -> 293 us (level)
  Pallas kernels: 123 us -> 119 us
  starting transfers between devices: 59.4 us -> 62.8 us
    pallas_call x3 -> x2, Pallas kernels: 31.7 us -> 27.5 us  [attend(): pl.pallas_call(functools.partial(attend_kernel, layout), out_shape=[jax.S...]
    ppermute x10, waiting for transfers between devices: 45.1 us -> 41 us  [along_z(): return lax.ppermute(array, 'z', [(i, (i + by) % LINE) for i in range(LINE)])]
    ppermute x13, starting transfers between devices: 8.67 us -> 11.8 us  [swap(): return lax.ppermute(array, 'head', [(0, 1), (1, 0)])]
    unnamed x63 -> x57, local copies, waits for them, and re-layouts: 9.02 us -> 9.02 us
  transfers between devices with their start and end apart: 34 -> 34, of which waited for: 7 -> 7; matrix products, arithmetic and copies ran while one was open for 5% -> 5% of each run, Pallas kernels for 35% -> 34%
where the time goes in v9:
time: 293 us; the launch traced here: 289 us
  Pallas kernels  119 us (41%)
  starting transfers between devices  62.8 us (21%)
  waiting for transfers between devices  56.6 us (19%)
  between operations  22.9 us (8%)
  local copies, waits for them, and re-layouts  21.1 us (7%)
  other arithmetic  6.6 us (2%)
    ppermute x10, waiting for transfers between devices, along_z(): return lax.ppermute(array, 'z', [(i, (i + by) % LINE) for i in range(LINE)])  41 us
    pallas_call x2, Pallas kernels, owner_project(): pl.pallas_call(functools.partial(owner_kernel, count), grid_spec=pltpu.Pr...  28.6 us
    pallas_call x2, Pallas kernels, attend(): pl.pallas_call(functools.partial(attend_kernel, layout), out_shape=[jax.S...  27.5 us
    ppermute x6, starting transfers between devices, along_img(): return lax.ppermute(array, IMG, pairs)  22.6 us
    pallas_call x1, Pallas kernels, home_project(): pl.pallas_call(project_kernel, grid_spec=pltpu.PrefetchScalarGridSpec(num...  15.2 us
    ppermute x10, starting transfers between devices, along_z(): return lax.ppermute(array, 'z', [(i, (i + by) % LINE) for i in range(LINE)])  14.9 us
    pallas_call x1, Pallas kernels, home_grad(): pl.pallas_call(grad_kernel, grid_spec=pltpu.PrefetchScalarGridSpec(num_sc...  14.9 us
    pallas_call x2, Pallas kernels, out_project(): pl.pallas_call(out_kernel, grid_spec=pltpu.PrefetchScalarGridSpec(num_sca...  13.9 us
  transfers between devices with their start and end apart: 34, of which 7 were waited for; matrix products, arithmetic and copies ran while one was open for 5% of the time, Pallas kernels for 34%

profile of v9, /device:TPU:31, one launch (start us, length us, event | category | flops | bytes accessed | tf_op | source)
XLA Modules:
  0.0 289.1 jit_solution(15100814635870993504)
XLA Ops:
  10.0 3.3 %collective-permute-start.1 = (bf16[50,768]{1,0:T(8,128)(2,1)S(1)}, bf16[50,768]{1,0:T(8,128)(2,1)S(1)}, u32[]{:S(2)}, u32[]{:S(2)}) collective-permute-start(bf16[50,768]{1,0:T(8,128)(2,1)S(1)} %get-tuple-element.107), channel_id=1, source_target_pairs={{0,64},{32,96},{64,0},{96,32},{1,65},{33,97},{65,1},{97,33},{2,66}... | collective-permute-start | bytes 230408 | tf_op jit(solution)/shard_map/ppermute | solution.py:26
  14.1 6.0 %norm.1.refs_0_ = bf16[2,128,3200]{2,1,0:T(8,128)(2,1)} custom-call(bf16[2,128,3200]{2,1,0:T(8,128)(2,1)} %tokens_ref.5), custom_call_target="tpu_custom_call" | custom-call | flops 1 | bytes 1 | tf_op jit(solution)/shard_map/norm/pallas_call | solution.py:84
  27.9 4.4 %constant_dynamic-slice_fusion = (bf16[1,256,2048]{2,1,0:T(8,128)(2,1)}, bf16[1,256,2048]{2,1,0:T(8,128)(2,1)}, bf16[1,256,2048]{2,1,0:T(8,128)(2,1)}, bf16[1,256,2048]{2,1,0:T(8,128)(2,1)}) fusion(bf16[6,256,2048]{2,1,0:T(8,128)(2,1)} %param.21, s32[]{:T(128)S(6)} %min.22, s32[]{:T(128)S(6)} %min.21, s32[]{:T(128)S(6)} %min.20, s32[]{:T(128)S(6)} %min.19), kind=kLoop, calls=%fused_computation.30 | loop fusion | bytes 8388624 | tf_op jit(solution)/shard_map/dynamic_slice | solution.py:479
  32.3 26.5 %collective-permute-done.4.refs_4_ = bf16[2,128,3200]{2,1,0:T(8,128)(2,1)S(1)} collective-permute-done((bf16[2,128,3200]{2,1,0:T(8,128)(2,1)S(1)}, bf16[2,128,3200]{2,1,0:T(8,128)(2,1)S(1)}, u32[]{:S(2)}, u32[]{:S(2)}) %collective-permute-start.4) | collective-permute-done | bytes 1638432 | tf_op jit(solution)/shard_map/ppermute | solution.py:26
  66.2 11.4 %collective-permute-done.8.refs_0_ = bf16[1,128,3200]{2,1,0:T(8,128)(2,1)} collective-permute-done((bf16[1,128,3200]{2,1,0:T(8,128)(2,1)S(1)}, bf16[1,128,3200]{2,1,0:T(8,128)(2,1)}, u32[]{:S(2)}, u32[]{:S(2)}) %collective-permute-start.8) | collective-permute-done | bytes 819232 | tf_op jit(solution)/shard_map/ppermute | solution.py:26
  77.6 3.3 %collective-permute-start.10 = (bf16[1,128,3200]{2,1,0:T(8,128)(2,1)}, bf16[1,128,3200]{2,1,0:T(8,128)(2,1)}, u32[]{:S(2)}, u32[]{:S(2)}) collective-permute-start(bf16[1,128,3200]{2,1,0:T(8,128)(2,1)} %collective-permute-done.8.refs_0_), channel_id=1, source_target_pairs={{0,1},{1,0},{2,3},{3,2},{4,5},{5,4},{6,7},{7,6},{8,9},{9,8},{10,11... | collective-permute-start | bytes 2457608 | tf_op jit(solution)/shard_map/ppermute | solution.py:22
  85.6 3.2 %collective-permute-start.7 = (bf16[1,256,2048]{2,1,0:T(8,128)(2,1)}, bf16[1,256,2048]{2,1,0:T(8,128)(2,1)S(1)}, u32[]{:S(2)}, u32[]{:S(2)}) collective-permute-start(bf16[1,256,2048]{2,1,0:T(8,128)(2,1)} %get-tuple-element.55), channel_id=1, source_target_pairs={{0,2},{2,4},{4,6},{6,8},{8,10},{10,12},{12,14},{14,16},{16,18},{18... | collective-permute-start | bytes 3145736 | tf_op jit(solution)/shard_map/ppermute | solution.py:32
  88.8 19.0 %attend.3 = (bf16[2,256,256]{2,1,0:T(8,128)(2,1)}, bf16[2,256,256]{2,1,0:T(8,128)(2,1)}, bf16[2,256,256]{2,1,0:T(8,128)(2,1)}) custom-call(bf16[1,128,3200]{2,1,0:T(8,128)(2,1)} %collective-permute-done.8.refs_0_, bf16[1,128,3200]{2,1,0:T(8,128)(2,1)} %collective-permute-done.9.refs_1_, bf16[1,128,3200]{2,1,0:T(8,128)(2,1)} %collective-permute-done.10.refs_2_, ...), custom_call_target="tpu_custom_call" | custom-call | flops 1 | bytes 1 | tf_op jit(solution)/shard_map/attend/pallas_call | solution.py:164
  107.9 3.3 %collective-permute-start.15 = (bf16[2,256,256]{2,1,0:T(8,128)(2,1)}, bf16[2,256,256]{2,1,0:T(8,128)(2,1)S(1)}, u32[]{:S(2)}, u32[]{:S(2)}) collective-permute-start(bf16[2,256,256]{2,1,0:T(8,128)(2,1)} %get-tuple-element.60), channel_id=1, source_target_pairs={{0,64},{32,96},{64,0},{96,32},{1,65},{33,97},{65,1},{97,33},{2,66}... | collective-permute-start | bytes 786440 | tf_op jit(solution)/shard_map/ppermute | solution.py:26
  112.0 8.6 %attend.2.refs_0_ = bf16[2,256,256]{2,1,0:T(8,128)(2,1)} custom-call(bf16[2,128,3200]{2,1,0:T(8,128)(2,1)} %norm.1.refs_0_, bf16[2,128,3200]{2,1,0:T(8,128)(2,1)} %collective-permute-done.3.refs_1_, bf16[3200,768]{1,0:T(8,128)(2,1)} %all-gather.2.cloned.1.call-done.refs_2_.refs_8_), custom_call_target="tpu_custom_call" | custom-call | flops 1 | bytes 1 | tf_op jit(solution)/shard_map/attend/pallas_call | solution.py:164
  120.6 3.2 %collective-permute-done.16.refs_3_ = bf16[2,256,256]{2,1,0:T(8,128)(2,1)S(1)} collective-permute-done((bf16[2,256,256]{2,1,0:T(8,128)(2,1)}, bf16[2,256,256]{2,1,0:T(8,128)(2,1)S(1)}, u32[]{:S(2)}, u32[]{:S(2)}) %collective-permute-start.16) | collective-permute-done | bytes 262176 | tf_op jit(solution)/shard_map/ppermute | solution.py:26
  124.5 7.1 %out.3 = bf16[2,128,3200]{2,1,0:T(8,128)(2,1)} custom-call(s32[1]{0:T(128)} %bitcast.4.line_ref, bf16[2,256,256]{2,1,0:T(8,128)(2,1)} %attend.2.refs_0_, bf16[2,256,256]{2,1,0:T(8,128)(2,1)} %copy-done.12, bf16[2,256,256]{2,1,0:T(8,128)(2,1)} %copy-done.13, bf16[2,256,256]{2,1,0:T(8,128)(2,1)} %copy-done.14, bf16[1024,3200]{1,0:T(8,128)(2,1)} %refs_4_.6), custom_call_target="tpu_custom_call" | custom-call | flops 1 | bytes 1 | tf_op jit(solution)/shard_map/out/pallas_call | solution.py:202
  132.1 7.7 %collective-permute-start.23 = (bf16[1,256,2048]{2,1,0:T(8,128)(2,1)S(1)}, bf16[1,256,2048]{2,1,0:T(8,128)(2,1)}, u32[]{:S(2)}, u32[]{:S(2)}) collective-permute-start(bf16[1,256,2048]{2,1,0:T(8,128)(2,1)S(1)} %copy-done.9), channel_id=1, source_target_pairs={{0,2},{2,4},{4,6},{6,8},{8,10},{10,12},{12,14},{14,16},{16,18},{18... | collective-permute-start | bytes 3145736 | tf_op jit(solution)/shard_map/ppermute | solution.py:32
  146.6 6.9 %out.2.own_ref = bf16[2,128,3200]{2,1,0:T(8,128)(2,1)} custom-call(s32[1]{0:T(128)} %bitcast.4.line_ref, bf16[2,256,256]{2,1,0:T(8,128)(2,1)} %attend.2.refs_0_, bf16[2,256,256]{2,1,0:T(8,128)(2,1)} %copy-done.12, bf16[2,256,256]{2,1,0:T(8,128)(2,1)} %copy-done.13, bf16[2,256,256]{2,1,0:T(8,128)(2,1)} %copy-done.14, bf16[1024,3200]{1,0:T(8,128)(2,1)} %refs_4_.6), custom_call_target="tpu_custom_call" | custom-call | flops 1 | bytes 1 | tf_op jit(solution)/shard_map/out/pallas_call | solution.py:202
  154.6 3.7 %join.2 = (bf16[1,128,3200]{2,1,0:T(8,128)(2,1)}, f32[1,128,128]{2,1,0:T(8,128)}) custom-call(f32[4]{0:T(128)} %exponential_divide_fusion.mixing_ref, bf16[2,128,3200]{2,1,0:T(8,128)(2,1)} %tokens_ref.5, bf16[2,128,3200]{2,1,0:T(8,128)(2,1)} %early_ref.3, bf16[2,128,3200]{2,1,0:T(8,128)(2,1)} %mid_ref.3, bf16[2,128,3200]{2,1,0:T(8,128)(2,1)} %out.2.own_ref, ...), custom_call_target="tpu_custom_call" | custom-call | flops 1 | bytes 1 | tf_op jit(solution)/shard_map/join/pallas_call | solution.py:241
  159.1 3.8 %join.3 = (bf16[1,128,3200]{2,1,0:T(8,128)(2,1)}, f32[1,128,128]{2,1,0:T(8,128)}) custom-call(f32[4]{0:T(128)} %exponential_divide_fusion.mixing_ref, bf16[2,128,3200]{2,1,0:T(8,128)(2,1)} %tokens_ref.5, bf16[2,128,3200]{2,1,0:T(8,128)(2,1)} %early_ref.3, bf16[2,128,3200]{2,1,0:T(8,128)(2,1)} %mid_ref.3, bf16[2,128,3200]{2,1,0:T(8,128)(2,1)} %out.2.own_ref, ...), custom_call_target="tpu_custom_call" | custom-call | flops 1 | bytes 1 | tf_op jit(solution)/shard_map/join/pallas_call | solution.py:241
  169.5 5.2 %collective-permute-start.21 = (bf16[1,128,3200]{2,1,0:T(8,128)(2,1)S(1)}, bf16[1,128,3200]{2,1,0:T(8,128)(2,1)}, u32[]{:S(2)}, u32[]{:S(2)}) collective-permute-start(bf16[1,128,3200]{2,1,0:T(8,128)(2,1)S(1)} %copy-done.4), channel_id=1, source_target_pairs={{4,0},{6,2},{8,4},{10,6},{12,8},{14,10},{16,12},{18,14},{20,16},{2... | collective-permute-start | bytes 2457608 | tf_op jit(solution)/shard_map/ppermute | solution.py:32
  174.7 15.2 %project.1 = (bf16[2,2,128,2048]{3,2,1,0:T(8,128)(2,1)}, f32[512,2048]{1,0:T(8,128)}) custom-call(s32[1]{0:T(128)} %bitcast.3.core_ref, bf16[1,128,3200]{2,1,0:T(8,128)(2,1)} %get-tuple-element.62.refs_0_.z_ref, bf16[1,128,3200]{2,1,0:T(8,128)(2,1)} %get-tuple-element.74.refs_1_.later_z_ref, bf16[1,128,3200]{2,1,0:T(8,128)(2,1)} %collective-permute-done.18.refs_2_, ...), custom_call_target="tpu_custom_call" | custom-call | flops 1 | bytes 1 | tf_op jit(solution)/shard_map/project/pallas_call | solution.py:319
  189.9 12.4 %collective-permute-done.23 = bf16[1,256,2048]{2,1,0:T(8,128)(2,1)} collective-permute-done((bf16[1,256,2048]{2,1,0:T(8,128)(2,1)S(1)}, bf16[1,256,2048]{2,1,0:T(8,128)(2,1)}, u32[]{:S(2)}, u32[]{:S(2)}) %collective-permute-start.23) | collective-permute-done | bytes 1048608 | tf_op jit(solution)/shard_map/ppermute | solution.py:32
  208.2 14.9 %grad.1 = (bf16[2,128,3200]{2,1,0:T(8,128)(2,1)}, bf16[2,128,3200]{2,1,0:T(8,128)(2,1)}) custom-call(s32[1]{0:T(128)} %bitcast.3.core_ref, f32[512,2048]{1,0:T(8,128)} %get-tuple-element.68.slope_ref, bf16[2,2,128,2048]{3,2,1,0:T(8,128)(2,1)} %pad_maximum_fusion.back_own_ref.back_other_ref, ...), custom_call_target="tpu_custom_call" | custom-call | flops 1 | bytes 1 | tf_op jit(solution)/shard_map/grad/pallas_call | solution.py:379
  228.5 6.3 %collective-permute-start.27 = (bf16[1,128,3200]{2,1,0:T(8,128)(2,1)}, bf16[1,128,3200]{2,1,0:T(8,128)(2,1)}, u32[]{:S(2)}, u32[]{:S(2)}) collective-permute-start(bf16[1,128,3200]{2,1,0:T(8,128)(2,1)} %copy-done.21), channel_id=1, source_target_pairs={{6,0},{0,2},{10,4},{4,6},{14,8},{8,10},{18,12},{12,14},{22,16},{16... | collective-permute-start | bytes 2457608 | tf_op jit(solution)/shard_map/ppermute | solution.py:49
  236.6 14.3 %owner.2 = bf16[2,2,128,2048]{3,2,1,0:T(8,128)(2,1)} custom-call(s32[1]{0:T(128)} %bitcast.3.core_ref, bf16[1,128,3200]{2,1,0:T(8,128)(2,1)} %collective-permute-done.20.refs_0_, bf16[1,128,3200]{2,1,0:T(8,128)(2,1)} %copy-done.16, bf16[1,128,3200]{2,1,0:T(8,128)(2,1)} %collective-permute-done.21.refs_2_, bf16[1,128,3200]{2,1,0:T(8,128)(2,1)} %copy-done.17, ...), custom_call_target="tpu_custom_call" | custom-call | flops 1 | bytes 1 | tf_op jit(solution)/shard_map/owner/pallas_call | solution.py:420
  252.1 5.4 %final.1 = bf16[2,128,3200]{2,1,0:T(8,128)(2,1)} custom-call(bf16[2,128,3200]{2,1,0:T(8,128)(2,1)} %get-tuple-element.78.own_ref, bf16[2,128,3200]{2,1,0:T(8,128)(2,1)} %copy-done.7, bf16[1,128,3200]{2,1,0:T(8,128)(2,1)} %get-tuple-element.62.refs_0_.z_ref, bf16[1,128,3200]{2,1,0:T(8,128)(2,1)} %get-tuple-element.74.refs_1_.later_z_ref, ...), custom_call_target="tpu_custom_call" | custom-call | flops 1 | bytes 1 | tf_op jit(solution)/shard_map/final/pallas_call | solution.py:277
  261.6 14.3 %owner.3 = bf16[2,2,128,2048]{3,2,1,0:T(8,128)(2,1)} custom-call(s32[1]{0:T(128)} %bitcast.3.core_ref, bf16[1,128,3200]{2,1,0:T(8,128)(2,1)} %copy-done.15, bf16[1,128,3200]{2,1,0:T(8,128)(2,1)} %collective-permute-done.31.refs_1_, bf16[1,128,3200]{2,1,0:T(8,128)(2,1)} %collective-permute-done.27.refs_2_, ...), custom_call_target="tpu_custom_call" | custom-call | flops 1 | bytes 1 | tf_op jit(solution)/shard_map/owner/pallas_call | solution.py:420
  (140 shorter events, 57.0 us)
Async XLA Ops:
  7.2 74.2 %all-gather.2.cloned.1.call-start = ((), (), s32[]{:S(2)}) async-start(), calls=%async_computation | async-start | bytes 5222400 | tf_op jit(solution)/shard_map/all_gather | solution.py:466
  8.3 11.8 %collective-permute-start = (bf16[50,768]{1,0:T(8,128)(2,1)S(1)}, bf16[50,768]{1,0:T(8,128)(2,1)S(1)}, u32[]{:S(2)}, u32[]{:S(2)}) collective-permute-start(bf16[50,768]{1,0:T(8,128)(2,1)S(1)} %get-tuple-element.105), channel_id=1, source_target_pairs={{0,32},{32,64},{64,96},{96,0},{1,33},{33,65},{65,97},{97,1},{2,34}... | collective-permute-start | bytes 230408 | tf_op jit(solution)/shard_map/ppermute | solution.py:26
  21.6 37.1 %collective-permute-start.4 = (bf16[2,128,3200]{2,1,0:T(8,128)(2,1)S(1)}, bf16[2,128,3200]{2,1,0:T(8,128)(2,1)S(1)}, u32[]{:S(2)}, u32[]{:S(2)}) collective-permute-start(bf16[2,128,3200]{2,1,0:T(8,128)(2,1)S(1)} %copy-done.1), channel_id=1, source_target_pairs={{0,32},{32,64},{64,96},{96,0},{1,33},{33,65},{65,97},{97,1},{2,34}... | collective-permute-start | bytes 4915208 | tf_op jit(solution)/shard_map/ppermute | solution.py:26
  22.4 36.4 %collective-permute-start.5 = (bf16[2,128,3200]{2,1,0:T(8,128)(2,1)S(1)}, bf16[2,128,3200]{2,1,0:T(8,128)(2,1)}, u32[]{:S(2)}, u32[]{:S(2)}) collective-permute-start(bf16[2,128,3200]{2,1,0:T(8,128)(2,1)S(1)} %copy-done.1), channel_id=1, source_target_pairs={{0,96},{32,0},{64,32},{96,64},{1,97},{33,1},{65,33},{97,65},{2,98}... | collective-permute-start | bytes 4915208 | tf_op jit(solution)/shard_map/ppermute | solution.py:26
  58.8 18.8 %collective-permute-start.8 = (bf16[1,128,3200]{2,1,0:T(8,128)(2,1)S(1)}, bf16[1,128,3200]{2,1,0:T(8,128)(2,1)}, u32[]{:S(2)}, u32[]{:S(2)}) collective-permute-start(bf16[1,128,3200]{2,1,0:T(8,128)(2,1)S(1)} %slice.28), channel_id=1, source_target_pairs={{0,32},{32,64},{64,96},{96,0},{1,33},{33,65},{65,97},{97,1},{2,34}... | collective-permute-start | bytes 2457608 | tf_op jit(solution)/shard_map/ppermute | solution.py:26
  60.5 20.3 %collective-permute-start.9 = (bf16[1,128,3200]{2,1,0:T(8,128)(2,1)S(1)}, bf16[1,128,3200]{2,1,0:T(8,128)(2,1)}, u32[]{:S(2)}, u32[]{:S(2)}) collective-permute-start(bf16[1,128,3200]{2,1,0:T(8,128)(2,1)S(1)} %slice.29), channel_id=1, source_target_pairs={{0,96},{32,0},{64,32},{96,64},{1,97},{33,1},{65,33},{97,65},{2,98}... | collective-permute-start | bytes 2457608 | tf_op jit(solution)/shard_map/ppermute | solution.py:26
  62.8 26.0 %collective-permute-start.12 = (bf16[2,128,3200]{2,1,0:T(8,128)(2,1)S(1)}, bf16[2,128,3200]{2,1,0:T(8,128)(2,1)}, u32[]{:S(2)}, u32[]{:S(2)}) collective-permute-start(bf16[2,128,3200]{2,1,0:T(8,128)(2,1)S(1)} %collective-permute-done.4.refs_4_), channel_id=1, source_target_pairs={{0,1},{1,0},{2,3},{3,2},{4,5},{5,4},{6,7},{7,6},{8,9},{9,8},{10,11... | collective-permute-start | bytes 4915208 | tf_op jit(solution)/shard_map/ppermute | solution.py:22
  65.7 23.1 %collective-permute-start.13 = (bf16[2,128,3200]{2,1,0:T(8,128)(2,1)}, bf16[2,128,3200]{2,1,0:T(8,128)(2,1)}, u32[]{:S(2)}, u32[]{:S(2)}) collective-permute-start(bf16[2,128,3200]{2,1,0:T(8,128)(2,1)} %collective-permute-done.5.refs_6_), channel_id=1, source_target_pairs={{0,1},{1,0},{2,3},{3,2},{4,5},{5,4},{6,7},{7,6},{8,9},{9,8},{10,11... | collective-permute-start | bytes 4915208 | tf_op jit(solution)/shard_map/ppermute | solution.py:22
  65.7 45.5 %collective-permute-start.3 = (bf16[2,128,3200]{2,1,0:T(8,128)(2,1)S(1)}, bf16[2,128,3200]{2,1,0:T(8,128)(2,1)}, u32[]{:S(2)}, u32[]{:S(2)}) collective-permute-start(bf16[2,128,3200]{2,1,0:T(8,128)(2,1)S(1)} %copy-done.1), channel_id=1, source_target_pairs={{0,1},{1,0},{2,3},{3,2},{4,5},{5,4},{6,7},{7,6},{8,9},{9,8},{10,11... | collective-permute-start | bytes 4915208 | tf_op jit(solution)/shard_map/ppermute | solution.py:22
  83.1 37.4 %collective-permute-start.6 = (bf16[1,256,2048]{2,1,0:T(8,128)(2,1)}, bf16[1,256,2048]{2,1,0:T(8,128)(2,1)}, u32[]{:S(2)}, u32[]{:S(2)}) collective-permute-start(bf16[1,256,2048]{2,1,0:T(8,128)(2,1)} %get-tuple-element.54), channel_id=1, source_target_pairs={{0,6},{2,0},{4,10},{6,4},{8,14},{10,8},{12,18},{14,12},{16,22},{18... | collective-permute-start | bytes 3145736 | tf_op jit(solution)/shard_map/ppermute | solution.py:48
  85.6 35.0 %collective-permute-start.7 = (bf16[1,256,2048]{2,1,0:T(8,128)(2,1)}, bf16[1,256,2048]{2,1,0:T(8,128)(2,1)S(1)}, u32[]{:S(2)}, u32[]{:S(2)}) collective-permute-start(bf16[1,256,2048]{2,1,0:T(8,128)(2,1)} %get-tuple-element.55), channel_id=1, source_target_pairs={{0,2},{2,4},{4,6},{6,8},{8,10},{10,12},{12,14},{14,16},{16,18},{18... | collective-permute-start | bytes 3145736 | tf_op jit(solution)/shard_map/ppermute | solution.py:32
  107.8 12.8 %collective-permute-start.14 = (bf16[2,256,256]{2,1,0:T(8,128)(2,1)}, bf16[2,256,256]{2,1,0:T(8,128)(2,1)S(1)}, u32[]{:S(2)}, u32[]{:S(2)}) collective-permute-start(bf16[2,256,256]{2,1,0:T(8,128)(2,1)} %get-tuple-element.59), channel_id=1, source_target_pairs={{0,96},{32,0},{64,32},{96,64},{1,97},{33,1},{65,33},{97,65},{2,98}... | collective-permute-start | bytes 786440 | tf_op jit(solution)/shard_map/ppermute | solution.py:26
  107.9 12.7 %collective-permute-start.15 = (bf16[2,256,256]{2,1,0:T(8,128)(2,1)}, bf16[2,256,256]{2,1,0:T(8,128)(2,1)S(1)}, u32[]{:S(2)}, u32[]{:S(2)}) collective-permute-start(bf16[2,256,256]{2,1,0:T(8,128)(2,1)} %get-tuple-element.60), channel_id=1, source_target_pairs={{0,64},{32,96},{64,0},{96,32},{1,65},{33,97},{65,1},{97,33},{2,66}... | collective-permute-start | bytes 786440 | tf_op jit(solution)/shard_map/ppermute | solution.py:26
  111.2 12.6 %collective-permute-start.16 = (bf16[2,256,256]{2,1,0:T(8,128)(2,1)}, bf16[2,256,256]{2,1,0:T(8,128)(2,1)S(1)}, u32[]{:S(2)}, u32[]{:S(2)}) collective-permute-start(bf16[2,256,256]{2,1,0:T(8,128)(2,1)} %get-tuple-element.61), channel_id=1, source_target_pairs={{0,32},{32,64},{64,96},{96,0},{1,33},{33,65},{65,97},{97,1},{2,34}... | collective-permute-start | bytes 786440 | tf_op jit(solution)/shard_map/ppermute | solution.py:26
  131.6 21.9 %collective-permute-start.17 = (bf16[2,128,3200]{2,1,0:T(8,128)(2,1)}, bf16[2,128,3200]{2,1,0:T(8,128)(2,1)S(1)}, u32[]{:S(2)}, u32[]{:S(2)}) collective-permute-start(bf16[2,128,3200]{2,1,0:T(8,128)(2,1)} %out.3), channel_id=1, source_target_pairs={{0,1},{1,0},{2,3},{3,2},{4,5},{5,4},{6,7},{7,6},{8,9},{9,8},{10,11... | collective-permute-start | bytes 4915208 | tf_op jit(solution)/shard_map/ppermute | solution.py:22
  132.1 70.3 %collective-permute-start.23 = (bf16[1,256,2048]{2,1,0:T(8,128)(2,1)S(1)}, bf16[1,256,2048]{2,1,0:T(8,128)(2,1)}, u32[]{:S(2)}, u32[]{:S(2)}) collective-permute-start(bf16[1,256,2048]{2,1,0:T(8,128)(2,1)S(1)} %copy-done.9), channel_id=1, source_target_pairs={{0,2},{2,4},{4,6},{6,8},{8,10},{10,12},{12,14},{14,16},{16,18},{18... | collective-permute-start | bytes 3145736 | tf_op jit(solution)/shard_map/ppermute | solution.py:32
  139.8 64.7 %collective-permute-start.25 = (bf16[1,256,2048]{2,1,0:T(8,128)(2,1)S(1)}, bf16[1,256,2048]{2,1,0:T(8,128)(2,1)}, u32[]{:S(2)}, u32[]{:S(2)}) collective-permute-start(bf16[1,256,2048]{2,1,0:T(8,128)(2,1)S(1)} %copy-done.8), channel_id=1, source_target_pairs={{0,4},{2,6},{4,8},{6,10},{8,12},{10,14},{12,16},{14,18},{16,20},{1... | collective-permute-start | bytes 3145736 | tf_op jit(solution)/shard_map/ppermute | solution.py:32
  141.7 62.8 %collective-permute-start.24 = (bf16[1,256,2048]{2,1,0:T(8,128)(2,1)}, bf16[1,256,2048]{2,1,0:T(8,128)(2,1)}, u32[]{:S(2)}, u32[]{:S(2)}) collective-permute-start(bf16[1,256,2048]{2,1,0:T(8,128)(2,1)} %collective-permute-done.6), channel_id=1, source_target_pairs={{6,4},{0,6},{10,8},{4,10},{14,12},{8,14},{18,16},{12,18},{22,20},{... | collective-permute-start | bytes 3145736 | tf_op jit(solution)/shard_map/ppermute | solution.py:49
  167.5 55.6 %collective-permute-start.20 = (bf16[1,128,3200]{2,1,0:T(8,128)(2,1)S(1)}, bf16[1,128,3200]{2,1,0:T(8,128)(2,1)}, u32[]{:S(2)}, u32[]{:S(2)}) collective-permute-start(bf16[1,128,3200]{2,1,0:T(8,128)(2,1)S(1)} %copy-done.4), channel_id=1, source_target_pairs={{2,0},{4,2},{6,4},{8,6},{10,8},{12,10},{14,12},{16,14},{18,16},{20... | collective-permute-start | bytes 2457608 | tf_op jit(solution)/shard_map/ppermute | solution.py:32
  169.5 53.7 %collective-permute-start.21 = (bf16[1,128,3200]{2,1,0:T(8,128)(2,1)S(1)}, bf16[1,128,3200]{2,1,0:T(8,128)(2,1)}, u32[]{:S(2)}, u32[]{:S(2)}) collective-permute-start(bf16[1,128,3200]{2,1,0:T(8,128)(2,1)S(1)} %copy-done.4), channel_id=1, source_target_pairs={{4,0},{6,2},{8,4},{10,6},{12,8},{14,10},{16,12},{18,14},{20,16},{2... | collective-permute-start | bytes 2457608 | tf_op jit(solution)/shard_map/ppermute | solution.py:32
  202.3 20.8 %collective-permute-start.22 = (bf16[1,128,3200]{2,1,0:T(8,128)(2,1)S(1)}, bf16[1,128,3200]{2,1,0:T(8,128)(2,1)S(1)}, u32[]{:S(2)}, u32[]{:S(2)}) collective-permute-start(bf16[1,128,3200]{2,1,0:T(8,128)(2,1)S(1)} %copy-done.5), channel_id=1, source_target_pairs={{4,6},{6,0},{8,10},{10,4},{12,14},{14,8},{16,18},{18,12},{20,22},{... | collective-permute-start | bytes 2457608 | tf_op jit(solution)/shard_map/ppermute | solution.py:48
  223.2 27.7 %collective-permute-start.30 = (bf16[2,128,3200]{2,1,0:T(8,128)(2,1)}, bf16[2,128,3200]{2,1,0:T(8,128)(2,1)S(1)}, u32[]{:S(2)}, u32[]{:S(2)}) collective-permute-start(bf16[2,128,3200]{2,1,0:T(8,128)(2,1)} %get-tuple-element.79), channel_id=1, source_target_pairs={{0,1},{1,0},{2,3},{3,2},{4,5},{5,4},{6,7},{7,6},{8,9},{9,8},{10,11... | collective-permute-start | bytes 4915208 | tf_op jit(solution)/shard_map/ppermute | solution.py:22
  225.7 31.8 %collective-permute-start.26 = (bf16[1,128,3200]{2,1,0:T(8,128)(2,1)S(1)}, bf16[1,128,3200]{2,1,0:T(8,128)(2,1)S(1)}, u32[]{:S(2)}, u32[]{:S(2)}) collective-permute-start(bf16[1,128,3200]{2,1,0:T(8,128)(2,1)S(1)} %copy-done.5), channel_id=1, source_target_pairs={{2,0},{4,2},{6,4},{8,6},{10,8},{12,10},{14,12},{16,14},{18,16},{20... | collective-permute-start | bytes 2457608 | tf_op jit(solution)/shard_map/ppermute | solution.py:32
  228.5 29.0 %collective-permute-start.27 = (bf16[1,128,3200]{2,1,0:T(8,128)(2,1)}, bf16[1,128,3200]{2,1,0:T(8,128)(2,1)}, u32[]{:S(2)}, u32[]{:S(2)}) collective-permute-start(bf16[1,128,3200]{2,1,0:T(8,128)(2,1)} %copy-done.21), channel_id=1, source_target_pairs={{6,0},{0,2},{10,4},{4,6},{14,8},{8,10},{18,12},{12,14},{22,16},{16... | collective-permute-start | bytes 2457608 | tf_op jit(solution)/shard_map/ppermute | solution.py:49
  (33 other events, 266.5 us)
Sparse Core Ops, SparseCore 0:
  21.2 52.7 all-gather.1

commit v10 on v9

--- a/solution.py
+++ b/solution.py
@@ -180,36 +180,43 @@
 
 
 def out_kernel(line_ref, *refs):
-    attended, weight_ref, part_ref, rows = refs[:LINE], refs[LINE], refs[LINE + 1], refs[LINE + 2]
-    tiles, half, block = part_ref.shape
+    attended, weight_ref, own_ref, other_ref, rows = refs[:LINE], *refs[LINE:]
+    tiles, half, block = own_ref.shape
     share = attended[0].shape[2]
+    count = tiles * half
 
     @pl.when(pl.program_id(0) == 0)
     def _():
         for distance, source in enumerate(attended):
             start = pl.multiple_of(lax.rem(line_ref[0] + distance, LINE) * share, share)
-            rows[:, pl.ds(start, share)] = source[...].reshape(tiles * half, share)
+            for part in range(2):
+                piece = source[:, part * half : (part + 1) * half].reshape(count, share)
+                rows[part * count : (part + 1) * count, pl.ds(start, share)] = piece
 
     total = jnp.dot(rows[...], weight_ref[...], preferred_element_type=jnp.float32)
-    part_ref[...] = total.astype(jnp.bfloat16).reshape(tiles, half, block)
-
-
-def out_project(line_arg, attended, out_weight, part):
+    total = total.astype(jnp.bfloat16)
+    own_ref[...] = total[:count].reshape(tiles, half, block)
+    other_ref[...] = total[count:].reshape(tiles, half, block)
+
+
+def out_project(line_arg, attended, out_weight):
     tiles, full, share = attended[0].shape
     half = full // 2
     depth = out_weight.shape[1]
     block = 640
+    part = pl.BlockSpec((tiles, half, block), lambda n, line: (0, 0, n))
+    shape = jax.ShapeDtypeStruct((tiles, half, depth), jnp.bfloat16)
     return pl.pallas_call(
         out_kernel,
         grid_spec=pltpu.PrefetchScalarGridSpec(
             num_scalar_prefetch=1,
             grid=(depth // block,),
-            in_specs=[pl.BlockSpec((tiles, half, share), lambda n, line: (0, part, 0))] * LINE
+            in_specs=[pl.BlockSpec((tiles, full, share), lambda n, line: (0, 0, 0))] * LINE
             + [pl.BlockSpec((LINE * share, block), lambda n, line: (0, n))],
-            out_specs=pl.BlockSpec((tiles, half, block), lambda n, line: (0, 0, n)),
-            scratch_shapes=[pltpu.VMEM((tiles * half, LINE * share), jnp.bfloat16)],
+            out_specs=[part, part],
+            scratch_shapes=[pltpu.VMEM((tiles * full, LINE * share), jnp.bfloat16)],
         ),
-        out_shape=jax.ShapeDtypeStruct((tiles, half, depth), jnp.bfloat16),
+        out_shape=[shape, shape],
         compiler_params=pltpu.CompilerParams(vmem_limit_bytes=VMEM_BYTES),
         cost_estimate=SMALL_COST,
         name="out",
@@ -499,8 +506,8 @@
     far_back[1] = far_on(halfway)
     attended = [att_own, att_low, att_far, att_high]
     line_arg = line_place.astype(jnp.int32).reshape(1)
-    part_other = swap(out_project(line_arg, attended, out_weight, 1))
-    part_own = out_project(line_arg, attended, out_weight, 0)
+    part_own, part_other = out_project(line_arg, attended, out_weight)
+    part_other = swap(part_other)
     raised_logits = jnp.exp(layer_logits)
     mixing = raised_logits / jnp.sum(raised_logits)
     scale = layer_scale.reshape(1, -1)

time: 293 us -> 294 us (level)
  waiting for transfers between devices: 56.6 us -> 63.7 us
  Pallas kernels: 119 us -> 114 us
    ppermute x6, waiting for transfers between devices: 12.4 us -> 19.1 us  [along_img(): return lax.ppermute(array, IMG, pairs)]
    pallas_call x2 -> x1, Pallas kernels: 13.9 us -> 8.62 us  [out_project(): pl.pallas_call(out_kernel, grid_spec=pltpu.PrefetchScalarGridSpec(num_sca...]
    unnamed x57 -> x55, local copies, waits for them, and re-layouts: 9.02 us -> 9.05 us
  transfers between devices with their start and end apart: 34 -> 34, of which waited for: 7 -> 8; matrix products, arithmetic and copies ran while one was open for 5% -> 5% of each run, Pallas kernels for 34% -> 31%
where the time goes in v10:
time: 294 us; the launch traced here: 290 us
  Pallas kernels  114 us (39%)
  waiting for transfers between devices  63.7 us (22%)
  starting transfers between devices  62.1 us (21%)
  between operations  22.9 us (8%)
  local copies, waits for them, and re-layouts  21.1 us (7%)
  other arithmetic  6.75 us (2%)
    ppermute x10, waiting for transfers between devices, along_z(): return lax.ppermute(array, 'z', [(i, (i + by) % LINE) for i in range(LINE)])  41 us
    pallas_call x2, Pallas kernels, owner_project(): pl.pallas_call(functools.partial(owner_kernel, count), grid_spec=pltpu.Pr...  28.6 us
    pallas_call x2, Pallas kernels, attend(): pl.pallas_call(functools.partial(attend_kernel, layout), out_shape=[jax.S...  27.5 us
    ppermute x6, starting transfers between devices, along_img(): return lax.ppermute(array, IMG, pairs)  22.9 us
    ppermute x6, waiting for transfers between devices, along_img(): return lax.ppermute(array, IMG, pairs)  19.1 us
    pallas_call x1, Pallas kernels, home_project(): pl.pallas_call(project_kernel, grid_spec=pltpu.PrefetchScalarGridSpec(num...  15.2 us
    ppermute x10, starting transfers between devices, along_z(): return lax.ppermute(array, 'z', [(i, (i + by) % LINE) for i in range(LINE)])  14.9 us
    pallas_call x1, Pallas kernels, home_grad(): pl.pallas_call(grad_kernel, grid_spec=pltpu.PrefetchScalarGridSpec(num_sc...  14.9 us
  transfers between devices with their start and end apart: 34, of which 8 were waited for; matrix products, arithmetic and copies ran while one was open for 5% of the time, Pallas kernels for 31%

profile of v10, /device:TPU:31, one launch (start us, length us, event | category | flops | bytes accessed | tf_op | source)
XLA Modules:
  0.0 290.4 jit_solution(13569766246205111559)
XLA Ops:
  10.0 3.3 %collective-permute-start.1 = (bf16[50,768]{1,0:T(8,128)(2,1)S(1)}, bf16[50,768]{1,0:T(8,128)(2,1)S(1)}, u32[]{:S(2)}, u32[]{:S(2)}) collective-permute-start(bf16[50,768]{1,0:T(8,128)(2,1)S(1)} %get-tuple-element.111), channel_id=1, source_target_pairs={{0,64},{32,96},{64,0},{96,32},{1,65},{33,97},{65,1},{97,33},{2,66}... | collective-permute-start | bytes 230408 | tf_op jit(solution)/shard_map/ppermute | solution.py:26
  14.1 6.0 %norm.1.refs_0_ = bf16[2,128,3200]{2,1,0:T(8,128)(2,1)} custom-call(bf16[2,128,3200]{2,1,0:T(8,128)(2,1)} %tokens_ref.5), custom_call_target="tpu_custom_call" | custom-call | flops 1 | bytes 1 | tf_op jit(solution)/shard_map/norm/pallas_call | solution.py:84
  27.9 4.4 %constant_dynamic-slice_fusion = (bf16[1,256,2048]{2,1,0:T(8,128)(2,1)}, bf16[1,256,2048]{2,1,0:T(8,128)(2,1)}, bf16[1,256,2048]{2,1,0:T(8,128)(2,1)}, bf16[1,256,2048]{2,1,0:T(8,128)(2,1)}) fusion(bf16[6,256,2048]{2,1,0:T(8,128)(2,1)} %param.21, s32[]{:T(128)S(6)} %min.22, s32[]{:T(128)S(6)} %min.21, s32[]{:T(128)S(6)} %min.20, s32[]{:T(128)S(6)} %min.19), kind=kLoop, calls=%fused_computation.30 | loop fusion | bytes 8388624 | tf_op jit(solution)/shard_map/dynamic_slice | solution.py:486
  32.3 26.5 %collective-permute-done.4.refs_4_ = bf16[2,128,3200]{2,1,0:T(8,128)(2,1)S(1)} collective-permute-done((bf16[2,128,3200]{2,1,0:T(8,128)(2,1)S(1)}, bf16[2,128,3200]{2,1,0:T(8,128)(2,1)S(1)}, u32[]{:S(2)}, u32[]{:S(2)}) %collective-permute-start.4) | collective-permute-done | bytes 1638432 | tf_op jit(solution)/shard_map/ppermute | solution.py:26
  66.2 11.4 %collective-permute-done.8.refs_0_ = bf16[1,128,3200]{2,1,0:T(8,128)(2,1)} collective-permute-done((bf16[1,128,3200]{2,1,0:T(8,128)(2,1)S(1)}, bf16[1,128,3200]{2,1,0:T(8,128)(2,1)}, u32[]{:S(2)}, u32[]{:S(2)}) %collective-permute-start.8) | collective-permute-done | bytes 819232 | tf_op jit(solution)/shard_map/ppermute | solution.py:26
  77.6 3.3 %collective-permute-start.10 = (bf16[1,128,3200]{2,1,0:T(8,128)(2,1)}, bf16[1,128,3200]{2,1,0:T(8,128)(2,1)}, u32[]{:S(2)}, u32[]{:S(2)}) collective-permute-start(bf16[1,128,3200]{2,1,0:T(8,128)(2,1)} %collective-permute-done.8.refs_0_), channel_id=1, source_target_pairs={{0,1},{1,0},{2,3},{3,2},{4,5},{5,4},{6,7},{7,6},{8,9},{9,8},{10,11... | collective-permute-start | bytes 2457608 | tf_op jit(solution)/shard_map/ppermute | solution.py:22
  85.6 3.2 %collective-permute-start.7 = (bf16[1,256,2048]{2,1,0:T(8,128)(2,1)}, bf16[1,256,2048]{2,1,0:T(8,128)(2,1)S(1)}, u32[]{:S(2)}, u32[]{:S(2)}) collective-permute-start(bf16[1,256,2048]{2,1,0:T(8,128)(2,1)} %get-tuple-element.57), channel_id=1, source_target_pairs={{0,2},{2,4},{4,6},{6,8},{8,10},{10,12},{12,14},{14,16},{16,18},{18... | collective-permute-start | bytes 3145736 | tf_op jit(solution)/shard_map/ppermute | solution.py:32
  88.8 19.0 %attend.3 = (bf16[2,256,256]{2,1,0:T(8,128)(2,1)}, bf16[2,256,256]{2,1,0:T(8,128)(2,1)}, bf16[2,256,256]{2,1,0:T(8,128)(2,1)}) custom-call(bf16[1,128,3200]{2,1,0:T(8,128)(2,1)} %collective-permute-done.8.refs_0_, bf16[1,128,3200]{2,1,0:T(8,128)(2,1)} %collective-permute-done.9.refs_1_, bf16[1,128,3200]{2,1,0:T(8,128)(2,1)} %collective-permute-done.10.refs_2_, ...), custom_call_target="tpu_custom_call" | custom-call | flops 1 | bytes 1 | tf_op jit(solution)/shard_map/attend/pallas_call | solution.py:164
  107.9 3.3 %collective-permute-start.15 = (bf16[2,256,256]{2,1,0:T(8,128)(2,1)}, bf16[2,256,256]{2,1,0:T(8,128)(2,1)S(1)}, u32[]{:S(2)}, u32[]{:S(2)}) collective-permute-start(bf16[2,256,256]{2,1,0:T(8,128)(2,1)} %get-tuple-element.62), channel_id=1, source_target_pairs={{0,64},{32,96},{64,0},{96,32},{1,65},{33,97},{65,1},{97,33},{2,66}... | collective-permute-start | bytes 786440 | tf_op jit(solution)/shard_map/ppermute | solution.py:26
  112.0 8.5 %attend.2.refs_0_ = bf16[2,256,256]{2,1,0:T(8,128)(2,1)} custom-call(bf16[2,128,3200]{2,1,0:T(8,128)(2,1)} %norm.1.refs_0_, bf16[2,128,3200]{2,1,0:T(8,128)(2,1)} %collective-permute-done.3.refs_1_, bf16[3200,768]{1,0:T(8,128)(2,1)} %all-gather.2.cloned.1.call-done.refs_2_.refs_8_), custom_call_target="tpu_custom_call" | custom-call | flops 1 | bytes 1 | tf_op jit(solution)/shard_map/attend/pallas_call | solution.py:164
  120.6 3.2 %collective-permute-done.16.refs_3_ = bf16[2,256,256]{2,1,0:T(8,128)(2,1)S(1)} collective-permute-done((bf16[2,256,256]{2,1,0:T(8,128)(2,1)}, bf16[2,256,256]{2,1,0:T(8,128)(2,1)S(1)}, u32[]{:S(2)}, u32[]{:S(2)}) %collective-permute-start.16) | collective-permute-done | bytes 262176 | tf_op jit(solution)/shard_map/ppermute | solution.py:26
  124.5 8.6 %out.1 = (bf16[2,128,3200]{2,1,0:T(8,128)(2,1)}, bf16[2,128,3200]{2,1,0:T(8,128)(2,1)}) custom-call(s32[1]{0:T(128)} %bitcast.4.line_ref, bf16[2,256,256]{2,1,0:T(8,128)(2,1)} %attend.2.refs_0_, bf16[2,256,256]{2,1,0:T(8,128)(2,1)} %copy-done.15, bf16[2,256,256]{2,1,0:T(8,128)(2,1)} %copy-done.16, bf16[2,256,256]{2,1,0:T(8,128)(2,1)} %copy-done.17, ...), custom_call_target="tpu_custom_call" | custom-call | flops 1 | bytes 1 | tf_op jit(solution)/shard_map/out/pallas_call | solution.py:209
  133.7 7.7 %collective-permute-start.23 = (bf16[1,256,2048]{2,1,0:T(8,128)(2,1)S(1)}, bf16[1,256,2048]{2,1,0:T(8,128)(2,1)}, u32[]{:S(2)}, u32[]{:S(2)}) collective-permute-start(bf16[1,256,2048]{2,1,0:T(8,128)(2,1)S(1)} %copy-done.9), channel_id=1, source_target_pairs={{0,2},{2,4},{4,6},{6,8},{8,10},{10,12},{12,14},{14,16},{16,18},{18... | collective-permute-start | bytes 3145736 | tf_op jit(solution)/shard_map/ppermute | solution.py:32
  149.5 3.8 %join.2 = (bf16[1,128,3200]{2,1,0:T(8,128)(2,1)}, f32[1,128,128]{2,1,0:T(8,128)}) custom-call(f32[4]{0:T(128)} %exponential_divide_fusion.mixing_ref, bf16[2,128,3200]{2,1,0:T(8,128)(2,1)} %tokens_ref.5, bf16[2,128,3200]{2,1,0:T(8,128)(2,1)} %early_ref.3, bf16[2,128,3200]{2,1,0:T(8,128)(2,1)} %mid_ref.3, bf16[2,128,3200]{2,1,0:T(8,128)(2,1)} %get-tuple-element.64.own_ref, ...), custom_call_target="tpu_custom_call" | custom-call | flops 1 | bytes 1 | tf_op jit(solution)/shard_map/join/pallas_call | solution.py:248
  154.0 3.8 %join.3 = (bf16[1,128,3200]{2,1,0:T(8,128)(2,1)}, f32[1,128,128]{2,1,0:T(8,128)}) custom-call(f32[4]{0:T(128)} %exponential_divide_fusion.mixing_ref, bf16[2,128,3200]{2,1,0:T(8,128)(2,1)} %tokens_ref.5, bf16[2,128,3200]{2,1,0:T(8,128)(2,1)} %early_ref.3, bf16[2,128,3200]{2,1,0:T(8,128)(2,1)} %mid_ref.3, bf16[2,128,3200]{2,1,0:T(8,128)(2,1)} %get-tuple-element.64.own_ref, ...), custom_call_target="tpu_custom_call" | custom-call | flops 1 | bytes 1 | tf_op jit(solution)/shard_map/join/pallas_call | solution.py:248
  164.4 5.2 %collective-permute-start.21 = (bf16[1,128,3200]{2,1,0:T(8,128)(2,1)S(1)}, bf16[1,128,3200]{2,1,0:T(8,128)(2,1)}, u32[]{:S(2)}, u32[]{:S(2)}) collective-permute-start(bf16[1,128,3200]{2,1,0:T(8,128)(2,1)S(1)} %copy-done.4), channel_id=1, source_target_pairs={{4,0},{6,2},{8,4},{10,6},{12,8},{14,10},{16,12},{18,14},{20,16},{2... | collective-permute-start | bytes 2457608 | tf_op jit(solution)/shard_map/ppermute | solution.py:32
  169.6 15.2 %project.1 = (bf16[2,2,128,2048]{3,2,1,0:T(8,128)(2,1)}, f32[512,2048]{1,0:T(8,128)}) custom-call(s32[1]{0:T(128)} %bitcast.3.core_ref, bf16[1,128,3200]{2,1,0:T(8,128)(2,1)} %get-tuple-element.66.refs_0_.z_ref, bf16[1,128,3200]{2,1,0:T(8,128)(2,1)} %get-tuple-element.78.refs_1_.later_z_ref, bf16[1,128,3200]{2,1,0:T(8,128)(2,1)} %collective-permute-done.18.refs_2_, ...), custom_call_target="tpu_custom_call" | custom-call | flops 1 | bytes 1 | tf_op jit(solution)/shard_map/project/pallas_call | solution.py:326
  184.8 19.1 %collective-permute-done.23 = bf16[1,256,2048]{2,1,0:T(8,128)(2,1)} collective-permute-done((bf16[1,256,2048]{2,1,0:T(8,128)(2,1)S(1)}, bf16[1,256,2048]{2,1,0:T(8,128)(2,1)}, u32[]{:S(2)}, u32[]{:S(2)}) %collective-permute-start.23) | collective-permute-done | bytes 1048608 | tf_op jit(solution)/shard_map/ppermute | solution.py:32
  209.6 14.9 %grad.1 = (bf16[2,128,3200]{2,1,0:T(8,128)(2,1)}, bf16[2,128,3200]{2,1,0:T(8,128)(2,1)}) custom-call(s32[1]{0:T(128)} %bitcast.3.core_ref, f32[512,2048]{1,0:T(8,128)} %get-tuple-element.72.slope_ref, bf16[2,2,128,2048]{3,2,1,0:T(8,128)(2,1)} %pad_maximum_fusion.back_own_ref.back_other_ref, ...), custom_call_target="tpu_custom_call" | custom-call | flops 1 | bytes 1 | tf_op jit(solution)/shard_map/grad/pallas_call | solution.py:386
  227.1 3.0 %collective-permute-start.26 = (bf16[1,128,3200]{2,1,0:T(8,128)(2,1)S(1)}, bf16[1,128,3200]{2,1,0:T(8,128)(2,1)S(1)}, u32[]{:S(2)}, u32[]{:S(2)}) collective-permute-start(bf16[1,128,3200]{2,1,0:T(8,128)(2,1)S(1)} %copy-done.5), channel_id=1, source_target_pairs={{2,0},{4,2},{6,4},{8,6},{10,8},{12,10},{14,12},{16,14},{18,16},{20... | collective-permute-start | bytes 2457608 | tf_op jit(solution)/shard_map/ppermute | solution.py:32
  230.1 5.9 %collective-permute-start.27 = (bf16[1,128,3200]{2,1,0:T(8,128)(2,1)}, bf16[1,128,3200]{2,1,0:T(8,128)(2,1)}, u32[]{:S(2)}, u32[]{:S(2)}) collective-permute-start(bf16[1,128,3200]{2,1,0:T(8,128)(2,1)} %collective-permute-done.22), channel_id=1, source_target_pairs={{6,0},{0,2},{10,4},{4,6},{14,8},{8,10},{18,12},{12,14},{22,16},{16... | collective-permute-start | bytes 2457608 | tf_op jit(solution)/shard_map/ppermute | solution.py:49
  237.8 14.3 %owner.2 = bf16[2,2,128,2048]{3,2,1,0:T(8,128)(2,1)} custom-call(s32[1]{0:T(128)} %bitcast.3.core_ref, bf16[1,128,3200]{2,1,0:T(8,128)(2,1)} %collective-permute-done.20.refs_0_, bf16[1,128,3200]{2,1,0:T(8,128)(2,1)} %copy-done.13, bf16[1,128,3200]{2,1,0:T(8,128)(2,1)} %collective-permute-done.21.refs_2_, bf16[1,128,3200]{2,1,0:T(8,128)(2,1)} %copy-done.14, ...), custom_call_target="tpu_custom_call" | custom-call | flops 1 | bytes 1 | tf_op jit(solution)/shard_map/owner/pallas_call | solution.py:427
  253.3 5.4 %final.1 = bf16[2,128,3200]{2,1,0:T(8,128)(2,1)} custom-call(bf16[2,128,3200]{2,1,0:T(8,128)(2,1)} %get-tuple-element.82.own_ref, bf16[2,128,3200]{2,1,0:T(8,128)(2,1)} %copy-done.7, bf16[1,128,3200]{2,1,0:T(8,128)(2,1)} %get-tuple-element.66.refs_0_.z_ref, bf16[1,128,3200]{2,1,0:T(8,128)(2,1)} %get-tuple-element.78.refs_1_.later_z_ref, ...), custom_call_target="tpu_custom_call" | custom-call | flops 1 | bytes 1 | tf_op jit(solution)/shard_map/final/pallas_call | solution.py:284
  262.9 14.3 %owner.3 = bf16[2,2,128,2048]{3,2,1,0:T(8,128)(2,1)} custom-call(s32[1]{0:T(128)} %bitcast.3.core_ref, bf16[1,128,3200]{2,1,0:T(8,128)(2,1)} %copy-done.12, bf16[1,128,3200]{2,1,0:T(8,128)(2,1)} %collective-permute-done.31.refs_1_, bf16[1,128,3200]{2,1,0:T(8,128)(2,1)} %collective-permute-done.27.refs_2_, ...), custom_call_target="tpu_custom_call" | custom-call | flops 1 | bytes 1 | tf_op jit(solution)/shard_map/owner/pallas_call | solution.py:427
  (137 shorter events, 54.2 us)
Async XLA Ops:
  7.2 74.2 %all-gather.2.cloned.1.call-start = ((), (), s32[]{:S(2)}) async-start(), calls=%async_computation | async-start | bytes 5222400 | tf_op jit(solution)/shard_map/all_gather | solution.py:473
  8.3 11.8 %collective-permute-start = (bf16[50,768]{1,0:T(8,128)(2,1)S(1)}, bf16[50,768]{1,0:T(8,128)(2,1)S(1)}, u32[]{:S(2)}, u32[]{:S(2)}) collective-permute-start(bf16[50,768]{1,0:T(8,128)(2,1)S(1)} %get-tuple-element.109), channel_id=1, source_target_pairs={{0,32},{32,64},{64,96},{96,0},{1,33},{33,65},{65,97},{97,1},{2,34}... | collective-permute-start | bytes 230408 | tf_op jit(solution)/shard_map/ppermute | solution.py:26
  21.6 37.1 %collective-permute-start.4 = (bf16[2,128,3200]{2,1,0:T(8,128)(2,1)S(1)}, bf16[2,128,3200]{2,1,0:T(8,128)(2,1)S(1)}, u32[]{:S(2)}, u32[]{:S(2)}) collective-permute-start(bf16[2,128,3200]{2,1,0:T(8,128)(2,1)S(1)} %copy-done.1), channel_id=1, source_target_pairs={{0,32},{32,64},{64,96},{96,0},{1,33},{33,65},{65,97},{97,1},{2,34}... | collective-permute-start | bytes 4915208 | tf_op jit(solution)/shard_map/ppermute | solution.py:26
  22.4 36.4 %collective-permute-start.5 = (bf16[2,128,3200]{2,1,0:T(8,128)(2,1)S(1)}, bf16[2,128,3200]{2,1,0:T(8,128)(2,1)}, u32[]{:S(2)}, u32[]{:S(2)}) collective-permute-start(bf16[2,128,3200]{2,1,0:T(8,128)(2,1)S(1)} %copy-done.1), channel_id=1, source_target_pairs={{0,96},{32,0},{64,32},{96,64},{1,97},{33,1},{65,33},{97,65},{2,98}... | collective-permute-start | bytes 4915208 | tf_op jit(solution)/shard_map/ppermute | solution.py:26
  58.8 18.8 %collective-permute-start.8 = (bf16[1,128,3200]{2,1,0:T(8,128)(2,1)S(1)}, bf16[1,128,3200]{2,1,0:T(8,128)(2,1)}, u32[]{:S(2)}, u32[]{:S(2)}) collective-permute-start(bf16[1,128,3200]{2,1,0:T(8,128)(2,1)S(1)} %slice.28), channel_id=1, source_target_pairs={{0,32},{32,64},{64,96},{96,0},{1,33},{33,65},{65,97},{97,1},{2,34}... | collective-permute-start | bytes 2457608 | tf_op jit(solution)/shard_map/ppermute | solution.py:26
  60.5 20.3 %collective-permute-start.9 = (bf16[1,128,3200]{2,1,0:T(8,128)(2,1)S(1)}, bf16[1,128,3200]{2,1,0:T(8,128)(2,1)}, u32[]{:S(2)}, u32[]{:S(2)}) collective-permute-start(bf16[1,128,3200]{2,1,0:T(8,128)(2,1)S(1)} %slice.29), channel_id=1, source_target_pairs={{0,96},{32,0},{64,32},{96,64},{1,97},{33,1},{65,33},{97,65},{2,98}... | collective-permute-start | bytes 2457608 | tf_op jit(solution)/shard_map/ppermute | solution.py:26
  62.8 26.0 %collective-permute-start.12 = (bf16[2,128,3200]{2,1,0:T(8,128)(2,1)S(1)}, bf16[2,128,3200]{2,1,0:T(8,128)(2,1)}, u32[]{:S(2)}, u32[]{:S(2)}) collective-permute-start(bf16[2,128,3200]{2,1,0:T(8,128)(2,1)S(1)} %collective-permute-done.4.refs_4_), channel_id=1, source_target_pairs={{0,1},{1,0},{2,3},{3,2},{4,5},{5,4},{6,7},{7,6},{8,9},{9,8},{10,11... | collective-permute-start | bytes 4915208 | tf_op jit(solution)/shard_map/ppermute | solution.py:22
  65.7 23.1 %collective-permute-start.13 = (bf16[2,128,3200]{2,1,0:T(8,128)(2,1)}, bf16[2,128,3200]{2,1,0:T(8,128)(2,1)}, u32[]{:S(2)}, u32[]{:S(2)}) collective-permute-start(bf16[2,128,3200]{2,1,0:T(8,128)(2,1)} %collective-permute-done.5.refs_6_), channel_id=1, source_target_pairs={{0,1},{1,0},{2,3},{3,2},{4,5},{5,4},{6,7},{7,6},{8,9},{9,8},{10,11... | collective-permute-start | bytes 4915208 | tf_op jit(solution)/shard_map/ppermute | solution.py:22
  65.7 45.5 %collective-permute-start.3 = (bf16[2,128,3200]{2,1,0:T(8,128)(2,1)S(1)}, bf16[2,128,3200]{2,1,0:T(8,128)(2,1)}, u32[]{:S(2)}, u32[]{:S(2)}) collective-permute-start(bf16[2,128,3200]{2,1,0:T(8,128)(2,1)S(1)} %copy-done.1), channel_id=1, source_target_pairs={{0,1},{1,0},{2,3},{3,2},{4,5},{5,4},{6,7},{7,6},{8,9},{9,8},{10,11... | collective-permute-start | bytes 4915208 | tf_op jit(solution)/shard_map/ppermute | solution.py:22
  83.1 37.4 %collective-permute-start.6 = (bf16[1,256,2048]{2,1,0:T(8,128)(2,1)}, bf16[1,256,2048]{2,1,0:T(8,128)(2,1)}, u32[]{:S(2)}, u32[]{:S(2)}) collective-permute-start(bf16[1,256,2048]{2,1,0:T(8,128)(2,1)} %get-tuple-element.56), channel_id=1, source_target_pairs={{0,6},{2,0},{4,10},{6,4},{8,14},{10,8},{12,18},{14,12},{16,22},{18... | collective-permute-start | bytes 3145736 | tf_op jit(solution)/shard_map/ppermute | solution.py:48
  85.6 35.0 %collective-permute-start.7 = (bf16[1,256,2048]{2,1,0:T(8,128)(2,1)}, bf16[1,256,2048]{2,1,0:T(8,128)(2,1)S(1)}, u32[]{:S(2)}, u32[]{:S(2)}) collective-permute-start(bf16[1,256,2048]{2,1,0:T(8,128)(2,1)} %get-tuple-element.57), channel_id=1, source_target_pairs={{0,2},{2,4},{4,6},{6,8},{8,10},{10,12},{12,14},{14,16},{16,18},{18... | collective-permute-start | bytes 3145736 | tf_op jit(solution)/shard_map/ppermute | solution.py:32
  107.8 12.8 %collective-permute-start.14 = (bf16[2,256,256]{2,1,0:T(8,128)(2,1)}, bf16[2,256,256]{2,1,0:T(8,128)(2,1)S(1)}, u32[]{:S(2)}, u32[]{:S(2)}) collective-permute-start(bf16[2,256,256]{2,1,0:T(8,128)(2,1)} %get-tuple-element.61), channel_id=1, source_target_pairs={{0,96},{32,0},{64,32},{96,64},{1,97},{33,1},{65,33},{97,65},{2,98}... | collective-permute-start | bytes 786440 | tf_op jit(solution)/shard_map/ppermute | solution.py:26
  107.9 12.7 %collective-permute-start.15 = (bf16[2,256,256]{2,1,0:T(8,128)(2,1)}, bf16[2,256,256]{2,1,0:T(8,128)(2,1)S(1)}, u32[]{:S(2)}, u32[]{:S(2)}) collective-permute-start(bf16[2,256,256]{2,1,0:T(8,128)(2,1)} %get-tuple-element.62), channel_id=1, source_target_pairs={{0,64},{32,96},{64,0},{96,32},{1,65},{33,97},{65,1},{97,33},{2,66}... | collective-permute-start | bytes 786440 | tf_op jit(solution)/shard_map/ppermute | solution.py:26
  111.2 12.6 %collective-permute-start.16 = (bf16[2,256,256]{2,1,0:T(8,128)(2,1)}, bf16[2,256,256]{2,1,0:T(8,128)(2,1)S(1)}, u32[]{:S(2)}, u32[]{:S(2)}) collective-permute-start(bf16[2,256,256]{2,1,0:T(8,128)(2,1)} %get-tuple-element.63), channel_id=1, source_target_pairs={{0,32},{32,64},{64,96},{96,0},{1,33},{33,65},{65,97},{97,1},{2,34}... | collective-permute-start | bytes 786440 | tf_op jit(solution)/shard_map/ppermute | solution.py:26
  133.2 15.2 %collective-permute-start.17 = (bf16[2,128,3200]{2,1,0:T(8,128)(2,1)}, bf16[2,128,3200]{2,1,0:T(8,128)(2,1)S(1)}, u32[]{:S(2)}, u32[]{:S(2)}) collective-permute-start(bf16[2,128,3200]{2,1,0:T(8,128)(2,1)} %get-tuple-element.65), channel_id=1, source_target_pairs={{0,1},{1,0},{2,3},{3,2},{4,5},{5,4},{6,7},{7,6},{8,9},{9,8},{10,11... | collective-permute-start | bytes 4915208 | tf_op jit(solution)/shard_map/ppermute | solution.py:22
  133.7 70.3 %collective-permute-start.23 = (bf16[1,256,2048]{2,1,0:T(8,128)(2,1)S(1)}, bf16[1,256,2048]{2,1,0:T(8,128)(2,1)}, u32[]{:S(2)}, u32[]{:S(2)}) collective-permute-start(bf16[1,256,2048]{2,1,0:T(8,128)(2,1)S(1)} %copy-done.9), channel_id=1, source_target_pairs={{0,2},{2,4},{4,6},{6,8},{8,10},{10,12},{12,14},{14,16},{16,18},{18... | collective-permute-start | bytes 3145736 | tf_op jit(solution)/shard_map/ppermute | solution.py:32
  141.4 64.5 %collective-permute-start.25 = (bf16[1,256,2048]{2,1,0:T(8,128)(2,1)S(1)}, bf16[1,256,2048]{2,1,0:T(8,128)(2,1)}, u32[]{:S(2)}, u32[]{:S(2)}) collective-permute-start(bf16[1,256,2048]{2,1,0:T(8,128)(2,1)S(1)} %copy-done.8), channel_id=1, source_target_pairs={{0,4},{2,6},{4,8},{6,10},{8,12},{10,14},{12,16},{14,18},{16,20},{1... | collective-permute-start | bytes 3145736 | tf_op jit(solution)/shard_map/ppermute | solution.py:32
  143.3 62.5 %collective-permute-start.24 = (bf16[1,256,2048]{2,1,0:T(8,128)(2,1)}, bf16[1,256,2048]{2,1,0:T(8,128)(2,1)}, u32[]{:S(2)}, u32[]{:S(2)}) collective-permute-start(bf16[1,256,2048]{2,1,0:T(8,128)(2,1)} %collective-permute-done.6), channel_id=1, source_target_pairs={{6,4},{0,6},{10,8},{4,10},{14,12},{8,14},{18,16},{12,18},{22,20},{... | collective-permute-start | bytes 3145736 | tf_op jit(solution)/shard_map/ppermute | solution.py:49
  162.5 62.0 %collective-permute-start.20 = (bf16[1,128,3200]{2,1,0:T(8,128)(2,1)S(1)}, bf16[1,128,3200]{2,1,0:T(8,128)(2,1)}, u32[]{:S(2)}, u32[]{:S(2)}) collective-permute-start(bf16[1,128,3200]{2,1,0:T(8,128)(2,1)S(1)} %copy-done.4), channel_id=1, source_target_pairs={{2,0},{4,2},{6,4},{8,6},{10,8},{12,10},{14,12},{16,14},{18,16},{20... | collective-permute-start | bytes 2457608 | tf_op jit(solution)/shard_map/ppermute | solution.py:32
  164.4 60.1 %collective-permute-start.21 = (bf16[1,128,3200]{2,1,0:T(8,128)(2,1)S(1)}, bf16[1,128,3200]{2,1,0:T(8,128)(2,1)}, u32[]{:S(2)}, u32[]{:S(2)}) collective-permute-start(bf16[1,128,3200]{2,1,0:T(8,128)(2,1)S(1)} %copy-done.4), channel_id=1, source_target_pairs={{4,0},{6,2},{8,4},{10,6},{12,8},{14,10},{16,12},{18,14},{20,16},{2... | collective-permute-start | bytes 2457608 | tf_op jit(solution)/shard_map/ppermute | solution.py:32
  204.0 20.9 %collective-permute-start.22 = (bf16[1,128,3200]{2,1,0:T(8,128)(2,1)S(1)}, bf16[1,128,3200]{2,1,0:T(8,128)(2,1)}, u32[]{:S(2)}, u32[]{:S(2)}) collective-permute-start(bf16[1,128,3200]{2,1,0:T(8,128)(2,1)S(1)} %copy-done.5), channel_id=1, source_target_pairs={{4,6},{6,0},{8,10},{10,4},{12,14},{14,8},{16,18},{18,12},{20,22},{... | collective-permute-start | bytes 2457608 | tf_op jit(solution)/shard_map/ppermute | solution.py:48
  224.9 27.3 %collective-permute-start.30 = (bf16[2,128,3200]{2,1,0:T(8,128)(2,1)}, bf16[2,128,3200]{2,1,0:T(8,128)(2,1)S(1)}, u32[]{:S(2)}, u32[]{:S(2)}) collective-permute-start(bf16[2,128,3200]{2,1,0:T(8,128)(2,1)} %get-tuple-element.83), channel_id=1, source_target_pairs={{0,1},{1,0},{2,3},{3,2},{4,5},{5,4},{6,7},{7,6},{8,9},{9,8},{10,11... | collective-permute-start | bytes 4915208 | tf_op jit(solution)/shard_map/ppermute | solution.py:22
  227.1 31.6 %collective-permute-start.26 = (bf16[1,128,3200]{2,1,0:T(8,128)(2,1)S(1)}, bf16[1,128,3200]{2,1,0:T(8,128)(2,1)S(1)}, u32[]{:S(2)}, u32[]{:S(2)}) collective-permute-start(bf16[1,128,3200]{2,1,0:T(8,128)(2,1)S(1)} %copy-done.5), channel_id=1, source_target_pairs={{2,0},{4,2},{6,4},{8,6},{10,8},{12,10},{14,12},{16,14},{18,16},{20... | collective-permute-start | bytes 2457608 | tf_op jit(solution)/shard_map/ppermute | solution.py:32
  230.1 28.6 %collective-permute-start.27 = (bf16[1,128,3200]{2,1,0:T(8,128)(2,1)}, bf16[1,128,3200]{2,1,0:T(8,128)(2,1)}, u32[]{:S(2)}, u32[]{:S(2)}) collective-permute-start(bf16[1,128,3200]{2,1,0:T(8,128)(2,1)} %collective-permute-done.22), channel_id=1, source_target_pairs={{6,0},{0,2},{10,4},{4,6},{14,8},{8,10},{18,12},{12,14},{22,16},{16... | collective-permute-start | bytes 2457608 | tf_op jit(solution)/shard_map/ppermute | solution.py:49
  (32 other events, 292.9 us)
Sparse Core Ops, SparseCore 0:
  21.2 52.7 all-gather.1
